TPU v7x, 256 devices: a whole 4x4x8 slice. The times are simulated.
256 devices in a mesh: ctx: 32 (over y, x, z_lo), kv: 8 (over z_hi, core).
Axes of the slice: x: 4, y: 4, z: 8 (z_hi: 4, z_lo: 2; z = z_hi * 2 + z_lo), core: 2. Of those that a mesh axis runs over, the one named last changes fastest.
Arguments:
- hidden: bfloat16 [4096, 4096], P('ctx', 'kv'), may hold values from -18 to 18, as said below
- block_ids: int32 [4096], P('ctx'), may hold values from 0 to 255, never falling along the last dimension, each value on 1 to 32 neighbouring positions
- decode_order: int32 [4096], P('ctx'), may hold values from 0 to 31
- step_cut: int32 [256], replicated, may hold values from 0 to 32
- mask_embed: bfloat16 [4096], replicated, may hold values from -6 to 6
- q_weight: bfloat16 [4096, 4096], P(None, 'kv'), may hold values from -0.09375 to 0.09375
- k_weight: bfloat16 [4096, 1024], P(None, 'kv'), may hold values from -0.09375 to 0.09375
- v_weight: bfloat16 [4096, 1024], P(None, 'kv'), may hold values from -0.09375 to 0.09375
Outputs:
- clean_out: bfloat16 [4096, 4096], P('ctx', 'kv')
- noisy_out: bfloat16 [4096, 4096], P('ctx', 'kv')
Inputs may be any that keep to these rules, and one draw needn't show every extreme that they name: `hidden`: activations; row scales differ. `block_ids`: never falling along the slab; each block has 1 to 32 tokens, one exactly 32.
All inputs are finite; a program needn't handle non-finite values.
Results may differ from a plain program's by a relative error of at most 0.013.
The roundings to bfloat16 on the way count: a program that leaves them out, or rounds other values in their place, can miss the bound.
Values may be sent and summed in bfloat16 or wider, within the bound.
No kernel may reach another device: no remote copies, remote signals or barrier semaphores. Data moves between devices by JAX's collectives and lax.ppermute only.
A program may use at most 128 MiB of HBM per device.

v0:
```python
import math

import jax
import jax.numpy as jnp
from jax import lax
from jax.sharding import PartitionSpec as P

HEAD_DIM = 128
BLOCK = 32


far_low = -1e30


def extended(block, sides, width):
    for axis, dim in sides:
        count = lax.axis_size(axis)
        forward = [(i, i + 1) for i in range(count - 1)]
        backward = [(target, source) for source, target in forward]
        low = lax.ppermute(
            lax.slice_in_dim(block, block.shape[dim] - width, None, axis=dim), axis, forward
        )
        high = lax.ppermute(lax.slice_in_dim(block, 0, width, axis=dim), axis, backward)
        block = jnp.concatenate([low, block, high], axis=dim)
    return block


def attend(state, queries, keys, values, allowed):
    top, total, accum = state
    scale = 1.0 / math.sqrt(queries.shape[-1])
    count = keys.shape[0]
    for begin in range(0, count, 1024):
        width = min(1024, count - begin)
        key_part = keys[begin : begin + width]
        value_part = values[begin : begin + width]
        permit = allowed[None, None, :, begin : begin + width]
        scores = (
            jnp.einsum("rgqd,sgd->gqrs", queries, key_part, preferred_element_type=jnp.float32)
            * scale
        )
        scores = jnp.where(permit, scores, far_low)
        new_top = jnp.maximum(top, jnp.max(scores, axis=-1))
        probs = jnp.where(permit, jnp.exp(scores - new_top[..., None]), 0.0)
        factor = jnp.exp(top - new_top)
        total = total * factor + jnp.sum(probs, axis=-1)
        accum = accum * factor[..., None] + jnp.einsum(
            "gqrs,sgd->gqrd",
            probs.astype(jnp.bfloat16),
            value_part,
            preferred_element_type=jnp.float32,
        )
        top = new_top
    return (top, total, accum)


def merge_state(first, second):
    top = jnp.maximum(first[0], second[0])
    factor_one = jnp.exp(first[0] - top)
    factor_two = jnp.exp(second[0] - top)
    total = first[1] * factor_one + second[1] * factor_two
    accum = first[2] * factor_one[..., None] + second[2] * factor_two[..., None]
    return (top, total, accum)


def empty_state(groups, group, count, head_dim):
    return (
        jnp.full((groups, group, count), far_low, jnp.float32),
        jnp.zeros((groups, group, count), jnp.float32),
        jnp.zeros((groups, group, count, head_dim), jnp.float32),
    )


def shards(hidden, block_ids, decode_order, step_cut, mask_embed, q_weight, k_weight, v_weight):
    rows = hidden.shape[0]
    half = rows // 2
    head_dim = HEAD_DIM
    groups = k_weight.shape[1] // head_dim
    match = block_ids[:, None] == jnp.arange(step_cut.shape[0], dtype=jnp.int32)[None, :]
    cut = jnp.sum(jnp.where(match, step_cut[None, :], 0), axis=1)
    masked = decode_order >= cut
    piece = lax.all_gather(hidden, "kv", axis=1, tiled=True)
    noisy_piece = jnp.where(masked[:, None], mask_embed[None, :], piece)
    results = []
    for index, weight in enumerate((q_weight, k_weight, v_weight)):
        weight_rows = weight
        results.append(jnp.dot(piece, weight_rows, preferred_element_type=jnp.float32))
    for index, weight in enumerate((q_weight, k_weight, v_weight)):
        weight_rows = weight
        results.append(jnp.dot(noisy_piece, weight_rows, preferred_element_type=jnp.float32))
    projected = tuple(results)
    q_clean, k_clean, v_clean, q_noisy, k_noisy, v_noisy = [
        p.astype(jnp.bfloat16) for p in projected
    ]
    group = q_clean.shape[1] // (groups * head_dim)
    clean_queries = q_clean.reshape(rows, groups, group, head_dim)
    noisy_queries = q_noisy.reshape(rows, groups, group, head_dim)
    late_clean = clean_queries[half:]
    late_noisy = noisy_queries[half:]
    late_ids = block_ids[half:]
    halves = (
        (jnp.concatenate([clean_queries[:half], noisy_queries[:half]], 0), block_ids[:half]),
        (jnp.concatenate([late_clean, late_noisy], 0), late_ids),
    )
    noisy_row = jnp.arange(2 * half) >= half
    fresh = (
        empty_state(groups, group, 2 * half, head_dim),
        empty_state(groups, group, 2 * half, head_dim),
    )
    stacked = jnp.stack([k_noisy, v_noisy], 1)
    rim_pairs, rim_ids = (
        extended(stacked, (("ctx", 0),), BLOCK),
        extended(block_ids + 1, (("ctx", 0),), BLOCK),
    )
    count = rim_pairs.shape[0]
    near = rim_ids[None, :] == (block_ids + 1)[:, None]
    rim_state = attend(
        empty_state(groups, group, rows, head_dim),
        noisy_queries,
        rim_pairs[:, 0].reshape(count, groups, head_dim),
        rim_pairs[:, 1].reshape(count, groups, head_dim),
        near,
    )
    keys = lax.all_gather(k_clean, "ctx", axis=0, tiled=True)
    values = lax.all_gather(v_clean, "ctx", axis=0, tiled=True)
    piece_ids = lax.all_gather(block_ids, "ctx", axis=0, tiled=True)
    count_here = keys.shape[0]
    key_part = keys.reshape(count_here, groups, head_dim)
    value_part = values.reshape(count_here, groups, head_dim)
    outcome = []
    for index in range(2):
        half_queries, half_ids = halves[index]
        query_blocks = jnp.concatenate([half_ids, half_ids], 0)
        before = piece_ids[None, :] < query_blocks[:, None]
        same = piece_ids[None, :] == query_blocks[:, None]
        permit = before | same & ~noisy_row[:, None]

        def work(current, half_queries=half_queries, permit=permit):
            return attend(current, half_queries, key_part, value_part, permit)

        outcome.append(work(fresh[index]))
    states = tuple(outcome)
    early_state, late_state = states
    whole = []
    for member in range(3):
        first = early_state[member]
        second = late_state[member]
        whole.append(
            jnp.concatenate(
                [first[:, :, :half], second[:, :, :half], first[:, :, half:], second[:, :, half:]],
                2,
            )
        )
    top, total, accum = whole
    noisy_part = merge_state((top[:, :, rows:], total[:, :, rows:], accum[:, :, rows:]), rim_state)
    top = jnp.concatenate([top[:, :, :rows], noisy_part[0]], 2)
    total = jnp.concatenate([total[:, :, :rows], noisy_part[1]], 2)
    accum = jnp.concatenate([accum[:, :, :rows], noisy_part[2]], 2)
    result = accum / total[..., None]
    result = (
        jnp.transpose(result, (2, 0, 1, 3))
        .reshape(2 * rows, groups * group * head_dim)
        .astype(jnp.bfloat16)
    )
    return (result[:rows], result[rows:])


def solution(mesh):
    return jax.shard_map(
        shards,
        mesh=mesh,
        in_specs=(
            P("ctx", "kv"),
            P("ctx"),
            P("ctx"),
            P(),
            P(),
            P(None, "kv"),
            P(None, "kv"),
            P(None, "kv"),
        ),
        out_specs=(P("ctx", "kv"), P("ctx", "kv")),
        check_vma=False,
    )
```

profile of v0, /device:TPU:24, one launch (start us, length us, event | category | flops | bytes accessed | tf_op | source)
XLA Modules:
  0.0 426.6 jit_solution(5532846870692307007)
XLA Ops:
  8.7 3.8 collective-permute-start
  12.5 5.0 %collective-permute-start.1 = (s32[32]{0:T(128)S(1)}, s32[32]{0:T(128)S(1)}, u32[]{:S(2)}, u32[]{:S(2)}) collective-permute-start(s32[32]{0:T(128)S(1)} %get-tuple-element.63), channel_id=1, source_target_pairs={{8,0},{16,8},{24,16},{32,24},{40,32},{48,40},{56,48},{64,56},{72,6... | collective-permute-start | bytes 392 | tf_op jit(solution)/shard_map/ppermute | solution.py:23
  17.6 0.8 fusion.174
  18.4 0.8 select_reduce_fusion
  19.2 67.0 %all-gather = s32[32,1,128]{2,1,0:T(1,128)S(1)} all-gather(s32[1,1,128]{2,1,0:T(1,128)} %bitcast.419), channel_id=1, replica_groups=mesh['ctx'=32,'kv'=8] {'ctx'}, dimensions={0}, use_global_device_ids=true | all-gather | bytes 16896 | tf_op jit(solution)/shard_map/all_gather | solution.py:125
  86.3 1.4 and_or_fusion.1
  90.0 2.4 convolution_convert_fusion.5
  94.2 2.2 collective-permute-start.2
  96.5 6.8 %collective-permute-start.3 = (bf16[32,2,128]{2,0,1:T(8,128)(2,1)}, bf16[32,2,128]{2,0,1:T(8,128)(2,1)}, u32[]{:S(2)}, u32[]{:S(2)}) collective-permute-start(bf16[32,2,128]{2,0,1:T(8,128)(2,1)} %get-tuple-element.35), channel_id=1, source_target_pairs={{8,0},{16,8},{24,16},{32,24},{40,32},{48,40},{56,48},{64,56},{72,6... | collective-permute-start | bytes 49160 | tf_op jit(solution)/shard_map/ppermute | solution.py:23
  104.7 1.0 convolution_convert_fusion.4
  105.8 3.0 convolution_convert_fusion
  111.1 1.0 fusion.175
  112.0 135.7 %all-gather.7.cloned.1.call-done = bf16[4096,128]{1,0:T(8,128)(2,1)} async-done(((bf16[128,128]{1,0:T(8,128)(2,1)}), bf16[4096,128]{1,0:T(8,128)(2,1)}) %all-gather.7.cloned.1.call-update) | async-done | bytes 1048592 | tf_op jit(solution)/shard_map/all_gather | solution.py:123
  247.7 1.5 fusion.4
  249.3 2.0 fusion.7
  252.3 0.8 subtract_exponential_fusion
  253.8 1.1 fusion.20
  254.9 1.1 fusion.18
  255.9 1.1 fusion.22
  257.1 1.1 fusion.16
  258.2 144.9 %all-gather.9.cloned.1.call-done = bf16[4096,128]{1,0:T(8,128)(2,1)} async-done(((bf16[128,128]{1,0:T(8,128)(2,1)}), bf16[4096,128]{1,0:T(8,128)(2,1)}) %all-gather.9.cloned.1.call-update) | async-done | bytes 1048592 | tf_op jit(solution)/shard_map/all_gather | solution.py:124
  403.1 2.6 fusion.31
  406.6 0.8 copy-done.4
  413.9 0.8 fusion.35
  (184 shorter events, 23.2 us)
Async XLA Ops:
  7.2 82.8 %copy-start = (bf16[4096,128]{1,0:T(8,128)(2,1)S(1)}, bf16[4096,128]{1,0:T(8,128)(2,1)}, u32[]{:S(2)}) copy-start(bf16[4096,128]{1,0:T(8,128)(2,1)} %param.14) | copy-start | bytes 3145732
  7.2 82.0 %copy-start.54 = (s32[128]{0:T(128)S(1)}, s32[128]{0:T(128)}, u32[]{:S(2)}) copy-start(s32[128]{0:T(128)} %param.10) | copy-start | bytes 1540
  7.2 82.8 %all-gather.5.cloned.1.call-start = ((), (), s32[]{:S(2)}) async-start(), calls=%async_computation | async-start | bytes 1179648 | tf_op jit(solution)/shard_map/all_gather | solution.py:81
  7.9 239.8 %all-gather.7.cloned.1.call-start = ((), (), s32[]{:S(2)}) async-start(), calls=%async_computation.1 | async-start | bytes 1081344 | tf_op jit(solution)/shard_map/all_gather | solution.py:123
  8.7 80.5 %collective-permute-start = (s32[32]{0:T(128)S(1)}, s32[32]{0:T(128)S(1)}, u32[]{:S(2)}, u32[]{:S(2)}) collective-permute-start(s32[32]{0:T(128)S(1)} %get-tuple-element.62), channel_id=1, source_target_pairs={{0,8},{8,16},{16,24},{24,32},{32,40},{40,48},{48,56},{56,64},{64,7... | collective-permute-start | bytes 392 | tf_op jit(solution)/shard_map/ppermute | solution.py:20
  12.5 76.7 %collective-permute-start.1 = (s32[32]{0:T(128)S(1)}, s32[32]{0:T(128)S(1)}, u32[]{:S(2)}, u32[]{:S(2)}) collective-permute-start(s32[32]{0:T(128)S(1)} %get-tuple-element.63), channel_id=1, source_target_pairs={{8,0},{16,8},{24,16},{32,24},{40,32},{48,40},{56,48},{64,56},{72,6... | collective-permute-start | bytes 392 | tf_op jit(solution)/shard_map/ppermute | solution.py:23
  87.7 4.8 %copy-start.53 = (bf16[4096]{0:T(1024)(128)(2,1)S(1)}, bf16[4096]{0:T(1024)(128)(2,1)}, u32[]{:S(2)}) copy-start(bf16[4096]{0:T(1024)(128)(2,1)} %param.12) | copy-start | bytes 24580
  89.2 3.8 copy-start.55
  92.5 310.7 %all-gather.9.cloned.1.call-start = ((), (), s32[]{:S(2)}) async-start(), calls=%async_computation.2 | async-start | bytes 1081344 | tf_op jit(solution)/shard_map/all_gather | solution.py:124
  92.5 10.7 %copy-start.2 = (bf16[4096,512]{1,0:T(8,128)(2,1)S(1)}, bf16[4096,512]{1,0:T(8,128)(2,1)}, u32[]{:S(2)}) copy-start(bf16[4096,512]{1,0:T(8,128)(2,1)} %param.13) | copy-start | bytes 12582916
  93.1 3.4 copy-start.21
  94.2 16.1 %collective-permute-start.2 = (bf16[32,2,128]{2,0,1:T(8,128)(2,1)}, bf16[32,2,128]{2,0,1:T(8,128)(2,1)S(1)}, u32[]{:S(2)}, u32[]{:S(2)}) collective-permute-start(bf16[32,2,128]{2,0,1:T(8,128)(2,1)} %get-tuple-element.34), channel_id=1, source_target_pairs={{0,8},{8,16},{16,24},{24,32},{32,40},{40,48},{48,56},{56,64},{64,7... | collective-permute-start | bytes 49160 | tf_op jit(solution)/shard_map/ppermute | solution.py:20
  96.5 13.8 %collective-permute-start.3 = (bf16[32,2,128]{2,0,1:T(8,128)(2,1)}, bf16[32,2,128]{2,0,1:T(8,128)(2,1)}, u32[]{:S(2)}, u32[]{:S(2)}) collective-permute-start(bf16[32,2,128]{2,0,1:T(8,128)(2,1)} %get-tuple-element.35), channel_id=1, source_target_pairs={{8,0},{16,8},{24,16},{32,24},{40,32},{48,40},{56,48},{64,56},{72,6... | collective-permute-start | bytes 49160 | tf_op jit(solution)/shard_map/ppermute | solution.py:23
  105.7 3.7 copy-start.19
  105.8 4.5 %copy-start.22 = (bf16[128,1,128]{2,0,1:T(8,128)(2,1)S(1)}, bf16[128,1,128]{2,0,1:T(8,128)(2,1)}, u32[]{:S(2)}) copy-start(bf16[128,1,128]{2,0,1:T(8,128)(2,1)} %copy-done.21) | copy-start | bytes 98308
  105.8 4.5 %copy-start.24 = (bf16[128,1,128]{2,0,1:T(8,128)(2,1)S(1)}, bf16[128,1,128]{2,0,1:T(8,128)(2,1)}, u32[]{:S(2)}) copy-start(bf16[128,1,128]{2,0,1:T(8,128)(2,1)} %copy-done.23) | copy-start | bytes 98308
  105.8 5.3 %copy-start.27 = (pred[128,192]{0,1:T(8,128)(4,1)S(1)}, pred[128,192]{0,1:T(8,128)(4,1)}, u32[]{:S(2)}) copy-start(pred[128,192]{0,1:T(8,128)(4,1)} %broadcast_compare_fusion) | copy-start | bytes 73732
  108.8 138.9 %copy-start.16 = (pred[128,1024]{0,1:T(8,128)(4,1)S(1)}, pred[128,1024]{0,1:T(8,128)(4,1)}, u32[]{:S(2)}) copy-start(pred[128,1024]{0,1:T(8,128)(4,1)} %get-tuple-element.20) | copy-start | bytes 393220
  109.5 139.7 %copy-start.31 = (bf16[64,1,4,128]{3,0,2,1:T(8,128)(2,1)}, bf16[64,1,4,128]{3,0,2,1:T(8,128)(2,1)S(1)}, u32[]{:S(2)}) copy-start(bf16[64,1,4,128]{3,0,2,1:T(8,128)(2,1)S(1)} %copy.63) | copy-start | bytes 196612
  110.2 139.0 %copy-start.33 = (bf16[64,1,4,128]{3,0,2,1:T(8,128)(2,1)}, bf16[64,1,4,128]{3,0,2,1:T(8,128)(2,1)S(1)}, u32[]{:S(2)}) copy-start(bf16[64,1,4,128]{3,0,2,1:T(8,128)(2,1)S(1)} %copy.64) | copy-start | bytes 196612
  111.0 138.2 %copy-start.25 = (bf16[192,2,128]{2,0,1:T(8,128)(2,1)}, bf16[192,2,128]{2,0,1:T(8,128)(2,1)S(1)}, u32[]{:S(2)}) copy-start(bf16[192,2,128]{2,0,1:T(8,128)(2,1)S(1)} %pad_maximum_fusion) | copy-start | bytes 294916
  247.7 3.6 copy-start.12
  249.2 7.8 %copy-start.5 = (f32[1024,128,4]{1,0,2:T(8,128)}, f32[1024,128,4]{1,0,2:T(8,128)S(1)}, u32[]{:S(2)}) copy-start(f32[1024,128,4]{1,0,2:T(8,128)S(1)} %get-tuple-element.81) | copy-start | bytes 6291460
  252.3 3.7 copy-start.6
  (39 other events, 69.4 us)
Sparse Core Ops, SparseCore 0:
  9.9 32.7 all-gather.4
  92.6 155.0 all-gather.6
  249.5 153.5 all-gather.8
where the time goes:
time: 434 us; the launch traced here: 427 us
  waiting for transfers between devices  281 us (65%)
  blocking collectives  67 us (15%)
  matrix products  23.8 us (5%)
  starting transfers between devices  18 us (4%)
  between operations  14.6 us (3%)
  other arithmetic  13.9 us (3%)
  local copies, waits for them, and re-layouts  8.02 us (2%)
    all_gather x1, waiting for transfers between devices, shards(): values = lax.all_gather(v_clean, 'ctx', axis=0, tiled=True)  145 us
    all_gather x1, waiting for transfers between devices, shards(): keys = lax.all_gather(k_clean, 'ctx', axis=0, tiled=True)  136 us
    all_gather x1, blocking collectives, shards(): piece_ids = lax.all_gather(block_ids, 'ctx', axis=0, tiled=True)  67 us
    ppermute x2, starting transfers between devices, extended(): lax.ppermute(lax.slice_in_dim(block, 0, width, axis=dim), axis, backward)  11.8 us
  transfers between devices with their start and end apart: 7, of which 2 were waited for; matrix products, arithmetic and copies ran while one was open for 6% of the time, Pallas kernels for 0%

commit v1 on v0

--- a/solution.py
+++ b/solution.py
@@ -23,6 +23,43 @@
         high = lax.ppermute(lax.slice_in_dim(block, 0, width, axis=dim), axis, backward)
         block = jnp.concatenate([low, block, high], axis=dim)
     return block
+
+
+def ctx_pairs(dy, dx, dz):
+    pairs = []
+    for i in range(32):
+        y, x, z = i // 8, (i // 2) % 4, i % 2
+        target = (((y + dy) % 4) * 4 + (x + dx) % 4) * 2 + (z + dz) % 2
+        pairs.append((i, target))
+    return pairs
+
+
+def kv_pairs(dz, dc):
+    pairs = []
+    for i in range(8):
+        z, c = i // 2, i % 2
+        pairs.append((i, ((z + dz) % 4) * 2 + (c + dc) % 2))
+    return pairs
+
+
+def gather_ctx(block):
+    block = jnp.stack([block, lax.ppermute(block, "ctx", ctx_pairs(0, 0, 1))])
+    block = jnp.stack([block] + [lax.ppermute(block, "ctx", ctx_pairs(0, d, 0)) for d in (1, 2, 3)])
+    block = jnp.stack([block] + [lax.ppermute(block, "ctx", ctx_pairs(d, 0, 0)) for d in (1, 2, 3)])
+    return block.reshape((-1,) + block.shape[4:] if block.ndim > 4 else (-1,))
+
+
+def gather_kv(block):
+    parts = [block] + [lax.ppermute(block, "kv", kv_pairs(d, 0)) for d in (1, 2, 3)]
+    block = jnp.stack(parts)
+    block = jnp.stack([block, lax.ppermute(block, "kv", kv_pairs(0, 1))], 1)
+    rows, width = block.shape[2:]
+    block = block.reshape(8, rows, width)
+    me = lax.axis_index("kv")
+    j = jnp.arange(8)
+    source = ((me // 2 - j // 2) % 4) * 2 + (me + j) % 2
+    block = block[source]
+    return jnp.transpose(block, (1, 0, 2)).reshape(rows, 8 * width)
 
 
 def attend(state, queries, keys, values, allowed):
@@ -78,7 +115,7 @@
     match = block_ids[:, None] == jnp.arange(step_cut.shape[0], dtype=jnp.int32)[None, :]
     cut = jnp.sum(jnp.where(match, step_cut[None, :], 0), axis=1)
     masked = decode_order >= cut
-    piece = lax.all_gather(hidden, "kv", axis=1, tiled=True)
+    piece = gather_kv(hidden)
     noisy_piece = jnp.where(masked[:, None], mask_embed[None, :], piece)
     results = []
     for index, weight in enumerate((q_weight, k_weight, v_weight)):
@@ -120,9 +157,9 @@
         rim_pairs[:, 1].reshape(count, groups, head_dim),
         near,
     )
-    keys = lax.all_gather(k_clean, "ctx", axis=0, tiled=True)
-    values = lax.all_gather(v_clean, "ctx", axis=0, tiled=True)
-    piece_ids = lax.all_gather(block_ids, "ctx", axis=0, tiled=True)
+    piece_ids = gather_ctx(block_ids)
+    both = gather_ctx(jnp.concatenate([k_clean, v_clean], 1))
+    keys, values = both[:, : k_clean.shape[1]], both[:, k_clean.shape[1] :]
     count_here = keys.shape[0]
     key_part = keys.reshape(count_here, groups, head_dim)
     value_part = values.reshape(count_here, groups, head_dim)

time: 434 us -> 124 us (0.29); the launches traced: 427 us -> 123 us
  waiting for transfers between devices: 281 us -> 31.1 us
  blocking collectives: 67 us -> 0 us
  starting transfers between devices: 18 us -> 44.5 us
  between operations: 14.6 us -> 1.2 us
  matrix products: 23.8 us -> 18.7 us
  local copies, waits for them, and re-layouts: 8.02 us -> 12.5 us
    all_gather x3 -> x0, waiting for transfers between devices: 281 us -> none  [the longest x1 145 us: shards(): values = lax.all_gather(v_clean, 'ctx', axis=0, tiled=True)]
    all_gather x1 -> x0, blocking collectives: 67 us -> none  [shards(): piece_ids = lax.all_gather(block_ids, 'ctx', axis=0, tiled=True)]
    ppermute x0 -> x18, waiting for transfers between devices: none -> 31.1 us  [the longest x6 24.1 us: gather_ctx(): lax.ppermute(block, 'ctx', ctx_pairs(d, 0, 0))]
    ppermute x0 -> x18, starting transfers between devices: none -> 26.8 us  [the longest x3 11.4 us: gather_kv(): lax.ppermute(block, 'kv', kv_pairs(d, 0))]
    another operation x0 -> x10, other arithmetic: none -> 4.47 us  [the longest x4 2.68 us: gather_ctx(): jnp.stack([block] + [lax.ppermute(block, 'ctx', ctx_pairs(d, 0, 0)) for d...]
  transfers between devices with their start and end apart: 7 -> 22, of which waited for: 2 -> 8; matrix products, arithmetic and copies ran while one was open for 6% -> 12% of each run, Pallas kernels for 0% -> 0%
where the time goes in v1:
time: 124 us; the launch traced here: 123 us
  starting transfers between devices  44.5 us (36%)
  waiting for transfers between devices  31.1 us (25%)
  matrix products  18.7 us (15%)
  other arithmetic  15.2 us (12%)
  local copies, waits for them, and re-layouts  12.5 us (10%)
    ppermute x6, waiting for transfers between devices, gather_ctx(): lax.ppermute(block, 'ctx', ctx_pairs(d, 0, 0))  24.1 us
    ppermute x3, starting transfers between devices, gather_kv(): lax.ppermute(block, 'kv', kv_pairs(d, 0))  11.4 us
    ppermute x2, starting transfers between devices, extended(): lax.ppermute(lax.slice_in_dim(block, 0, width, axis=dim), axis, backward)  10.9 us
    ppermute x6, starting transfers between devices, gather_ctx(): lax.ppermute(block, 'ctx', ctx_pairs(0, d, 0))  7.55 us
    ppermute x6, waiting for transfers between devices, gather_ctx(): lax.ppermute(block, 'ctx', ctx_pairs(0, d, 0))  6.94 us
    dot_general x9, matrix products, attend(): jnp.einsum('gqrs,sgd->gqrd', probs.astype(jnp.bfloat16), value_part, pref...  6.89 us
    ppermute x2, starting transfers between devices, extended(): lax.ppermute(lax.slice_in_dim(block, block.shape[dim] - width, None, axis...  6.81 us
    dot_general x9, matrix products, attend(): jnp.einsum('rgqd,sgd->gqrs', queries, key_part, preferred_element_type=jn...  6.52 us
  transfers between devices with their start and end apart: 22, of which 8 were waited for; matrix products, arithmetic and copies ran while one was open for 12% of the time, Pallas kernels for 0%

profile of v1, /device:TPU:24, one launch (start us, length us, event | category | flops | bytes accessed | tf_op | source)
XLA Modules:
  0.0 123.1 jit_solution(1762076929516658883)
XLA Ops:
  0.6 3.3 %collective-permute-start.7 = (bf16[128,512]{1,0:T(8,128)(2,1)}, bf16[128,512]{1,0:T(8,128)(2,1)S(1)}, u32[]{:S(2)}, u32[]{:S(2)}) collective-permute-start(bf16[128,512]{1,0:T(8,128)(2,1)} %param.8), channel_id=1, source_target_pairs={{0,2},{1,3},{2,4},{3,5},{4,6},{5,7},{6,0},{7,1},{8,10},{9,11},{10,... | collective-permute-start | bytes 393224 | tf_op jit(solution)/shard_map/ppermute | solution.py:53
  4.0 3.1 %collective-permute-start.9 = (bf16[128,512]{1,0:T(8,128)(2,1)}, bf16[128,512]{1,0:T(8,128)(2,1)S(1)}, u32[]{:S(2)}, u32[]{:S(2)}) collective-permute-start(bf16[128,512]{1,0:T(8,128)(2,1)} %param.8), channel_id=1, source_target_pairs={{0,6},{1,7},{2,0},{3,1},{4,2},{5,3},{6,4},{7,5},{8,14},{9,15},{10,... | collective-permute-start | bytes 393224 | tf_op jit(solution)/shard_map/ppermute | solution.py:53
  8.9 2.9 %collective-permute-start.18 = (s32[32]{0:T(128)S(1)}, s32[32]{0:T(128)S(1)}, u32[]{:S(2)}, u32[]{:S(2)}) collective-permute-start(s32[32]{0:T(128)S(1)} %get-tuple-element.70), channel_id=1, source_target_pairs={{0,8},{8,16},{16,24},{24,32},{32,40},{40,48},{48,56},{56,64},{64,7... | collective-permute-start | bytes 392 | tf_op jit(solution)/shard_map/ppermute | solution.py:20
  11.8 5.9 %collective-permute-start.19 = (s32[32]{0:T(128)S(1)}, s32[32]{0:T(128)S(1)}, u32[]{:S(2)}, u32[]{:S(2)}) collective-permute-start(s32[32]{0:T(128)S(1)} %get-tuple-element.71), channel_id=1, source_target_pairs={{8,0},{16,8},{24,16},{32,24},{40,32},{48,40},{56,48},{64,56},{72,6... | collective-permute-start | bytes 392 | tf_op jit(solution)/shard_map/ppermute | solution.py:23
  22.4 2.6 %collective-permute-start.3 = (s32[2,128]{1,0:T(2,128)S(1)}, s32[2,128]{1,0:T(2,128)S(1)}, u32[]{:S(2)}, u32[]{:S(2)}) collective-permute-start(s32[2,128]{1,0:T(2,128)S(1)} %get-tuple-element.69), channel_id=1, source_target_pairs={{0,48},{8,56},{16,0},{24,8},{32,16},{40,24},{48,32},{56,40},{64,11... | collective-permute-start | bytes 3080 | tf_op jit(solution)/shard_map/ppermute | solution.py:47
  25.9 4.9 %collective-permute-start.8 = (bf16[128,512]{1,0:T(8,128)(2,1)}, bf16[128,512]{1,0:T(8,128)(2,1)S(1)}, u32[]{:S(2)}, u32[]{:S(2)}) collective-permute-start(bf16[128,512]{1,0:T(8,128)(2,1)} %param.8), channel_id=1, source_target_pairs={{0,4},{1,5},{2,6},{3,7},{4,0},{5,1},{6,2},{7,3},{8,12},{9,13},{10,... | collective-permute-start | bytes 393224 | tf_op jit(solution)/shard_map/ppermute | solution.py:53
  30.9 1.3 %collective-permute-start.5 = (s32[4,2,128]{2,1,0:T(2,128)S(1)}, s32[4,2,128]{2,1,0:T(2,128)S(1)}, u32[]{:S(2)}, u32[]{:S(2)}) collective-permute-start(s32[4,2,128]{2,1,0:T(2,128)S(1)} %pad_add_fusion.1), channel_id=1, source_target_pairs={{0,128},{8,136},{16,144},{24,152},{32,160},{40,168},{48,176},{56,1... | collective-permute-start | bytes 12296 | tf_op jit(solution)/shard_map/ppermute | solution.py:48
  32.9 2.2 %collective-permute-start.4 = (s32[4,2,128]{2,1,0:T(2,128)S(1)}, s32[4,2,128]{2,1,0:T(2,128)S(1)}, u32[]{:S(2)}, u32[]{:S(2)}) collective-permute-start(s32[4,2,128]{2,1,0:T(2,128)S(1)} %pad_add_fusion.1), channel_id=1, source_target_pairs={{0,64},{8,72},{16,80},{24,88},{32,96},{40,104},{48,112},{56,120},{... | collective-permute-start | bytes 12296 | tf_op jit(solution)/shard_map/ppermute | solution.py:48
  36.8 4.1 %collective-permute-done.6 = s32[4,2,128]{2,1,0:T(2,128)S(1)} collective-permute-done((s32[4,2,128]{2,1,0:T(2,128)S(1)}, s32[4,2,128]{2,1,0:T(2,128)S(1)}, u32[]{:S(2)}, u32[]{:S(2)}) %collective-permute-start.6) | collective-permute-done | bytes 4128 | tf_op jit(solution)/shard_map/ppermute | solution.py:48
  42.2 1.4 %and_or_fusion.1 = (pred[128,4096]{0,1:T(8,128)(4,1)S(1)}, pred[128,4096]{0,1:T(8,128)(4,1)S(1)}) fusion(s32[128]{0:T(128)S(1)} %get-tuple-element.92, pred[128]{0:T(512)(128)(4,1)S(1)} %compare_not_fusion, s32[4096]{0:T(1024)S(1)} %bitcast.491, s32[128]{0:T(128)S(1)} %get-tuple-element.93), kind=kLoop, calls=%fused_computation.19 | loop fusion | flops 4194304 | bytes 1066112 | tf_op jit(solution)/shard_map/or | solution.py:172
  50.3 1.5 %convolution_convert_fusion = bf16[128,512]{1,0:T(8,128)(2,1)S(1)} fusion(bf16[4096,512]{1,0:T(8,128)(2,1)S(1)} %copy-done.1, bf16[128,4096]{0,1:T(8,128)(2,1)S(1)} %bitcast.459, pred[128]{0:T(512)(128)(4,1)S(1)} %ge.17, bf16[4096]{0:T(1024)(128)(2,1)S(1)} %copy-done.19), kind=kOutput, calls=%fused_computation.67 | convolution fusion | flops 537460736 | bytes 5382272 | tf_op jit(solution)/shard_map/dot_general | solution.py:126
  53.3 3.9 %collective-permute-start.20 = (bf16[32,2,128]{2,0,1:T(8,128)(2,1)}, bf16[32,2,128]{2,0,1:T(8,128)(2,1)S(1)}, u32[]{:S(2)}, u32[]{:S(2)}) collective-permute-start(bf16[32,2,128]{2,0,1:T(8,128)(2,1)} %get-tuple-element.38), channel_id=1, source_target_pairs={{0,8},{8,16},{16,24},{24,32},{32,40},{40,48},{48,56},{56,64},{64,7... | collective-permute-start | bytes 49160 | tf_op jit(solution)/shard_map/ppermute | solution.py:20
  57.2 4.9 %collective-permute-start.21 = (bf16[32,2,128]{2,0,1:T(8,128)(2,1)}, bf16[32,2,128]{2,0,1:T(8,128)(2,1)}, u32[]{:S(2)}, u32[]{:S(2)}) collective-permute-start(bf16[32,2,128]{2,0,1:T(8,128)(2,1)} %get-tuple-element.39), channel_id=1, source_target_pairs={{8,0},{16,8},{24,16},{32,24},{40,32},{48,40},{56,48},{64,56},{72,6... | collective-permute-start | bytes 49160 | tf_op jit(solution)/shard_map/ppermute | solution.py:23
  62.4 3.2 %collective-permute-start.14 = (bf16[2,128,256]{1,2,0:T(8,128)(2,1)S(1)}, bf16[2,128,256]{1,2,0:T(8,128)(2,1)S(1)}, u32[]{:S(2)}, u32[]{:S(2)}) collective-permute-start(bf16[2,128,256]{1,2,0:T(8,128)(2,1)S(1)} %get-tuple-element.37), channel_id=1, source_target_pairs={{0,48},{8,56},{16,0},{24,8},{32,16},{40,24},{48,32},{56,40},{64,11... | collective-permute-start | bytes 393224 | tf_op jit(solution)/shard_map/ppermute | solution.py:47
  65.6 4.5 %collective-permute-done.13 = bf16[2,128,256]{1,2,0:T(8,128)(2,1)S(1)} collective-permute-done((bf16[2,128,256]{1,2,0:T(8,128)(2,1)S(1)}, bf16[2,128,256]{1,2,0:T(8,128)(2,1)S(1)}, u32[]{:S(2)}, u32[]{:S(2)}) %collective-permute-start.13) | collective-permute-done | bytes 131104 | tf_op jit(solution)/shard_map/ppermute | solution.py:47
  70.2 1.6 %collective-permute-done.12 = bf16[2,128,256]{1,2,0:T(8,128)(2,1)S(1)} collective-permute-done((bf16[2,128,256]{1,2,0:T(8,128)(2,1)S(1)}, bf16[2,128,256]{1,2,0:T(8,128)(2,1)S(1)}, u32[]{:S(2)}, u32[]{:S(2)}) %collective-permute-start.12) | collective-permute-done | bytes 131104 | tf_op jit(solution)/shard_map/ppermute | solution.py:47
  72.6 2.2 %collective-permute-start.15 = (bf16[4,2,128,256]{2,3,1,0:T(8,128)(2,1)S(1)}, bf16[4,2,128,256]{2,3,1,0:T(8,128)(2,1)S(1)}, u32[]{:S(2)}, u32[]{:S(2)}) collective-permute-start(bf16[4,2,128,256]{2,3,1,0:T(8,128)(2,1)S(1)} %get-tuple-element.23), channel_id=1, source_target_pairs={{0,64},{8,72},{16,80},{24,88},{32,96},{40,104},{48,112},{56,120},{... | collective-permute-start | bytes 1572872 | tf_op jit(solution)/shard_map/ppermute | solution.py:48
  78.2 1.7 %fusion.189 = (f32[4,128]{1,0:T(4,128)S(1)}, f32[1,4,128,192]{2,3,1,0:T(8,128)}) fusion(bf16[192,2,128]{2,0,1:T(8,128)(2,1)S(1)} %pad_maximum_fusion.5, pred[128,192]{0,1:T(8,128)(4,1)} %broadcast_compare_fusion, bf16[128,512]{1,0:T(8,128)(2,1)S(1)} %convolution_convert_fusion), kind=kOutput, calls=%fused_computation.303 | convolution fusion | flops 25460224 | bytes 600064 | tf_op jit(solution)/shard_map/rgqd,sgd->gqrs/dot_general | solution.py:75
  79.9 9.1 %collective-permute-done.16 = bf16[4,2,128,256]{2,3,1,0:T(8,128)(2,1)} collective-permute-done((bf16[4,2,128,256]{2,3,1,0:T(8,128)(2,1)S(1)}, bf16[4,2,128,256]{2,3,1,0:T(8,128)(2,1)}, u32[]{:S(2)}, u32[]{:S(2)}) %collective-permute-start.16) | collective-permute-done | bytes 524320 | tf_op jit(solution)/shard_map/ppermute | solution.py:48
  89.1 6.2 %collective-permute-done.15 = bf16[4,2,128,256]{2,3,1,0:T(8,128)(2,1)S(1)} collective-permute-done((bf16[4,2,128,256]{2,3,1,0:T(8,128)(2,1)S(1)}, bf16[4,2,128,256]{2,3,1,0:T(8,128)(2,1)S(1)}, u32[]{:S(2)}, u32[]{:S(2)}) %collective-permute-start.15) | collective-permute-done | bytes 524320 | tf_op jit(solution)/shard_map/ppermute | solution.py:48
  95.3 3.7 %collective-permute-done.17 = bf16[4,2,128,256]{2,3,1,0:T(8,128)(2,1)S(1)} collective-permute-done((bf16[4,2,128,256]{2,3,1,0:T(8,128)(2,1)S(1)}, bf16[4,2,128,256]{2,3,1,0:T(8,128)(2,1)S(1)}, u32[]{:S(2)}, u32[]{:S(2)}) %collective-permute-start.17) | collective-permute-done | bytes 524320 | tf_op jit(solution)/shard_map/ppermute | solution.py:48
  99.8 1.8 %pad_maximum_fusion = bf16[4,4,2,128,256]{3,4,2,1,0:T(8,128)(2,1)S(1)} fusion(bf16[1,4,2,128,256]{3,4,2,1,0:T(8,128)(2,1)} %bitcast.483, bf16[1,4,2,128,256]{3,4,2,1,0:T(8,128)(2,1)} %bitcast.30, bf16[1,4,2,128,256]{3,4,2,1,0:T(8,128)(2,1)} %bitcast.482, bf16[1,4,2,128,256]{3,4,2,1,0:T(8,128)(2,1)} %get-tuple-element.22), kind=kLoop, calls=%fused_computation.1 | loop fusion | flops 3145728 | bytes 4194304 | tf_op jit(solution)/shard_map/stack | solution.py:48
  101.6 2.4 %copy.45 = bf16[4,4,2,128,256]{4,3,2,1,0:T(8,128)(2,1)} copy(bf16[4,4,2,128,256]{3,4,2,1,0:T(8,128)(2,1)S(1)} %pad_maximum_fusion) | data formatting | bytes 4194304 | tf_op jit(solution)/shard_map/stack | solution.py:48
  104.0 1.6 %fusion.4 = (f32[4,128]{1,0:T(4,128)S(1)}, f32[1024,128,4]{1,0,2:T(8,128)S(1)}) fusion(pred[128,1024]{0,1:T(8,128)(4,1)} %get-tuple-element.18, bf16[64,1,4,128]{3,0,2,1:T(8,128)(2,1)} %copy.53, bf16[64,1,4,128]{3,0,2,1:T(8,128)(2,1)} %copy.52, bf16[4096,256]{1,0:T(8,128)(2,1)} %bitcast.463), kind=kOutput, calls=%fused_computation.24 | convolution fusion | flops 136052224 | bytes 2623488 | tf_op jit(solution)/shard_map/rgqd,sgd->gqrs/dot_general | solution.py:75
  (153 shorter events, 41.7 us)
Async XLA Ops:
  0.6 45.9 %copy-start = (bf16[4096,128]{1,0:T(8,128)(2,1)S(1)}, bf16[4096,128]{1,0:T(8,128)(2,1)}, u32[]{:S(2)}) copy-start(bf16[4096,128]{1,0:T(8,128)(2,1)} %param.15) | copy-start | bytes 3145732
  0.6 40.3 %collective-permute-start.7 = (bf16[128,512]{1,0:T(8,128)(2,1)}, bf16[128,512]{1,0:T(8,128)(2,1)S(1)}, u32[]{:S(2)}, u32[]{:S(2)}) collective-permute-start(bf16[128,512]{1,0:T(8,128)(2,1)} %param.8), channel_id=1, source_target_pairs={{0,2},{1,3},{2,4},{3,5},{4,6},{5,7},{6,0},{7,1},{8,10},{9,11},{10,... | collective-permute-start | bytes 393224 | tf_op jit(solution)/shard_map/ppermute | solution.py:53
  4.0 36.9 %collective-permute-start.9 = (bf16[128,512]{1,0:T(8,128)(2,1)}, bf16[128,512]{1,0:T(8,128)(2,1)S(1)}, u32[]{:S(2)}, u32[]{:S(2)}) collective-permute-start(bf16[128,512]{1,0:T(8,128)(2,1)} %param.8), channel_id=1, source_target_pairs={{0,6},{1,7},{2,0},{3,1},{4,2},{5,3},{6,4},{7,5},{8,14},{9,15},{10,... | collective-permute-start | bytes 393224 | tf_op jit(solution)/shard_map/ppermute | solution.py:53
  7.1 13.1 %collective-permute-start = (s32[128]{0:T(128)}, s32[128]{0:T(128)S(1)}, u32[]{:S(2)}, u32[]{:S(2)}) collective-permute-start(s32[128]{0:T(128)} %param.9), channel_id=1, source_target_pairs={{0,8},{8,0},{16,24},{24,16},{32,40},{40,32},{48,56},{56,48},{64,72... | collective-permute-start | bytes 1544 | tf_op jit(solution)/shard_map/ppermute | solution.py:46
  8.9 12.9 %collective-permute-start.18 = (s32[32]{0:T(128)S(1)}, s32[32]{0:T(128)S(1)}, u32[]{:S(2)}, u32[]{:S(2)}) collective-permute-start(s32[32]{0:T(128)S(1)} %get-tuple-element.70), channel_id=1, source_target_pairs={{0,8},{8,16},{16,24},{24,32},{32,40},{40,48},{48,56},{56,64},{64,7... | collective-permute-start | bytes 392 | tf_op jit(solution)/shard_map/ppermute | solution.py:20
  11.8 10.6 %collective-permute-start.19 = (s32[32]{0:T(128)S(1)}, s32[32]{0:T(128)S(1)}, u32[]{:S(2)}, u32[]{:S(2)}) collective-permute-start(s32[32]{0:T(128)S(1)} %get-tuple-element.71), channel_id=1, source_target_pairs={{8,0},{16,8},{24,16},{32,24},{40,32},{48,40},{56,48},{64,56},{72,6... | collective-permute-start | bytes 392 | tf_op jit(solution)/shard_map/ppermute | solution.py:23
  20.9 5.1 %collective-permute-start.2 = (s32[2,128]{1,0:T(2,128)S(1)}, s32[2,128]{1,0:T(2,128)S(1)}, u32[]{:S(2)}, u32[]{:S(2)}) collective-permute-start(s32[2,128]{1,0:T(2,128)S(1)} %get-tuple-element.69), channel_id=1, source_target_pairs={{0,32},{8,40},{16,48},{24,56},{32,0},{40,8},{48,16},{56,24},{64,96... | collective-permute-start | bytes 3080 | tf_op jit(solution)/shard_map/ppermute | solution.py:47
  21.8 9.1 %collective-permute-start.1 = (s32[2,128]{1,0:T(2,128)S(1)}, s32[2,128]{1,0:T(2,128)S(1)}, u32[]{:S(2)}, u32[]{:S(2)}) collective-permute-start(s32[2,128]{1,0:T(2,128)S(1)} %get-tuple-element.69), channel_id=1, source_target_pairs={{0,16},{8,24},{16,32},{24,40},{32,48},{40,56},{48,0},{56,8},{64,80... | collective-permute-start | bytes 3080 | tf_op jit(solution)/shard_map/ppermute | solution.py:47
  22.4 8.5 %collective-permute-start.3 = (s32[2,128]{1,0:T(2,128)S(1)}, s32[2,128]{1,0:T(2,128)S(1)}, u32[]{:S(2)}, u32[]{:S(2)}) collective-permute-start(s32[2,128]{1,0:T(2,128)S(1)} %get-tuple-element.69), channel_id=1, source_target_pairs={{0,48},{8,56},{16,0},{24,8},{32,16},{40,24},{48,32},{56,40},{64,11... | collective-permute-start | bytes 3080 | tf_op jit(solution)/shard_map/ppermute | solution.py:47
  25.9 15.0 %collective-permute-start.8 = (bf16[128,512]{1,0:T(8,128)(2,1)}, bf16[128,512]{1,0:T(8,128)(2,1)S(1)}, u32[]{:S(2)}, u32[]{:S(2)}) collective-permute-start(bf16[128,512]{1,0:T(8,128)(2,1)} %param.8), channel_id=1, source_target_pairs={{0,4},{1,5},{2,6},{3,7},{4,0},{5,1},{6,2},{7,3},{8,12},{9,13},{10,... | collective-permute-start | bytes 393224 | tf_op jit(solution)/shard_map/ppermute | solution.py:53
  30.9 5.2 %collective-permute-start.5 = (s32[4,2,128]{2,1,0:T(2,128)S(1)}, s32[4,2,128]{2,1,0:T(2,128)S(1)}, u32[]{:S(2)}, u32[]{:S(2)}) collective-permute-start(s32[4,2,128]{2,1,0:T(2,128)S(1)} %pad_add_fusion.1), channel_id=1, source_target_pairs={{0,128},{8,136},{16,144},{24,152},{32,160},{40,168},{48,176},{56,1... | collective-permute-start | bytes 12296 | tf_op jit(solution)/shard_map/ppermute | solution.py:48
  32.9 3.9 %collective-permute-start.4 = (s32[4,2,128]{2,1,0:T(2,128)S(1)}, s32[4,2,128]{2,1,0:T(2,128)S(1)}, u32[]{:S(2)}, u32[]{:S(2)}) collective-permute-start(s32[4,2,128]{2,1,0:T(2,128)S(1)} %pad_add_fusion.1), channel_id=1, source_target_pairs={{0,64},{8,72},{16,80},{24,88},{32,96},{40,104},{48,112},{56,120},{... | collective-permute-start | bytes 12296 | tf_op jit(solution)/shard_map/ppermute | solution.py:48
  36.1 4.8 %collective-permute-start.6 = (s32[4,2,128]{2,1,0:T(2,128)S(1)}, s32[4,2,128]{2,1,0:T(2,128)S(1)}, u32[]{:S(2)}, u32[]{:S(2)}) collective-permute-start(s32[4,2,128]{2,1,0:T(2,128)S(1)} %pad_add_fusion.1), channel_id=1, source_target_pairs={{0,192},{8,200},{16,208},{24,216},{32,224},{40,232},{48,240},{56,2... | collective-permute-start | bytes 12296 | tf_op jit(solution)/shard_map/ppermute | solution.py:48
  41.9 3.2 %collective-permute-start.10 = (bf16[4,128,512]{2,1,0:T(8,128)(2,1)S(1)}, bf16[4,128,512]{2,1,0:T(8,128)(2,1)S(1)}, u32[]{:S(2)}, u32[]{:S(2)}) collective-permute-start(bf16[4,128,512]{2,1,0:T(8,128)(2,1)S(1)} %get-tuple-element.25), channel_id=1, source_target_pairs={{0,1},{1,0},{2,3},{3,2},{4,5},{5,4},{6,7},{7,6},{8,9},{9,8},{10,11... | collective-permute-start | bytes 1572872 | tf_op jit(solution)/shard_map/ppermute | solution.py:55
  52.6 9.6 %collective-permute-start.11 = (bf16[128,256]{0,1:T(8,128)(2,1)S(1)}, bf16[128,256]{0,1:T(8,128)(2,1)S(1)}, u32[]{:S(2)}, u32[]{:S(2)}) collective-permute-start(bf16[128,256]{0,1:T(8,128)(2,1)S(1)} %get-tuple-element.41), channel_id=1, source_target_pairs={{0,8},{8,0},{16,24},{24,16},{32,40},{40,32},{48,56},{56,48},{64,72... | collective-permute-start | bytes 196616 | tf_op jit(solution)/shard_map/ppermute | solution.py:46
  53.3 24.2 %collective-permute-start.20 = (bf16[32,2,128]{2,0,1:T(8,128)(2,1)}, bf16[32,2,128]{2,0,1:T(8,128)(2,1)S(1)}, u32[]{:S(2)}, u32[]{:S(2)}) collective-permute-start(bf16[32,2,128]{2,0,1:T(8,128)(2,1)} %get-tuple-element.38), channel_id=1, source_target_pairs={{0,8},{8,16},{16,24},{24,32},{32,40},{40,48},{48,56},{56,64},{64,7... | collective-permute-start | bytes 49160 | tf_op jit(solution)/shard_map/ppermute | solution.py:20
  57.2 20.3 %collective-permute-start.21 = (bf16[32,2,128]{2,0,1:T(8,128)(2,1)}, bf16[32,2,128]{2,0,1:T(8,128)(2,1)}, u32[]{:S(2)}, u32[]{:S(2)}) collective-permute-start(bf16[32,2,128]{2,0,1:T(8,128)(2,1)} %get-tuple-element.39), channel_id=1, source_target_pairs={{8,0},{16,8},{24,16},{32,24},{40,32},{48,40},{56,48},{64,56},{72,6... | collective-permute-start | bytes 49160 | tf_op jit(solution)/shard_map/ppermute | solution.py:23
  62.2 8.0 %collective-permute-start.13 = (bf16[2,128,256]{1,2,0:T(8,128)(2,1)S(1)}, bf16[2,128,256]{1,2,0:T(8,128)(2,1)S(1)}, u32[]{:S(2)}, u32[]{:S(2)}) collective-permute-start(bf16[2,128,256]{1,2,0:T(8,128)(2,1)S(1)} %get-tuple-element.37), channel_id=1, source_target_pairs={{0,32},{8,40},{16,48},{24,56},{32,0},{40,8},{48,16},{56,24},{64,96... | collective-permute-start | bytes 393224 | tf_op jit(solution)/shard_map/ppermute | solution.py:47
  62.3 9.4 %collective-permute-start.12 = (bf16[2,128,256]{1,2,0:T(8,128)(2,1)S(1)}, bf16[2,128,256]{1,2,0:T(8,128)(2,1)S(1)}, u32[]{:S(2)}, u32[]{:S(2)}) collective-permute-start(bf16[2,128,256]{1,2,0:T(8,128)(2,1)S(1)} %get-tuple-element.37), channel_id=1, source_target_pairs={{0,16},{8,24},{16,32},{24,40},{32,48},{40,56},{48,0},{56,8},{64,80... | collective-permute-start | bytes 393224 | tf_op jit(solution)/shard_map/ppermute | solution.py:47
  62.4 9.3 %collective-permute-start.14 = (bf16[2,128,256]{1,2,0:T(8,128)(2,1)S(1)}, bf16[2,128,256]{1,2,0:T(8,128)(2,1)S(1)}, u32[]{:S(2)}, u32[]{:S(2)}) collective-permute-start(bf16[2,128,256]{1,2,0:T(8,128)(2,1)S(1)} %get-tuple-element.37), channel_id=1, source_target_pairs={{0,48},{8,56},{16,0},{24,8},{32,16},{40,24},{48,32},{56,40},{64,11... | collective-permute-start | bytes 393224 | tf_op jit(solution)/shard_map/ppermute | solution.py:47
  72.6 16.5 %collective-permute-start.16 = (bf16[4,2,128,256]{2,3,1,0:T(8,128)(2,1)S(1)}, bf16[4,2,128,256]{2,3,1,0:T(8,128)(2,1)}, u32[]{:S(2)}, u32[]{:S(2)}) collective-permute-start(bf16[4,2,128,256]{2,3,1,0:T(8,128)(2,1)S(1)} %get-tuple-element.23), channel_id=1, source_target_pairs={{0,128},{8,136},{16,144},{24,152},{32,160},{40,168},{48,176},{56,1... | collective-permute-start | bytes 1572872 | tf_op jit(solution)/shard_map/ppermute | solution.py:48
  72.6 22.7 %collective-permute-start.15 = (bf16[4,2,128,256]{2,3,1,0:T(8,128)(2,1)S(1)}, bf16[4,2,128,256]{2,3,1,0:T(8,128)(2,1)S(1)}, u32[]{:S(2)}, u32[]{:S(2)}) collective-permute-start(bf16[4,2,128,256]{2,3,1,0:T(8,128)(2,1)S(1)} %get-tuple-element.23), channel_id=1, source_target_pairs={{0,64},{8,72},{16,80},{24,88},{32,96},{40,104},{48,112},{56,120},{... | collective-permute-start | bytes 1572872 | tf_op jit(solution)/shard_map/ppermute | solution.py:48
  74.8 24.2 %collective-permute-start.17 = (bf16[4,2,128,256]{2,3,1,0:T(8,128)(2,1)S(1)}, bf16[4,2,128,256]{2,3,1,0:T(8,128)(2,1)S(1)}, u32[]{:S(2)}, u32[]{:S(2)}) collective-permute-start(bf16[4,2,128,256]{2,3,1,0:T(8,128)(2,1)S(1)} %get-tuple-element.23), channel_id=1, source_target_pairs={{0,192},{8,200},{16,208},{24,216},{32,224},{40,232},{48,240},{56,2... | collective-permute-start | bytes 1572872 | tf_op jit(solution)/shard_map/ppermute | solution.py:48
  78.2 20.8 %copy-start.12 = (bf16[192,2,128]{2,0,1:T(8,128)(2,1)}, bf16[192,2,128]{2,0,1:T(8,128)(2,1)S(1)}, u32[]{:S(2)}) copy-start(bf16[192,2,128]{2,0,1:T(8,128)(2,1)S(1)} %pad_maximum_fusion.5) | copy-start | bytes 294916
  (18 other events, 27.4 us)

commit v2 on v0

v2 whole, which is shorter than its diff:
```python
import math

import jax
import jax.numpy as jnp
from jax import lax
from jax.experimental import pallas as pl
from jax.experimental.pallas import tpu as pltpu
from jax.sharding import PartitionSpec as P

ROWS = 128
HEAD = 128
GROUP = 4
WIDTH = 512
BLOCK = 32
LAST = 31
LOW = -1e30
FAR = 1e6
POWER = math.log2(math.e) / math.sqrt(HEAD)
LIMIT = 48 * 1024 * 1024
F32 = jnp.float32
BF16 = jnp.bfloat16


def ctx_pairs(dy, dx, dz):
    pairs = []
    for i in range(32):
        y, x, z = i // 8, (i // 2) % 4, i % 2
        pairs.append((i, (((y + dy) % 4) * 4 + (x + dx) % 4) * 2 + (z + dz) % 2))
    return pairs


def kv_pairs(dz, dc):
    pairs = []
    for i in range(8):
        z, c = i // 2, i % 2
        pairs.append((i, ((z + dz) % 4) * 2 + (c + dc) % 2))
    return pairs


def dot(a, b):
    return jnp.dot(a, b, preferred_element_type=F32)


def dot_t(a, b):
    return lax.dot_general(a, b, (((1,), (1,)), ((), ())), preferred_element_type=F32)


def call(kernel, outs, args, cost, scratch=()):
    spec = pl.BlockSpec(memory_space=pltpu.VMEM)
    return pl.pallas_call(
        kernel,
        out_shape=[jax.ShapeDtypeStruct(s, t) for s, t in outs],
        in_specs=[spec] * len(args),
        out_specs=[spec] * len(outs),
        scratch_shapes=list(scratch),
        compiler_params=pltpu.CompilerParams(vmem_limit_bytes=LIMIT),
        cost_estimate=pl.CostEstimate(flops=cost[0], bytes_accessed=cost[1], transcendentals=0),
    )(*args)


def column(row):
    square = (ROWS, ROWS)
    same = lax.broadcasted_iota(jnp.int32, square, 0) == lax.broadcasted_iota(jnp.int32, square, 1)
    return jnp.sum(jnp.where(same, jnp.broadcast_to(row, square), 0.0), axis=1, keepdims=True)


def mask_kernel(ids_ref, order_ref, cut_ref, embed_ref, wq_ref, wk_ref, wv_ref, flag_ref, mq_ref, mkv_ref):
    ids = column(ids_ref[...].astype(F32))
    order = column(order_ref[...].astype(F32))
    blocks = cut_ref.shape[1]
    spots = lax.broadcasted_iota(jnp.int32, (ROWS, blocks), 1).astype(F32)
    cuts = jnp.broadcast_to(cut_ref[...].astype(F32), (ROWS, blocks))
    cut = jnp.sum(jnp.where(spots == ids, cuts, 0.0), axis=1, keepdims=True)
    flag_ref[...] = jnp.broadcast_to(jnp.where(order >= cut, 1.0, 0.0), (ROWS, HEAD))
    embed = jnp.broadcast_to(embed_ref[...], (16, embed_ref.shape[1]))
    mq_ref[...] = dot(embed, wq_ref[...]).astype(BF16)
    mkv_ref[:, :HEAD] = dot(embed, wk_ref[...]).astype(BF16)
    mkv_ref[:, HEAD:] = dot(embed, wv_ref[...]).astype(BF16)


def kv_kernel(*refs):
    pieces = refs[:8]
    wk_ref, wv_ref, flag_ref, mkv_ref, ids_ref = refs[8:13]
    x_ref, kv_ref, kvn_ref, up_ref, down_ref = refs[13:]
    me = lax.axis_index("kv")
    for dz in range(4):
        for dc in range(2):
            source = lax.rem(me // 2 + 4 - dz, 4) * 2 + lax.rem(me + dc, 2)
            x_ref[:, pl.ds(pl.multiple_of(source * WIDTH, WIDTH), WIDTH)] = pieces[2 * dz + dc][...]
    x = x_ref[...]
    masked = flag_ref[...] > 0.5
    for part, w_ref in enumerate((wk_ref, wv_ref)):
        lanes = slice(part * HEAD, (part + 1) * HEAD)
        clean = dot(x, w_ref[...])
        fixed = jnp.broadcast_to(mkv_ref[0:1, lanes].astype(F32), (ROWS, HEAD))
        noisy = jnp.where(masked, fixed, clean).astype(BF16)
        clean = clean.astype(BF16)
        kv_ref[:, lanes] = clean
        kvn_ref[:, lanes] = noisy
        up_ref[0:ROWS, lanes] = clean
        up_ref[ROWS : ROWS + BLOCK, lanes] = noisy[ROWS - BLOCK :]
        down_ref[0:BLOCK, lanes] = clean[:BLOCK]
        down_ref[BLOCK : 2 * BLOCK, lanes] = noisy[:BLOCK]
        ids = jnp.broadcast_to(ids_ref[...].astype(F32), (16, ROWS)).astype(BF16)
        up_ref[ROWS + BLOCK :, lanes] = ids
        down_ref[2 * BLOCK :, lanes] = ids


def q_kernel(x_ref, wq_ref, flag_ref, mq_ref, q_ref):
    masked = flag_ref[...] > 0.5
    x = x_ref[...]
    for h in range(GROUP):
        lanes = slice(h * HEAD, (h + 1) * HEAD)
        clean = dot(x, wq_ref[:, lanes])
        fixed = jnp.broadcast_to(mq_ref[0:1, lanes].astype(F32), (ROWS, HEAD))
        q_ref[h, :ROWS, :] = clean.astype(BF16)
        q_ref[h, ROWS:, :] = jnp.where(masked, fixed, clean).astype(BF16)


def near_kernel(q_ref, kv_ref, kvn_ref, up_ref, down_ref, ids_ref, top_ref, total_ref, accum_ref, k_ref, v_ref):
    me = lax.axis_index("ctx")
    for ref, lanes in ((k_ref, slice(0, HEAD)), (v_ref, slice(HEAD, 2 * HEAD))):
        ref[0:128, :] = up_ref[0:ROWS, lanes]
        ref[128:256, :] = kv_ref[:, lanes]
        ref[256:288, :] = down_ref[0:BLOCK, lanes]
        ref[288:320, :] = up_ref[ROWS : ROWS + BLOCK, lanes]
        ref[320:352, :] = down_ref[BLOCK : 2 * BLOCK, lanes]
        ref[352:384, :] = jnp.zeros((BLOCK, HEAD), BF16)
        ref[384:512, :] = kvn_ref[:, lanes]
    own = jnp.broadcast_to(ids_ref[...].astype(F32), (8, ROWS))
    before = up_ref[ROWS + BLOCK :, 0:ROWS].astype(F32)[:8]
    after = down_ref[2 * BLOCK :, 0:ROWS].astype(F32)[:8]
    before = jnp.where(me > 0, before, FAR)
    after = jnp.where(me < LAST, after, FAR)
    lane = lax.broadcasted_iota(jnp.int32, (8, ROWS), 1)
    mixed = jnp.where(
        lane < 32,
        after,
        jnp.where(lane < 64, pltpu.roll(before, 64, 1), jnp.where(lane < 96, pltpu.roll(after, 64, 1), -5.0)),
    )
    query = jnp.broadcast_to(column(ids_ref[...].astype(F32)), (ROWS, ROWS))
    keys = [jnp.broadcast_to(row[0:1], (ROWS, ROWS)) for row in (before, own, mixed, own)]
    early = lax.broadcasted_iota(jnp.int32, (ROWS, ROWS), 1) < 32
    zero = jnp.zeros((ROWS, ROWS), F32)
    low = jnp.full((ROWS, ROWS), LOW, F32)
    clean_bias = [
        jnp.where(keys[0] <= query, zero, low),
        jnp.where(keys[1] <= query, zero, low),
        jnp.where(early, jnp.where(keys[2] <= query, zero, low), low),
        low,
    ]
    noisy_bias = [
        jnp.where(keys[0] < query, zero, low),
        jnp.where(keys[1] < query, zero, low),
        jnp.where(early, jnp.where(keys[2] < query, zero, low), jnp.where(keys[2] == query, zero, low)),
        jnp.where(keys[3] == query, zero, low),
    ]
    bias = jnp.concatenate(
        [jnp.concatenate(clean_bias, axis=1), jnp.concatenate(noisy_bias, axis=1)], axis=0
    )
    for h in range(GROUP):
        scores = dot_t(q_ref[h], k_ref[...])
        scores = jnp.where(bias < -1.0, LOW, scores)
        top = jnp.max(scores, axis=1, keepdims=True)
        probs = jnp.exp2((scores - top) * POWER)
        top_ref[h] = jnp.broadcast_to(top, (2 * ROWS, HEAD))
        total_ref[h] = probs[:, 0:128] + probs[:, 128:256] + probs[:, 256:384] + probs[:, 384:512]
        accum_ref[h] = dot(probs.astype(BF16), v_ref[...])


def far_kernel(*refs):
    q_ref = refs[0]
    k_refs, v_refs = refs[1:5], refs[5:9]
    top_in, total_in, accum_in = refs[9:12]
    clean_ref, noisy_ref = refs[12:14]
    top_ref, total_ref, accum_ref = refs[14:]
    me = lax.axis_index("ctx")
    y, x, z = me // 8, lax.rem(me // 2, 4), lax.rem(me, 2)
    top_ref[...] = top_in[...]
    total_ref[...] = total_in[...]
    accum_ref[...] = accum_in[...]

    def chunk(h, dy, partial):
        keys = k_refs[dy][...].reshape(8 * ROWS, HEAD)
        scores = dot_t(q_ref[h], keys)
        parts = [scores[:, j * ROWS : (j + 1) * ROWS] for j in range(8)]
        if partial:
            for j in range(8):
                dx, dz = j // 2, j % 2
                index = lax.rem(y + 4 - dy, 4) * 8 + lax.rem(x + 4 - dx, 4) * 2 + lax.rem(z + dz, 2)
                parts[j] = jnp.where(index < me - 1, parts[j], LOW)
        best = parts[0]
        for part in parts[1:]:
            best = jnp.maximum(best, part)
        old = top_ref[h]
        top = jnp.maximum(old, jnp.max(best, axis=1, keepdims=True))
        factor = jnp.exp2((old - top) * POWER)
        probs = [jnp.exp2((part - top) * POWER) for part in parts]
        total = total_ref[h] * factor
        for part in probs:
            total = total + part
        accum = accum_ref[h] * factor
        probs = jnp.concatenate([part.astype(BF16) for part in probs], axis=1)
        for dx in range(4):
            values = v_refs[dx][dy].reshape(2 * ROWS, HEAD)
            accum = accum + dot(probs[:, dx * 256 : (dx + 1) * 256], values)
        top_ref[h] = top
        total_ref[h] = total
        accum_ref[h] = accum

    for dy in range(4):
        if dy == 0:
            some, whole = me - y * 8 > 1, me < 0
        else:
            whole = (y >= dy) & ((dy > 1) | (x + z > 0))
            some = (y >= dy) & jnp.logical_not(whole)
        for partial, when in ((True, some), (False, whole)):
            if dy == 0 and not partial or dy > 1 and partial:
                continue

            @pl.when(when)
            def _(dy=dy, partial=partial):
                def body(h, carry):
                    chunk(h, dy, partial)
                    return carry

                lax.fori_loop(0, GROUP, body, 0)

    for h in range(GROUP):
        lanes = slice(h * HEAD, (h + 1) * HEAD)
        total = jnp.sum(total_ref[h], axis=1, keepdims=True)
        result = (accum_ref[h] / total).astype(BF16)
        clean_ref[:, lanes] = result[:ROWS]
        noisy_ref[:, lanes] = result[ROWS:]


def shards(hidden, block_ids, decode_order, step_cut, mask_embed, q_weight, k_weight, v_weight):
    ids = block_ids.reshape(1, ROWS)
    flag, mask_q, mask_kv = call(
        mask_kernel,
        [((ROWS, HEAD), F32), ((16, GROUP * HEAD), BF16), ((16, 2 * HEAD), BF16)],
        [ids, decode_order.reshape(1, ROWS), step_cut.reshape(1, -1), mask_embed.reshape(1, -1), q_weight, k_weight, v_weight],
        (1 << 28, 6 << 20),
    )
    mine = [hidden] + [lax.ppermute(hidden, "kv", kv_pairs(d, 0)) for d in (1, 2, 3)]
    pieces = []
    for piece in mine:
        pieces += [piece, lax.ppermute(piece, "kv", kv_pairs(0, 1))]
    x, kv, kv_noisy, up, down = call(
        kv_kernel,
        [
            ((ROWS, 8 * WIDTH), BF16),
            ((ROWS, 2 * HEAD), BF16),
            ((ROWS, 2 * HEAD), BF16),
            ((ROWS + BLOCK + 16, 2 * HEAD), BF16),
            ((2 * BLOCK + 16, 2 * HEAD), BF16),
        ],
        pieces + [k_weight, v_weight, flag, mask_kv, ids],
        (1 << 29, 3 << 20),
    )
    pair = lax.ppermute(kv, "ctx", ctx_pairs(0, 0, 1))
    k = jnp.stack([kv[:, :HEAD], pair[:, :HEAD]])
    v = jnp.stack([kv[:, HEAD:], pair[:, HEAD:]])
    ks = jnp.stack([k] + [lax.ppermute(k, "ctx", ctx_pairs(0, d, 0)) for d in (1, 2, 3)])
    vs = jnp.stack([v] + [lax.ppermute(v, "ctx", ctx_pairs(d, 0, 0)) for d in (1, 2, 3)])
    count = 32
    up = lax.ppermute(up, "ctx", [(i, (i + 1) % count) for i in range(count)])
    down = lax.ppermute(down, "ctx", [(i, (i - 1) % count) for i in range(count)])
    (q,) = call(
        q_kernel,
        [((GROUP, 2 * ROWS, HEAD), BF16)],
        [x, q_weight, flag, mask_q],
        (1 << 30, 5 << 20),
    )
    state = [((GROUP, 2 * ROWS, HEAD), F32)] * 3
    near = call(
        near_kernel,
        state,
        [q, kv, kv_noisy, up, down, ids],
        (1 << 30, 2 << 20),
        [pltpu.VMEM((4 * ROWS, HEAD), BF16)] * 2,
    )
    all_k = [ks] + [lax.ppermute(ks, "ctx", ctx_pairs(d, 0, 0)) for d in (1, 2, 3)]
    all_v = [vs] + [lax.ppermute(vs, "ctx", ctx_pairs(0, d, 0)) for d in (1, 2, 3)]
    return tuple(
        call(
            far_kernel,
            [((ROWS, GROUP * HEAD), BF16)] * 2,
            [q, *all_k, *all_v, *near],
            (1 << 32, 4 << 20),
            [pltpu.VMEM((GROUP, 2 * ROWS, HEAD), F32)] * 3,
        )
    )


def solution(mesh):
    return jax.shard_map(
        shards,
        mesh=mesh,
        in_specs=(
            P("ctx", "kv"),
            P("ctx"),
            P("ctx"),
            P(),
            P(),
            P(None, "kv"),
            P(None, "kv"),
            P(None, "kv"),
        ),
        out_specs=(P("ctx", "kv"), P("ctx", "kv")),
        check_vma=False,
    )
```

time: 434 us -> 81 us (0.19); the launches traced: 427 us -> 80.2 us
  waiting for transfers between devices: 281 us -> 23.8 us
  blocking collectives: 67 us -> 0 us
  matrix products: 23.8 us -> 0 us
  starting transfers between devices: 18 us -> 34.1 us
  Pallas kernels: 0 us -> 15.4 us
  between operations: 14.6 us -> 0.77 us
  other arithmetic: 13.9 us -> 0.09 us
    all_gather x3 -> x0, waiting for transfers between devices: 281 us -> none  [the longest x1 145 us: shards(): values = lax.all_gather(v_clean, 'ctx', axis=0, tiled=True)]
    all_gather x1 -> x0, blocking collectives: 67 us -> none  [shards(): piece_ids = lax.all_gather(block_ids, 'ctx', axis=0, tiled=True)]
    ppermute x4 -> x22, waiting for transfers between devices: 0.01 us -> 23.8 us  [the longest x3 8.59 us: shards(): lax.ppermute(hidden, 'kv', kv_pairs(d, 0))]
    dot_general x24 -> x0, matrix products: 23.8 us -> none  [the longest x9 8.44 us: attend(): jnp.einsum('gqrs,sgd->gqrd', probs.astype(jnp.bfloat16), value_part, pref...]
    ppermute x4 -> x22, starting transfers between devices: 17.9 us -> 34.1 us  [the longest x3 11.4 us: shards(): lax.ppermute(hidden, 'kv', kv_pairs(d, 0))]
    pallas_call x0 -> x5, Pallas kernels: none -> 15.4 us  [call(): pl.pallas_call(kernel, out_shape=[jax.ShapeDtypeStruct(s, t) for s, t in...]
    reduce_sum x10 -> x0, other arithmetic: 7.68 us -> none  [the longest x9 6.83 us: attend(): total = total * factor + jnp.sum(probs, axis=-1)]
    slice x21 -> x0, local copies, waits for them, and re-layouts: 4.89 us -> none  [the longest x2 1.48 us: attend(): permit = allowed[None, None, :, begin:begin + width]]
  transfers between devices with their start and end apart: 7 -> 22, of which waited for: 2 -> 11; matrix products, arithmetic and copies ran while one was open for 6% -> 1% of each run, Pallas kernels for 0% -> 7%
where the time goes in v2:
time: 81 us; the launch traced here: 80.2 us
  starting transfers between devices  34.1 us (42%)
  waiting for transfers between devices  23.8 us (29%)
  Pallas kernels  15.4 us (19%)
  local copies, waits for them, and re-layouts  6.06 us (7%)
    pallas_call x5, Pallas kernels, call(): pl.pallas_call(kernel, out_shape=[jax.ShapeDtypeStruct(s, t) for s, t in...  15.4 us
    ppermute x3, starting transfers between devices, shards(): lax.ppermute(hidden, 'kv', kv_pairs(d, 0))  11.4 us
    ppermute x3, waiting for transfers between devices, shards(): lax.ppermute(hidden, 'kv', kv_pairs(d, 0))  8.59 us
    ppermute x3, starting transfers between devices, shards(): lax.ppermute(k, 'ctx', ctx_pairs(0, d, 0))  6.35 us
    ppermute x3, waiting for transfers between devices, shards(): lax.ppermute(vs, 'ctx', ctx_pairs(0, d, 0))  6.14 us
    unnamed x18, local copies, waits for them, and re-layouts  5.34 us
    ppermute x1, starting transfers between devices, shards(): lax.ppermute(down, 'ctx', [(i, (i - 1) % count) for i in range(count)])  4.74 us
    ppermute x3, starting transfers between devices, shards(): lax.ppermute(vs, 'ctx', ctx_pairs(0, d, 0))  3.87 us
  transfers between devices with their start and end apart: 22, of which 11 were waited for; matrix products, arithmetic and copies ran while one was open for 1% of the time, Pallas kernels for 7%

profile of v2, /device:TPU:24, one launch (start us, length us, event | category | flops | bytes accessed | tf_op | source)
XLA Modules:
  0.0 80.2 jit_solution(12005911489796640782)
XLA Ops:
  0.6 7.3 %collective-permute-start.3 = (bf16[128,512]{1,0:T(8,128)(2,1)}, bf16[128,512]{1,0:T(8,128)(2,1)S(1)}, u32[]{:S(2)}, u32[]{:S(2)}) collective-permute-start(bf16[128,512]{1,0:T(8,128)(2,1)} %refs_0_.1), channel_id=1, source_target_pairs={{0,4},{1,5},{2,6},{3,7},{4,0},{5,1},{6,2},{7,3},{8,12},{9,13},{10,... | collective-permute-start | bytes 393224 | tf_op jit(solution)/shard_map/ppermute | solution.py:245
  7.9 1.5 %collective-permute-start.1 = (bf16[128,512]{1,0:T(8,128)(2,1)}, bf16[128,512]{1,0:T(8,128)(2,1)S(1)}, u32[]{:S(2)}, u32[]{:S(2)}) collective-permute-start(bf16[128,512]{1,0:T(8,128)(2,1)} %refs_0_.1), channel_id=1, source_target_pairs={{0,2},{1,3},{2,4},{3,5},{4,6},{5,7},{6,0},{7,1},{8,10},{9,11},{10,... | collective-permute-start | bytes 393224 | tf_op jit(solution)/shard_map/ppermute | solution.py:245
  9.4 2.7 %collective-permute-start.5 = (bf16[128,512]{1,0:T(8,128)(2,1)}, bf16[128,512]{1,0:T(8,128)(2,1)S(1)}, u32[]{:S(2)}, u32[]{:S(2)}) collective-permute-start(bf16[128,512]{1,0:T(8,128)(2,1)} %refs_0_.1), channel_id=1, source_target_pairs={{0,6},{1,7},{2,0},{3,1},{4,2},{5,3},{6,4},{7,5},{8,14},{9,15},{10,... | collective-permute-start | bytes 393224 | tf_op jit(solution)/shard_map/ppermute | solution.py:245
  12.0 2.6 %collective-permute-done.3.refs_4_ = bf16[128,512]{1,0:T(8,128)(2,1)S(1)} collective-permute-done((bf16[128,512]{1,0:T(8,128)(2,1)}, bf16[128,512]{1,0:T(8,128)(2,1)S(1)}, u32[]{:S(2)}, u32[]{:S(2)}) %collective-permute-start.3) | collective-permute-done | bytes 131104 | tf_op jit(solution)/shard_map/ppermute | solution.py:245
  14.6 4.2 %collective-permute-done.1.refs_2_ = bf16[128,512]{1,0:T(8,128)(2,1)S(1)} collective-permute-done((bf16[128,512]{1,0:T(8,128)(2,1)}, bf16[128,512]{1,0:T(8,128)(2,1)S(1)}, u32[]{:S(2)}, u32[]{:S(2)}) %collective-permute-start.1) | collective-permute-done | bytes 131104 | tf_op jit(solution)/shard_map/ppermute | solution.py:245
  18.8 1.8 %collective-permute-done.5.refs_6_ = bf16[128,512]{1,0:T(8,128)(2,1)S(1)} collective-permute-done((bf16[128,512]{1,0:T(8,128)(2,1)}, bf16[128,512]{1,0:T(8,128)(2,1)S(1)}, u32[]{:S(2)}, u32[]{:S(2)}) %collective-permute-start.5) | collective-permute-done | bytes 131104 | tf_op jit(solution)/shard_map/ppermute | solution.py:245
  21.4 1.2 %copy-done.1 = bf16[4096,128]{1,0:T(8,128)(2,1)S(1)} copy-done((bf16[4096,128]{1,0:T(8,128)(2,1)S(1)}, bf16[4096,128]{1,0:T(8,128)(2,1)}, u32[]{:S(2)}) %copy-start.1) | copy-done | bytes 1048600
  22.6 1.2 %copy-done.3 = bf16[4096,128]{1,0:T(8,128)(2,1)S(1)} copy-done((bf16[4096,128]{1,0:T(8,128)(2,1)S(1)}, bf16[4096,128]{1,0:T(8,128)(2,1)}, u32[]{:S(2)}) %copy-start.3) | copy-done | bytes 1048600
  25.8 3.3 %shard_map.95 = (f32[128,128]{1,0:T(8,128)S(1)}, bf16[16,512]{1,0:T(8,128)(2,1)S(1)}, bf16[16,256]{1,0:T(8,128)(2,1)S(1)}) custom-call(s32[1,128]{1,0:T(1,128)S(1)} %bitcast.21, s32[1,128]{1,0:T(1,128)S(1)} %bitcast.25, s32[1,256]{1,0:T(1,128)S(1)} %bitcast.24, bf16[1,4096]{1,0:T(2,128)(2,1)S(1)} %reshape.19.embed_ref, bf16[4096,512]{1,0:T(8,128)(2,1)} %wq_ref.3, ...), custom_call_target="tpu_custom_call" | custom-call | flops 268435456 | bytes 6291456 | tf_op jit(solution)/shard_map/pallas_call | solution.py:50
  31.8 3.7 %collective-permute-done.7 = bf16[128,256]{1,0:T(8,128)(2,1)S(1)} collective-permute-done((bf16[128,256]{1,0:T(8,128)(2,1)S(1)}, bf16[128,256]{1,0:T(8,128)(2,1)S(1)}, u32[]{:S(2)}, u32[]{:S(2)}) %collective-permute-start.7) | collective-permute-done | bytes 65568 | tf_op jit(solution)/shard_map/ppermute | solution.py:261
  35.4 3.1 %collective-permute-start.9 = (bf16[2,128,128]{2,1,0:T(8,128)(2,1)S(1)}, bf16[2,128,128]{2,1,0:T(8,128)(2,1)S(1)}, u32[]{:S(2)}, u32[]{:S(2)}) collective-permute-start(bf16[2,128,128]{2,1,0:T(8,128)(2,1)S(1)} %get-tuple-element.31), channel_id=1, source_target_pairs={{0,32},{8,40},{16,48},{24,56},{32,0},{40,8},{48,16},{56,24},{64,96... | collective-permute-start | bytes 196616 | tf_op jit(solution)/shard_map/ppermute | solution.py:264
  39.1 2.6 %collective-permute-start.10 = (bf16[2,128,128]{2,1,0:T(8,128)(2,1)S(1)}, bf16[2,128,128]{2,1,0:T(8,128)(2,1)S(1)}, u32[]{:S(2)}, u32[]{:S(2)}) collective-permute-start(bf16[2,128,128]{2,1,0:T(8,128)(2,1)S(1)} %get-tuple-element.31), channel_id=1, source_target_pairs={{0,48},{8,56},{16,0},{24,8},{32,16},{40,24},{48,32},{56,40},{64,11... | collective-permute-start | bytes 196616 | tf_op jit(solution)/shard_map/ppermute | solution.py:264
  41.8 2.2 %collective-permute-done.8 = bf16[2,128,128]{2,1,0:T(8,128)(2,1)S(1)} collective-permute-done((bf16[2,128,128]{2,1,0:T(8,128)(2,1)S(1)}, bf16[2,128,128]{2,1,0:T(8,128)(2,1)S(1)}, u32[]{:S(2)}, u32[]{:S(2)}) %collective-permute-start.8) | collective-permute-done | bytes 65568 | tf_op jit(solution)/shard_map/ppermute | solution.py:264
  45.9 2.2 %collective-permute-start.14 = (bf16[2,128,128]{2,1,0:T(8,128)(2,1)S(1)}, bf16[2,128,128]{2,1,0:T(8,128)(2,1)S(1)}, u32[]{:S(2)}, u32[]{:S(2)}) collective-permute-start(bf16[2,128,128]{2,1,0:T(8,128)(2,1)S(1)} %get-tuple-element.25), channel_id=1, source_target_pairs={{0,64},{8,72},{16,80},{24,88},{32,96},{40,104},{48,112},{56,120},{... | collective-permute-start | bytes 196616 | tf_op jit(solution)/shard_map/ppermute | solution.py:265
  48.3 4.7 %collective-permute-start.21 = (bf16[80,256]{1,0:T(8,128)(2,1)S(1)}, bf16[80,256]{1,0:T(8,128)(2,1)S(1)}, u32[]{:S(2)}, u32[]{:S(2)}) collective-permute-start(bf16[80,256]{1,0:T(8,128)(2,1)S(1)} %get-tuple-element.20), channel_id=1, source_target_pairs={{0,248},{8,0},{16,8},{24,16},{32,24},{40,32},{48,40},{56,48},{64,5... | collective-permute-start | bytes 122888 | tf_op jit(solution)/shard_map/ppermute | solution.py:268
  53.1 2.5 %collective-permute-start.12 = (bf16[4,2,128,128]{3,2,1,0:T(8,128)(2,1)S(1)}, bf16[4,2,128,128]{3,2,1,0:T(8,128)(2,1)S(1)}, u32[]{:S(2)}, u32[]{:S(2)}) collective-permute-start(bf16[4,2,128,128]{3,2,1,0:T(8,128)(2,1)S(1)} %pad_maximum_fusion.refs_1_), channel_id=1, source_target_pairs={{0,128},{8,136},{16,144},{24,152},{32,160},{40,168},{48,176},{56,1... | collective-permute-start | bytes 786440 | tf_op jit(solution)/shard_map/ppermute | solution.py:283
  55.6 1.9 %collective-permute-done.16 = bf16[2,128,128]{2,1,0:T(8,128)(2,1)S(1)} collective-permute-done((bf16[2,128,128]{2,1,0:T(8,128)(2,1)S(1)}, bf16[2,128,128]{2,1,0:T(8,128)(2,1)S(1)}, u32[]{:S(2)}, u32[]{:S(2)}) %collective-permute-start.16) | collective-permute-done | bytes 65568 | tf_op jit(solution)/shard_map/ppermute | solution.py:265
  57.5 3.0 %collective-permute-start.19 = (bf16[4,2,128,128]{3,2,1,0:T(8,128)(2,1)S(1)}, bf16[4,2,128,128]{3,2,1,0:T(8,128)(2,1)S(1)}, u32[]{:S(2)}, u32[]{:S(2)}) collective-permute-start(bf16[4,2,128,128]{3,2,1,0:T(8,128)(2,1)S(1)} %pad_maximum_fusion.1.refs_5_), channel_id=1, source_target_pairs={{0,48},{8,56},{16,0},{24,8},{32,16},{40,24},{48,32},{56,40},{64,11... | collective-permute-start | bytes 786440 | tf_op jit(solution)/shard_map/ppermute | solution.py:284
  61.8 1.3 %shard_map.97.q_ref.refs_0_ = bf16[4,256,128]{2,1,0:T(8,128)(2,1)S(1)} custom-call(bf16[128,4096]{1,0:T(8,128)(2,1)S(1)} %get-tuple-element.15.x_ref, bf16[4096,512]{1,0:T(8,128)(2,1)S(1)} %copy-done, f32[128,128]{1,0:T(8,128)S(1)} %get-tuple-element.13.refs_10_.flag_ref, bf16[16,512]{1,0:T(8,128)(2,1)S(1)} %get-tuple-element.16.mq_ref), custom_call_target="tpu_custom_call" | custom-call | flops 1073741824 | bytes 5242880 | tf_op jit(solution)/shard_map/pallas_call | solution.py:50
  63.1 1.4 %shard_map.98 = (f32[4,256,128]{2,1,0:T(8,128)S(1)}, f32[4,256,128]{2,1,0:T(8,128)S(1)}, f32[4,256,128]{2,1,0:T(8,128)S(1)}) custom-call(bf16[4,256,128]{2,1,0:T(8,128)(2,1)S(1)} %shard_map.97.q_ref.refs_0_, bf16[128,256]{1,0:T(8,128)(2,1)S(1)} %get-tuple-element.17.kv_ref, bf16[128,256]{1,0:T(8,128)(2,1)S(1)} %get-tuple-element.18.kvn_ref, ...), custom_call_target="tpu_custom_call" | custom-call | flops 1073741824 | bytes 2097152 | tf_op jit(solution)/shard_map/pallas_call | solution.py:50
  65.4 1.9 %collective-permute-done.19.refs_8_ = bf16[4,2,128,128]{3,2,1,0:T(8,128)(2,1)S(1)} collective-permute-done((bf16[4,2,128,128]{3,2,1,0:T(8,128)(2,1)S(1)}, bf16[4,2,128,128]{3,2,1,0:T(8,128)(2,1)S(1)}, u32[]{:S(2)}, u32[]{:S(2)}) %collective-permute-start.19) | collective-permute-done | bytes 262176 | tf_op jit(solution)/shard_map/ppermute | solution.py:284
  67.3 1.7 %collective-permute-done.18.refs_7_ = bf16[4,2,128,128]{3,2,1,0:T(8,128)(2,1)S(1)} collective-permute-done((bf16[4,2,128,128]{3,2,1,0:T(8,128)(2,1)S(1)}, bf16[4,2,128,128]{3,2,1,0:T(8,128)(2,1)S(1)}, u32[]{:S(2)}, u32[]{:S(2)}) %collective-permute-start.18) | collective-permute-done | bytes 262176 | tf_op jit(solution)/shard_map/ppermute | solution.py:284
  69.0 2.6 %collective-permute-done.17.refs_6_ = bf16[4,2,128,128]{3,2,1,0:T(8,128)(2,1)S(1)} collective-permute-done((bf16[4,2,128,128]{3,2,1,0:T(8,128)(2,1)S(1)}, bf16[4,2,128,128]{3,2,1,0:T(8,128)(2,1)S(1)}, u32[]{:S(2)}, u32[]{:S(2)}) %collective-permute-start.17) | collective-permute-done | bytes 262176 | tf_op jit(solution)/shard_map/ppermute | solution.py:284
  71.5 8.7 %shard_map.99 = (bf16[128,512]{1,0:T(8,128)(2,1)}, bf16[128,512]{1,0:T(8,128)(2,1)}) custom-call(bf16[4,256,128]{2,1,0:T(8,128)(2,1)S(1)} %shard_map.97.q_ref.refs_0_, bf16[4,2,128,128]{3,2,1,0:T(8,128)(2,1)S(1)} %pad_maximum_fusion.refs_1_, bf16[4,2,128,128]{3,2,1,0:T(8,128)(2,1)S(1)} %collective-permute-done.11.refs_2_, ...), custom_call_target="tpu_custom_call" | custom-call | flops 4294967296 | bytes 4194304 | tf_op jit(solution)/shard_map/pallas_call | solution.py:50
  (50 shorter events, 10.3 us)
Async XLA Ops:
  0.6 14.0 %collective-permute-start.3 = (bf16[128,512]{1,0:T(8,128)(2,1)}, bf16[128,512]{1,0:T(8,128)(2,1)S(1)}, u32[]{:S(2)}, u32[]{:S(2)}) collective-permute-start(bf16[128,512]{1,0:T(8,128)(2,1)} %refs_0_.1), channel_id=1, source_target_pairs={{0,4},{1,5},{2,6},{3,7},{4,0},{5,1},{6,2},{7,3},{8,12},{9,13},{10,... | collective-permute-start | bytes 393224 | tf_op jit(solution)/shard_map/ppermute | solution.py:245
  7.9 10.9 %collective-permute-start.1 = (bf16[128,512]{1,0:T(8,128)(2,1)}, bf16[128,512]{1,0:T(8,128)(2,1)S(1)}, u32[]{:S(2)}, u32[]{:S(2)}) collective-permute-start(bf16[128,512]{1,0:T(8,128)(2,1)} %refs_0_.1), channel_id=1, source_target_pairs={{0,2},{1,3},{2,4},{3,5},{4,6},{5,7},{6,0},{7,1},{8,10},{9,11},{10,... | collective-permute-start | bytes 393224 | tf_op jit(solution)/shard_map/ppermute | solution.py:245
  9.4 11.3 %collective-permute-start.5 = (bf16[128,512]{1,0:T(8,128)(2,1)}, bf16[128,512]{1,0:T(8,128)(2,1)S(1)}, u32[]{:S(2)}, u32[]{:S(2)}) collective-permute-start(bf16[128,512]{1,0:T(8,128)(2,1)} %refs_0_.1), channel_id=1, source_target_pairs={{0,6},{1,7},{2,0},{3,1},{4,2},{5,3},{6,4},{7,5},{8,14},{9,15},{10,... | collective-permute-start | bytes 393224 | tf_op jit(solution)/shard_map/ppermute | solution.py:245
  12.0 17.0 %collective-permute-start = (bf16[128,512]{1,0:T(8,128)(2,1)}, bf16[128,512]{1,0:T(8,128)(2,1)S(1)}, u32[]{:S(2)}, u32[]{:S(2)}) collective-permute-start(bf16[128,512]{1,0:T(8,128)(2,1)} %refs_0_.1), channel_id=1, source_target_pairs={{0,1},{1,0},{2,3},{3,2},{4,5},{5,4},{6,7},{7,6},{8,9},{9,8},{10,11... | collective-permute-start | bytes 393224 | tf_op jit(solution)/shard_map/ppermute | solution.py:248
  14.6 14.4 %collective-permute-start.4 = (bf16[128,512]{1,0:T(8,128)(2,1)S(1)}, bf16[128,512]{1,0:T(8,128)(2,1)S(1)}, u32[]{:S(2)}, u32[]{:S(2)}) collective-permute-start(bf16[128,512]{1,0:T(8,128)(2,1)S(1)} %collective-permute-done.3.refs_4_), channel_id=1, source_target_pairs={{0,1},{1,0},{2,3},{3,2},{4,5},{5,4},{6,7},{7,6},{8,9},{9,8},{10,11... | collective-permute-start | bytes 393224 | tf_op jit(solution)/shard_map/ppermute | solution.py:248
  18.8 10.3 %collective-permute-start.2 = (bf16[128,512]{1,0:T(8,128)(2,1)S(1)}, bf16[128,512]{1,0:T(8,128)(2,1)S(1)}, u32[]{:S(2)}, u32[]{:S(2)}) collective-permute-start(bf16[128,512]{1,0:T(8,128)(2,1)S(1)} %collective-permute-done.1.refs_2_), channel_id=1, source_target_pairs={{0,1},{1,0},{2,3},{3,2},{4,5},{5,4},{6,7},{7,6},{8,9},{9,8},{10,11... | collective-permute-start | bytes 393224 | tf_op jit(solution)/shard_map/ppermute | solution.py:248
  20.6 8.5 %collective-permute-start.6 = (bf16[128,512]{1,0:T(8,128)(2,1)S(1)}, bf16[128,512]{1,0:T(8,128)(2,1)S(1)}, u32[]{:S(2)}, u32[]{:S(2)}) collective-permute-start(bf16[128,512]{1,0:T(8,128)(2,1)S(1)} %collective-permute-done.5.refs_6_), channel_id=1, source_target_pairs={{0,1},{1,0},{2,3},{3,2},{4,5},{5,4},{6,7},{7,6},{8,9},{9,8},{10,11... | collective-permute-start | bytes 393224 | tf_op jit(solution)/shard_map/ppermute | solution.py:248
  25.8 3.3 %copy-start.4 = (bf16[4096,128]{1,0:T(8,128)(2,1)S(1)}, bf16[4096,128]{1,0:T(8,128)(2,1)}, u32[]{:S(2)}) copy-start(bf16[4096,128]{1,0:T(8,128)(2,1)} %refs_9_.1) | copy-start | bytes 3145732
  25.8 36.0 %copy-start = (bf16[4096,512]{1,0:T(8,128)(2,1)S(1)}, bf16[4096,512]{1,0:T(8,128)(2,1)}, u32[]{:S(2)}) copy-start(bf16[4096,512]{1,0:T(8,128)(2,1)} %wq_ref.3) | copy-start | bytes 12582916
  30.8 4.6 %collective-permute-start.7 = (bf16[128,256]{1,0:T(8,128)(2,1)S(1)}, bf16[128,256]{1,0:T(8,128)(2,1)S(1)}, u32[]{:S(2)}, u32[]{:S(2)}) collective-permute-start(bf16[128,256]{1,0:T(8,128)(2,1)S(1)} %get-tuple-element.17.kv_ref), channel_id=1, source_target_pairs={{0,8},{8,0},{16,24},{24,16},{32,40},{40,32},{48,56},{56,48},{64,72... | collective-permute-start | bytes 196616 | tf_op jit(solution)/shard_map/ppermute | solution.py:261
  35.4 6.3 %collective-permute-start.9 = (bf16[2,128,128]{2,1,0:T(8,128)(2,1)S(1)}, bf16[2,128,128]{2,1,0:T(8,128)(2,1)S(1)}, u32[]{:S(2)}, u32[]{:S(2)}) collective-permute-start(bf16[2,128,128]{2,1,0:T(8,128)(2,1)S(1)} %get-tuple-element.31), channel_id=1, source_target_pairs={{0,32},{8,40},{16,48},{24,56},{32,0},{40,8},{48,16},{56,24},{64,96... | collective-permute-start | bytes 196616 | tf_op jit(solution)/shard_map/ppermute | solution.py:264
  38.5 5.5 %collective-permute-start.8 = (bf16[2,128,128]{2,1,0:T(8,128)(2,1)S(1)}, bf16[2,128,128]{2,1,0:T(8,128)(2,1)S(1)}, u32[]{:S(2)}, u32[]{:S(2)}) collective-permute-start(bf16[2,128,128]{2,1,0:T(8,128)(2,1)S(1)} %get-tuple-element.31), channel_id=1, source_target_pairs={{0,16},{8,24},{16,32},{24,40},{32,48},{40,56},{48,0},{56,8},{64,80... | collective-permute-start | bytes 196616 | tf_op jit(solution)/shard_map/ppermute | solution.py:264
  39.1 4.9 %collective-permute-start.10 = (bf16[2,128,128]{2,1,0:T(8,128)(2,1)S(1)}, bf16[2,128,128]{2,1,0:T(8,128)(2,1)S(1)}, u32[]{:S(2)}, u32[]{:S(2)}) collective-permute-start(bf16[2,128,128]{2,1,0:T(8,128)(2,1)S(1)} %get-tuple-element.31), channel_id=1, source_target_pairs={{0,48},{8,56},{16,0},{24,8},{32,16},{40,24},{48,32},{56,40},{64,11... | collective-permute-start | bytes 196616 | tf_op jit(solution)/shard_map/ppermute | solution.py:264
  44.1 16.9 %collective-permute-start.13 = (bf16[4,2,128,128]{3,2,1,0:T(8,128)(2,1)S(1)}, bf16[4,2,128,128]{3,2,1,0:T(8,128)(2,1)S(1)}, u32[]{:S(2)}, u32[]{:S(2)}) collective-permute-start(bf16[4,2,128,128]{3,2,1,0:T(8,128)(2,1)S(1)} %pad_maximum_fusion.refs_1_), channel_id=1, source_target_pairs={{0,192},{8,200},{16,208},{24,216},{32,224},{40,232},{48,240},{56,2... | collective-permute-start | bytes 786440 | tf_op jit(solution)/shard_map/ppermute | solution.py:283
  44.9 8.2 %collective-permute-start.15 = (bf16[2,128,128]{2,1,0:T(8,128)(2,1)S(1)}, bf16[2,128,128]{2,1,0:T(8,128)(2,1)S(1)}, u32[]{:S(2)}, u32[]{:S(2)}) collective-permute-start(bf16[2,128,128]{2,1,0:T(8,128)(2,1)S(1)} %get-tuple-element.25), channel_id=1, source_target_pairs={{0,128},{8,136},{16,144},{24,152},{32,160},{40,168},{48,176},{56,1... | collective-permute-start | bytes 196616 | tf_op jit(solution)/shard_map/ppermute | solution.py:265
  45.9 7.2 %collective-permute-start.14 = (bf16[2,128,128]{2,1,0:T(8,128)(2,1)S(1)}, bf16[2,128,128]{2,1,0:T(8,128)(2,1)S(1)}, u32[]{:S(2)}, u32[]{:S(2)}) collective-permute-start(bf16[2,128,128]{2,1,0:T(8,128)(2,1)S(1)} %get-tuple-element.25), channel_id=1, source_target_pairs={{0,64},{8,72},{16,80},{24,88},{32,96},{40,104},{48,112},{56,120},{... | collective-permute-start | bytes 196616 | tf_op jit(solution)/shard_map/ppermute | solution.py:265
  48.1 9.4 %collective-permute-start.16 = (bf16[2,128,128]{2,1,0:T(8,128)(2,1)S(1)}, bf16[2,128,128]{2,1,0:T(8,128)(2,1)S(1)}, u32[]{:S(2)}, u32[]{:S(2)}) collective-permute-start(bf16[2,128,128]{2,1,0:T(8,128)(2,1)S(1)} %get-tuple-element.25), channel_id=1, source_target_pairs={{0,192},{8,200},{16,208},{24,216},{32,224},{40,232},{48,240},{56,2... | collective-permute-start | bytes 196616 | tf_op jit(solution)/shard_map/ppermute | solution.py:265
  48.3 9.2 %collective-permute-start.21 = (bf16[80,256]{1,0:T(8,128)(2,1)S(1)}, bf16[80,256]{1,0:T(8,128)(2,1)S(1)}, u32[]{:S(2)}, u32[]{:S(2)}) collective-permute-start(bf16[80,256]{1,0:T(8,128)(2,1)S(1)} %get-tuple-element.20), channel_id=1, source_target_pairs={{0,248},{8,0},{16,8},{24,16},{32,24},{40,32},{48,40},{56,48},{64,5... | collective-permute-start | bytes 122888 | tf_op jit(solution)/shard_map/ppermute | solution.py:268
  53.1 7.9 %collective-permute-start.20 = (bf16[176,256]{1,0:T(8,128)(2,1)S(1)}, bf16[176,256]{1,0:T(8,128)(2,1)S(1)}, u32[]{:S(2)}, u32[]{:S(2)}) collective-permute-start(bf16[176,256]{1,0:T(8,128)(2,1)S(1)} %get-tuple-element.19), channel_id=1, source_target_pairs={{0,8},{8,16},{16,24},{24,32},{32,40},{40,48},{48,56},{56,64},{64,7... | collective-permute-start | bytes 270344 | tf_op jit(solution)/shard_map/ppermute | solution.py:267
  53.1 11.5 %collective-permute-start.12 = (bf16[4,2,128,128]{3,2,1,0:T(8,128)(2,1)S(1)}, bf16[4,2,128,128]{3,2,1,0:T(8,128)(2,1)S(1)}, u32[]{:S(2)}, u32[]{:S(2)}) collective-permute-start(bf16[4,2,128,128]{3,2,1,0:T(8,128)(2,1)S(1)} %pad_maximum_fusion.refs_1_), channel_id=1, source_target_pairs={{0,128},{8,136},{16,144},{24,152},{32,160},{40,168},{48,176},{56,1... | collective-permute-start | bytes 786440 | tf_op jit(solution)/shard_map/ppermute | solution.py:283
  57.5 7.9 %collective-permute-start.11 = (bf16[4,2,128,128]{3,2,1,0:T(8,128)(2,1)S(1)}, bf16[4,2,128,128]{3,2,1,0:T(8,128)(2,1)S(1)}, u32[]{:S(2)}, u32[]{:S(2)}) collective-permute-start(bf16[4,2,128,128]{3,2,1,0:T(8,128)(2,1)S(1)} %pad_maximum_fusion.refs_1_), channel_id=1, source_target_pairs={{0,64},{8,72},{16,80},{24,88},{32,96},{40,104},{48,112},{56,120},{... | collective-permute-start | bytes 786440 | tf_op jit(solution)/shard_map/ppermute | solution.py:283
  57.5 9.7 %collective-permute-start.19 = (bf16[4,2,128,128]{3,2,1,0:T(8,128)(2,1)S(1)}, bf16[4,2,128,128]{3,2,1,0:T(8,128)(2,1)S(1)}, u32[]{:S(2)}, u32[]{:S(2)}) collective-permute-start(bf16[4,2,128,128]{3,2,1,0:T(8,128)(2,1)S(1)} %pad_maximum_fusion.1.refs_5_), channel_id=1, source_target_pairs={{0,48},{8,56},{16,0},{24,8},{32,16},{40,24},{48,32},{56,40},{64,11... | collective-permute-start | bytes 786440 | tf_op jit(solution)/shard_map/ppermute | solution.py:284
  61.0 8.0 %collective-permute-start.18 = (bf16[4,2,128,128]{3,2,1,0:T(8,128)(2,1)S(1)}, bf16[4,2,128,128]{3,2,1,0:T(8,128)(2,1)S(1)}, u32[]{:S(2)}, u32[]{:S(2)}) collective-permute-start(bf16[4,2,128,128]{3,2,1,0:T(8,128)(2,1)S(1)} %pad_maximum_fusion.1.refs_5_), channel_id=1, source_target_pairs={{0,32},{8,40},{16,48},{24,56},{32,0},{40,8},{48,16},{56,24},{64,96... | collective-permute-start | bytes 786440 | tf_op jit(solution)/shard_map/ppermute | solution.py:284
  61.0 10.5 %collective-permute-start.17 = (bf16[4,2,128,128]{3,2,1,0:T(8,128)(2,1)S(1)}, bf16[4,2,128,128]{3,2,1,0:T(8,128)(2,1)S(1)}, u32[]{:S(2)}, u32[]{:S(2)}) collective-permute-start(bf16[4,2,128,128]{3,2,1,0:T(8,128)(2,1)S(1)} %pad_maximum_fusion.1.refs_5_), channel_id=1, source_target_pairs={{0,16},{8,24},{16,32},{24,40},{32,48},{40,56},{48,0},{56,8},{64,80... | collective-permute-start | bytes 786440 | tf_op jit(solution)/shard_map/ppermute | solution.py:284
  (7 other events, 8.7 us)

commit v3 on v2

v3 whole, which is shorter than its diff:
```python
import math

import jax
import jax.numpy as jnp
from jax import lax
from jax.experimental import pallas as pl
from jax.experimental.pallas import tpu as pltpu
from jax.sharding import PartitionSpec as P

ROWS = 128
HEAD = 128
GROUP = 4
WIDTH = 512
BLOCK = 32
LAST = 31
LOW = -1e30
FAR = 1e6
POWER = math.log2(math.e) / math.sqrt(HEAD)
LIMIT = 48 * 1024 * 1024
F32 = jnp.float32
BF16 = jnp.bfloat16


def ctx_pairs(dy, dx, dz):
    pairs = []
    for i in range(32):
        y, x, z = i // 8, (i // 2) % 4, i % 2
        pairs.append((i, (((y + dy) % 4) * 4 + (x + dx) % 4) * 2 + (z + dz) % 2))
    return pairs


def kv_pairs(dz, dc):
    pairs = []
    for i in range(8):
        z, c = i // 2, i % 2
        pairs.append((i, ((z + dz) % 4) * 2 + (c + dc) % 2))
    return pairs


def dot(a, b):
    return jnp.dot(a, b, preferred_element_type=F32)


def dot_t(a, b):
    return lax.dot_general(a, b, (((1,), (1,)), ((), ())), preferred_element_type=F32)


def call(kernel, outs, args, cost, scratch=()):
    spec = pl.BlockSpec(memory_space=pltpu.VMEM)
    return pl.pallas_call(
        kernel,
        out_shape=[jax.ShapeDtypeStruct(s, t) for s, t in outs],
        in_specs=[spec] * len(args),
        out_specs=[spec] * len(outs),
        scratch_shapes=list(scratch),
        compiler_params=pltpu.CompilerParams(vmem_limit_bytes=LIMIT),
        cost_estimate=pl.CostEstimate(flops=cost[0], bytes_accessed=cost[1], transcendentals=0),
    )(*args)


def column(row):
    square = (ROWS, ROWS)
    same = lax.broadcasted_iota(jnp.int32, square, 0) == lax.broadcasted_iota(jnp.int32, square, 1)
    return jnp.sum(jnp.where(same, jnp.broadcast_to(row, square), 0.0), axis=1, keepdims=True)


def mask_kernel(ids_ref, order_ref, cut_ref, embed_ref, wq_ref, wk_ref, wv_ref, flag_ref, code_ref, mq_ref, mkv_ref):
    code_ref[...] = jnp.broadcast_to(ids_ref[...] * 32 + order_ref[...], (8, ROWS))
    ids = column(ids_ref[...].astype(F32))
    order = column(order_ref[...].astype(F32))
    blocks = cut_ref.shape[1]
    spots = lax.broadcasted_iota(jnp.int32, (ROWS, blocks), 1).astype(F32)
    cuts = jnp.broadcast_to(cut_ref[...].astype(F32), (ROWS, blocks))
    cut = jnp.sum(jnp.where(spots == ids, cuts, 0.0), axis=1, keepdims=True)
    flag_ref[...] = jnp.broadcast_to(jnp.where(order >= cut, 1.0, 0.0), (ROWS, HEAD))
    embed = jnp.broadcast_to(embed_ref[...], (16, embed_ref.shape[1]))
    mq_ref[...] = dot(embed, wq_ref[...]).astype(BF16)
    mkv_ref[:, :HEAD] = dot(embed, wk_ref[...]).astype(BF16)
    mkv_ref[:, HEAD:] = dot(embed, wv_ref[...]).astype(BF16)


def kv_kernel(*refs):
    pieces = refs[:8]
    wk_ref, wv_ref, flag_ref, mkv_ref = refs[8:12]
    x_ref, kv_ref, kvn_ref = refs[12:]
    me = lax.axis_index("kv")
    for dz in range(4):
        for dc in range(2):
            source = lax.rem(me // 2 + 4 - dz, 4) * 2 + lax.rem(me + dc, 2)
            x_ref[:, pl.ds(pl.multiple_of(source * WIDTH, WIDTH), WIDTH)] = pieces[2 * dz + dc][...]
    x = x_ref[...]
    masked = flag_ref[...] > 0.5
    for part, w_ref in enumerate((wk_ref, wv_ref)):
        lanes = slice(part * HEAD, (part + 1) * HEAD)
        clean = dot(x, w_ref[...])
        fixed = jnp.broadcast_to(mkv_ref[0:1, lanes].astype(F32), (ROWS, HEAD))
        kv_ref[:, lanes] = clean.astype(BF16)
        kvn_ref[:, lanes] = jnp.where(masked, fixed, clean).astype(BF16)


def q_kernel(x_ref, wq_ref, flag_ref, mq_ref, q_ref):
    masked = flag_ref[...] > 0.5
    x = x_ref[...]
    for h in range(GROUP):
        lanes = slice(h * HEAD, (h + 1) * HEAD)
        clean = dot(x, wq_ref[:, lanes])
        fixed = jnp.broadcast_to(mq_ref[0:1, lanes].astype(F32), (ROWS, HEAD))
        q_ref[h, :ROWS, :] = clean.astype(BF16)
        q_ref[h, ROWS:, :] = jnp.where(masked, fixed, clean).astype(BF16)


def near_kernel(q_ref, kv_ref, kvn_ref, ids_ref, top_ref, total_ref, accum_ref):
    row = ids_ref[...].astype(F32)
    query = jnp.broadcast_to(column(row), (ROWS, ROWS))
    key = jnp.broadcast_to(row, (ROWS, ROWS))
    zero = jnp.zeros((ROWS, ROWS), F32)
    low = jnp.full((ROWS, ROWS), LOW, F32)
    clean_bias = jnp.concatenate([jnp.where(key <= query, zero, low), low], axis=1)
    noisy_bias = jnp.concatenate([jnp.where(key < query, zero, low), jnp.where(key == query, zero, low)], axis=1)
    bias = jnp.concatenate([clean_bias, noisy_bias], axis=0)
    keys = jnp.concatenate([kv_ref[:, :HEAD], kvn_ref[:, :HEAD]], axis=0)
    values = jnp.concatenate([kv_ref[:, HEAD:], kvn_ref[:, HEAD:]], axis=0)
    for h in range(GROUP):
        scores = jnp.where(bias < -1.0, LOW, dot_t(q_ref[h], keys))
        top = jnp.max(scores, axis=1, keepdims=True)
        probs = jnp.exp2((scores - top) * POWER)
        top_ref[h] = jnp.broadcast_to(top, (2 * ROWS, HEAD))
        total_ref[h] = probs[:, :HEAD] + probs[:, HEAD:]
        accum_ref[h] = dot(probs.astype(BF16), values)


def far_kernel(*refs):
    q_ref = refs[0]
    k_refs, v_refs = refs[1:5], refs[5:9]
    top_in, total_in, accum_in = refs[9:12]
    ids_ref, code_ref, up_ref, down_ref, cut_ref, mkv_ref = refs[12:18]
    clean_ref, noisy_ref = refs[18:20]
    top_ref, total_ref, accum_ref = refs[20:]
    me = lax.axis_index("ctx")
    y, x, z = me // 8, lax.rem(me // 2, 4), lax.rem(me, 2)

    hop = jnp.where(z == 0, 1, 0)
    wrap = (z == 0) & (x == 0)
    old_y = jnp.where(wrap, 1, 0)
    step = jnp.where(z == 0, 0, 3)
    beyond = (z == 1) & (x == 3)
    new_y = jnp.where(beyond, 3, 0)
    k_old = jnp.where(wrap, k_refs[1][hop, 1], k_refs[0][hop, 1])
    v_old = jnp.where(z == 0, v_refs[1][old_y, 1], v_refs[0][old_y, 1])
    k_new = jnp.where(beyond, k_refs[3][step, 1], k_refs[0][step, 1])[:BLOCK]
    v_new = jnp.where(z == 0, v_refs[0][new_y, 1], v_refs[3][new_y, 1])[:BLOCK]

    code = code_ref[...]
    own = (code // 32).astype(F32)
    old_ids = jnp.where(me > 0, (up_ref[...] // 32).astype(F32), FAR)
    new_ids = jnp.where(me < LAST, (down_ref[...] // 32).astype(F32), FAR)
    old_order = lax.rem(up_ref[...], 32).astype(F32)
    new_order = lax.rem(down_ref[...], 32).astype(F32)
    blocks = cut_ref.shape[1]
    spots = lax.broadcasted_iota(jnp.int32, (8, blocks), 1).astype(F32)
    cuts = jnp.broadcast_to(cut_ref[...].astype(F32), (8, blocks))
    first_cut = jnp.sum(jnp.where(spots == own[:, 0:1], cuts, 0.0), axis=1, keepdims=True)
    last_cut = jnp.sum(jnp.where(spots == own[:, ROWS - 1 : ROWS], cuts, 0.0), axis=1, keepdims=True)
    old_masked = column(jnp.where(old_order >= first_cut, 1.0, 0.0)[0:1])[ROWS - BLOCK :]
    new_masked = column(jnp.where(new_order >= last_cut, 1.0, 0.0)[0:1])[:BLOCK]

    def noisy(masked, clean, lanes):
        fixed = jnp.broadcast_to(mkv_ref[0:1, lanes].astype(F32), clean.shape)
        flag = jnp.broadcast_to(masked, clean.shape) > 0.5
        return jnp.where(flag, fixed, clean.astype(F32)).astype(BF16)

    def rim(old, new, lanes):
        parts = [old, new, noisy(old_masked, old[ROWS - BLOCK :], lanes), noisy(new_masked, new, lanes)]
        return jnp.concatenate(parts + [jnp.zeros((BLOCK, HEAD), BF16)], axis=0)

    k_rim = rim(k_old, k_new, slice(0, HEAD))
    v_rim = rim(v_old, v_new, slice(HEAD, 2 * HEAD))
    lane = lax.broadcasted_iota(jnp.int32, (8, ROWS), 1)
    mixed = jnp.where(
        lane < 32,
        new_ids,
        jnp.where(lane < 64, pltpu.roll(old_ids, 64, 1), jnp.where(lane < 96, pltpu.roll(new_ids, 64, 1), -5.0)),
    )
    square = (ROWS, ROWS)
    query = jnp.broadcast_to(column(own[0:1]), square)
    old_key = jnp.broadcast_to(old_ids[0:1], square)
    mixed_key = jnp.broadcast_to(mixed[0:1], square)
    early = lax.broadcasted_iota(jnp.int32, square, 1) < 32
    zero = jnp.zeros(square, F32)
    low = jnp.full(square, LOW, F32)
    clean_bias = [
        jnp.where(old_key <= query, zero, low),
        jnp.where(early, jnp.where(mixed_key <= query, zero, low), low),
    ]
    noisy_bias = [
        jnp.where(old_key < query, zero, low),
        jnp.where(early, jnp.where(mixed_key < query, zero, low), jnp.where(mixed_key == query, zero, low)),
    ]
    bias = jnp.concatenate([jnp.concatenate(clean_bias, axis=1), jnp.concatenate(noisy_bias, axis=1)], axis=0)

    def scores_of(step):
        dy, h = step
        if dy < 0:
            return jnp.where(bias < -1.0, LOW, dot_t(q_ref[h], k_rim))
        return dot_t(q_ref[h], k_refs[dy][...].reshape(8 * ROWS, HEAD))

    def absorb(step, scores):
        dy, h = step
        parts = [scores[:, j : j + ROWS] for j in range(0, scores.shape[1], ROWS)]
        if dy in (0, 1):
            for j in range(8):
                there = lax.rem(y + 4 - dy, 4) * 8 + lax.rem(x + 4 - j // 2, 4) * 2 + lax.rem(z + j, 2)
                parts[j] = jnp.where(there < me - 1, parts[j], LOW)
        best = parts[0]
        for part in parts[1:]:
            best = jnp.maximum(best, part)
        best = jnp.max(best, axis=1, keepdims=True)
        if dy > 1:
            best = jnp.where(y >= dy, best, LOW)
        old = top_in[h] if dy < 0 else top_ref[h]
        top = jnp.maximum(old, best)
        factor = jnp.exp2((old - top) * POWER)
        level = jnp.where(y >= dy, top, -LOW) if dy > 1 else top
        probs = [jnp.exp2((part - level) * POWER) for part in parts]
        total = (total_in[h] if dy < 0 else total_ref[h]) * factor
        for part in probs:
            total = total + part
        if dy < 0:
            values = v_rim
        else:
            values = jnp.concatenate([v_refs[dx][dy].reshape(2 * ROWS, HEAD) for dx in range(4)], axis=0)
        probs = jnp.concatenate([part.astype(BF16) for part in probs], axis=1)
        accum = (accum_in[h] if dy < 0 else accum_ref[h]) * factor + dot(probs, values)
        if dy < 3:
            top_ref[h] = top
            total_ref[h] = total
            accum_ref[h] = accum
            return
        lanes = slice(h * HEAD, (h + 1) * HEAD)
        result = (accum / jnp.sum(total, axis=1, keepdims=True)).astype(BF16)
        clean_ref[:, lanes] = result[:ROWS]
        noisy_ref[:, lanes] = result[ROWS:]

    steps = [(dy, h) for dy in (-1, 0, 1, 2, 3) for h in range(GROUP)]
    scores = scores_of(steps[0])
    for now, later in zip(steps, steps[1:] + [None]):
        following = None if later is None else scores_of(later)
        absorb(now, scores)
        scores = following


def shards(hidden, block_ids, decode_order, step_cut, mask_embed, q_weight, k_weight, v_weight):
    ids = block_ids.reshape(1, ROWS)
    order = decode_order.reshape(1, ROWS)
    cuts = step_cut.reshape(1, -1)
    flag, code, mask_q, mask_kv = call(
        mask_kernel,
        [((ROWS, HEAD), F32), ((8, ROWS), jnp.int32), ((16, GROUP * HEAD), BF16), ((16, 2 * HEAD), BF16)],
        [ids, order, cuts, mask_embed.reshape(1, -1), q_weight, k_weight, v_weight],
        (1 << 28, 6 << 20),
    )
    moved = [lax.ppermute(hidden, "kv", kv_pairs(d, 0)) for d in (1, 2, 3)]
    count = 32
    up = lax.ppermute(code, "ctx", [(i, (i + 1) % count) for i in range(count)])
    down = lax.ppermute(code, "ctx", [(i, (i - 1) % count) for i in range(count)])
    flag, code, mask_q, mask_kv, up, down = lax.optimization_barrier((flag, code, mask_q, mask_kv, up, down))
    pieces = [hidden, lax.ppermute(hidden, "kv", kv_pairs(0, 1))]
    for piece in moved:
        piece, _, _ = lax.optimization_barrier((piece, up, flag))
        pieces += [piece, lax.ppermute(piece, "kv", kv_pairs(0, 1))]
    x, kv, kv_noisy = call(
        kv_kernel,
        [((ROWS, 8 * WIDTH), BF16), ((ROWS, 2 * HEAD), BF16), ((ROWS, 2 * HEAD), BF16)],
        [*pieces, k_weight, v_weight, flag, mask_kv],
        (1 << 29, 3 << 20),
    )
    pair = lax.ppermute(kv, "ctx", ctx_pairs(0, 0, 1))
    k = jnp.stack([kv[:, :HEAD], pair[:, :HEAD]])
    v = jnp.stack([kv[:, HEAD:], pair[:, HEAD:]])
    ks = jnp.stack([k] + [lax.ppermute(k, "ctx", ctx_pairs(0, d, 0)) for d in (1, 2, 3)])
    vs = jnp.stack([v] + [lax.ppermute(v, "ctx", ctx_pairs(d, 0, 0)) for d in (1, 2, 3)])
    (q,) = call(
        q_kernel,
        [((GROUP, 2 * ROWS, HEAD), BF16)],
        [x, q_weight, flag, mask_q],
        (1 << 30, 5 << 20),
    )
    near = call(
        near_kernel,
        [((GROUP, 2 * ROWS, HEAD), F32)] * 3,
        [q, kv, kv_noisy, ids],
        (1 << 30, 2 << 20),
    )
    all_k = [ks] + [lax.ppermute(ks, "ctx", ctx_pairs(d, 0, 0)) for d in (1, 2, 3)]
    all_v = [vs] + [lax.ppermute(vs, "ctx", ctx_pairs(0, d, 0)) for d in (1, 2, 3)]
    return tuple(
        call(
            far_kernel,
            [((ROWS, GROUP * HEAD), BF16)] * 2,
            [q, *all_k, *all_v, *near, ids, code, up, down, cuts, mask_kv],
            (1 << 32, 4 << 20),
            [pltpu.VMEM((GROUP, 2 * ROWS, HEAD), F32)] * 3,
        )
    )


def solution(mesh):
    return jax.shard_map(
        shards,
        mesh=mesh,
        in_specs=(
            P("ctx", "kv"),
            P("ctx"),
            P("ctx"),
            P(),
            P(),
            P(None, "kv"),
            P(None, "kv"),
            P(None, "kv"),
        ),
        out_specs=(P("ctx", "kv"), P("ctx", "kv")),
        check_vma=False,
    )
```

time: 81 us -> 81 us (level)
  waiting for transfers between devices: 23.8 us -> 29.1 us
  starting transfers between devices: 34.1 us -> 30 us
  Pallas kernels: 15.4 us -> 13.4 us
    ppermute x3, waiting for transfers between devices: 1.86 us -> 6.41 us  [shards(): lax.ppermute(v, 'ctx', ctx_pairs(d, 0, 0))]
    ppermute x3, starting transfers between devices: 3.44 us -> 6.83 us  [shards(): lax.ppermute(v, 'ctx', ctx_pairs(d, 0, 0))]
    ppermute x3, starting transfers between devices: 6.35 us -> 3.41 us  [shards(): lax.ppermute(k, 'ctx', ctx_pairs(0, d, 0))]
    ppermute x3, starting transfers between devices: 3.36 us -> 0.62 us  [shards(): lax.ppermute(ks, 'ctx', ctx_pairs(d, 0, 0))]
    ppermute x5 -> x6, waiting for transfers between devices: 9.03 us -> 6.62 us  [the longest x1 5.28 us: shards(): up = lax.ppermute(code, 'ctx', [(i, (i + 1) % count) for i in range(count)])]
    pallas_call x5, Pallas kernels: 15.4 us -> 13.4 us  [call(): pl.pallas_call(kernel, out_shape=[jax.ShapeDtypeStruct(s, t) for s, t in...]
    ppermute x5 -> x6, starting transfers between devices: 16.1 us -> 14.9 us  [the longest x3 11.4 us: shards(): moved = [lax.ppermute(hidden, 'kv', kv_pairs(d, 0)) for d in (1, 2, 3)]]
    ppermute x4 -> x3, waiting for transfers between devices: 0.02 us -> 1.25 us  [shards(): pieces += [piece, lax.ppermute(piece, 'kv', kv_pairs(0, 1))]]
  transfers between devices with their start and end apart: 22 -> 22, of which waited for: 11 -> 13; matrix products, arithmetic and copies ran while one was open for 1% -> 1% of each run, Pallas kernels for 7% -> 7%
where the time goes in v3:
time: 81 us; the launch traced here: 79.4 us
  starting transfers between devices  30 us (37%)
  waiting for transfers between devices  29.1 us (36%)
  Pallas kernels  13.4 us (17%)
  local copies, waits for them, and re-layouts  6.08 us (8%)
    pallas_call x5, Pallas kernels, call(): pl.pallas_call(kernel, out_shape=[jax.ShapeDtypeStruct(s, t) for s, t in...  13.4 us
    ppermute x3, starting transfers between devices, shards(): moved = [lax.ppermute(hidden, 'kv', kv_pairs(d, 0)) for d in (1, 2, 3)]  11.4 us
    ppermute x3, waiting for transfers between devices, shards(): lax.ppermute(vs, 'ctx', ctx_pairs(0, d, 0))  6.98 us
    ppermute x3, starting transfers between devices, shards(): lax.ppermute(v, 'ctx', ctx_pairs(d, 0, 0))  6.83 us
    ppermute x3, waiting for transfers between devices, shards(): lax.ppermute(v, 'ctx', ctx_pairs(d, 0, 0))  6.41 us
    unnamed x22, local copies, waits for them, and re-layouts  5.36 us
    ppermute x1, waiting for transfers between devices, shards(): up = lax.ppermute(code, 'ctx', [(i, (i + 1) % count) for i in range(count)])  5.28 us
    ppermute x1, waiting for transfers between devices, shards(): pair = lax.ppermute(kv, 'ctx', ctx_pairs(0, 0, 1))  4.24 us
  transfers between devices with their start and end apart: 22, of which 13 were waited for; matrix products, arithmetic and copies ran while one was open for 1% of the time, Pallas kernels for 7%

profile of v3, /device:TPU:24, one launch (start us, length us, event | category | flops | bytes accessed | tf_op | source)
XLA Modules:
  0.0 79.4 jit_solution(3199972210219985664)
XLA Ops:
  0.6 7.3 %collective-permute-start.5 = (bf16[128,512]{1,0:T(8,128)(2,1)}, bf16[128,512]{1,0:T(8,128)(2,1)S(1)}, u32[]{:S(2)}, u32[]{:S(2)}) collective-permute-start(bf16[128,512]{1,0:T(8,128)(2,1)} %refs_0_.1), channel_id=1, source_target_pairs={{0,4},{1,5},{2,6},{3,7},{4,0},{5,1},{6,2},{7,3},{8,12},{9,13},{10,... | collective-permute-start | bytes 393224 | tf_op jit(solution)/shard_map/ppermute | solution.py:262
  7.9 1.5 %collective-permute-start.1 = (bf16[128,512]{1,0:T(8,128)(2,1)}, bf16[128,512]{1,0:T(8,128)(2,1)S(1)}, u32[]{:S(2)}, u32[]{:S(2)}) collective-permute-start(bf16[128,512]{1,0:T(8,128)(2,1)} %refs_0_.1), channel_id=1, source_target_pairs={{0,2},{1,3},{2,4},{3,5},{4,6},{5,7},{6,0},{7,1},{8,10},{9,11},{10,... | collective-permute-start | bytes 393224 | tf_op jit(solution)/shard_map/ppermute | solution.py:262
  9.4 2.7 %collective-permute-start.7 = (bf16[128,512]{1,0:T(8,128)(2,1)}, bf16[128,512]{1,0:T(8,128)(2,1)S(1)}, u32[]{:S(2)}, u32[]{:S(2)}) collective-permute-start(bf16[128,512]{1,0:T(8,128)(2,1)} %refs_0_.1), channel_id=1, source_target_pairs={{0,6},{1,7},{2,0},{3,1},{4,2},{5,3},{6,4},{7,5},{8,14},{9,15},{10,... | collective-permute-start | bytes 393224 | tf_op jit(solution)/shard_map/ppermute | solution.py:262
  12.8 1.2 %copy-done.1 = bf16[4096,128]{1,0:T(8,128)(2,1)S(1)} copy-done((bf16[4096,128]{1,0:T(8,128)(2,1)S(1)}, bf16[4096,128]{1,0:T(8,128)(2,1)}, u32[]{:S(2)}) %copy-start.1) | copy-done | bytes 1048600
  14.0 1.2 %copy-done.3 = bf16[4096,128]{1,0:T(8,128)(2,1)S(1)} copy-done((bf16[4096,128]{1,0:T(8,128)(2,1)S(1)}, bf16[4096,128]{1,0:T(8,128)(2,1)}, u32[]{:S(2)}) %copy-start.3) | copy-done | bytes 1048600
  17.2 3.3 %shard_map.95 = (f32[128,128]{1,0:T(8,128)S(1)}, s32[8,128]{1,0:T(8,128)S(1)}, bf16[16,512]{1,0:T(8,128)(2,1)S(1)}, bf16[16,256]{1,0:T(8,128)(2,1)S(1)}) custom-call(s32[1,128]{1,0:T(1,128)S(1)} %bitcast.24, s32[1,128]{1,0:T(1,128)S(1)} %bitcast.23, s32[1,256]{1,0:T(1,128)S(1)} %bitcast.21, bf16[1,4096]{1,0:T(2,128)(2,1)S(1)} %reshape.19.embed_ref, ...), custom_call_target="tpu_custom_call" | custom-call | flops 268435456 | bytes 6291456 | tf_op jit(solution)/shard_map/pallas_call | solution.py:50
  20.5 3.5 %collective-permute-start.3 = (s32[8,128]{1,0:T(8,128)S(1)}, s32[8,128]{1,0:T(8,128)S(1)}, u32[]{:S(2)}, u32[]{:S(2)}) collective-permute-start(s32[8,128]{1,0:T(8,128)S(1)} %get-tuple-element.38.refs_13_), channel_id=1, source_target_pairs={{0,248},{8,0},{16,8},{24,16},{32,24},{40,32},{48,40},{56,48},{64,5... | collective-permute-start | bytes 12296 | tf_op jit(solution)/shard_map/ppermute | solution.py:265
  23.9 1.3 %collective-permute-done.3.refs_15_ = s32[8,128]{1,0:T(8,128)S(1)} collective-permute-done((s32[8,128]{1,0:T(8,128)S(1)}, s32[8,128]{1,0:T(8,128)S(1)}, u32[]{:S(2)}, u32[]{:S(2)}) %collective-permute-start.3) | collective-permute-done | bytes 4128 | tf_op jit(solution)/shard_map/ppermute | solution.py:265
  25.3 5.3 %collective-permute-done.2.refs_14_ = s32[8,128]{1,0:T(8,128)S(1)} collective-permute-done((s32[8,128]{1,0:T(8,128)S(1)}, s32[8,128]{1,0:T(8,128)S(1)}, u32[]{:S(2)}, u32[]{:S(2)}) %collective-permute-start.2) | collective-permute-done | bytes 4128 | tf_op jit(solution)/shard_map/ppermute | solution.py:264
  32.4 0.9 %copy-done.5 = bf16[128,512]{1,0:T(8,128)(2,1)S(1)} copy-done((bf16[128,512]{1,0:T(8,128)(2,1)S(1)}, bf16[128,512]{1,0:T(8,128)(2,1)}, u32[]{:S(2)}) %copy-start.5) | copy-done | bytes 131096
  34.2 4.2 %collective-permute-done.9 = bf16[128,256]{1,0:T(8,128)(2,1)S(1)} collective-permute-done((bf16[128,256]{1,0:T(8,128)(2,1)S(1)}, bf16[128,256]{1,0:T(8,128)(2,1)S(1)}, u32[]{:S(2)}, u32[]{:S(2)}) %collective-permute-start.9) | collective-permute-done | bytes 65568 | tf_op jit(solution)/shard_map/ppermute | solution.py:277
  38.6 0.9 %collective-permute-start.10 = (bf16[2,128,128]{2,1,0:T(8,128)(2,1)S(1)}, bf16[2,128,128]{2,1,0:T(8,128)(2,1)S(1)}, u32[]{:S(2)}, u32[]{:S(2)}) collective-permute-start(bf16[2,128,128]{2,1,0:T(8,128)(2,1)S(1)} %get-tuple-element.47), channel_id=1, source_target_pairs={{0,16},{8,24},{16,32},{24,40},{32,48},{40,56},{48,0},{56,8},{64,80... | collective-permute-start | bytes 196616 | tf_op jit(solution)/shard_map/ppermute | solution.py:280
  39.5 2.4 %collective-permute-start.12 = (bf16[2,128,128]{2,1,0:T(8,128)(2,1)S(1)}, bf16[2,128,128]{2,1,0:T(8,128)(2,1)S(1)}, u32[]{:S(2)}, u32[]{:S(2)}) collective-permute-start(bf16[2,128,128]{2,1,0:T(8,128)(2,1)S(1)} %get-tuple-element.47), channel_id=1, source_target_pairs={{0,48},{8,56},{16,0},{24,8},{32,16},{40,24},{48,32},{56,40},{64,11... | collective-permute-start | bytes 196616 | tf_op jit(solution)/shard_map/ppermute | solution.py:280
  41.9 2.5 %collective-permute-done.11 = bf16[2,128,128]{2,1,0:T(8,128)(2,1)S(1)} collective-permute-done((bf16[2,128,128]{2,1,0:T(8,128)(2,1)S(1)}, bf16[2,128,128]{2,1,0:T(8,128)(2,1)S(1)}, u32[]{:S(2)}, u32[]{:S(2)}) %collective-permute-start.11) | collective-permute-done | bytes 65568 | tf_op jit(solution)/shard_map/ppermute | solution.py:280
  45.4 4.8 %collective-permute-start.17 = (bf16[2,128,128]{2,1,0:T(8,128)(2,1)S(1)}, bf16[2,128,128]{2,1,0:T(8,128)(2,1)S(1)}, u32[]{:S(2)}, u32[]{:S(2)}) collective-permute-start(bf16[2,128,128]{2,1,0:T(8,128)(2,1)S(1)} %get-tuple-element.41), channel_id=1, source_target_pairs={{0,128},{8,136},{16,144},{24,152},{32,160},{40,168},{48,176},{56,1... | collective-permute-start | bytes 196616 | tf_op jit(solution)/shard_map/ppermute | solution.py:281
  50.2 2.0 %collective-permute-start.18 = (bf16[2,128,128]{2,1,0:T(8,128)(2,1)S(1)}, bf16[2,128,128]{2,1,0:T(8,128)(2,1)S(1)}, u32[]{:S(2)}, u32[]{:S(2)}) collective-permute-start(bf16[2,128,128]{2,1,0:T(8,128)(2,1)S(1)} %get-tuple-element.41), channel_id=1, source_target_pairs={{0,192},{8,200},{16,208},{24,216},{32,224},{40,232},{48,240},{56,2... | collective-permute-start | bytes 196616 | tf_op jit(solution)/shard_map/ppermute | solution.py:281
  52.4 6.4 %collective-permute-done.17 = bf16[2,128,128]{2,1,0:T(8,128)(2,1)S(1)} collective-permute-done((bf16[2,128,128]{2,1,0:T(8,128)(2,1)S(1)}, bf16[2,128,128]{2,1,0:T(8,128)(2,1)S(1)}, u32[]{:S(2)}, u32[]{:S(2)}) %collective-permute-start.17) | collective-permute-done | bytes 65568 | tf_op jit(solution)/shard_map/ppermute | solution.py:281
  58.8 2.6 %collective-permute-start.21 = (bf16[4,2,128,128]{3,2,1,0:T(8,128)(2,1)S(1)}, bf16[4,2,128,128]{3,2,1,0:T(8,128)(2,1)S(1)}, u32[]{:S(2)}, u32[]{:S(2)}) collective-permute-start(bf16[4,2,128,128]{3,2,1,0:T(8,128)(2,1)S(1)} %pad_maximum_fusion.1.refs_5_), channel_id=1, source_target_pairs={{0,48},{8,56},{16,0},{24,8},{32,16},{40,24},{48,32},{56,40},{64,11... | collective-permute-start | bytes 786440 | tf_op jit(solution)/shard_map/ppermute | solution.py:295
  61.4 0.9 %collective-permute-start.20 = (bf16[4,2,128,128]{3,2,1,0:T(8,128)(2,1)S(1)}, bf16[4,2,128,128]{3,2,1,0:T(8,128)(2,1)S(1)}, u32[]{:S(2)}, u32[]{:S(2)}) collective-permute-start(bf16[4,2,128,128]{3,2,1,0:T(8,128)(2,1)S(1)} %pad_maximum_fusion.1.refs_5_), channel_id=1, source_target_pairs={{0,32},{8,40},{16,48},{24,56},{32,0},{40,8},{48,16},{56,24},{64,96... | collective-permute-start | bytes 786440 | tf_op jit(solution)/shard_map/ppermute | solution.py:295
  62.4 1.3 %shard_map.97.q_ref.refs_0_ = bf16[4,256,128]{2,1,0:T(8,128)(2,1)S(1)} custom-call(bf16[128,4096]{1,0:T(8,128)(2,1)S(1)} %get-tuple-element.31.x_ref, bf16[4096,512]{1,0:T(8,128)(2,1)S(1)} %copy-done, f32[128,128]{1,0:T(8,128)S(1)} %get-tuple-element.26.refs_10_.flag_ref, bf16[16,512]{1,0:T(8,128)(2,1)S(1)} %get-tuple-element.32.mq_ref), custom_call_target="tpu_custom_call" | custom-call | flops 1073741824 | bytes 5242880 | tf_op jit(solution)/shard_map/pallas_call | solution.py:50
  65.1 3.0 %collective-permute-done.21.refs_8_ = bf16[4,2,128,128]{3,2,1,0:T(8,128)(2,1)S(1)} collective-permute-done((bf16[4,2,128,128]{3,2,1,0:T(8,128)(2,1)S(1)}, bf16[4,2,128,128]{3,2,1,0:T(8,128)(2,1)S(1)}, u32[]{:S(2)}, u32[]{:S(2)}) %collective-permute-start.21) | collective-permute-done | bytes 262176 | tf_op jit(solution)/shard_map/ppermute | solution.py:295
  68.2 1.2 %collective-permute-done.20.refs_7_ = bf16[4,2,128,128]{3,2,1,0:T(8,128)(2,1)S(1)} collective-permute-done((bf16[4,2,128,128]{3,2,1,0:T(8,128)(2,1)S(1)}, bf16[4,2,128,128]{3,2,1,0:T(8,128)(2,1)S(1)}, u32[]{:S(2)}, u32[]{:S(2)}) %collective-permute-start.20) | collective-permute-done | bytes 262176 | tf_op jit(solution)/shard_map/ppermute | solution.py:295
  69.4 2.7 %collective-permute-done.19.refs_6_ = bf16[4,2,128,128]{3,2,1,0:T(8,128)(2,1)S(1)} collective-permute-done((bf16[4,2,128,128]{3,2,1,0:T(8,128)(2,1)S(1)}, bf16[4,2,128,128]{3,2,1,0:T(8,128)(2,1)S(1)}, u32[]{:S(2)}, u32[]{:S(2)}) %collective-permute-start.19) | collective-permute-done | bytes 262176 | tf_op jit(solution)/shard_map/ppermute | solution.py:295
  72.1 7.3 %shard_map.99 = (bf16[128,512]{1,0:T(8,128)(2,1)}, bf16[128,512]{1,0:T(8,128)(2,1)}) custom-call(bf16[4,256,128]{2,1,0:T(8,128)(2,1)S(1)} %shard_map.97.q_ref.refs_0_, bf16[4,2,128,128]{3,2,1,0:T(8,128)(2,1)S(1)} %pad_maximum_fusion.refs_1_, bf16[4,2,128,128]{3,2,1,0:T(8,128)(2,1)S(1)} %collective-permute-done.13.refs_2_, ...), custom_call_target="tpu_custom_call" | custom-call | flops 4294967296 | bytes 4194304 | tf_op jit(solution)/shard_map/pallas_call | solution.py:50
  (54 shorter events, 8.2 us)
Async XLA Ops:
  0.6 29.9 %collective-permute-start.5 = (bf16[128,512]{1,0:T(8,128)(2,1)}, bf16[128,512]{1,0:T(8,128)(2,1)S(1)}, u32[]{:S(2)}, u32[]{:S(2)}) collective-permute-start(bf16[128,512]{1,0:T(8,128)(2,1)} %refs_0_.1), channel_id=1, source_target_pairs={{0,4},{1,5},{2,6},{3,7},{4,0},{5,1},{6,2},{7,3},{8,12},{9,13},{10,... | collective-permute-start | bytes 393224 | tf_op jit(solution)/shard_map/ppermute | solution.py:262
  7.9 22.6 %collective-permute-start.1 = (bf16[128,512]{1,0:T(8,128)(2,1)}, bf16[128,512]{1,0:T(8,128)(2,1)S(1)}, u32[]{:S(2)}, u32[]{:S(2)}) collective-permute-start(bf16[128,512]{1,0:T(8,128)(2,1)} %refs_0_.1), channel_id=1, source_target_pairs={{0,2},{1,3},{2,4},{3,5},{4,6},{5,7},{6,0},{7,1},{8,10},{9,11},{10,... | collective-permute-start | bytes 393224 | tf_op jit(solution)/shard_map/ppermute | solution.py:262
  9.4 21.7 %collective-permute-start.7 = (bf16[128,512]{1,0:T(8,128)(2,1)}, bf16[128,512]{1,0:T(8,128)(2,1)S(1)}, u32[]{:S(2)}, u32[]{:S(2)}) collective-permute-start(bf16[128,512]{1,0:T(8,128)(2,1)} %refs_0_.1), channel_id=1, source_target_pairs={{0,6},{1,7},{2,0},{3,1},{4,2},{5,3},{6,4},{7,5},{8,14},{9,15},{10,... | collective-permute-start | bytes 393224 | tf_op jit(solution)/shard_map/ppermute | solution.py:262
  17.2 45.2 %copy-start = (bf16[4096,512]{1,0:T(8,128)(2,1)S(1)}, bf16[4096,512]{1,0:T(8,128)(2,1)}, u32[]{:S(2)}) copy-start(bf16[4096,512]{1,0:T(8,128)(2,1)} %wq_ref.3) | copy-start | bytes 12582916
  20.5 4.8 %collective-permute-start.3 = (s32[8,128]{1,0:T(8,128)S(1)}, s32[8,128]{1,0:T(8,128)S(1)}, u32[]{:S(2)}, u32[]{:S(2)}) collective-permute-start(s32[8,128]{1,0:T(8,128)S(1)} %get-tuple-element.38.refs_13_), channel_id=1, source_target_pairs={{0,248},{8,0},{16,8},{24,16},{32,24},{40,32},{48,40},{56,48},{64,5... | collective-permute-start | bytes 12296 | tf_op jit(solution)/shard_map/ppermute | solution.py:265
  23.9 6.6 %collective-permute-start.2 = (s32[8,128]{1,0:T(8,128)S(1)}, s32[8,128]{1,0:T(8,128)S(1)}, u32[]{:S(2)}, u32[]{:S(2)}) collective-permute-start(s32[8,128]{1,0:T(8,128)S(1)} %get-tuple-element.38.refs_13_), channel_id=1, source_target_pairs={{0,8},{8,16},{16,24},{24,32},{32,40},{40,48},{48,56},{56,64},{64,7... | collective-permute-start | bytes 12296 | tf_op jit(solution)/shard_map/ppermute | solution.py:264
  25.2 5.9 %collective-permute-start = (bf16[128,512]{1,0:T(8,128)(2,1)}, bf16[128,512]{1,0:T(8,128)(2,1)S(1)}, u32[]{:S(2)}, u32[]{:S(2)}) collective-permute-start(bf16[128,512]{1,0:T(8,128)(2,1)} %refs_0_.1), channel_id=1, source_target_pairs={{0,1},{1,0},{2,3},{3,2},{4,5},{5,4},{6,7},{7,6},{8,9},{9,8},{10,11... | collective-permute-start | bytes 393224 | tf_op jit(solution)/shard_map/ppermute | solution.py:267
  30.5 1.3 %collective-permute-start.6 = (bf16[128,512]{1,0:T(8,128)(2,1)S(1)}, bf16[128,512]{1,0:T(8,128)(2,1)S(1)}, u32[]{:S(2)}, u32[]{:S(2)}) collective-permute-start(bf16[128,512]{1,0:T(8,128)(2,1)S(1)} %collective-permute-done.5.refs_4_), channel_id=1, source_target_pairs={{0,1},{1,0},{2,3},{3,2},{4,5},{5,4},{6,7},{7,6},{8,9},{9,8},{10,11... | collective-permute-start | bytes 393224 | tf_op jit(solution)/shard_map/ppermute | solution.py:270
  30.5 1.5 %collective-permute-start.4 = (bf16[128,512]{1,0:T(8,128)(2,1)S(1)}, bf16[128,512]{1,0:T(8,128)(2,1)S(1)}, u32[]{:S(2)}, u32[]{:S(2)}) collective-permute-start(bf16[128,512]{1,0:T(8,128)(2,1)S(1)} %collective-permute-done.1.refs_2_), channel_id=1, source_target_pairs={{0,1},{1,0},{2,3},{3,2},{4,5},{5,4},{6,7},{7,6},{8,9},{9,8},{10,11... | collective-permute-start | bytes 393224 | tf_op jit(solution)/shard_map/ppermute | solution.py:270
  31.1 1.3 %collective-permute-start.8 = (bf16[128,512]{1,0:T(8,128)(2,1)S(1)}, bf16[128,512]{1,0:T(8,128)(2,1)S(1)}, u32[]{:S(2)}, u32[]{:S(2)}) collective-permute-start(bf16[128,512]{1,0:T(8,128)(2,1)S(1)} %collective-permute-done.7.refs_6_), channel_id=1, source_target_pairs={{0,1},{1,0},{2,3},{3,2},{4,5},{5,4},{6,7},{7,6},{8,9},{9,8},{10,11... | collective-permute-start | bytes 393224 | tf_op jit(solution)/shard_map/ppermute | solution.py:270
  34.1 29.5 %copy-start.10 = (s32[128]{0:T(128)S(1)}, s32[128]{0:T(128)}, u32[]{:S(2)}) copy-start(s32[128]{0:T(128)} %param.9) | copy-start | bytes 1540
  34.1 4.4 %collective-permute-start.9 = (bf16[128,256]{1,0:T(8,128)(2,1)S(1)}, bf16[128,256]{1,0:T(8,128)(2,1)S(1)}, u32[]{:S(2)}, u32[]{:S(2)}) collective-permute-start(bf16[128,256]{1,0:T(8,128)(2,1)S(1)} %get-tuple-element.33.kv_ref), channel_id=1, source_target_pairs={{0,8},{8,0},{16,24},{24,16},{32,40},{40,32},{48,56},{56,48},{64,72... | collective-permute-start | bytes 196616 | tf_op jit(solution)/shard_map/ppermute | solution.py:277
  38.5 6.0 %collective-permute-start.11 = (bf16[2,128,128]{2,1,0:T(8,128)(2,1)S(1)}, bf16[2,128,128]{2,1,0:T(8,128)(2,1)S(1)}, u32[]{:S(2)}, u32[]{:S(2)}) collective-permute-start(bf16[2,128,128]{2,1,0:T(8,128)(2,1)S(1)} %get-tuple-element.47), channel_id=1, source_target_pairs={{0,32},{8,40},{16,48},{24,56},{32,0},{40,8},{48,16},{56,24},{64,96... | collective-permute-start | bytes 196616 | tf_op jit(solution)/shard_map/ppermute | solution.py:280
  38.6 6.3 %collective-permute-start.10 = (bf16[2,128,128]{2,1,0:T(8,128)(2,1)S(1)}, bf16[2,128,128]{2,1,0:T(8,128)(2,1)S(1)}, u32[]{:S(2)}, u32[]{:S(2)}) collective-permute-start(bf16[2,128,128]{2,1,0:T(8,128)(2,1)S(1)} %get-tuple-element.47), channel_id=1, source_target_pairs={{0,16},{8,24},{16,32},{24,40},{32,48},{40,56},{48,0},{56,8},{64,80... | collective-permute-start | bytes 196616 | tf_op jit(solution)/shard_map/ppermute | solution.py:280
  39.5 5.3 %collective-permute-start.12 = (bf16[2,128,128]{2,1,0:T(8,128)(2,1)S(1)}, bf16[2,128,128]{2,1,0:T(8,128)(2,1)S(1)}, u32[]{:S(2)}, u32[]{:S(2)}) collective-permute-start(bf16[2,128,128]{2,1,0:T(8,128)(2,1)S(1)} %get-tuple-element.47), channel_id=1, source_target_pairs={{0,48},{8,56},{16,0},{24,8},{32,16},{40,24},{48,32},{56,40},{64,11... | collective-permute-start | bytes 196616 | tf_op jit(solution)/shard_map/ppermute | solution.py:280
  44.9 17.4 %collective-permute-start.15 = (bf16[4,2,128,128]{3,2,1,0:T(8,128)(2,1)S(1)}, bf16[4,2,128,128]{3,2,1,0:T(8,128)(2,1)S(1)}, u32[]{:S(2)}, u32[]{:S(2)}) collective-permute-start(bf16[4,2,128,128]{3,2,1,0:T(8,128)(2,1)S(1)} %pad_maximum_fusion.refs_1_), channel_id=1, source_target_pairs={{0,192},{8,200},{16,208},{24,216},{32,224},{40,232},{48,240},{56,2... | collective-permute-start | bytes 786440 | tf_op jit(solution)/shard_map/ppermute | solution.py:294
  45.4 13.3 %collective-permute-start.17 = (bf16[2,128,128]{2,1,0:T(8,128)(2,1)S(1)}, bf16[2,128,128]{2,1,0:T(8,128)(2,1)S(1)}, u32[]{:S(2)}, u32[]{:S(2)}) collective-permute-start(bf16[2,128,128]{2,1,0:T(8,128)(2,1)S(1)} %get-tuple-element.41), channel_id=1, source_target_pairs={{0,128},{8,136},{16,144},{24,152},{32,160},{40,168},{48,176},{56,1... | collective-permute-start | bytes 196616 | tf_op jit(solution)/shard_map/ppermute | solution.py:281
  50.2 8.5 %collective-permute-start.16 = (bf16[2,128,128]{2,1,0:T(8,128)(2,1)S(1)}, bf16[2,128,128]{2,1,0:T(8,128)(2,1)S(1)}, u32[]{:S(2)}, u32[]{:S(2)}) collective-permute-start(bf16[2,128,128]{2,1,0:T(8,128)(2,1)S(1)} %get-tuple-element.41), channel_id=1, source_target_pairs={{0,64},{8,72},{16,80},{24,88},{32,96},{40,104},{48,112},{56,120},{... | collective-permute-start | bytes 196616 | tf_op jit(solution)/shard_map/ppermute | solution.py:281
  50.2 8.5 %collective-permute-start.18 = (bf16[2,128,128]{2,1,0:T(8,128)(2,1)S(1)}, bf16[2,128,128]{2,1,0:T(8,128)(2,1)S(1)}, u32[]{:S(2)}, u32[]{:S(2)}) collective-permute-start(bf16[2,128,128]{2,1,0:T(8,128)(2,1)S(1)} %get-tuple-element.41), channel_id=1, source_target_pairs={{0,192},{8,200},{16,208},{24,216},{32,224},{40,232},{48,240},{56,2... | collective-permute-start | bytes 196616 | tf_op jit(solution)/shard_map/ppermute | solution.py:281
  52.3 12.2 %collective-permute-start.14 = (bf16[4,2,128,128]{3,2,1,0:T(8,128)(2,1)S(1)}, bf16[4,2,128,128]{3,2,1,0:T(8,128)(2,1)S(1)}, u32[]{:S(2)}, u32[]{:S(2)}) collective-permute-start(bf16[4,2,128,128]{3,2,1,0:T(8,128)(2,1)S(1)} %pad_maximum_fusion.refs_1_), channel_id=1, source_target_pairs={{0,128},{8,136},{16,144},{24,152},{32,160},{40,168},{48,176},{56,1... | collective-permute-start | bytes 786440 | tf_op jit(solution)/shard_map/ppermute | solution.py:294
  58.8 6.4 %collective-permute-start.13 = (bf16[4,2,128,128]{3,2,1,0:T(8,128)(2,1)S(1)}, bf16[4,2,128,128]{3,2,1,0:T(8,128)(2,1)S(1)}, u32[]{:S(2)}, u32[]{:S(2)}) collective-permute-start(bf16[4,2,128,128]{3,2,1,0:T(8,128)(2,1)S(1)} %pad_maximum_fusion.refs_1_), channel_id=1, source_target_pairs={{0,64},{8,72},{16,80},{24,88},{32,96},{40,104},{48,112},{56,120},{... | collective-permute-start | bytes 786440 | tf_op jit(solution)/shard_map/ppermute | solution.py:294
  58.8 9.3 %collective-permute-start.21 = (bf16[4,2,128,128]{3,2,1,0:T(8,128)(2,1)S(1)}, bf16[4,2,128,128]{3,2,1,0:T(8,128)(2,1)S(1)}, u32[]{:S(2)}, u32[]{:S(2)}) collective-permute-start(bf16[4,2,128,128]{3,2,1,0:T(8,128)(2,1)S(1)} %pad_maximum_fusion.1.refs_5_), channel_id=1, source_target_pairs={{0,48},{8,56},{16,0},{24,8},{32,16},{40,24},{48,32},{56,40},{64,11... | collective-permute-start | bytes 786440 | tf_op jit(solution)/shard_map/ppermute | solution.py:295
  61.4 8.0 %collective-permute-start.20 = (bf16[4,2,128,128]{3,2,1,0:T(8,128)(2,1)S(1)}, bf16[4,2,128,128]{3,2,1,0:T(8,128)(2,1)S(1)}, u32[]{:S(2)}, u32[]{:S(2)}) collective-permute-start(bf16[4,2,128,128]{3,2,1,0:T(8,128)(2,1)S(1)} %pad_maximum_fusion.1.refs_5_), channel_id=1, source_target_pairs={{0,32},{8,40},{16,48},{24,56},{32,0},{40,8},{48,16},{56,24},{64,96... | collective-permute-start | bytes 786440 | tf_op jit(solution)/shard_map/ppermute | solution.py:295
  62.3 9.8 %collective-permute-start.19 = (bf16[4,2,128,128]{3,2,1,0:T(8,128)(2,1)S(1)}, bf16[4,2,128,128]{3,2,1,0:T(8,128)(2,1)S(1)}, u32[]{:S(2)}, u32[]{:S(2)}) collective-permute-start(bf16[4,2,128,128]{3,2,1,0:T(8,128)(2,1)S(1)} %pad_maximum_fusion.1.refs_5_), channel_id=1, source_target_pairs={{0,16},{8,24},{16,32},{24,40},{32,48},{40,56},{48,0},{56,8},{64,80... | collective-permute-start | bytes 786440 | tf_op jit(solution)/shard_map/ppermute | solution.py:295
  (9 other events, 45.5 us)

commit v4 on v3

--- a/solution.py
+++ b/solution.py
@@ -10,6 +10,7 @@
 ROWS = 128
 HEAD = 128
 GROUP = 4
+PAD = 16
 WIDTH = 512
 BLOCK = 32
 LAST = 31
@@ -45,12 +46,12 @@
     return lax.dot_general(a, b, (((1,), (1,)), ((), ())), preferred_element_type=F32)
 
 
-def call(kernel, outs, args, cost, scratch=()):
+def call(kernel, outs, args, cost, scratch=(), space=pltpu.VMEM):
     spec = pl.BlockSpec(memory_space=pltpu.VMEM)
     return pl.pallas_call(
         kernel,
         out_shape=[jax.ShapeDtypeStruct(s, t) for s, t in outs],
-        in_specs=[spec] * len(args),
+        in_specs=[pl.BlockSpec(memory_space=space)] * len(args),
         out_specs=[spec] * len(outs),
         scratch_shapes=list(scratch),
         compiler_params=pltpu.CompilerParams(vmem_limit_bytes=LIMIT),
@@ -64,53 +65,77 @@
     return jnp.sum(jnp.where(same, jnp.broadcast_to(row, square), 0.0), axis=1, keepdims=True)
 
 
-def mask_kernel(ids_ref, order_ref, cut_ref, embed_ref, wq_ref, wk_ref, wv_ref, flag_ref, code_ref, mq_ref, mkv_ref):
-    code_ref[...] = jnp.broadcast_to(ids_ref[...] * 32 + order_ref[...], (8, ROWS))
-    ids = column(ids_ref[...].astype(F32))
-    order = column(order_ref[...].astype(F32))
+def prep_kernel(*refs):
+    hidden_hbm, wk_hbm, wv_hbm, ids_hbm, order_hbm, embed_hbm = refs[:6]
+    own_ref, wk_ref, wv_ref, code_ref, pad_ref = refs[6:11]
+    ids_ref, order_ref, embed_ref, sems = refs[11:]
+    pairs = (
+        (ids_hbm, ids_ref),
+        (order_hbm, order_ref),
+        (embed_hbm, embed_ref),
+        (hidden_hbm, own_ref),
+        (wk_hbm, wk_ref),
+        (wv_hbm, wv_ref),
+    )
+    copies = [pltpu.make_async_copy(a, b, sems.at[i]) for i, (a, b) in enumerate(pairs)]
+    for copy in copies:
+        copy.start()
+    for copy in copies:
+        copy.wait()
+    ids = jnp.broadcast_to(ids_ref[...].astype(F32), (8, ROWS))
+    order = jnp.broadcast_to(order_ref[...].astype(F32), (8, ROWS))
+    code_ref[...] = jnp.concatenate([ids, order], axis=0).astype(BF16)
+    pad_ref[...] = jnp.broadcast_to(embed_ref[...], pad_ref.shape)
+
+
+def kv_kernel(*refs):
+    pieces = refs[:8]
+    pad_ref, wk_ref, wv_ref, code_ref = refs[8:12]
+    x_ref, kv_ref, mkv_ref = refs[12:]
+    me = lax.axis_index("kv")
+    for dz in range(4):
+        for dc in range(2):
+            source = lax.rem(me // 2 + 4 - dz, 4) * 2 + lax.rem(me + dc, 2)
+            x_ref[:ROWS, pl.ds(pl.multiple_of(source * WIDTH, WIDTH), WIDTH)] = pieces[2 * dz + dc][...]
+    x_ref[ROWS:, :] = pad_ref[...]
+    x = x_ref[...]
+    for part, w_ref in enumerate((wk_ref, wv_ref)):
+        lanes = slice(part * HEAD, (part + 1) * HEAD)
+        product = dot(x, w_ref[...]).astype(BF16)
+        kv_ref[:ROWS, lanes] = product[:ROWS]
+        kv_ref[ROWS:, lanes] = code_ref[...]
+        mkv_ref[:, lanes] = product[ROWS:]
+
+
+def q_kernel(x_ref, wq_ref, code_ref, cut_ref, q_ref, flag_ref, own_cut_ref):
+    code = code_ref[...].astype(F32)
+    ids = column(code[0:1])
+    order = column(code[8:9])
     blocks = cut_ref.shape[1]
     spots = lax.broadcasted_iota(jnp.int32, (ROWS, blocks), 1).astype(F32)
     cuts = jnp.broadcast_to(cut_ref[...].astype(F32), (ROWS, blocks))
     cut = jnp.sum(jnp.where(spots == ids, cuts, 0.0), axis=1, keepdims=True)
-    flag_ref[...] = jnp.broadcast_to(jnp.where(order >= cut, 1.0, 0.0), (ROWS, HEAD))
-    embed = jnp.broadcast_to(embed_ref[...], (16, embed_ref.shape[1]))
-    mq_ref[...] = dot(embed, wq_ref[...]).astype(BF16)
-    mkv_ref[:, :HEAD] = dot(embed, wk_ref[...]).astype(BF16)
-    mkv_ref[:, HEAD:] = dot(embed, wv_ref[...]).astype(BF16)
-
-
-def kv_kernel(*refs):
-    pieces = refs[:8]
-    wk_ref, wv_ref, flag_ref, mkv_ref = refs[8:12]
-    x_ref, kv_ref, kvn_ref = refs[12:]
-    me = lax.axis_index("kv")
-    for dz in range(4):
-        for dc in range(2):
-            source = lax.rem(me // 2 + 4 - dz, 4) * 2 + lax.rem(me + dc, 2)
-            x_ref[:, pl.ds(pl.multiple_of(source * WIDTH, WIDTH), WIDTH)] = pieces[2 * dz + dc][...]
-    x = x_ref[...]
-    masked = flag_ref[...] > 0.5
-    for part, w_ref in enumerate((wk_ref, wv_ref)):
-        lanes = slice(part * HEAD, (part + 1) * HEAD)
-        clean = dot(x, w_ref[...])
-        fixed = jnp.broadcast_to(mkv_ref[0:1, lanes].astype(F32), (ROWS, HEAD))
-        kv_ref[:, lanes] = clean.astype(BF16)
-        kvn_ref[:, lanes] = jnp.where(masked, fixed, clean).astype(BF16)
-
-
-def q_kernel(x_ref, wq_ref, flag_ref, mq_ref, q_ref):
-    masked = flag_ref[...] > 0.5
+    flag = jnp.broadcast_to(jnp.where(order >= cut, 1.0, 0.0), (ROWS, HEAD))
+    flag_ref[...] = flag
+    own_cut_ref[...] = jnp.broadcast_to(cut, (ROWS, HEAD))
     x = x_ref[...]
     for h in range(GROUP):
-        lanes = slice(h * HEAD, (h + 1) * HEAD)
-        clean = dot(x, wq_ref[:, lanes])
-        fixed = jnp.broadcast_to(mq_ref[0:1, lanes].astype(F32), (ROWS, HEAD))
+        product = dot(x, wq_ref[:, h * HEAD : (h + 1) * HEAD])
+        clean = product[:ROWS]
+        fixed = jnp.broadcast_to(product[ROWS : ROWS + 1], (ROWS, HEAD))
         q_ref[h, :ROWS, :] = clean.astype(BF16)
-        q_ref[h, ROWS:, :] = jnp.where(masked, fixed, clean).astype(BF16)
-
-
-def near_kernel(q_ref, kv_ref, kvn_ref, ids_ref, top_ref, total_ref, accum_ref):
-    row = ids_ref[...].astype(F32)
+        q_ref[h, ROWS:, :] = jnp.where(flag > 0.5, fixed, clean).astype(BF16)
+
+
+def near_kernel(q_ref, kv_ref, mkv_ref, flag_ref, code_ref, top_ref, total_ref, accum_ref):
+    masked = flag_ref[...] > 0.5
+
+    def both(lanes):
+        clean = kv_ref[:ROWS, lanes]
+        fixed = jnp.broadcast_to(mkv_ref[0:1, lanes].astype(F32), (ROWS, HEAD))
+        return jnp.concatenate([clean, jnp.where(masked, fixed, clean.astype(F32)).astype(BF16)], axis=0)
+
+    row = code_ref[...].astype(F32)[0:1]
     query = jnp.broadcast_to(column(row), (ROWS, ROWS))
     key = jnp.broadcast_to(row, (ROWS, ROWS))
     zero = jnp.zeros((ROWS, ROWS), F32)
@@ -118,8 +143,8 @@
     clean_bias = jnp.concatenate([jnp.where(key <= query, zero, low), low], axis=1)
     noisy_bias = jnp.concatenate([jnp.where(key < query, zero, low), jnp.where(key == query, zero, low)], axis=1)
     bias = jnp.concatenate([clean_bias, noisy_bias], axis=0)
-    keys = jnp.concatenate([kv_ref[:, :HEAD], kvn_ref[:, :HEAD]], axis=0)
-    values = jnp.concatenate([kv_ref[:, HEAD:], kvn_ref[:, HEAD:]], axis=0)
+    keys = both(slice(0, HEAD))
+    values = both(slice(HEAD, 2 * HEAD))
     for h in range(GROUP):
         scores = jnp.where(bias < -1.0, LOW, dot_t(q_ref[h], keys))
         top = jnp.max(scores, axis=1, keepdims=True)
@@ -133,9 +158,9 @@
     q_ref = refs[0]
     k_refs, v_refs = refs[1:5], refs[5:9]
     top_in, total_in, accum_in = refs[9:12]
-    ids_ref, code_ref, up_ref, down_ref, cut_ref, mkv_ref = refs[12:18]
-    clean_ref, noisy_ref = refs[18:20]
-    top_ref, total_ref, accum_ref = refs[20:]
+    code_ref, pair_ref, swap_ref, own_cut_ref, mkv_ref = refs[12:17]
+    clean_ref, noisy_ref = refs[17:19]
+    top_ref, total_ref, accum_ref = refs[19:]
     me = lax.axis_index("ctx")
     y, x, z = me // 8, lax.rem(me // 2, 4), lax.rem(me, 2)
 
@@ -150,19 +175,17 @@
     k_new = jnp.where(beyond, k_refs[3][step, 1], k_refs[0][step, 1])[:BLOCK]
     v_new = jnp.where(z == 0, v_refs[0][new_y, 1], v_refs[3][new_y, 1])[:BLOCK]
 
-    code = code_ref[...]
-    own = (code // 32).astype(F32)
-    old_ids = jnp.where(me > 0, (up_ref[...] // 32).astype(F32), FAR)
-    new_ids = jnp.where(me < LAST, (down_ref[...] // 32).astype(F32), FAR)
-    old_order = lax.rem(up_ref[...], 32).astype(F32)
-    new_order = lax.rem(down_ref[...], 32).astype(F32)
-    blocks = cut_ref.shape[1]
-    spots = lax.broadcasted_iota(jnp.int32, (8, blocks), 1).astype(F32)
-    cuts = jnp.broadcast_to(cut_ref[...].astype(F32), (8, blocks))
-    first_cut = jnp.sum(jnp.where(spots == own[:, 0:1], cuts, 0.0), axis=1, keepdims=True)
-    last_cut = jnp.sum(jnp.where(spots == own[:, ROWS - 1 : ROWS], cuts, 0.0), axis=1, keepdims=True)
-    old_masked = column(jnp.where(old_order >= first_cut, 1.0, 0.0)[0:1])[ROWS - BLOCK :]
-    new_masked = column(jnp.where(new_order >= last_cut, 1.0, 0.0)[0:1])[:BLOCK]
+    own = code_ref[...].astype(F32)[:8]
+    partner = pair_ref[ROWS:, :HEAD].astype(F32)
+    other = swap_ref[...].astype(F32)
+    old_code = jnp.where(z == 0, other, partner)
+    new_code = jnp.where(z == 0, partner, other)
+    old_ids, old_order = jnp.where(me > 0, old_code[:8], FAR), old_code[8:]
+    new_ids, new_order = jnp.where(me < LAST, new_code[:8], FAR), new_code[8:]
+    first_cut = own_cut_ref[0:1, :]
+    last_cut = own_cut_ref[ROWS - 1 : ROWS, :]
+    old_masked = column(jnp.where(old_order[0:1] >= first_cut, 1.0, 0.0))[ROWS - BLOCK :]
+    new_masked = column(jnp.where(new_order[0:1] >= last_cut, 1.0, 0.0))[:BLOCK]
 
     def noisy(masked, clean, lanes):
         fixed = jnp.broadcast_to(mkv_ref[0:1, lanes].astype(F32), clean.shape)
@@ -253,42 +276,54 @@
     ids = block_ids.reshape(1, ROWS)
     order = decode_order.reshape(1, ROWS)
     cuts = step_cut.reshape(1, -1)
-    flag, code, mask_q, mask_kv = call(
-        mask_kernel,
-        [((ROWS, HEAD), F32), ((8, ROWS), jnp.int32), ((16, GROUP * HEAD), BF16), ((16, 2 * HEAD), BF16)],
-        [ids, order, cuts, mask_embed.reshape(1, -1), q_weight, k_weight, v_weight],
-        (1 << 28, 6 << 20),
-    )
     moved = [lax.ppermute(hidden, "kv", kv_pairs(d, 0)) for d in (1, 2, 3)]
-    count = 32
-    up = lax.ppermute(code, "ctx", [(i, (i + 1) % count) for i in range(count)])
-    down = lax.ppermute(code, "ctx", [(i, (i - 1) % count) for i in range(count)])
-    flag, code, mask_q, mask_kv, up, down = lax.optimization_barrier((flag, code, mask_q, mask_kv, up, down))
-    pieces = [hidden, lax.ppermute(hidden, "kv", kv_pairs(0, 1))]
-    for piece in moved:
-        piece, _, _ = lax.optimization_barrier((piece, up, flag))
+    own, wk, wv, code, pad = call(
+        prep_kernel,
+        [
+            (hidden.shape, BF16),
+            (k_weight.shape, BF16),
+            (v_weight.shape, BF16),
+            ((PAD, ROWS), BF16),
+            ((PAD, 8 * WIDTH), BF16),
+        ],
+        [hidden, k_weight, v_weight, ids, order, mask_embed.reshape(1, -1)],
+        (1 << 20, 4 << 20),
+        [
+            pltpu.VMEM(ids.shape, jnp.int32),
+            pltpu.VMEM(ids.shape, jnp.int32),
+            pltpu.VMEM((1, 8 * WIDTH), BF16),
+            pltpu.SemaphoreType.DMA((6,)),
+        ],
+        pltpu.HBM,
+    )
+    pieces = []
+    for piece in (own, *moved):
+        piece, _ = lax.optimization_barrier((piece, pad))
         pieces += [piece, lax.ppermute(piece, "kv", kv_pairs(0, 1))]
-    x, kv, kv_noisy = call(
+    x, kv, mask_kv = call(
         kv_kernel,
-        [((ROWS, 8 * WIDTH), BF16), ((ROWS, 2 * HEAD), BF16), ((ROWS, 2 * HEAD), BF16)],
-        [*pieces, k_weight, v_weight, flag, mask_kv],
+        [((ROWS + PAD, 8 * WIDTH), BF16), ((ROWS + PAD, 2 * HEAD), BF16), ((PAD, 2 * HEAD), BF16)],
+        [*pieces, pad, wk, wv, code],
         (1 << 29, 3 << 20),
     )
     pair = lax.ppermute(kv, "ctx", ctx_pairs(0, 0, 1))
-    k = jnp.stack([kv[:, :HEAD], pair[:, :HEAD]])
-    v = jnp.stack([kv[:, HEAD:], pair[:, HEAD:]])
+    swap = lax.ppermute(code, "ctx", [(i, (i + 2 * (i % 2) - 1) % 32) for i in range(32)])
+    pair, swap = lax.optimization_barrier((pair, swap))
+    k = jnp.stack([kv[:ROWS, :HEAD], pair[:ROWS, :HEAD]])
+    v = jnp.stack([kv[:ROWS, HEAD:], pair[:ROWS, HEAD:]])
+    k, v = lax.optimization_barrier((k, v))
     ks = jnp.stack([k] + [lax.ppermute(k, "ctx", ctx_pairs(0, d, 0)) for d in (1, 2, 3)])
     vs = jnp.stack([v] + [lax.ppermute(v, "ctx", ctx_pairs(d, 0, 0)) for d in (1, 2, 3)])
-    (q,) = call(
+    q, flag, own_cut = call(
         q_kernel,
-        [((GROUP, 2 * ROWS, HEAD), BF16)],
-        [x, q_weight, flag, mask_q],
+        [((GROUP, 2 * ROWS, HEAD), BF16), ((ROWS, HEAD), F32), ((ROWS, HEAD), F32)],
+        [x, q_weight, code, cuts],
         (1 << 30, 5 << 20),
     )
     near = call(
         near_kernel,
         [((GROUP, 2 * ROWS, HEAD), F32)] * 3,
-        [q, kv, kv_noisy, ids],
+        [q, kv, mask_kv, flag, code],
         (1 << 30, 2 << 20),
     )
     all_k = [ks] + [lax.ppermute(ks, "ctx", ctx_pairs(d, 0, 0)) for d in (1, 2, 3)]
@@ -297,7 +332,7 @@
         call(
             far_kernel,
             [((ROWS, GROUP * HEAD), BF16)] * 2,
-            [q, *all_k, *all_v, *near, ids, code, up, down, cuts, mask_kv],
+            [q, *all_k, *all_v, *near, code, pair, swap, own_cut, mask_kv],
             (1 << 32, 4 << 20),
             [pltpu.VMEM((GROUP, 2 * ROWS, HEAD), F32)] * 3,
         )

time: 81 us -> 72.3 us (0.89)
  the two profiles are of different devices: /device:TPU:24 before, /device:TPU:8 now
where the time goes in v4:
time: 72.3 us; the launch traced here: 72.1 us
  starting transfers between devices  32.7 us (45%)
  waiting for transfers between devices  22.3 us (31%)
  Pallas kernels  10.9 us (15%)
  local copies, waits for them, and re-layouts  5.38 us (7%)
  between operations  0.76 us (1%)
    ppermute x3, starting transfers between devices, shards(): moved = [lax.ppermute(hidden, 'kv', kv_pairs(d, 0)) for d in (1, 2, 3)]  11.4 us
    pallas_call x5, Pallas kernels, call(): pl.pallas_call(kernel, out_shape=[jax.ShapeDtypeStruct(s, t) for s, t in...  10.9 us
    ppermute x3, waiting for transfers between devices, shards(): lax.ppermute(ks, 'ctx', ctx_pairs(d, 0, 0))  6.33 us
    ppermute x3, starting transfers between devices, shards(): lax.ppermute(vs, 'ctx', ctx_pairs(0, d, 0))  6.28 us
    ppermute x3, waiting for transfers between devices, shards(): lax.ppermute(k, 'ctx', ctx_pairs(0, d, 0))  5.48 us
    ppermute x3, starting transfers between devices, shards(): lax.ppermute(v, 'ctx', ctx_pairs(d, 0, 0))  5 us
    ppermute x3, starting transfers between devices, shards(): lax.ppermute(k, 'ctx', ctx_pairs(0, d, 0))  4.75 us
    unnamed x14, local copies, waits for them, and re-layouts  4.67 us
  transfers between devices with their start and end apart: 21, of which 12 were waited for; matrix products, arithmetic and copies ran while one was open for 1% of the time, Pallas kernels for 5%

profile of v4, /device:TPU:8, one launch (start us, length us, event | category | flops | bytes accessed | tf_op | source)
XLA Modules:
  0.0 72.1 jit_solution(6437971545310235988)
XLA Ops:
  0.6 3.3 %collective-permute-start.1 = (bf16[128,512]{1,0:T(8,128)(2,1)}, bf16[128,512]{1,0:T(8,128)(2,1)S(1)}, u32[]{:S(2)}, u32[]{:S(2)}) collective-permute-start(bf16[128,512]{1,0:T(8,128)(2,1)} %refs_0_.1), channel_id=1, source_target_pairs={{0,2},{1,3},{2,4},{3,5},{4,6},{5,7},{6,0},{7,1},{8,10},{9,11},{10,... | collective-permute-start | bytes 393224 | tf_op jit(solution)/shard_map/ppermute | solution.py:279
  4.0 5.4 %collective-permute-start.3 = (bf16[128,512]{1,0:T(8,128)(2,1)}, bf16[128,512]{1,0:T(8,128)(2,1)S(1)}, u32[]{:S(2)}, u32[]{:S(2)}) collective-permute-start(bf16[128,512]{1,0:T(8,128)(2,1)} %refs_0_.1), channel_id=1, source_target_pairs={{0,4},{1,5},{2,6},{3,7},{4,0},{5,1},{6,2},{7,3},{8,12},{9,13},{10,... | collective-permute-start | bytes 393224 | tf_op jit(solution)/shard_map/ppermute | solution.py:279
  9.4 2.7 %collective-permute-start.5 = (bf16[128,512]{1,0:T(8,128)(2,1)}, bf16[128,512]{1,0:T(8,128)(2,1)S(1)}, u32[]{:S(2)}, u32[]{:S(2)}) collective-permute-start(bf16[128,512]{1,0:T(8,128)(2,1)} %refs_0_.1), channel_id=1, source_target_pairs={{0,6},{1,7},{2,0},{3,1},{4,2},{5,3},{6,4},{7,5},{8,14},{9,15},{10,... | collective-permute-start | bytes 393224 | tf_op jit(solution)/shard_map/ppermute | solution.py:279
  12.8 1.2 %copy-done.1 = bf16[4096,128]{1,0:T(8,128)(2,1)S(1)} copy-done((bf16[4096,128]{1,0:T(8,128)(2,1)S(1)}, bf16[4096,128]{1,0:T(8,128)(2,1)}, u32[]{:S(2)}) %copy-start.1) | copy-done | bytes 1048600
  14.0 1.2 %copy-done.2 = bf16[4096,128]{1,0:T(8,128)(2,1)S(1)} copy-done((bf16[4096,128]{1,0:T(8,128)(2,1)S(1)}, bf16[4096,128]{1,0:T(8,128)(2,1)}, u32[]{:S(2)}) %copy-start.2) | copy-done | bytes 1048600
  18.6 3.2 %collective-permute-done.5.refs_6_ = bf16[128,512]{1,0:T(8,128)(2,1)S(1)} collective-permute-done((bf16[128,512]{1,0:T(8,128)(2,1)}, bf16[128,512]{1,0:T(8,128)(2,1)S(1)}, u32[]{:S(2)}, u32[]{:S(2)}) %collective-permute-start.5) | collective-permute-done | bytes 131104 | tf_op jit(solution)/shard_map/ppermute | solution.py:279
  24.0 1.7 %collective-permute-start.7 = (bf16[144,256]{1,0:T(8,128)(2,1)S(1)}, bf16[144,256]{1,0:T(8,128)(2,1)S(1)}, u32[]{:S(2)}, u32[]{:S(2)}) collective-permute-start(bf16[144,256]{1,0:T(8,128)(2,1)S(1)} %get-tuple-element.35.kv_ref), channel_id=1, source_target_pairs={{0,8},{8,0},{16,24},{24,16},{32,40},{40,32},{48,56},{56,48},{64,72... | collective-permute-start | bytes 221192 | tf_op jit(solution)/shard_map/ppermute | solution.py:309
  25.7 2.7 %collective-permute-done.8.refs_14_ = bf16[16,128]{1,0:T(8,128)(2,1)S(1)} collective-permute-done((bf16[16,128]{1,0:T(8,128)(2,1)S(1)}, bf16[16,128]{1,0:T(8,128)(2,1)S(1)}, u32[]{:S(2)}, u32[]{:S(2)}) %collective-permute-start.8) | collective-permute-done | bytes 4128 | tf_op jit(solution)/shard_map/ppermute | solution.py:310
  28.5 1.7 %collective-permute-start.15 = (bf16[2,128,128]{2,1,0:T(8,128)(2,1)S(1)}, bf16[2,128,128]{2,1,0:T(8,128)(2,1)S(1)}, u32[]{:S(2)}, u32[]{:S(2)}) collective-permute-start(bf16[2,128,128]{2,1,0:T(8,128)(2,1)S(1)} %get-tuple-element.38), channel_id=1, source_target_pairs={{0,64},{8,72},{16,80},{24,88},{32,96},{40,104},{48,112},{56,120},{... | collective-permute-start | bytes 196616 | tf_op jit(solution)/shard_map/ppermute | solution.py:316
  30.1 3.0 %collective-permute-start.16 = (bf16[2,128,128]{2,1,0:T(8,128)(2,1)S(1)}, bf16[2,128,128]{2,1,0:T(8,128)(2,1)S(1)}, u32[]{:S(2)}, u32[]{:S(2)}) collective-permute-start(bf16[2,128,128]{2,1,0:T(8,128)(2,1)S(1)} %get-tuple-element.38), channel_id=1, source_target_pairs={{0,128},{8,136},{16,144},{24,152},{32,160},{40,168},{48,176},{56,1... | collective-permute-start | bytes 196616 | tf_op jit(solution)/shard_map/ppermute | solution.py:316
  33.6 2.4 %collective-permute-done.16 = bf16[2,128,128]{2,1,0:T(8,128)(2,1)S(1)} collective-permute-done((bf16[2,128,128]{2,1,0:T(8,128)(2,1)S(1)}, bf16[2,128,128]{2,1,0:T(8,128)(2,1)S(1)}, u32[]{:S(2)}, u32[]{:S(2)}) %collective-permute-start.16) | collective-permute-done | bytes 65568 | tf_op jit(solution)/shard_map/ppermute | solution.py:316
  36.0 1.4 %collective-permute-done.17 = bf16[2,128,128]{2,1,0:T(8,128)(2,1)S(1)} collective-permute-done((bf16[2,128,128]{2,1,0:T(8,128)(2,1)S(1)}, bf16[2,128,128]{2,1,0:T(8,128)(2,1)S(1)}, u32[]{:S(2)}, u32[]{:S(2)}) %collective-permute-start.17) | collective-permute-done | bytes 65568 | tf_op jit(solution)/shard_map/ppermute | solution.py:316
  37.6 3.1 %collective-permute-start.11 = (bf16[2,128,128]{2,1,0:T(8,128)(2,1)S(1)}, bf16[2,128,128]{2,1,0:T(8,128)(2,1)S(1)}, u32[]{:S(2)}, u32[]{:S(2)}) collective-permute-start(bf16[2,128,128]{2,1,0:T(8,128)(2,1)S(1)} %get-tuple-element.37), channel_id=1, source_target_pairs={{0,48},{8,56},{16,0},{24,8},{32,16},{40,24},{48,32},{56,40},{64,11... | collective-permute-start | bytes 196616 | tf_op jit(solution)/shard_map/ppermute | solution.py:315
  40.8 1.6 %collective-permute-start.10 = (bf16[2,128,128]{2,1,0:T(8,128)(2,1)S(1)}, bf16[2,128,128]{2,1,0:T(8,128)(2,1)S(1)}, u32[]{:S(2)}, u32[]{:S(2)}) collective-permute-start(bf16[2,128,128]{2,1,0:T(8,128)(2,1)S(1)} %get-tuple-element.37), channel_id=1, source_target_pairs={{0,32},{8,40},{16,48},{24,56},{32,0},{40,8},{48,16},{56,24},{64,96... | collective-permute-start | bytes 196616 | tf_op jit(solution)/shard_map/ppermute | solution.py:315
  42.4 1.9 %collective-permute-start.19 = (bf16[4,2,128,128]{3,2,1,0:T(8,128)(2,1)S(1)}, bf16[4,2,128,128]{3,2,1,0:T(8,128)(2,1)S(1)}, u32[]{:S(2)}, u32[]{:S(2)}) collective-permute-start(bf16[4,2,128,128]{3,2,1,0:T(8,128)(2,1)S(1)} %pad_maximum_fusion.1.refs_5_), channel_id=1, source_target_pairs={{0,32},{8,40},{16,48},{24,56},{32,0},{40,8},{48,16},{56,24},{64,96... | collective-permute-start | bytes 786440 | tf_op jit(solution)/shard_map/ppermute | solution.py:330
  44.3 2.3 %collective-permute-done.11 = bf16[2,128,128]{2,1,0:T(8,128)(2,1)S(1)} collective-permute-done((bf16[2,128,128]{2,1,0:T(8,128)(2,1)S(1)}, bf16[2,128,128]{2,1,0:T(8,128)(2,1)S(1)}, u32[]{:S(2)}, u32[]{:S(2)}) %collective-permute-start.11) | collective-permute-done | bytes 65568 | tf_op jit(solution)/shard_map/ppermute | solution.py:315
  46.6 4.2 %collective-permute-start.20 = (bf16[4,2,128,128]{3,2,1,0:T(8,128)(2,1)S(1)}, bf16[4,2,128,128]{3,2,1,0:T(8,128)(2,1)S(1)}, u32[]{:S(2)}, u32[]{:S(2)}) collective-permute-start(bf16[4,2,128,128]{3,2,1,0:T(8,128)(2,1)S(1)} %pad_maximum_fusion.1.refs_5_), channel_id=1, source_target_pairs={{0,48},{8,56},{16,0},{24,8},{32,16},{40,24},{48,32},{56,40},{64,11... | collective-permute-start | bytes 786440 | tf_op jit(solution)/shard_map/ppermute | solution.py:330
  50.8 3.1 %collective-permute-done.9 = bf16[2,128,128]{2,1,0:T(8,128)(2,1)S(1)} collective-permute-done((bf16[2,128,128]{2,1,0:T(8,128)(2,1)S(1)}, bf16[2,128,128]{2,1,0:T(8,128)(2,1)S(1)}, u32[]{:S(2)}, u32[]{:S(2)}) %collective-permute-start.9) | collective-permute-done | bytes 65568 | tf_op jit(solution)/shard_map/ppermute | solution.py:315
  54.5 1.7 %collective-permute-start.14 = (bf16[4,2,128,128]{3,2,1,0:T(8,128)(2,1)S(1)}, bf16[4,2,128,128]{3,2,1,0:T(8,128)(2,1)S(1)}, u32[]{:S(2)}, u32[]{:S(2)}) collective-permute-start(bf16[4,2,128,128]{3,2,1,0:T(8,128)(2,1)S(1)} %pad_maximum_fusion.refs_1_), channel_id=1, source_target_pairs={{0,192},{8,200},{16,208},{24,216},{32,224},{40,232},{48,240},{56,2... | collective-permute-start | bytes 786440 | tf_op jit(solution)/shard_map/ppermute | solution.py:329
  56.1 1.4 %shard_map.97 = (bf16[4,256,128]{2,1,0:T(8,128)(2,1)S(1)}, f32[128,128]{1,0:T(8,128)S(1)}, f32[128,128]{1,0:T(8,128)S(1)}) custom-call(bf16[144,4096]{1,0:T(8,128)(2,1)S(1)} %get-tuple-element.33.x_ref, bf16[4096,512]{1,0:T(8,128)(2,1)S(1)} %copy-done, bf16[16,128]{1,0:T(8,128)(2,1)S(1)} %get-tuple-element.32.refs_11_.code_ref.refs_12_, s32[1,256]{1,0:T(1,128)S(1)} %bitcast.19), custom_call_target="tpu_custom_call" | custom-call | flops 1073741824 | bytes 5242880 | tf_op jit(solution)/shard_map/pallas_call | solution.py:51
  58.4 2.0 %collective-permute-done.12.refs_2_ = bf16[4,2,128,128]{3,2,1,0:T(8,128)(2,1)S(1)} collective-permute-done((bf16[4,2,128,128]{3,2,1,0:T(8,128)(2,1)S(1)}, bf16[4,2,128,128]{3,2,1,0:T(8,128)(2,1)S(1)}, u32[]{:S(2)}, u32[]{:S(2)}) %collective-permute-start.12) | collective-permute-done | bytes 262176 | tf_op jit(solution)/shard_map/ppermute | solution.py:329
  60.5 1.7 %collective-permute-done.13.refs_3_ = bf16[4,2,128,128]{3,2,1,0:T(8,128)(2,1)S(1)} collective-permute-done((bf16[4,2,128,128]{3,2,1,0:T(8,128)(2,1)S(1)}, bf16[4,2,128,128]{3,2,1,0:T(8,128)(2,1)S(1)}, u32[]{:S(2)}, u32[]{:S(2)}) %collective-permute-start.13) | collective-permute-done | bytes 262176 | tf_op jit(solution)/shard_map/ppermute | solution.py:329
  62.2 2.6 %collective-permute-done.14.refs_4_ = bf16[4,2,128,128]{3,2,1,0:T(8,128)(2,1)S(1)} collective-permute-done((bf16[4,2,128,128]{3,2,1,0:T(8,128)(2,1)S(1)}, bf16[4,2,128,128]{3,2,1,0:T(8,128)(2,1)S(1)}, u32[]{:S(2)}, u32[]{:S(2)}) %collective-permute-start.14) | collective-permute-done | bytes 262176 | tf_op jit(solution)/shard_map/ppermute | solution.py:329
  64.7 7.4 %shard_map.99 = (bf16[128,512]{1,0:T(8,128)(2,1)}, bf16[128,512]{1,0:T(8,128)(2,1)}) custom-call(bf16[4,256,128]{2,1,0:T(8,128)(2,1)S(1)} %get-tuple-element.34.q_ref.refs_0_, bf16[4,2,128,128]{3,2,1,0:T(8,128)(2,1)S(1)} %pad_maximum_fusion.refs_1_, bf16[4,2,128,128]{3,2,1,0:T(8,128)(2,1)S(1)} %collective-permute-done.12.refs_2_, ...), custom_call_target="tpu_custom_call" | custom-call | flops 4294967296 | bytes 4194304 | tf_op jit(solution)/shard_map/pallas_call | solution.py:51
  (43 shorter events, 8.3 us)
Async XLA Ops:
  0.6 55.5 %copy-start = (bf16[4096,512]{1,0:T(8,128)(2,1)S(1)}, bf16[4096,512]{1,0:T(8,128)(2,1)}, u32[]{:S(2)}) copy-start(bf16[4096,512]{1,0:T(8,128)(2,1)} %wq_ref.1) | copy-start | bytes 12582916
  0.6 17.3 %collective-permute-start.1 = (bf16[128,512]{1,0:T(8,128)(2,1)}, bf16[128,512]{1,0:T(8,128)(2,1)S(1)}, u32[]{:S(2)}, u32[]{:S(2)}) collective-permute-start(bf16[128,512]{1,0:T(8,128)(2,1)} %refs_0_.1), channel_id=1, source_target_pairs={{0,2},{1,3},{2,4},{3,5},{4,6},{5,7},{6,0},{7,1},{8,10},{9,11},{10,... | collective-permute-start | bytes 393224 | tf_op jit(solution)/shard_map/ppermute | solution.py:279
  4.0 14.5 %collective-permute-start.3 = (bf16[128,512]{1,0:T(8,128)(2,1)}, bf16[128,512]{1,0:T(8,128)(2,1)S(1)}, u32[]{:S(2)}, u32[]{:S(2)}) collective-permute-start(bf16[128,512]{1,0:T(8,128)(2,1)} %refs_0_.1), channel_id=1, source_target_pairs={{0,4},{1,5},{2,6},{3,7},{4,0},{5,1},{6,2},{7,3},{8,12},{9,13},{10,... | collective-permute-start | bytes 393224 | tf_op jit(solution)/shard_map/ppermute | solution.py:279
  9.4 12.4 %collective-permute-start.5 = (bf16[128,512]{1,0:T(8,128)(2,1)}, bf16[128,512]{1,0:T(8,128)(2,1)S(1)}, u32[]{:S(2)}, u32[]{:S(2)}) collective-permute-start(bf16[128,512]{1,0:T(8,128)(2,1)} %refs_0_.1), channel_id=1, source_target_pairs={{0,6},{1,7},{2,0},{3,1},{4,2},{5,3},{6,4},{7,5},{8,14},{9,15},{10,... | collective-permute-start | bytes 393224 | tf_op jit(solution)/shard_map/ppermute | solution.py:279
  12.8 1.2 %copy-start.1 = (bf16[4096,128]{1,0:T(8,128)(2,1)S(1)}, bf16[4096,128]{1,0:T(8,128)(2,1)}, u32[]{:S(2)}) copy-start(bf16[4096,128]{1,0:T(8,128)(2,1)} %refs_1_.1) | copy-start | bytes 3145732
  17.4 38.7 %copy-start.4 = (s32[256]{0:T(256)S(1)}, s32[256]{0:T(256)}, u32[]{:S(2)}) copy-start(s32[256]{0:T(256)} %param.11) | copy-start | bytes 3076
  17.8 4.7 %collective-permute-start = (bf16[128,512]{1,0:T(8,128)(2,1)S(1)}, bf16[128,512]{1,0:T(8,128)(2,1)S(1)}, u32[]{:S(2)}, u32[]{:S(2)}) collective-permute-start(bf16[128,512]{1,0:T(8,128)(2,1)S(1)} %get-tuple-element.26.refs_0_), channel_id=1, source_target_pairs={{0,1},{1,0},{2,3},{3,2},{4,5},{5,4},{6,7},{7,6},{8,9},{9,8},{10,11... | collective-permute-start | bytes 393224 | tf_op jit(solution)/shard_map/ppermute | solution.py:302
  18.0 4.6 %collective-permute-start.2 = (bf16[128,512]{1,0:T(8,128)(2,1)S(1)}, bf16[128,512]{1,0:T(8,128)(2,1)S(1)}, u32[]{:S(2)}, u32[]{:S(2)}) collective-permute-start(bf16[128,512]{1,0:T(8,128)(2,1)S(1)} %collective-permute-done.1.refs_2_), channel_id=1, source_target_pairs={{0,1},{1,0},{2,3},{3,2},{4,5},{5,4},{6,7},{7,6},{8,9},{9,8},{10,11... | collective-permute-start | bytes 393224 | tf_op jit(solution)/shard_map/ppermute | solution.py:302
  18.5 4.1 %collective-permute-start.4 = (bf16[128,512]{1,0:T(8,128)(2,1)S(1)}, bf16[128,512]{1,0:T(8,128)(2,1)S(1)}, u32[]{:S(2)}, u32[]{:S(2)}) collective-permute-start(bf16[128,512]{1,0:T(8,128)(2,1)S(1)} %collective-permute-done.3.refs_4_), channel_id=1, source_target_pairs={{0,1},{1,0},{2,3},{3,2},{4,5},{5,4},{6,7},{7,6},{8,9},{9,8},{10,11... | collective-permute-start | bytes 393224 | tf_op jit(solution)/shard_map/ppermute | solution.py:302
  21.8 1.3 %collective-permute-start.6 = (bf16[128,512]{1,0:T(8,128)(2,1)S(1)}, bf16[128,512]{1,0:T(8,128)(2,1)S(1)}, u32[]{:S(2)}, u32[]{:S(2)}) collective-permute-start(bf16[128,512]{1,0:T(8,128)(2,1)S(1)} %collective-permute-done.5.refs_6_), channel_id=1, source_target_pairs={{0,1},{1,0},{2,3},{3,2},{4,5},{5,4},{6,7},{7,6},{8,9},{9,8},{10,11... | collective-permute-start | bytes 393224 | tf_op jit(solution)/shard_map/ppermute | solution.py:302
  21.8 6.6 %collective-permute-start.8 = (bf16[16,128]{1,0:T(8,128)(2,1)S(1)}, bf16[16,128]{1,0:T(8,128)(2,1)S(1)}, u32[]{:S(2)}, u32[]{:S(2)}) collective-permute-start(bf16[16,128]{1,0:T(8,128)(2,1)S(1)} %get-tuple-element.32.refs_11_.code_ref.refs_12_), channel_id=1, source_target_pairs={{0,248},{8,16},{16,8},{24,32},{32,24},{40,48},{48,40},{56,64},{64,... | collective-permute-start | bytes 12296 | tf_op jit(solution)/shard_map/ppermute | solution.py:310
  24.0 4.4 %collective-permute-start.7 = (bf16[144,256]{1,0:T(8,128)(2,1)S(1)}, bf16[144,256]{1,0:T(8,128)(2,1)S(1)}, u32[]{:S(2)}, u32[]{:S(2)}) collective-permute-start(bf16[144,256]{1,0:T(8,128)(2,1)S(1)} %get-tuple-element.35.kv_ref), channel_id=1, source_target_pairs={{0,8},{8,0},{16,24},{24,16},{32,40},{40,32},{48,56},{56,48},{64,72... | collective-permute-start | bytes 221192 | tf_op jit(solution)/shard_map/ppermute | solution.py:309
  28.5 5.2 %collective-permute-start.15 = (bf16[2,128,128]{2,1,0:T(8,128)(2,1)S(1)}, bf16[2,128,128]{2,1,0:T(8,128)(2,1)S(1)}, u32[]{:S(2)}, u32[]{:S(2)}) collective-permute-start(bf16[2,128,128]{2,1,0:T(8,128)(2,1)S(1)} %get-tuple-element.38), channel_id=1, source_target_pairs={{0,64},{8,72},{16,80},{24,88},{32,96},{40,104},{48,112},{56,120},{... | collective-permute-start | bytes 196616 | tf_op jit(solution)/shard_map/ppermute | solution.py:316
  30.1 5.9 %collective-permute-start.16 = (bf16[2,128,128]{2,1,0:T(8,128)(2,1)S(1)}, bf16[2,128,128]{2,1,0:T(8,128)(2,1)S(1)}, u32[]{:S(2)}, u32[]{:S(2)}) collective-permute-start(bf16[2,128,128]{2,1,0:T(8,128)(2,1)S(1)} %get-tuple-element.38), channel_id=1, source_target_pairs={{0,128},{8,136},{16,144},{24,152},{32,160},{40,168},{48,176},{56,1... | collective-permute-start | bytes 196616 | tf_op jit(solution)/shard_map/ppermute | solution.py:316
  33.1 4.3 %collective-permute-start.17 = (bf16[2,128,128]{2,1,0:T(8,128)(2,1)S(1)}, bf16[2,128,128]{2,1,0:T(8,128)(2,1)S(1)}, u32[]{:S(2)}, u32[]{:S(2)}) collective-permute-start(bf16[2,128,128]{2,1,0:T(8,128)(2,1)S(1)} %get-tuple-element.38), channel_id=1, source_target_pairs={{0,192},{8,200},{16,208},{24,216},{32,224},{40,232},{48,240},{56,2... | collective-permute-start | bytes 196616 | tf_op jit(solution)/shard_map/ppermute | solution.py:316
  37.5 17.0 %collective-permute-start.18 = (bf16[4,2,128,128]{3,2,1,0:T(8,128)(2,1)S(1)}, bf16[4,2,128,128]{3,2,1,0:T(8,128)(2,1)S(1)}, u32[]{:S(2)}, u32[]{:S(2)}) collective-permute-start(bf16[4,2,128,128]{3,2,1,0:T(8,128)(2,1)S(1)} %pad_maximum_fusion.1.refs_5_), channel_id=1, source_target_pairs={{0,16},{8,24},{16,32},{24,40},{32,48},{40,56},{48,0},{56,8},{64,80... | collective-permute-start | bytes 786440 | tf_op jit(solution)/shard_map/ppermute | solution.py:330
  37.6 9.0 %collective-permute-start.11 = (bf16[2,128,128]{2,1,0:T(8,128)(2,1)S(1)}, bf16[2,128,128]{2,1,0:T(8,128)(2,1)S(1)}, u32[]{:S(2)}, u32[]{:S(2)}) collective-permute-start(bf16[2,128,128]{2,1,0:T(8,128)(2,1)S(1)} %get-tuple-element.37), channel_id=1, source_target_pairs={{0,48},{8,56},{16,0},{24,8},{32,16},{40,24},{48,32},{56,40},{64,11... | collective-permute-start | bytes 196616 | tf_op jit(solution)/shard_map/ppermute | solution.py:315
  40.8 13.2 %collective-permute-start.9 = (bf16[2,128,128]{2,1,0:T(8,128)(2,1)S(1)}, bf16[2,128,128]{2,1,0:T(8,128)(2,1)S(1)}, u32[]{:S(2)}, u32[]{:S(2)}) collective-permute-start(bf16[2,128,128]{2,1,0:T(8,128)(2,1)S(1)} %get-tuple-element.37), channel_id=1, source_target_pairs={{0,16},{8,24},{16,32},{24,40},{32,48},{40,56},{48,0},{56,8},{64,80... | collective-permute-start | bytes 196616 | tf_op jit(solution)/shard_map/ppermute | solution.py:315
  40.8 13.2 %collective-permute-start.10 = (bf16[2,128,128]{2,1,0:T(8,128)(2,1)S(1)}, bf16[2,128,128]{2,1,0:T(8,128)(2,1)S(1)}, u32[]{:S(2)}, u32[]{:S(2)}) collective-permute-start(bf16[2,128,128]{2,1,0:T(8,128)(2,1)S(1)} %get-tuple-element.37), channel_id=1, source_target_pairs={{0,32},{8,40},{16,48},{24,56},{32,0},{40,8},{48,16},{56,24},{64,96... | collective-permute-start | bytes 196616 | tf_op jit(solution)/shard_map/ppermute | solution.py:315
  42.4 16.0 %collective-permute-start.19 = (bf16[4,2,128,128]{3,2,1,0:T(8,128)(2,1)S(1)}, bf16[4,2,128,128]{3,2,1,0:T(8,128)(2,1)S(1)}, u32[]{:S(2)}, u32[]{:S(2)}) collective-permute-start(bf16[4,2,128,128]{3,2,1,0:T(8,128)(2,1)S(1)} %pad_maximum_fusion.1.refs_5_), channel_id=1, source_target_pairs={{0,32},{8,40},{16,48},{24,56},{32,0},{40,8},{48,16},{56,24},{64,96... | collective-permute-start | bytes 786440 | tf_op jit(solution)/shard_map/ppermute | solution.py:330
  46.6 11.8 %collective-permute-start.20 = (bf16[4,2,128,128]{3,2,1,0:T(8,128)(2,1)S(1)}, bf16[4,2,128,128]{3,2,1,0:T(8,128)(2,1)S(1)}, u32[]{:S(2)}, u32[]{:S(2)}) collective-permute-start(bf16[4,2,128,128]{3,2,1,0:T(8,128)(2,1)S(1)} %pad_maximum_fusion.1.refs_5_), channel_id=1, source_target_pairs={{0,48},{8,56},{16,0},{24,8},{32,16},{40,24},{48,32},{56,40},{64,11... | collective-permute-start | bytes 786440 | tf_op jit(solution)/shard_map/ppermute | solution.py:330
  54.0 6.4 %collective-permute-start.12 = (bf16[4,2,128,128]{3,2,1,0:T(8,128)(2,1)S(1)}, bf16[4,2,128,128]{3,2,1,0:T(8,128)(2,1)S(1)}, u32[]{:S(2)}, u32[]{:S(2)}) collective-permute-start(bf16[4,2,128,128]{3,2,1,0:T(8,128)(2,1)S(1)} %pad_maximum_fusion.refs_1_), channel_id=1, source_target_pairs={{0,64},{8,72},{16,80},{24,88},{32,96},{40,104},{48,112},{56,120},{... | collective-permute-start | bytes 786440 | tf_op jit(solution)/shard_map/ppermute | solution.py:329
  54.1 8.1 %collective-permute-start.13 = (bf16[4,2,128,128]{3,2,1,0:T(8,128)(2,1)S(1)}, bf16[4,2,128,128]{3,2,1,0:T(8,128)(2,1)S(1)}, u32[]{:S(2)}, u32[]{:S(2)}) collective-permute-start(bf16[4,2,128,128]{3,2,1,0:T(8,128)(2,1)S(1)} %pad_maximum_fusion.refs_1_), channel_id=1, source_target_pairs={{0,128},{8,136},{16,144},{24,152},{32,160},{40,168},{48,176},{56,1... | collective-permute-start | bytes 786440 | tf_op jit(solution)/shard_map/ppermute | solution.py:329
  54.5 10.3 %collective-permute-start.14 = (bf16[4,2,128,128]{3,2,1,0:T(8,128)(2,1)S(1)}, bf16[4,2,128,128]{3,2,1,0:T(8,128)(2,1)S(1)}, u32[]{:S(2)}, u32[]{:S(2)}) collective-permute-start(bf16[4,2,128,128]{3,2,1,0:T(8,128)(2,1)S(1)} %pad_maximum_fusion.refs_1_), channel_id=1, source_target_pairs={{0,192},{8,200},{16,208},{24,216},{32,224},{40,232},{48,240},{56,2... | collective-permute-start | bytes 786440 | tf_op jit(solution)/shard_map/ppermute | solution.py:329
  (4 other events, 3.4 us)

commit v5 on v4

--- a/solution.py
+++ b/solution.py
@@ -91,13 +91,14 @@
 def kv_kernel(*refs):
     pieces = refs[:8]
     pad_ref, wk_ref, wv_ref, code_ref = refs[8:12]
-    x_ref, kv_ref, mkv_ref = refs[12:]
+    x_ref, kv_ref, mkv_ref, send_ref = refs[12:]
     me = lax.axis_index("kv")
     for dz in range(4):
         for dc in range(2):
             source = lax.rem(me // 2 + 4 - dz, 4) * 2 + lax.rem(me + dc, 2)
             x_ref[:ROWS, pl.ds(pl.multiple_of(source * WIDTH, WIDTH), WIDTH)] = pieces[2 * dz + dc][...]
     x_ref[ROWS:, :] = pad_ref[...]
+    send_ref[...] = code_ref[...]
     x = x_ref[...]
     for part, w_ref in enumerate((wk_ref, wv_ref)):
         lanes = slice(part * HEAD, (part + 1) * HEAD)
@@ -300,20 +301,29 @@
     for piece in (own, *moved):
         piece, _ = lax.optimization_barrier((piece, pad))
         pieces += [piece, lax.ppermute(piece, "kv", kv_pairs(0, 1))]
-    x, kv, mask_kv = call(
+    x, kv, mask_kv, send = call(
         kv_kernel,
-        [((ROWS + PAD, 8 * WIDTH), BF16), ((ROWS + PAD, 2 * HEAD), BF16), ((PAD, 2 * HEAD), BF16)],
+        [
+            ((ROWS + PAD, 8 * WIDTH), BF16),
+            ((ROWS + PAD, 2 * HEAD), BF16),
+            ((PAD, 2 * HEAD), BF16),
+            ((PAD, ROWS), BF16),
+        ],
         [*pieces, pad, wk, wv, code],
         (1 << 29, 3 << 20),
     )
     pair = lax.ppermute(kv, "ctx", ctx_pairs(0, 0, 1))
-    swap = lax.ppermute(code, "ctx", [(i, (i + 2 * (i % 2) - 1) % 32) for i in range(32)])
+    swap = lax.ppermute(send, "ctx", [(i, (i + 2 * (i % 2) - 1) % 32) for i in range(32)])
     pair, swap = lax.optimization_barrier((pair, swap))
     k = jnp.stack([kv[:ROWS, :HEAD], pair[:ROWS, :HEAD]])
     v = jnp.stack([kv[:ROWS, HEAD:], pair[:ROWS, HEAD:]])
     k, v = lax.optimization_barrier((k, v))
-    ks = jnp.stack([k] + [lax.ppermute(k, "ctx", ctx_pairs(0, d, 0)) for d in (1, 2, 3)])
-    vs = jnp.stack([v] + [lax.ppermute(v, "ctx", ctx_pairs(d, 0, 0)) for d in (1, 2, 3)])
+    ks = [lax.ppermute(k, "ctx", ctx_pairs(0, d, 0)) for d in (1, 2, 3)]
+    vs = [lax.ppermute(v, "ctx", ctx_pairs(d, 0, 0)) for d in (1, 2, 3)]
+    moved = lax.optimization_barrier((*ks, *vs))
+    ks = jnp.stack([k, *moved[:3]])
+    vs = jnp.stack([v, *moved[3:]])
+    ks, vs = lax.optimization_barrier((ks, vs))
     q, flag, own_cut = call(
         q_kernel,
         [((GROUP, 2 * ROWS, HEAD), BF16), ((ROWS, HEAD), F32), ((ROWS, HEAD), F32)],

time: 72.3 us -> 68.9 us (0.953)
  the two profiles are of different devices: /device:TPU:8 before, /device:TPU:24 now
where the time goes in v5:
time: 68.9 us; the launch traced here: 68.4 us
  starting transfers between devices  32.2 us (47%)
  waiting for transfers between devices  19 us (28%)
  Pallas kernels  10.9 us (16%)
  local copies, waits for them, and re-layouts  5.38 us (8%)
  between operations  0.74 us (1%)
    pallas_call x5, Pallas kernels, call(): pl.pallas_call(kernel, out_shape=[jax.ShapeDtypeStruct(s, t) for s, t in...  10.9 us
    ppermute x3, starting transfers between devices, shards(): moved = [lax.ppermute(hidden, 'kv', kv_pairs(d, 0)) for d in (1, 2, 3)]  10.2 us
    ppermute x3, waiting for transfers between devices, shards(): lax.ppermute(vs, 'ctx', ctx_pairs(0, d, 0))  5.95 us
    ppermute x3, starting transfers between devices, shards(): lax.ppermute(vs, 'ctx', ctx_pairs(0, d, 0))  5.92 us
    ppermute x3, starting transfers between devices, shards(): vs = [lax.ppermute(v, 'ctx', ctx_pairs(d, 0, 0)) for d in (1, 2, 3)]  4.71 us
    unnamed x14, local copies, waits for them, and re-layouts  4.67 us
    ppermute x3, starting transfers between devices, shards(): lax.ppermute(ks, 'ctx', ctx_pairs(d, 0, 0))  4.45 us
    ppermute x1, starting transfers between devices, shards(): lax.ppermute(send, 'ctx', [(i, (i + 2 * (i % 2) - 1) % 32) for i in range...  4.23 us
  transfers between devices with their start and end apart: 21, of which 15 were waited for; matrix products, arithmetic and copies ran while one was open for 1% of the time, Pallas kernels for 4%

profile of v5, /device:TPU:24, one launch (start us, length us, event | category | flops | bytes accessed | tf_op | source)
XLA Modules:
  0.0 68.4 jit_solution(12941030492581673584)
XLA Ops:
  0.6 6.4 %collective-permute-start.5 = (bf16[128,512]{1,0:T(8,128)(2,1)}, bf16[128,512]{1,0:T(8,128)(2,1)S(1)}, u32[]{:S(2)}, u32[]{:S(2)}) collective-permute-start(bf16[128,512]{1,0:T(8,128)(2,1)} %refs_0_.1), channel_id=1, source_target_pairs={{0,6},{1,7},{2,0},{3,1},{4,2},{5,3},{6,4},{7,5},{8,14},{9,15},{10,... | collective-permute-start | bytes 393224 | tf_op jit(solution)/shard_map/ppermute | solution.py:280
  7.0 1.0 %collective-permute-start.3 = (bf16[128,512]{1,0:T(8,128)(2,1)}, bf16[128,512]{1,0:T(8,128)(2,1)S(1)}, u32[]{:S(2)}, u32[]{:S(2)}) collective-permute-start(bf16[128,512]{1,0:T(8,128)(2,1)} %refs_0_.1), channel_id=1, source_target_pairs={{0,4},{1,5},{2,6},{3,7},{4,0},{5,1},{6,2},{7,3},{8,12},{9,13},{10,... | collective-permute-start | bytes 393224 | tf_op jit(solution)/shard_map/ppermute | solution.py:280
  8.0 2.8 %collective-permute-start.1 = (bf16[128,512]{1,0:T(8,128)(2,1)}, bf16[128,512]{1,0:T(8,128)(2,1)S(1)}, u32[]{:S(2)}, u32[]{:S(2)}) collective-permute-start(bf16[128,512]{1,0:T(8,128)(2,1)} %refs_0_.1), channel_id=1, source_target_pairs={{0,2},{1,3},{2,4},{3,5},{4,6},{5,7},{6,0},{7,1},{8,10},{9,11},{10,... | collective-permute-start | bytes 393224 | tf_op jit(solution)/shard_map/ppermute | solution.py:280
  11.6 1.2 %copy-done.1 = bf16[4096,128]{1,0:T(8,128)(2,1)S(1)} copy-done((bf16[4096,128]{1,0:T(8,128)(2,1)S(1)}, bf16[4096,128]{1,0:T(8,128)(2,1)}, u32[]{:S(2)}) %copy-start.1) | copy-done | bytes 1048600
  12.8 1.2 %copy-done.2 = bf16[4096,128]{1,0:T(8,128)(2,1)S(1)} copy-done((bf16[4096,128]{1,0:T(8,128)(2,1)S(1)}, bf16[4096,128]{1,0:T(8,128)(2,1)}, u32[]{:S(2)}) %copy-start.2) | copy-done | bytes 1048600
  14.0 0.9 %copy-done.3 = bf16[128,512]{1,0:T(8,128)(2,1)S(1)} copy-done((bf16[128,512]{1,0:T(8,128)(2,1)S(1)}, bf16[128,512]{1,0:T(8,128)(2,1)}, u32[]{:S(2)}) %copy-start.3) | copy-done | bytes 131096
  16.7 1.8 %collective-permute-done.5.refs_6_ = bf16[128,512]{1,0:T(8,128)(2,1)S(1)} collective-permute-done((bf16[128,512]{1,0:T(8,128)(2,1)}, bf16[128,512]{1,0:T(8,128)(2,1)S(1)}, u32[]{:S(2)}, u32[]{:S(2)}) %collective-permute-start.5) | collective-permute-done | bytes 131104 | tf_op jit(solution)/shard_map/ppermute | solution.py:280
  18.5 1.8 %collective-permute-done.3.refs_4_ = bf16[128,512]{1,0:T(8,128)(2,1)S(1)} collective-permute-done((bf16[128,512]{1,0:T(8,128)(2,1)}, bf16[128,512]{1,0:T(8,128)(2,1)S(1)}, u32[]{:S(2)}, u32[]{:S(2)}) %collective-permute-start.3) | collective-permute-done | bytes 131104 | tf_op jit(solution)/shard_map/ppermute | solution.py:280
  23.1 4.2 %collective-permute-start.8 = (bf16[16,128]{1,0:T(8,128)(2,1)S(1)}, bf16[16,128]{1,0:T(8,128)(2,1)S(1)}, u32[]{:S(2)}, u32[]{:S(2)}) collective-permute-start(bf16[16,128]{1,0:T(8,128)(2,1)S(1)} %get-tuple-element.45), channel_id=1, source_target_pairs={{0,248},{8,16},{16,8},{24,32},{32,24},{40,48},{48,40},{56,64},{64,... | collective-permute-start | bytes 12296 | tf_op jit(solution)/shard_map/ppermute | solution.py:316
  27.3 2.5 %collective-permute-done.8.refs_14_ = bf16[16,128]{1,0:T(8,128)(2,1)S(1)} collective-permute-done((bf16[16,128]{1,0:T(8,128)(2,1)S(1)}, bf16[16,128]{1,0:T(8,128)(2,1)S(1)}, u32[]{:S(2)}, u32[]{:S(2)}) %collective-permute-start.8) | collective-permute-done | bytes 4128 | tf_op jit(solution)/shard_map/ppermute | solution.py:316
  29.8 1.9 %collective-permute-done.7.refs_13_ = bf16[144,256]{1,0:T(8,128)(2,1)S(1)} collective-permute-done((bf16[144,256]{1,0:T(8,128)(2,1)S(1)}, bf16[144,256]{1,0:T(8,128)(2,1)S(1)}, u32[]{:S(2)}, u32[]{:S(2)}) %collective-permute-start.7) | collective-permute-done | bytes 73760 | tf_op jit(solution)/shard_map/ppermute | solution.py:315
  34.5 3.2 %collective-permute-start.13 = (bf16[2,128,128]{2,1,0:T(8,128)(2,1)S(1)}, bf16[2,128,128]{2,1,0:T(8,128)(2,1)S(1)}, u32[]{:S(2)}, u32[]{:S(2)}) collective-permute-start(bf16[2,128,128]{2,1,0:T(8,128)(2,1)S(1)} %get-tuple-element.48), channel_id=1, source_target_pairs={{0,128},{8,136},{16,144},{24,152},{32,160},{40,168},{48,176},{56,1... | collective-permute-start | bytes 196616 | tf_op jit(solution)/shard_map/ppermute | solution.py:322
  39.3 1.4 %collective-permute-done.13 = bf16[2,128,128]{2,1,0:T(8,128)(2,1)S(1)} collective-permute-done((bf16[2,128,128]{2,1,0:T(8,128)(2,1)S(1)}, bf16[2,128,128]{2,1,0:T(8,128)(2,1)S(1)}, u32[]{:S(2)}, u32[]{:S(2)}) %collective-permute-start.13) | collective-permute-done | bytes 65568 | tf_op jit(solution)/shard_map/ppermute | solution.py:322
  40.7 1.3 %collective-permute-done.12 = bf16[2,128,128]{2,1,0:T(8,128)(2,1)S(1)} collective-permute-done((bf16[2,128,128]{2,1,0:T(8,128)(2,1)S(1)}, bf16[2,128,128]{2,1,0:T(8,128)(2,1)S(1)}, u32[]{:S(2)}, u32[]{:S(2)}) %collective-permute-start.12) | collective-permute-done | bytes 65568 | tf_op jit(solution)/shard_map/ppermute | solution.py:322
  42.3 3.3 %collective-permute-start.16 = (bf16[4,2,128,128]{3,2,1,0:T(8,128)(2,1)S(1)}, bf16[4,2,128,128]{3,2,1,0:T(8,128)(2,1)S(1)}, u32[]{:S(2)}, u32[]{:S(2)}) collective-permute-start(bf16[4,2,128,128]{3,2,1,0:T(8,128)(2,1)S(1)} %pad_maximum_fusion.refs_1_), channel_id=1, source_target_pairs={{0,128},{8,136},{16,144},{24,152},{32,160},{40,168},{48,176},{56,1... | collective-permute-start | bytes 786440 | tf_op jit(solution)/shard_map/ppermute | solution.py:339
  45.6 0.9 %collective-permute-start.15 = (bf16[4,2,128,128]{3,2,1,0:T(8,128)(2,1)S(1)}, bf16[4,2,128,128]{3,2,1,0:T(8,128)(2,1)S(1)}, u32[]{:S(2)}, u32[]{:S(2)}) collective-permute-start(bf16[4,2,128,128]{3,2,1,0:T(8,128)(2,1)S(1)} %pad_maximum_fusion.refs_1_), channel_id=1, source_target_pairs={{0,64},{8,72},{16,80},{24,88},{32,96},{40,104},{48,112},{56,120},{... | collective-permute-start | bytes 786440 | tf_op jit(solution)/shard_map/ppermute | solution.py:339
  46.5 2.7 %collective-permute-start.20 = (bf16[4,2,128,128]{3,2,1,0:T(8,128)(2,1)S(1)}, bf16[4,2,128,128]{3,2,1,0:T(8,128)(2,1)S(1)}, u32[]{:S(2)}, u32[]{:S(2)}) collective-permute-start(bf16[4,2,128,128]{3,2,1,0:T(8,128)(2,1)S(1)} %pad_maximum_fusion.1.refs_5_), channel_id=1, source_target_pairs={{0,48},{8,56},{16,0},{24,8},{32,16},{40,24},{48,32},{56,40},{64,11... | collective-permute-start | bytes 786440 | tf_op jit(solution)/shard_map/ppermute | solution.py:340
  49.2 1.8 %collective-permute-start.19 = (bf16[4,2,128,128]{3,2,1,0:T(8,128)(2,1)S(1)}, bf16[4,2,128,128]{3,2,1,0:T(8,128)(2,1)S(1)}, u32[]{:S(2)}, u32[]{:S(2)}) collective-permute-start(bf16[4,2,128,128]{3,2,1,0:T(8,128)(2,1)S(1)} %pad_maximum_fusion.1.refs_5_), channel_id=1, source_target_pairs={{0,32},{8,40},{16,48},{24,56},{32,0},{40,8},{48,16},{56,24},{64,96... | collective-permute-start | bytes 786440 | tf_op jit(solution)/shard_map/ppermute | solution.py:340
  51.3 1.4 %collective-permute-start.18 = (bf16[4,2,128,128]{3,2,1,0:T(8,128)(2,1)S(1)}, bf16[4,2,128,128]{3,2,1,0:T(8,128)(2,1)S(1)}, u32[]{:S(2)}, u32[]{:S(2)}) collective-permute-start(bf16[4,2,128,128]{3,2,1,0:T(8,128)(2,1)S(1)} %pad_maximum_fusion.1.refs_5_), channel_id=1, source_target_pairs={{0,16},{8,24},{16,32},{24,40},{32,48},{40,56},{48,0},{56,8},{64,80... | collective-permute-start | bytes 786440 | tf_op jit(solution)/shard_map/ppermute | solution.py:340
  52.8 1.4 %shard_map.97 = (bf16[4,256,128]{2,1,0:T(8,128)(2,1)S(1)}, f32[128,128]{1,0:T(8,128)S(1)}, f32[128,128]{1,0:T(8,128)S(1)}) custom-call(bf16[144,4096]{1,0:T(8,128)(2,1)S(1)} %get-tuple-element.42.x_ref, bf16[4096,512]{1,0:T(8,128)(2,1)S(1)} %copy-done, bf16[16,128]{1,0:T(8,128)(2,1)S(1)} %get-tuple-element.41.refs_11_.code_ref.refs_12_, s32[1,256]{1,0:T(1,128)S(1)} %bitcast.19), custom_call_target="tpu_custom_call" | custom-call | flops 1073741824 | bytes 5242880 | tf_op jit(solution)/shard_map/pallas_call | solution.py:51
  55.0 1.5 %collective-permute-done.20.refs_8_ = bf16[4,2,128,128]{3,2,1,0:T(8,128)(2,1)S(1)} collective-permute-done((bf16[4,2,128,128]{3,2,1,0:T(8,128)(2,1)S(1)}, bf16[4,2,128,128]{3,2,1,0:T(8,128)(2,1)S(1)}, u32[]{:S(2)}, u32[]{:S(2)}) %collective-permute-start.20) | collective-permute-done | bytes 262176 | tf_op jit(solution)/shard_map/ppermute | solution.py:340
  56.5 1.3 %collective-permute-done.19.refs_7_ = bf16[4,2,128,128]{3,2,1,0:T(8,128)(2,1)S(1)} collective-permute-done((bf16[4,2,128,128]{3,2,1,0:T(8,128)(2,1)S(1)}, bf16[4,2,128,128]{3,2,1,0:T(8,128)(2,1)S(1)}, u32[]{:S(2)}, u32[]{:S(2)}) %collective-permute-start.19) | collective-permute-done | bytes 262176 | tf_op jit(solution)/shard_map/ppermute | solution.py:340
  57.8 3.2 %collective-permute-done.18.refs_6_ = bf16[4,2,128,128]{3,2,1,0:T(8,128)(2,1)S(1)} collective-permute-done((bf16[4,2,128,128]{3,2,1,0:T(8,128)(2,1)S(1)}, bf16[4,2,128,128]{3,2,1,0:T(8,128)(2,1)S(1)}, u32[]{:S(2)}, u32[]{:S(2)}) %collective-permute-start.18) | collective-permute-done | bytes 262176 | tf_op jit(solution)/shard_map/ppermute | solution.py:340
  61.0 7.4 %shard_map.99 = (bf16[128,512]{1,0:T(8,128)(2,1)}, bf16[128,512]{1,0:T(8,128)(2,1)}) custom-call(bf16[4,256,128]{2,1,0:T(8,128)(2,1)S(1)} %get-tuple-element.43.q_ref.refs_0_, bf16[4,2,128,128]{3,2,1,0:T(8,128)(2,1)S(1)} %pad_maximum_fusion.refs_1_, bf16[4,2,128,128]{3,2,1,0:T(8,128)(2,1)S(1)} %collective-permute-done.15.refs_2_, ...), custom_call_target="tpu_custom_call" | custom-call | flops 4294967296 | bytes 4194304 | tf_op jit(solution)/shard_map/pallas_call | solution.py:51
  (43 shorter events, 11.1 us)
Async XLA Ops:
  0.6 52.1 %copy-start = (bf16[4096,512]{1,0:T(8,128)(2,1)S(1)}, bf16[4096,512]{1,0:T(8,128)(2,1)}, u32[]{:S(2)}) copy-start(bf16[4096,512]{1,0:T(8,128)(2,1)} %wq_ref.1) | copy-start | bytes 12582916
  0.6 17.9 %collective-permute-start.5 = (bf16[128,512]{1,0:T(8,128)(2,1)}, bf16[128,512]{1,0:T(8,128)(2,1)S(1)}, u32[]{:S(2)}, u32[]{:S(2)}) collective-permute-start(bf16[128,512]{1,0:T(8,128)(2,1)} %refs_0_.1), channel_id=1, source_target_pairs={{0,6},{1,7},{2,0},{3,1},{4,2},{5,3},{6,4},{7,5},{8,14},{9,15},{10,... | collective-permute-start | bytes 393224 | tf_op jit(solution)/shard_map/ppermute | solution.py:280
  7.0 13.3 %collective-permute-start.3 = (bf16[128,512]{1,0:T(8,128)(2,1)}, bf16[128,512]{1,0:T(8,128)(2,1)S(1)}, u32[]{:S(2)}, u32[]{:S(2)}) collective-permute-start(bf16[128,512]{1,0:T(8,128)(2,1)} %refs_0_.1), channel_id=1, source_target_pairs={{0,4},{1,5},{2,6},{3,7},{4,0},{5,1},{6,2},{7,3},{8,12},{9,13},{10,... | collective-permute-start | bytes 393224 | tf_op jit(solution)/shard_map/ppermute | solution.py:280
  8.0 12.3 %collective-permute-start.1 = (bf16[128,512]{1,0:T(8,128)(2,1)}, bf16[128,512]{1,0:T(8,128)(2,1)S(1)}, u32[]{:S(2)}, u32[]{:S(2)}) collective-permute-start(bf16[128,512]{1,0:T(8,128)(2,1)} %refs_0_.1), channel_id=1, source_target_pairs={{0,2},{1,3},{2,4},{3,5},{4,6},{5,7},{6,0},{7,1},{8,10},{9,11},{10,... | collective-permute-start | bytes 393224 | tf_op jit(solution)/shard_map/ppermute | solution.py:280
  11.5 1.2 %copy-start.1 = (bf16[4096,128]{1,0:T(8,128)(2,1)S(1)}, bf16[4096,128]{1,0:T(8,128)(2,1)}, u32[]{:S(2)}) copy-start(bf16[4096,128]{1,0:T(8,128)(2,1)} %refs_1_.1) | copy-start | bytes 3145732
  16.2 36.5 %copy-start.4 = (s32[256]{0:T(256)S(1)}, s32[256]{0:T(256)}, u32[]{:S(2)}) copy-start(s32[256]{0:T(256)} %param.11) | copy-start | bytes 3076
  16.6 4.2 %collective-permute-start = (bf16[128,512]{1,0:T(8,128)(2,1)S(1)}, bf16[128,512]{1,0:T(8,128)(2,1)S(1)}, u32[]{:S(2)}, u32[]{:S(2)}) collective-permute-start(bf16[128,512]{1,0:T(8,128)(2,1)S(1)} %get-tuple-element.35.refs_0_), channel_id=1, source_target_pairs={{0,1},{1,0},{2,3},{3,2},{4,5},{5,4},{6,7},{7,6},{8,9},{9,8},{10,11... | collective-permute-start | bytes 393224 | tf_op jit(solution)/shard_map/ppermute | solution.py:303
  20.3 1.3 %collective-permute-start.2 = (bf16[128,512]{1,0:T(8,128)(2,1)S(1)}, bf16[128,512]{1,0:T(8,128)(2,1)S(1)}, u32[]{:S(2)}, u32[]{:S(2)}) collective-permute-start(bf16[128,512]{1,0:T(8,128)(2,1)S(1)} %collective-permute-done.1.refs_2_), channel_id=1, source_target_pairs={{0,1},{1,0},{2,3},{3,2},{4,5},{5,4},{6,7},{7,6},{8,9},{9,8},{10,11... | collective-permute-start | bytes 393224 | tf_op jit(solution)/shard_map/ppermute | solution.py:303
  20.3 1.5 %collective-permute-start.4 = (bf16[128,512]{1,0:T(8,128)(2,1)S(1)}, bf16[128,512]{1,0:T(8,128)(2,1)S(1)}, u32[]{:S(2)}, u32[]{:S(2)}) collective-permute-start(bf16[128,512]{1,0:T(8,128)(2,1)S(1)} %collective-permute-done.3.refs_4_), channel_id=1, source_target_pairs={{0,1},{1,0},{2,3},{3,2},{4,5},{5,4},{6,7},{7,6},{8,9},{9,8},{10,11... | collective-permute-start | bytes 393224 | tf_op jit(solution)/shard_map/ppermute | solution.py:303
  20.8 1.3 %collective-permute-start.6 = (bf16[128,512]{1,0:T(8,128)(2,1)S(1)}, bf16[128,512]{1,0:T(8,128)(2,1)S(1)}, u32[]{:S(2)}, u32[]{:S(2)}) collective-permute-start(bf16[128,512]{1,0:T(8,128)(2,1)S(1)} %collective-permute-done.5.refs_6_), channel_id=1, source_target_pairs={{0,1},{1,0},{2,3},{3,2},{4,5},{5,4},{6,7},{7,6},{8,9},{9,8},{10,11... | collective-permute-start | bytes 393224 | tf_op jit(solution)/shard_map/ppermute | solution.py:303
  23.1 6.7 %collective-permute-start.8 = (bf16[16,128]{1,0:T(8,128)(2,1)S(1)}, bf16[16,128]{1,0:T(8,128)(2,1)S(1)}, u32[]{:S(2)}, u32[]{:S(2)}) collective-permute-start(bf16[16,128]{1,0:T(8,128)(2,1)S(1)} %get-tuple-element.45), channel_id=1, source_target_pairs={{0,248},{8,16},{16,8},{24,32},{32,24},{40,48},{48,40},{56,64},{64,... | collective-permute-start | bytes 12296 | tf_op jit(solution)/shard_map/ppermute | solution.py:316
  27.3 4.4 %collective-permute-start.7 = (bf16[144,256]{1,0:T(8,128)(2,1)S(1)}, bf16[144,256]{1,0:T(8,128)(2,1)S(1)}, u32[]{:S(2)}, u32[]{:S(2)}) collective-permute-start(bf16[144,256]{1,0:T(8,128)(2,1)S(1)} %get-tuple-element.44.kv_ref), channel_id=1, source_target_pairs={{0,8},{8,0},{16,24},{24,16},{32,40},{40,32},{48,56},{56,48},{64,72... | collective-permute-start | bytes 221192 | tf_op jit(solution)/shard_map/ppermute | solution.py:315
  31.7 6.1 %collective-permute-start.11 = (bf16[2,128,128]{2,1,0:T(8,128)(2,1)S(1)}, bf16[2,128,128]{2,1,0:T(8,128)(2,1)S(1)}, u32[]{:S(2)}, u32[]{:S(2)}) collective-permute-start(bf16[2,128,128]{2,1,0:T(8,128)(2,1)S(1)} %get-tuple-element.47), channel_id=1, source_target_pairs={{0,48},{8,56},{16,0},{24,8},{32,16},{40,24},{48,32},{56,40},{64,11... | collective-permute-start | bytes 196616 | tf_op jit(solution)/shard_map/ppermute | solution.py:321
  32.4 6.1 %collective-permute-start.10 = (bf16[2,128,128]{2,1,0:T(8,128)(2,1)S(1)}, bf16[2,128,128]{2,1,0:T(8,128)(2,1)S(1)}, u32[]{:S(2)}, u32[]{:S(2)}) collective-permute-start(bf16[2,128,128]{2,1,0:T(8,128)(2,1)S(1)} %get-tuple-element.47), channel_id=1, source_target_pairs={{0,32},{8,40},{16,48},{24,56},{32,0},{40,8},{48,16},{56,24},{64,96... | collective-permute-start | bytes 196616 | tf_op jit(solution)/shard_map/ppermute | solution.py:321
  32.9 6.0 %collective-permute-start.9 = (bf16[2,128,128]{2,1,0:T(8,128)(2,1)S(1)}, bf16[2,128,128]{2,1,0:T(8,128)(2,1)S(1)}, u32[]{:S(2)}, u32[]{:S(2)}) collective-permute-start(bf16[2,128,128]{2,1,0:T(8,128)(2,1)S(1)} %get-tuple-element.47), channel_id=1, source_target_pairs={{0,16},{8,24},{16,32},{24,40},{32,48},{40,56},{48,0},{56,8},{64,80... | collective-permute-start | bytes 196616 | tf_op jit(solution)/shard_map/ppermute | solution.py:321
  33.8 5.5 %collective-permute-start.14 = (bf16[2,128,128]{2,1,0:T(8,128)(2,1)S(1)}, bf16[2,128,128]{2,1,0:T(8,128)(2,1)S(1)}, u32[]{:S(2)}, u32[]{:S(2)}) collective-permute-start(bf16[2,128,128]{2,1,0:T(8,128)(2,1)S(1)} %get-tuple-element.48), channel_id=1, source_target_pairs={{0,192},{8,200},{16,208},{24,216},{32,224},{40,232},{48,240},{56,2... | collective-permute-start | bytes 196616 | tf_op jit(solution)/shard_map/ppermute | solution.py:322
  34.5 6.1 %collective-permute-start.13 = (bf16[2,128,128]{2,1,0:T(8,128)(2,1)S(1)}, bf16[2,128,128]{2,1,0:T(8,128)(2,1)S(1)}, u32[]{:S(2)}, u32[]{:S(2)}) collective-permute-start(bf16[2,128,128]{2,1,0:T(8,128)(2,1)S(1)} %get-tuple-element.48), channel_id=1, source_target_pairs={{0,128},{8,136},{16,144},{24,152},{32,160},{40,168},{48,176},{56,1... | collective-permute-start | bytes 196616 | tf_op jit(solution)/shard_map/ppermute | solution.py:322
  37.7 4.3 %collective-permute-start.12 = (bf16[2,128,128]{2,1,0:T(8,128)(2,1)S(1)}, bf16[2,128,128]{2,1,0:T(8,128)(2,1)S(1)}, u32[]{:S(2)}, u32[]{:S(2)}) collective-permute-start(bf16[2,128,128]{2,1,0:T(8,128)(2,1)S(1)} %get-tuple-element.48), channel_id=1, source_target_pairs={{0,64},{8,72},{16,80},{24,88},{32,96},{40,104},{48,112},{56,120},{... | collective-permute-start | bytes 196616 | tf_op jit(solution)/shard_map/ppermute | solution.py:322
  42.1 9.3 %collective-permute-start.17 = (bf16[4,2,128,128]{3,2,1,0:T(8,128)(2,1)S(1)}, bf16[4,2,128,128]{3,2,1,0:T(8,128)(2,1)S(1)}, u32[]{:S(2)}, u32[]{:S(2)}) collective-permute-start(bf16[4,2,128,128]{3,2,1,0:T(8,128)(2,1)S(1)} %pad_maximum_fusion.refs_1_), channel_id=1, source_target_pairs={{0,192},{8,200},{16,208},{24,216},{32,224},{40,232},{48,240},{56,2... | collective-permute-start | bytes 786440 | tf_op jit(solution)/shard_map/ppermute | solution.py:339
  42.3 12.7 %collective-permute-start.16 = (bf16[4,2,128,128]{3,2,1,0:T(8,128)(2,1)S(1)}, bf16[4,2,128,128]{3,2,1,0:T(8,128)(2,1)S(1)}, u32[]{:S(2)}, u32[]{:S(2)}) collective-permute-start(bf16[4,2,128,128]{3,2,1,0:T(8,128)(2,1)S(1)} %pad_maximum_fusion.refs_1_), channel_id=1, source_target_pairs={{0,128},{8,136},{16,144},{24,152},{32,160},{40,168},{48,176},{56,1... | collective-permute-start | bytes 786440 | tf_op jit(solution)/shard_map/ppermute | solution.py:339
  45.6 9.4 %collective-permute-start.15 = (bf16[4,2,128,128]{3,2,1,0:T(8,128)(2,1)S(1)}, bf16[4,2,128,128]{3,2,1,0:T(8,128)(2,1)S(1)}, u32[]{:S(2)}, u32[]{:S(2)}) collective-permute-start(bf16[4,2,128,128]{3,2,1,0:T(8,128)(2,1)S(1)} %pad_maximum_fusion.refs_1_), channel_id=1, source_target_pairs={{0,64},{8,72},{16,80},{24,88},{32,96},{40,104},{48,112},{56,120},{... | collective-permute-start | bytes 786440 | tf_op jit(solution)/shard_map/ppermute | solution.py:339
  46.5 10.0 %collective-permute-start.20 = (bf16[4,2,128,128]{3,2,1,0:T(8,128)(2,1)S(1)}, bf16[4,2,128,128]{3,2,1,0:T(8,128)(2,1)S(1)}, u32[]{:S(2)}, u32[]{:S(2)}) collective-permute-start(bf16[4,2,128,128]{3,2,1,0:T(8,128)(2,1)S(1)} %pad_maximum_fusion.1.refs_5_), channel_id=1, source_target_pairs={{0,48},{8,56},{16,0},{24,8},{32,16},{40,24},{48,32},{56,40},{64,11... | collective-permute-start | bytes 786440 | tf_op jit(solution)/shard_map/ppermute | solution.py:340
  49.2 8.6 %collective-permute-start.19 = (bf16[4,2,128,128]{3,2,1,0:T(8,128)(2,1)S(1)}, bf16[4,2,128,128]{3,2,1,0:T(8,128)(2,1)S(1)}, u32[]{:S(2)}, u32[]{:S(2)}) collective-permute-start(bf16[4,2,128,128]{3,2,1,0:T(8,128)(2,1)S(1)} %pad_maximum_fusion.1.refs_5_), channel_id=1, source_target_pairs={{0,32},{8,40},{16,48},{24,56},{32,0},{40,8},{48,16},{56,24},{64,96... | collective-permute-start | bytes 786440 | tf_op jit(solution)/shard_map/ppermute | solution.py:340
  51.3 9.7 %collective-permute-start.18 = (bf16[4,2,128,128]{3,2,1,0:T(8,128)(2,1)S(1)}, bf16[4,2,128,128]{3,2,1,0:T(8,128)(2,1)S(1)}, u32[]{:S(2)}, u32[]{:S(2)}) collective-permute-start(bf16[4,2,128,128]{3,2,1,0:T(8,128)(2,1)S(1)} %pad_maximum_fusion.1.refs_5_), channel_id=1, source_target_pairs={{0,16},{8,24},{16,32},{24,40},{32,48},{40,56},{48,0},{56,8},{64,80... | collective-permute-start | bytes 786440 | tf_op jit(solution)/shard_map/ppermute | solution.py:340
  (4 other events, 3.4 us)

commit v6 on v5

--- a/solution.py
+++ b/solution.py
@@ -82,23 +82,23 @@
         copy.start()
     for copy in copies:
         copy.wait()
-    ids = jnp.broadcast_to(ids_ref[...].astype(F32), (8, ROWS))
-    order = jnp.broadcast_to(order_ref[...].astype(F32), (8, ROWS))
-    code_ref[...] = jnp.concatenate([ids, order], axis=0).astype(BF16)
+    ids = jnp.broadcast_to(ids_ref[...].astype(F32), (PAD, ROWS))
+    order = jnp.broadcast_to(order_ref[...].astype(F32), (PAD, ROWS))
+    row = lax.broadcasted_iota(jnp.int32, (PAD, ROWS), 0)
+    code_ref[...] = jnp.where(lax.rem(row, 2) == 0, ids, order).astype(BF16)
     pad_ref[...] = jnp.broadcast_to(embed_ref[...], pad_ref.shape)
 
 
 def kv_kernel(*refs):
     pieces = refs[:8]
     pad_ref, wk_ref, wv_ref, code_ref = refs[8:12]
-    x_ref, kv_ref, mkv_ref, send_ref = refs[12:]
+    x_ref, kv_ref, mkv_ref = refs[12:]
     me = lax.axis_index("kv")
     for dz in range(4):
         for dc in range(2):
             source = lax.rem(me // 2 + 4 - dz, 4) * 2 + lax.rem(me + dc, 2)
             x_ref[:ROWS, pl.ds(pl.multiple_of(source * WIDTH, WIDTH), WIDTH)] = pieces[2 * dz + dc][...]
     x_ref[ROWS:, :] = pad_ref[...]
-    send_ref[...] = code_ref[...]
     x = x_ref[...]
     for part, w_ref in enumerate((wk_ref, wv_ref)):
         lanes = slice(part * HEAD, (part + 1) * HEAD)
@@ -108,10 +108,38 @@
         mkv_ref[:, lanes] = product[ROWS:]
 
 
+def pair_kernel(own_ref, other_ref, k_ref, v_ref):
+    for i, ref in enumerate((own_ref, other_ref)):
+        rows = slice(i * ROWS, (i + 1) * ROWS)
+        k_ref[rows, :] = ref[:ROWS, :HEAD]
+        v_ref[rows, :] = ref[:ROWS, HEAD:]
+    row = lax.broadcasted_iota(jnp.int32, (PAD, HEAD), 0)
+    first = ref_tail(own_ref, ROWS)
+    code = jnp.where(lax.rem(row, 4) < 2, first, ref_tail(other_ref, ROWS))
+    k_ref[2 * ROWS :, :] = code.astype(BF16)
+
+
+def ref_tail(ref, start):
+    return ref[start:, :HEAD].astype(F32)
+
+
+def stack_kernel(*refs):
+    ks, vs = refs[:4], refs[4:8]
+    k_ref, v_ref = refs[8:]
+    row = lax.broadcasted_iota(jnp.int32, (PAD, HEAD), 0)
+    code = jnp.zeros((PAD, HEAD), F32)
+    for i in range(4):
+        rows = slice(i * 2 * ROWS, (i + 1) * 2 * ROWS)
+        k_ref[rows, :] = ks[i][: 2 * ROWS, :]
+        v_ref[rows, :] = vs[i][...]
+        code = jnp.where(row // 4 == i, ref_tail(ks[i], 2 * ROWS), code)
+    k_ref[8 * ROWS :, :] = code.astype(BF16)
+
+
 def q_kernel(x_ref, wq_ref, code_ref, cut_ref, q_ref, flag_ref, own_cut_ref):
     code = code_ref[...].astype(F32)
     ids = column(code[0:1])
-    order = column(code[8:9])
+    order = column(code[1:2])
     blocks = cut_ref.shape[1]
     spots = lax.broadcasted_iota(jnp.int32, (ROWS, blocks), 1).astype(F32)
     cuts = jnp.broadcast_to(cut_ref[...].astype(F32), (ROWS, blocks))
@@ -155,38 +183,111 @@
         accum_ref[h] = dot(probs.astype(BF16), values)
 
 
+def place():
+    me = lax.axis_index("ctx")
+    return me, me // 8, lax.rem(me // 2, 4), lax.rem(me, 2)
+
+
+def pipeline(q_ref, pieces, state_in, state, finish):
+    top_ref, total_ref, accum_ref = state
+
+    def scores_of(step):
+        h, chunk, _, _ = step
+        keys, _, mask, _ = pieces[chunk]
+        scores = dot_t(q_ref[h], keys())
+        parts = [scores[:, j : j + ROWS] for j in range(0, scores.shape[1], ROWS)]
+        return mask(parts) if mask is not None else parts
+
+    def absorb(step, parts):
+        h, chunk, first, last = step
+        _, values, _, seen = pieces[chunk]
+        best = parts[0]
+        for part in parts[1:]:
+            best = jnp.maximum(best, part)
+        best = jnp.max(best, axis=1, keepdims=True)
+        if seen is not None:
+            best = jnp.where(seen, best, LOW)
+        source = state_in if first else state
+        old = source[0][h]
+        top = jnp.maximum(old, best)
+        factor = jnp.exp2((old - top) * POWER)
+        level = top if seen is None else jnp.where(seen, top, -LOW)
+        probs = [jnp.exp2((part - level) * POWER) for part in parts]
+        total = source[1][h] * factor
+        for part in probs:
+            total = total + part
+        probs = jnp.concatenate([part.astype(BF16) for part in probs], axis=1)
+        accum = source[2][h] * factor + dot(probs, values())
+        if last and finish is not None:
+            finish(h, accum, total)
+        else:
+            top_ref[h] = top
+            total_ref[h] = total
+            accum_ref[h] = accum
+
+    order = [(h, i, i == 0, i == len(pieces) - 1) for i in range(len(pieces)) for h in range(GROUP)]
+    parts = scores_of(order[0])
+    for now, later in zip(order, order[1:] + [None]):
+        following = None if later is None else scores_of(later)
+        absorb(now, parts)
+        parts = following
+
+
+def blocks_of(ref, which):
+    return jnp.concatenate([ref[i * 2 * ROWS : (i + 1) * 2 * ROWS, :] for i in which], axis=0)
+
+
+def shard_mask(where, spots):
+    me, y, x, z = where
+
+    def mask(parts):
+        kept = []
+        for j, part in enumerate(parts):
+            dy, dx = spots[j // 2]
+            there = lax.rem(y + 4 - dy, 4) * 8 + lax.rem(x + 4 - dx, 4) * 2 + lax.rem(z + j, 2)
+            kept.append(jnp.where(there < me - 1, part, LOW))
+        return kept
+
+    return mask
+
+
 def far_kernel(*refs):
     q_ref = refs[0]
-    k_refs, v_refs = refs[1:5], refs[5:9]
-    top_in, total_in, accum_in = refs[9:12]
-    code_ref, pair_ref, swap_ref, own_cut_ref, mkv_ref = refs[12:17]
-    clean_ref, noisy_ref = refs[17:19]
-    top_ref, total_ref, accum_ref = refs[19:]
-    me = lax.axis_index("ctx")
-    y, x, z = me // 8, lax.rem(me // 2, 4), lax.rem(me, 2)
-
-    hop = jnp.where(z == 0, 1, 0)
+    k_refs = dict(zip((0, 1, 3), refs[1:4]))
+    v_refs = dict(zip((0, 1, 3), refs[4:7]))
+    state_in = refs[7:10]
+    code_ref, own_cut_ref, mkv_ref = refs[10:13]
+    state = refs[13:16]
+    me, y, x, z = place()
+
     wrap = (z == 0) & (x == 0)
-    old_y = jnp.where(wrap, 1, 0)
-    step = jnp.where(z == 0, 0, 3)
     beyond = (z == 1) & (x == 3)
-    new_y = jnp.where(beyond, 3, 0)
-    k_old = jnp.where(wrap, k_refs[1][hop, 1], k_refs[0][hop, 1])
-    v_old = jnp.where(z == 0, v_refs[1][old_y, 1], v_refs[0][old_y, 1])
-    k_new = jnp.where(beyond, k_refs[3][step, 1], k_refs[0][step, 1])[:BLOCK]
-    v_new = jnp.where(z == 0, v_refs[0][new_y, 1], v_refs[3][new_y, 1])[:BLOCK]
-
-    own = code_ref[...].astype(F32)[:8]
-    partner = pair_ref[ROWS:, :HEAD].astype(F32)
-    other = swap_ref[...].astype(F32)
-    old_code = jnp.where(z == 0, other, partner)
-    new_code = jnp.where(z == 0, partner, other)
-    old_ids, old_order = jnp.where(me > 0, old_code[:8], FAR), old_code[8:]
-    new_ids, new_order = jnp.where(me < LAST, new_code[:8], FAR), new_code[8:]
+
+    def block(ref, index):
+        return ref[index * ROWS : (index + 1) * ROWS, :]
+
+    k_old = jnp.where(wrap, block(k_refs[1], 3), jnp.where(z == 0, block(k_refs[0], 3), block(k_refs[0], 1)))
+    v_old = jnp.where(wrap, block(v_refs[1], 3), jnp.where(z == 0, block(v_refs[1], 1), block(v_refs[0], 1)))
+    k_new = jnp.where(beyond, block(k_refs[3], 7), jnp.where(z == 1, block(k_refs[0], 7), block(k_refs[0], 1)))
+    v_new = jnp.where(beyond, block(v_refs[3], 7), jnp.where(z == 1, block(v_refs[3], 1), block(v_refs[0], 1)))
+    k_new, v_new = k_new[:BLOCK], v_new[:BLOCK]
+
+    own = code_ref[...].astype(F32)[0:1]
+    tails = {dy: ref_tail(k_refs[dy], 8 * ROWS) for dy in (0, 1, 3)}
+
+    def line(i):
+        old = jnp.where(wrap, tails[1][6 + i : 7 + i], jnp.where(z == 0, tails[0][6 + i : 7 + i], tails[0][2 + i : 3 + i]))
+        new = jnp.where(beyond, tails[3][14 + i : 15 + i], jnp.where(z == 1, tails[0][14 + i : 15 + i], tails[0][2 + i : 3 + i]))
+        return old, new
+
+    old_ids, new_ids = line(0)
+    old_order, new_order = line(1)
+    old_ids = jnp.broadcast_to(jnp.where(me > 0, old_ids, FAR), (8, ROWS))
+    new_ids = jnp.broadcast_to(jnp.where(me < LAST, new_ids, FAR), (8, ROWS))
     first_cut = own_cut_ref[0:1, :]
     last_cut = own_cut_ref[ROWS - 1 : ROWS, :]
-    old_masked = column(jnp.where(old_order[0:1] >= first_cut, 1.0, 0.0))[ROWS - BLOCK :]
-    new_masked = column(jnp.where(new_order[0:1] >= last_cut, 1.0, 0.0))[:BLOCK]
+    old_masked = column(jnp.where(old_order >= first_cut, 1.0, 0.0))[ROWS - BLOCK :]
+    new_masked = column(jnp.where(new_order >= last_cut, 1.0, 0.0))[:BLOCK]
 
     def noisy(masked, clean, lanes):
         fixed = jnp.broadcast_to(mkv_ref[0:1, lanes].astype(F32), clean.shape)
@@ -206,7 +307,7 @@
         jnp.where(lane < 64, pltpu.roll(old_ids, 64, 1), jnp.where(lane < 96, pltpu.roll(new_ids, 64, 1), -5.0)),
     )
     square = (ROWS, ROWS)
-    query = jnp.broadcast_to(column(own[0:1]), square)
+    query = jnp.broadcast_to(column(own), square)
     old_key = jnp.broadcast_to(old_ids[0:1], square)
     mixed_key = jnp.broadcast_to(mixed[0:1], square)
     early = lax.broadcasted_iota(jnp.int32, square, 1) < 32
@@ -222,55 +323,52 @@
     ]
     bias = jnp.concatenate([jnp.concatenate(clean_bias, axis=1), jnp.concatenate(noisy_bias, axis=1)], axis=0)
 
-    def scores_of(step):
-        dy, h = step
-        if dy < 0:
-            return jnp.where(bias < -1.0, LOW, dot_t(q_ref[h], k_rim))
-        return dot_t(q_ref[h], k_refs[dy][...].reshape(8 * ROWS, HEAD))
-
-    def absorb(step, scores):
-        dy, h = step
-        parts = [scores[:, j : j + ROWS] for j in range(0, scores.shape[1], ROWS)]
-        if dy in (0, 1):
-            for j in range(8):
-                there = lax.rem(y + 4 - dy, 4) * 8 + lax.rem(x + 4 - j // 2, 4) * 2 + lax.rem(z + j, 2)
-                parts[j] = jnp.where(there < me - 1, parts[j], LOW)
-        best = parts[0]
-        for part in parts[1:]:
-            best = jnp.maximum(best, part)
-        best = jnp.max(best, axis=1, keepdims=True)
-        if dy > 1:
-            best = jnp.where(y >= dy, best, LOW)
-        old = top_in[h] if dy < 0 else top_ref[h]
-        top = jnp.maximum(old, best)
-        factor = jnp.exp2((old - top) * POWER)
-        level = jnp.where(y >= dy, top, -LOW) if dy > 1 else top
-        probs = [jnp.exp2((part - level) * POWER) for part in parts]
-        total = (total_in[h] if dy < 0 else total_ref[h]) * factor
-        for part in probs:
-            total = total + part
-        if dy < 0:
-            values = v_rim
-        else:
-            values = jnp.concatenate([v_refs[dx][dy].reshape(2 * ROWS, HEAD) for dx in range(4)], axis=0)
-        probs = jnp.concatenate([part.astype(BF16) for part in probs], axis=1)
-        accum = (accum_in[h] if dy < 0 else accum_ref[h]) * factor + dot(probs, values)
-        if dy < 3:
-            top_ref[h] = top
-            total_ref[h] = total
-            accum_ref[h] = accum
-            return
+    def rim_mask(parts):
+        return [jnp.where(bias[:, j * ROWS : (j + 1) * ROWS] < -1.0, LOW, part) for j, part in enumerate(parts)]
+
+    near = (0, 1, 3)
+    pieces = [(lambda: k_rim, lambda: v_rim, rim_mask, None)]
+    for dy in near:
+        pieces.append(
+            (
+                lambda dy=dy: blocks_of(k_refs[dy], near),
+                lambda dy=dy: jnp.concatenate([blocks_of(v_refs[dx], (dy,)) for dx in near], axis=0),
+                shard_mask((me, y, x, z), [(dy, dx) for dx in near]) if dy < 3 else None,
+                y >= dy if dy == 3 else None,
+            )
+        )
+    pipeline(q_ref, pieces, state_in, state, None)
+
+
+def last_kernel(*refs):
+    q_ref, k_refs, v_refs = refs[0], refs[1:5], refs[5:9]
+    state_in = refs[9:12]
+    clean_ref, noisy_ref = refs[12:14]
+    state = refs[14:]
+    where = place()
+    near = (0, 1, 3)
+    pieces = [
+        (
+            lambda: blocks_of(k_refs[2], range(4)),
+            lambda: jnp.concatenate([blocks_of(v_refs[dx], (2,)) for dx in range(4)], axis=0),
+            None,
+            where[1] >= 2,
+        ),
+        (
+            lambda: jnp.concatenate([blocks_of(k_refs[dy], (2,)) for dy in near], axis=0),
+            lambda: blocks_of(v_refs[2], near),
+            shard_mask(where, [(dy, 2) for dy in near]),
+            None,
+        ),
+    ]
+
+    def finish(h, accum, total):
         lanes = slice(h * HEAD, (h + 1) * HEAD)
         result = (accum / jnp.sum(total, axis=1, keepdims=True)).astype(BF16)
         clean_ref[:, lanes] = result[:ROWS]
         noisy_ref[:, lanes] = result[ROWS:]
 
-    steps = [(dy, h) for dy in (-1, 0, 1, 2, 3) for h in range(GROUP)]
-    scores = scores_of(steps[0])
-    for now, later in zip(steps, steps[1:] + [None]):
-        following = None if later is None else scores_of(later)
-        absorb(now, scores)
-        scores = following
+    pipeline(q_ref, pieces, state_in, state, finish)
 
 
 def shards(hidden, block_ids, decode_order, step_cut, mask_embed, q_weight, k_weight, v_weight):
@@ -301,29 +399,31 @@
     for piece in (own, *moved):
         piece, _ = lax.optimization_barrier((piece, pad))
         pieces += [piece, lax.ppermute(piece, "kv", kv_pairs(0, 1))]
-    x, kv, mask_kv, send = call(
+    x, kv, mask_kv = call(
         kv_kernel,
         [
             ((ROWS + PAD, 8 * WIDTH), BF16),
             ((ROWS + PAD, 2 * HEAD), BF16),
             ((PAD, 2 * HEAD), BF16),
-            ((PAD, ROWS), BF16),
         ],
         [*pieces, pad, wk, wv, code],
         (1 << 29, 3 << 20),
     )
     pair = lax.ppermute(kv, "ctx", ctx_pairs(0, 0, 1))
-    swap = lax.ppermute(send, "ctx", [(i, (i + 2 * (i % 2) - 1) % 32) for i in range(32)])
-    pair, swap = lax.optimization_barrier((pair, swap))
-    k = jnp.stack([kv[:ROWS, :HEAD], pair[:ROWS, :HEAD]])
-    v = jnp.stack([kv[:ROWS, HEAD:], pair[:ROWS, HEAD:]])
-    k, v = lax.optimization_barrier((k, v))
+    k, v = call(
+        pair_kernel,
+        [((2 * ROWS + PAD, HEAD), BF16), ((2 * ROWS, HEAD), BF16)],
+        [kv, pair],
+        (1 << 10, 1 << 18),
+    )
     ks = [lax.ppermute(k, "ctx", ctx_pairs(0, d, 0)) for d in (1, 2, 3)]
     vs = [lax.ppermute(v, "ctx", ctx_pairs(d, 0, 0)) for d in (1, 2, 3)]
-    moved = lax.optimization_barrier((*ks, *vs))
-    ks = jnp.stack([k, *moved[:3]])
-    vs = jnp.stack([v, *moved[3:]])
-    ks, vs = lax.optimization_barrier((ks, vs))
+    ks, vs = call(
+        stack_kernel,
+        [((8 * ROWS + PAD, HEAD), BF16), ((8 * ROWS, HEAD), BF16)],
+        [k, *ks, v, *vs],
+        (1 << 10, 1 << 20),
+    )
     q, flag, own_cut = call(
         q_kernel,
         [((GROUP, 2 * ROWS, HEAD), BF16), ((ROWS, HEAD), F32), ((ROWS, HEAD), F32)],
@@ -338,12 +438,19 @@
     )
     all_k = [ks] + [lax.ppermute(ks, "ctx", ctx_pairs(d, 0, 0)) for d in (1, 2, 3)]
     all_v = [vs] + [lax.ppermute(vs, "ctx", ctx_pairs(0, d, 0)) for d in (1, 2, 3)]
+    state = [((GROUP, 2 * ROWS, HEAD), F32)] * 3
+    far = call(
+        far_kernel,
+        state,
+        [q, *[all_k[d] for d in (0, 1, 3)], *[all_v[d] for d in (0, 1, 3)], *near, code, own_cut, mask_kv],
+        (1 << 31, 4 << 20),
+    )
     return tuple(
         call(
-            far_kernel,
+            last_kernel,
             [((ROWS, GROUP * HEAD), BF16)] * 2,
-            [q, *all_k, *all_v, *near, code, pair, swap, own_cut, mask_kv],
-            (1 << 32, 4 << 20),
+            [q, *all_k, *all_v, *far],
+            (1 << 31, 4 << 20),
             [pltpu.VMEM((GROUP, 2 * ROWS, HEAD), F32)] * 3,
         )
     )

time: 68.9 us -> 65.8 us (0.955)
  starting transfers between devices: 32.2 us -> 25.9 us
  waiting for transfers between devices: 19 us -> 21.9 us
  Pallas kernels: 10.9 us -> 11.6 us
    ppermute x1 -> x0, starting transfers between devices: 4.23 us -> none  [shards(): lax.ppermute(send, 'ctx', [(i, (i + 2 * (i % 2) - 1) % 32) for i in range...]
    ppermute x3, waiting for transfers between devices: 0.32 us -> 4.27 us  [shards(): lax.ppermute(ks, 'ctx', ctx_pairs(d, 0, 0))]
    ppermute x3, starting transfers between devices: 2.12 us -> 5.05 us  [shards(): ks = [lax.ppermute(k, 'ctx', ctx_pairs(0, d, 0)) for d in (1, 2, 3)]]
    ppermute x3, waiting for transfers between devices: 5.95 us -> 3.18 us  [shards(): lax.ppermute(vs, 'ctx', ctx_pairs(0, d, 0))]
    ppermute x3, starting transfers between devices: 5.92 us -> 3.32 us  [shards(): lax.ppermute(vs, 'ctx', ctx_pairs(0, d, 0))]
    ppermute x1 -> x0, waiting for transfers between devices: 2.47 us -> none  [shards(): lax.ppermute(send, 'ctx', [(i, (i + 2 * (i % 2) - 1) % 32) for i in range...]
    ppermute x1, waiting for transfers between devices: 1.88 us -> 4.34 us  [shards(): pair = lax.ppermute(kv, 'ctx', ctx_pairs(0, 0, 1))]
    ppermute x3, waiting for transfers between devices: 3.13 us -> 5.48 us  [shards(): vs = [lax.ppermute(v, 'ctx', ctx_pairs(d, 0, 0)) for d in (1, 2, 3)]]
  transfers between devices with their start and end apart: 21 -> 20, of which waited for: 15 -> 8; matrix products, arithmetic and copies ran while one was open for 1% -> 1% of each run, Pallas kernels for 4% -> 11%
where the time goes in v6:
time: 65.8 us; the launch traced here: 65.6 us
  starting transfers between devices  25.9 us (39%)
  waiting for transfers between devices  21.9 us (33%)
  Pallas kernels  11.6 us (18%)
  local copies, waits for them, and re-layouts  5.37 us (8%)
  between operations  0.77 us (1%)
    pallas_call x8, Pallas kernels, call(): pl.pallas_call(kernel, out_shape=[jax.ShapeDtypeStruct(s, t) for s, t in...  11.6 us
    ppermute x3, starting transfers between devices, shards(): moved = [lax.ppermute(hidden, 'kv', kv_pairs(d, 0)) for d in (1, 2, 3)]  11.4 us
    ppermute x3, waiting for transfers between devices, shards(): vs = [lax.ppermute(v, 'ctx', ctx_pairs(d, 0, 0)) for d in (1, 2, 3)]  5.48 us
    ppermute x3, starting transfers between devices, shards(): ks = [lax.ppermute(k, 'ctx', ctx_pairs(0, d, 0)) for d in (1, 2, 3)]  5.05 us
    unnamed x14, local copies, waits for them, and re-layouts  4.67 us
    ppermute x1, waiting for transfers between devices, shards(): pair = lax.ppermute(kv, 'ctx', ctx_pairs(0, 0, 1))  4.34 us
    ppermute x3, waiting for transfers between devices, shards(): lax.ppermute(ks, 'ctx', ctx_pairs(d, 0, 0))  4.27 us
    ppermute x3, waiting for transfers between devices, shards(): moved = [lax.ppermute(hidden, 'kv', kv_pairs(d, 0)) for d in (1, 2, 3)]  3.32 us
  transfers between devices with their start and end apart: 20, of which 8 were waited for; matrix products, arithmetic and copies ran while one was open for 1% of the time, Pallas kernels for 11%

profile of v6, /device:TPU:24, one launch (start us, length us, event | category | flops | bytes accessed | tf_op | source)
XLA Modules:
  0.0 65.6 jit_solution(6621161061035869161)
XLA Ops:
  0.6 3.3 %collective-permute-start.1 = (bf16[128,512]{1,0:T(8,128)(2,1)}, bf16[128,512]{1,0:T(8,128)(2,1)S(1)}, u32[]{:S(2)}, u32[]{:S(2)}) collective-permute-start(bf16[128,512]{1,0:T(8,128)(2,1)} %refs_0_.1), channel_id=1, source_target_pairs={{0,2},{1,3},{2,4},{3,5},{4,6},{5,7},{6,0},{7,1},{8,10},{9,11},{10,... | collective-permute-start | bytes 393224 | tf_op jit(solution)/shard_map/ppermute | solution.py:378
  4.0 5.4 %collective-permute-start.3 = (bf16[128,512]{1,0:T(8,128)(2,1)}, bf16[128,512]{1,0:T(8,128)(2,1)S(1)}, u32[]{:S(2)}, u32[]{:S(2)}) collective-permute-start(bf16[128,512]{1,0:T(8,128)(2,1)} %refs_0_.1), channel_id=1, source_target_pairs={{0,4},{1,5},{2,6},{3,7},{4,0},{5,1},{6,2},{7,3},{8,12},{9,13},{10,... | collective-permute-start | bytes 393224 | tf_op jit(solution)/shard_map/ppermute | solution.py:378
  9.4 2.7 %collective-permute-start.5 = (bf16[128,512]{1,0:T(8,128)(2,1)}, bf16[128,512]{1,0:T(8,128)(2,1)S(1)}, u32[]{:S(2)}, u32[]{:S(2)}) collective-permute-start(bf16[128,512]{1,0:T(8,128)(2,1)} %refs_0_.1), channel_id=1, source_target_pairs={{0,6},{1,7},{2,0},{3,1},{4,2},{5,3},{6,4},{7,5},{8,14},{9,15},{10,... | collective-permute-start | bytes 393224 | tf_op jit(solution)/shard_map/ppermute | solution.py:378
  12.8 1.2 %copy-done.1 = bf16[4096,128]{1,0:T(8,128)(2,1)S(1)} copy-done((bf16[4096,128]{1,0:T(8,128)(2,1)S(1)}, bf16[4096,128]{1,0:T(8,128)(2,1)}, u32[]{:S(2)}) %copy-start.1) | copy-done | bytes 1048600
  14.0 1.2 %copy-done.2 = bf16[4096,128]{1,0:T(8,128)(2,1)S(1)} copy-done((bf16[4096,128]{1,0:T(8,128)(2,1)S(1)}, bf16[4096,128]{1,0:T(8,128)(2,1)}, u32[]{:S(2)}) %copy-start.2) | copy-done | bytes 1048600
  15.2 0.9 %copy-done.3 = bf16[128,512]{1,0:T(8,128)(2,1)S(1)} copy-done((bf16[128,512]{1,0:T(8,128)(2,1)S(1)}, bf16[128,512]{1,0:T(8,128)(2,1)}, u32[]{:S(2)}) %copy-start.3) | copy-done | bytes 131096
  18.6 3.2 %collective-permute-done.5.refs_6_ = bf16[128,512]{1,0:T(8,128)(2,1)S(1)} collective-permute-done((bf16[128,512]{1,0:T(8,128)(2,1)}, bf16[128,512]{1,0:T(8,128)(2,1)S(1)}, u32[]{:S(2)}, u32[]{:S(2)}) %collective-permute-start.5) | collective-permute-done | bytes 131104 | tf_op jit(solution)/shard_map/ppermute | solution.py:378
  21.8 1.3 %collective-permute-done.6.refs_7_ = bf16[128,512]{1,0:T(8,128)(2,1)S(1)} collective-permute-done((bf16[128,512]{1,0:T(8,128)(2,1)S(1)}, bf16[128,512]{1,0:T(8,128)(2,1)S(1)}, u32[]{:S(2)}, u32[]{:S(2)}) %collective-permute-start.6) | collective-permute-done | bytes 131104 | tf_op jit(solution)/shard_map/ppermute | solution.py:401
  23.1 0.9 %shard_map.96 = (bf16[144,4096]{1,0:T(8,128)(2,1)S(1)}, bf16[144,256]{1,0:T(8,128)(2,1)S(1)}, bf16[16,256]{1,0:T(8,128)(2,1)S(1)}) custom-call(bf16[128,512]{1,0:T(8,128)(2,1)S(1)} %get-tuple-element.29.refs_0_, bf16[128,512]{1,0:T(8,128)(2,1)S(1)} %collective-permute-done.refs_1_, bf16[128,512]{1,0:T(8,128)(2,1)S(1)} %collective-permute-done.1.refs_2_, ...), custom_call_target="tpu_custom_call" | custom-call | flops 536870912 | bytes 3145728 | tf_op jit(solution)/shard_map/pallas_call | solution.py:51
  24.1 4.3 %collective-permute-done.7.other_ref = bf16[144,256]{1,0:T(8,128)(2,1)S(1)} collective-permute-done((bf16[144,256]{1,0:T(8,128)(2,1)S(1)}, bf16[144,256]{1,0:T(8,128)(2,1)S(1)}, u32[]{:S(2)}, u32[]{:S(2)}) %collective-permute-start.7) | collective-permute-done | bytes 73760 | tf_op jit(solution)/shard_map/ppermute | solution.py:412
  28.8 2.8 %collective-permute-start.10 = (bf16[272,128]{1,0:T(8,128)(2,1)S(1)}, bf16[272,128]{1,0:T(8,128)(2,1)S(1)}, u32[]{:S(2)}, u32[]{:S(2)}) collective-permute-start(bf16[272,128]{1,0:T(8,128)(2,1)S(1)} %get-tuple-element.39.refs_0_), channel_id=1, source_target_pairs={{0,48},{8,56},{16,0},{24,8},{32,16},{40,24},{48,32},{56,40},{64,11... | collective-permute-start | bytes 208904 | tf_op jit(solution)/shard_map/ppermute | solution.py:419
  31.5 2.3 %collective-permute-start.9 = (bf16[272,128]{1,0:T(8,128)(2,1)S(1)}, bf16[272,128]{1,0:T(8,128)(2,1)S(1)}, u32[]{:S(2)}, u32[]{:S(2)}) collective-permute-start(bf16[272,128]{1,0:T(8,128)(2,1)S(1)} %get-tuple-element.39.refs_0_), channel_id=1, source_target_pairs={{0,32},{8,40},{16,48},{24,56},{32,0},{40,8},{48,16},{56,24},{64,96... | collective-permute-start | bytes 208904 | tf_op jit(solution)/shard_map/ppermute | solution.py:419
  33.8 2.6 %collective-permute-start.12 = (bf16[256,128]{1,0:T(8,128)(2,1)S(1)}, bf16[256,128]{1,0:T(8,128)(2,1)S(1)}, u32[]{:S(2)}, u32[]{:S(2)}) collective-permute-start(bf16[256,128]{1,0:T(8,128)(2,1)S(1)} %get-tuple-element.40.refs_4_), channel_id=1, source_target_pairs={{0,128},{8,136},{16,144},{24,152},{32,160},{40,168},{48,176},{56,1... | collective-permute-start | bytes 196616 | tf_op jit(solution)/shard_map/ppermute | solution.py:420
  36.4 3.2 %collective-permute-done.12.refs_6_ = bf16[256,128]{1,0:T(8,128)(2,1)S(1)} collective-permute-done((bf16[256,128]{1,0:T(8,128)(2,1)S(1)}, bf16[256,128]{1,0:T(8,128)(2,1)S(1)}, u32[]{:S(2)}, u32[]{:S(2)}) %collective-permute-start.12) | collective-permute-done | bytes 65568 | tf_op jit(solution)/shard_map/ppermute | solution.py:420
  39.6 2.3 %collective-permute-done.13.refs_7_ = bf16[256,128]{1,0:T(8,128)(2,1)S(1)} collective-permute-done((bf16[256,128]{1,0:T(8,128)(2,1)S(1)}, bf16[256,128]{1,0:T(8,128)(2,1)S(1)}, u32[]{:S(2)}, u32[]{:S(2)}) %collective-permute-start.13) | collective-permute-done | bytes 65568 | tf_op jit(solution)/shard_map/ppermute | solution.py:420
  42.0 1.9 %collective-permute-start.17 = (bf16[1024,128]{1,0:T(8,128)(2,1)S(1)}, bf16[1024,128]{1,0:T(8,128)(2,1)S(1)}, u32[]{:S(2)}, u32[]{:S(2)}) collective-permute-start(bf16[1024,128]{1,0:T(8,128)(2,1)S(1)} %get-tuple-element.42.refs_4_.refs_5_), channel_id=1, source_target_pairs={{0,16},{8,24},{16,32},{24,40},{32,48},{40,56},{48,0},{56,8},{64,80... | collective-permute-start | bytes 786440 | tf_op jit(solution)/shard_map/ppermute | solution.py:440
  43.8 1.1 %collective-permute-start.14 = (bf16[1040,128]{1,0:T(8,128)(2,1)S(1)}, bf16[1040,128]{1,0:T(8,128)(2,1)S(1)}, u32[]{:S(2)}, u32[]{:S(2)}) collective-permute-start(bf16[1040,128]{1,0:T(8,128)(2,1)S(1)} %get-tuple-element.41.refs_1_), channel_id=1, source_target_pairs={{0,64},{8,72},{16,80},{24,88},{32,96},{40,104},{48,112},{56,120},{... | collective-permute-start | bytes 798728 | tf_op jit(solution)/shard_map/ppermute | solution.py:439
  45.0 0.9 %collective-permute-start.16 = (bf16[1040,128]{1,0:T(8,128)(2,1)S(1)}, bf16[1040,128]{1,0:T(8,128)(2,1)S(1)}, u32[]{:S(2)}, u32[]{:S(2)}) collective-permute-start(bf16[1040,128]{1,0:T(8,128)(2,1)S(1)} %get-tuple-element.41.refs_1_), channel_id=1, source_target_pairs={{0,192},{8,200},{16,208},{24,216},{32,224},{40,232},{48,240},{56,2... | collective-permute-start | bytes 798728 | tf_op jit(solution)/shard_map/ppermute | solution.py:439
  45.9 1.4 %collective-permute-start.19 = (bf16[1024,128]{1,0:T(8,128)(2,1)S(1)}, bf16[1024,128]{1,0:T(8,128)(2,1)S(1)}, u32[]{:S(2)}, u32[]{:S(2)}) collective-permute-start(bf16[1024,128]{1,0:T(8,128)(2,1)S(1)} %get-tuple-element.42.refs_4_.refs_5_), channel_id=1, source_target_pairs={{0,48},{8,56},{16,0},{24,8},{32,16},{40,24},{48,32},{56,40},{64,11... | collective-permute-start | bytes 786440 | tf_op jit(solution)/shard_map/ppermute | solution.py:440
  47.3 1.4 %shard_map.97 = (bf16[4,256,128]{2,1,0:T(8,128)(2,1)S(1)}, f32[128,128]{1,0:T(8,128)S(1)}, f32[128,128]{1,0:T(8,128)S(1)}) custom-call(bf16[144,4096]{1,0:T(8,128)(2,1)S(1)} %get-tuple-element.36.x_ref, bf16[4096,512]{1,0:T(8,128)(2,1)S(1)} %copy-done, bf16[16,128]{1,0:T(8,128)(2,1)S(1)} %get-tuple-element.35.refs_11_.code_ref.refs_10_, s32[1,256]{1,0:T(1,128)S(1)} %bitcast.3), custom_call_target="tpu_custom_call" | custom-call | flops 1073741824 | bytes 5242880 | tf_op jit(solution)/shard_map/pallas_call | solution.py:51
  49.3 3.2 %collective-permute-done.17.refs_5_.refs_6_ = bf16[1024,128]{1,0:T(8,128)(2,1)S(1)} collective-permute-done((bf16[1024,128]{1,0:T(8,128)(2,1)S(1)}, bf16[1024,128]{1,0:T(8,128)(2,1)S(1)}, u32[]{:S(2)}, u32[]{:S(2)}) %collective-permute-start.17) | collective-permute-done | bytes 262176 | tf_op jit(solution)/shard_map/ppermute | solution.py:440
  53.3 4.3 %collective-permute-done.16.refs_3_.refs_4_ = bf16[1040,128]{1,0:T(8,128)(2,1)S(1)} collective-permute-done((bf16[1040,128]{1,0:T(8,128)(2,1)S(1)}, bf16[1040,128]{1,0:T(8,128)(2,1)S(1)}, u32[]{:S(2)}, u32[]{:S(2)}) %collective-permute-start.16) | collective-permute-done | bytes 266272 | tf_op jit(solution)/shard_map/ppermute | solution.py:439
  57.5 4.4 %shard_map.101 = (f32[4,256,128]{2,1,0:T(8,128)S(1)}, f32[4,256,128]{2,1,0:T(8,128)S(1)}, f32[4,256,128]{2,1,0:T(8,128)S(1)}) custom-call(bf16[4,256,128]{2,1,0:T(8,128)(2,1)S(1)} %get-tuple-element.37.q_ref.refs_0_, bf16[1040,128]{1,0:T(8,128)(2,1)S(1)} %get-tuple-element.41.refs_1_, bf16[1040,128]{1,0:T(8,128)(2,1)S(1)} %collective-permute-done.14.refs_2_, ...), custom_call_target="tpu_custom_call" | custom-call | flops 2147483648 | bytes 4194304 | tf_op jit(solution)/shard_map/pallas_call | solution.py:51
  62.0 3.6 %shard_map.102 = (bf16[128,512]{1,0:T(8,128)(2,1)}, bf16[128,512]{1,0:T(8,128)(2,1)}) custom-call(bf16[4,256,128]{2,1,0:T(8,128)(2,1)S(1)} %get-tuple-element.37.q_ref.refs_0_, bf16[1040,128]{1,0:T(8,128)(2,1)S(1)} %get-tuple-element.41.refs_1_, bf16[1040,128]{1,0:T(8,128)(2,1)S(1)} %collective-permute-done.14.refs_2_, ...), custom_call_target="tpu_custom_call" | custom-call | flops 2147483648 | bytes 4194304 | tf_op jit(solution)/shard_map/pallas_call | solution.py:51
  (39 shorter events, 5.0 us)
Async XLA Ops:
  0.6 46.7 %copy-start = (bf16[4096,512]{1,0:T(8,128)(2,1)S(1)}, bf16[4096,512]{1,0:T(8,128)(2,1)}, u32[]{:S(2)}) copy-start(bf16[4096,512]{1,0:T(8,128)(2,1)} %wq_ref.1) | copy-start | bytes 12582916
  0.6 17.3 %collective-permute-start.1 = (bf16[128,512]{1,0:T(8,128)(2,1)}, bf16[128,512]{1,0:T(8,128)(2,1)S(1)}, u32[]{:S(2)}, u32[]{:S(2)}) collective-permute-start(bf16[128,512]{1,0:T(8,128)(2,1)} %refs_0_.1), channel_id=1, source_target_pairs={{0,2},{1,3},{2,4},{3,5},{4,6},{5,7},{6,0},{7,1},{8,10},{9,11},{10,... | collective-permute-start | bytes 393224 | tf_op jit(solution)/shard_map/ppermute | solution.py:378
  4.0 14.5 %collective-permute-start.3 = (bf16[128,512]{1,0:T(8,128)(2,1)}, bf16[128,512]{1,0:T(8,128)(2,1)S(1)}, u32[]{:S(2)}, u32[]{:S(2)}) collective-permute-start(bf16[128,512]{1,0:T(8,128)(2,1)} %refs_0_.1), channel_id=1, source_target_pairs={{0,4},{1,5},{2,6},{3,7},{4,0},{5,1},{6,2},{7,3},{8,12},{9,13},{10,... | collective-permute-start | bytes 393224 | tf_op jit(solution)/shard_map/ppermute | solution.py:378
  9.4 12.4 %collective-permute-start.5 = (bf16[128,512]{1,0:T(8,128)(2,1)}, bf16[128,512]{1,0:T(8,128)(2,1)S(1)}, u32[]{:S(2)}, u32[]{:S(2)}) collective-permute-start(bf16[128,512]{1,0:T(8,128)(2,1)} %refs_0_.1), channel_id=1, source_target_pairs={{0,6},{1,7},{2,0},{3,1},{4,2},{5,3},{6,4},{7,5},{8,14},{9,15},{10,... | collective-permute-start | bytes 393224 | tf_op jit(solution)/shard_map/ppermute | solution.py:378
  12.8 1.2 %copy-start.1 = (bf16[4096,128]{1,0:T(8,128)(2,1)S(1)}, bf16[4096,128]{1,0:T(8,128)(2,1)}, u32[]{:S(2)}) copy-start(bf16[4096,128]{1,0:T(8,128)(2,1)} %refs_1_.1) | copy-start | bytes 3145732
  14.0 1.2 %copy-start.2 = (bf16[4096,128]{1,0:T(8,128)(2,1)S(1)}, bf16[4096,128]{1,0:T(8,128)(2,1)}, u32[]{:S(2)}) copy-start(bf16[4096,128]{1,0:T(8,128)(2,1)} %refs_2_.1) | copy-start | bytes 3145732
  17.4 29.9 %copy-start.4 = (s32[256]{0:T(256)S(1)}, s32[256]{0:T(256)}, u32[]{:S(2)}) copy-start(s32[256]{0:T(256)} %param.11) | copy-start | bytes 3076
  17.8 4.0 %collective-permute-start = (bf16[128,512]{1,0:T(8,128)(2,1)S(1)}, bf16[128,512]{1,0:T(8,128)(2,1)S(1)}, u32[]{:S(2)}, u32[]{:S(2)}) collective-permute-start(bf16[128,512]{1,0:T(8,128)(2,1)S(1)} %get-tuple-element.29.refs_0_), channel_id=1, source_target_pairs={{0,1},{1,0},{2,3},{3,2},{4,5},{5,4},{6,7},{7,6},{8,9},{9,8},{10,11... | collective-permute-start | bytes 393224 | tf_op jit(solution)/shard_map/ppermute | solution.py:401
  18.0 3.9 %collective-permute-start.2 = (bf16[128,512]{1,0:T(8,128)(2,1)S(1)}, bf16[128,512]{1,0:T(8,128)(2,1)S(1)}, u32[]{:S(2)}, u32[]{:S(2)}) collective-permute-start(bf16[128,512]{1,0:T(8,128)(2,1)S(1)} %collective-permute-done.1.refs_2_), channel_id=1, source_target_pairs={{0,1},{1,0},{2,3},{3,2},{4,5},{5,4},{6,7},{7,6},{8,9},{9,8},{10,11... | collective-permute-start | bytes 393224 | tf_op jit(solution)/shard_map/ppermute | solution.py:401
  18.5 3.3 %collective-permute-start.4 = (bf16[128,512]{1,0:T(8,128)(2,1)S(1)}, bf16[128,512]{1,0:T(8,128)(2,1)S(1)}, u32[]{:S(2)}, u32[]{:S(2)}) collective-permute-start(bf16[128,512]{1,0:T(8,128)(2,1)S(1)} %collective-permute-done.3.refs_4_), channel_id=1, source_target_pairs={{0,1},{1,0},{2,3},{3,2},{4,5},{5,4},{6,7},{7,6},{8,9},{9,8},{10,11... | collective-permute-start | bytes 393224 | tf_op jit(solution)/shard_map/ppermute | solution.py:401
  21.8 1.3 %collective-permute-start.6 = (bf16[128,512]{1,0:T(8,128)(2,1)S(1)}, bf16[128,512]{1,0:T(8,128)(2,1)S(1)}, u32[]{:S(2)}, u32[]{:S(2)}) collective-permute-start(bf16[128,512]{1,0:T(8,128)(2,1)S(1)} %collective-permute-done.5.refs_6_), channel_id=1, source_target_pairs={{0,1},{1,0},{2,3},{3,2},{4,5},{5,4},{6,7},{7,6},{8,9},{9,8},{10,11... | collective-permute-start | bytes 393224 | tf_op jit(solution)/shard_map/ppermute | solution.py:401
  24.0 4.4 %collective-permute-start.7 = (bf16[144,256]{1,0:T(8,128)(2,1)S(1)}, bf16[144,256]{1,0:T(8,128)(2,1)S(1)}, u32[]{:S(2)}, u32[]{:S(2)}) collective-permute-start(bf16[144,256]{1,0:T(8,128)(2,1)S(1)} %get-tuple-element.38.own_ref.kv_ref), channel_id=1, source_target_pairs={{0,8},{8,0},{16,24},{24,16},{32,40},{40,32},{48,56},{56,48},{64,72... | collective-permute-start | bytes 221192 | tf_op jit(solution)/shard_map/ppermute | solution.py:412
  28.5 7.9 %collective-permute-start.11 = (bf16[256,128]{1,0:T(8,128)(2,1)S(1)}, bf16[256,128]{1,0:T(8,128)(2,1)S(1)}, u32[]{:S(2)}, u32[]{:S(2)}) collective-permute-start(bf16[256,128]{1,0:T(8,128)(2,1)S(1)} %get-tuple-element.40.refs_4_), channel_id=1, source_target_pairs={{0,64},{8,72},{16,80},{24,88},{32,96},{40,104},{48,112},{56,120},{... | collective-permute-start | bytes 196616 | tf_op jit(solution)/shard_map/ppermute | solution.py:420
  28.8 13.1 %collective-permute-start.10 = (bf16[272,128]{1,0:T(8,128)(2,1)S(1)}, bf16[272,128]{1,0:T(8,128)(2,1)S(1)}, u32[]{:S(2)}, u32[]{:S(2)}) collective-permute-start(bf16[272,128]{1,0:T(8,128)(2,1)S(1)} %get-tuple-element.39.refs_0_), channel_id=1, source_target_pairs={{0,48},{8,56},{16,0},{24,8},{32,16},{40,24},{48,32},{56,40},{64,11... | collective-permute-start | bytes 208904 | tf_op jit(solution)/shard_map/ppermute | solution.py:419
  31.5 10.4 %collective-permute-start.8 = (bf16[272,128]{1,0:T(8,128)(2,1)S(1)}, bf16[272,128]{1,0:T(8,128)(2,1)S(1)}, u32[]{:S(2)}, u32[]{:S(2)}) collective-permute-start(bf16[272,128]{1,0:T(8,128)(2,1)S(1)} %get-tuple-element.39.refs_0_), channel_id=1, source_target_pairs={{0,16},{8,24},{16,32},{24,40},{32,48},{40,56},{48,0},{56,8},{64,80... | collective-permute-start | bytes 208904 | tf_op jit(solution)/shard_map/ppermute | solution.py:419
  31.5 10.4 %collective-permute-start.9 = (bf16[272,128]{1,0:T(8,128)(2,1)S(1)}, bf16[272,128]{1,0:T(8,128)(2,1)S(1)}, u32[]{:S(2)}, u32[]{:S(2)}) collective-permute-start(bf16[272,128]{1,0:T(8,128)(2,1)S(1)} %get-tuple-element.39.refs_0_), channel_id=1, source_target_pairs={{0,32},{8,40},{16,48},{24,56},{32,0},{40,8},{48,16},{56,24},{64,96... | collective-permute-start | bytes 208904 | tf_op jit(solution)/shard_map/ppermute | solution.py:419
  33.8 5.8 %collective-permute-start.12 = (bf16[256,128]{1,0:T(8,128)(2,1)S(1)}, bf16[256,128]{1,0:T(8,128)(2,1)S(1)}, u32[]{:S(2)}, u32[]{:S(2)}) collective-permute-start(bf16[256,128]{1,0:T(8,128)(2,1)S(1)} %get-tuple-element.40.refs_4_), channel_id=1, source_target_pairs={{0,128},{8,136},{16,144},{24,152},{32,160},{40,168},{48,176},{56,1... | collective-permute-start | bytes 196616 | tf_op jit(solution)/shard_map/ppermute | solution.py:420
  36.4 5.5 %collective-permute-start.13 = (bf16[256,128]{1,0:T(8,128)(2,1)S(1)}, bf16[256,128]{1,0:T(8,128)(2,1)S(1)}, u32[]{:S(2)}, u32[]{:S(2)}) collective-permute-start(bf16[256,128]{1,0:T(8,128)(2,1)S(1)} %get-tuple-element.40.refs_4_), channel_id=1, source_target_pairs={{0,192},{8,200},{16,208},{24,216},{32,224},{40,232},{48,240},{56,2... | collective-permute-start | bytes 196616 | tf_op jit(solution)/shard_map/ppermute | solution.py:420
  42.0 10.5 %collective-permute-start.17 = (bf16[1024,128]{1,0:T(8,128)(2,1)S(1)}, bf16[1024,128]{1,0:T(8,128)(2,1)S(1)}, u32[]{:S(2)}, u32[]{:S(2)}) collective-permute-start(bf16[1024,128]{1,0:T(8,128)(2,1)S(1)} %get-tuple-element.42.refs_4_.refs_5_), channel_id=1, source_target_pairs={{0,16},{8,24},{16,32},{24,40},{32,48},{40,56},{48,0},{56,8},{64,80... | collective-permute-start | bytes 786440 | tf_op jit(solution)/shard_map/ppermute | solution.py:440
  43.8 9.4 %collective-permute-start.14 = (bf16[1040,128]{1,0:T(8,128)(2,1)S(1)}, bf16[1040,128]{1,0:T(8,128)(2,1)S(1)}, u32[]{:S(2)}, u32[]{:S(2)}) collective-permute-start(bf16[1040,128]{1,0:T(8,128)(2,1)S(1)} %get-tuple-element.41.refs_1_), channel_id=1, source_target_pairs={{0,64},{8,72},{16,80},{24,88},{32,96},{40,104},{48,112},{56,120},{... | collective-permute-start | bytes 798728 | tf_op jit(solution)/shard_map/ppermute | solution.py:439
  45.0 12.6 %collective-permute-start.16 = (bf16[1040,128]{1,0:T(8,128)(2,1)S(1)}, bf16[1040,128]{1,0:T(8,128)(2,1)S(1)}, u32[]{:S(2)}, u32[]{:S(2)}) collective-permute-start(bf16[1040,128]{1,0:T(8,128)(2,1)S(1)} %get-tuple-element.41.refs_1_), channel_id=1, source_target_pairs={{0,192},{8,200},{16,208},{24,216},{32,224},{40,232},{48,240},{56,2... | collective-permute-start | bytes 798728 | tf_op jit(solution)/shard_map/ppermute | solution.py:439
  45.9 7.4 %collective-permute-start.19 = (bf16[1024,128]{1,0:T(8,128)(2,1)S(1)}, bf16[1024,128]{1,0:T(8,128)(2,1)S(1)}, u32[]{:S(2)}, u32[]{:S(2)}) collective-permute-start(bf16[1024,128]{1,0:T(8,128)(2,1)S(1)} %get-tuple-element.42.refs_4_.refs_5_), channel_id=1, source_target_pairs={{0,48},{8,56},{16,0},{24,8},{32,16},{40,24},{48,32},{56,40},{64,11... | collective-permute-start | bytes 786440 | tf_op jit(solution)/shard_map/ppermute | solution.py:440
  48.7 13.2 %collective-permute-start.15 = (bf16[1040,128]{1,0:T(8,128)(2,1)S(1)}, bf16[1040,128]{1,0:T(8,128)(2,1)S(1)}, u32[]{:S(2)}, u32[]{:S(2)}) collective-permute-start(bf16[1040,128]{1,0:T(8,128)(2,1)S(1)} %get-tuple-element.41.refs_1_), channel_id=1, source_target_pairs={{0,128},{8,136},{16,144},{24,152},{32,160},{40,168},{48,176},{56,1... | collective-permute-start | bytes 798728 | tf_op jit(solution)/shard_map/ppermute | solution.py:439
  52.4 9.5 %collective-permute-start.18 = (bf16[1024,128]{1,0:T(8,128)(2,1)S(1)}, bf16[1024,128]{1,0:T(8,128)(2,1)S(1)}, u32[]{:S(2)}, u32[]{:S(2)}) collective-permute-start(bf16[1024,128]{1,0:T(8,128)(2,1)S(1)} %get-tuple-element.42.refs_4_.refs_5_), channel_id=1, source_target_pairs={{0,32},{8,40},{16,48},{24,56},{32,0},{40,8},{48,16},{56,24},{64,96... | collective-permute-start | bytes 786440 | tf_op jit(solution)/shard_map/ppermute | solution.py:440
  (3 other events, 2.2 us)

commit v7 on v6

--- a/solution.py
+++ b/solution.py
@@ -59,6 +59,10 @@
     )(*args)
 
 
+def held(array):
+    return pltpu.with_memory_space_constraint(array, pltpu.HBM)
+
+
 def column(row):
     square = (ROWS, ROWS)
     same = lax.broadcasted_iota(jnp.int32, square, 0) == lax.broadcasted_iota(jnp.int32, square, 1)
@@ -89,15 +93,31 @@
     pad_ref[...] = jnp.broadcast_to(embed_ref[...], pad_ref.shape)
 
 
+def low_kernel(source_ref, out_ref):
+    out_ref[...] = source_ref[: out_ref.shape[0], :]
+
+
+def high_kernel(source_ref, out_ref):
+    rows = out_ref.shape[0]
+    out_ref[...] = source_ref[rows : 2 * rows, :]
+
+
+def half(kernel, array, rows):
+    (out,) = call(kernel, [((rows, array.shape[1]), BF16)], [array], (1 << 10, 1 << 16))
+    return out
+
+
 def kv_kernel(*refs):
-    pieces = refs[:8]
-    pad_ref, wk_ref, wv_ref, code_ref = refs[8:12]
-    x_ref, kv_ref, mkv_ref = refs[12:]
+    pieces = refs[:10]
+    pad_ref, wk_ref, wv_ref, code_ref = refs[10:14]
+    x_ref, kv_ref, mkv_ref = refs[14:]
     me = lax.axis_index("kv")
-    for dz in range(4):
+    spots = ((0, 0, ROWS), (1, 0, ROWS), (3, 0, ROWS), (2, 0, ROWS // 2), (2, ROWS // 2, ROWS // 2))
+    for i, (dz, start, count) in enumerate(spots):
         for dc in range(2):
             source = lax.rem(me // 2 + 4 - dz, 4) * 2 + lax.rem(me + dc, 2)
-            x_ref[:ROWS, pl.ds(pl.multiple_of(source * WIDTH, WIDTH), WIDTH)] = pieces[2 * dz + dc][...]
+            lanes = pl.ds(pl.multiple_of(source * WIDTH, WIDTH), WIDTH)
+            x_ref[start : start + count, lanes] = pieces[2 * i + dc][...]
     x_ref[ROWS:, :] = pad_ref[...]
     x = x_ref[...]
     for part, w_ref in enumerate((wk_ref, wv_ref)):
@@ -375,7 +395,9 @@
     ids = block_ids.reshape(1, ROWS)
     order = decode_order.reshape(1, ROWS)
     cuts = step_cut.reshape(1, -1)
-    moved = [lax.ppermute(hidden, "kv", kv_pairs(d, 0)) for d in (1, 2, 3)]
+    moved = [lax.ppermute(hidden, "kv", kv_pairs(d, 0)) for d in (1, 3)]
+    moved.append(lax.ppermute(half(low_kernel, moved[0], ROWS // 2), "kv", kv_pairs(1, 0)))
+    moved.append(lax.ppermute(half(high_kernel, moved[1], ROWS // 2), "kv", kv_pairs(3, 0)))
     own, wk, wv, code, pad = call(
         prep_kernel,
         [
@@ -385,7 +407,7 @@
             ((PAD, ROWS), BF16),
             ((PAD, 8 * WIDTH), BF16),
         ],
-        [hidden, k_weight, v_weight, ids, order, mask_embed.reshape(1, -1)],
+        [held(a) for a in (hidden, k_weight, v_weight, ids, order, mask_embed.reshape(1, -1))],
         (1 << 20, 4 << 20),
         [
             pltpu.VMEM(ids.shape, jnp.int32),
@@ -393,7 +415,7 @@
             pltpu.VMEM((1, 8 * WIDTH), BF16),
             pltpu.SemaphoreType.DMA((6,)),
         ],
-        pltpu.HBM,
+        pl.ANY,
     )
     pieces = []
     for piece in (own, *moved):

time: 65.8 us -> 67.1 us (1.020); the launches traced: 65.6 us -> 66.1 us
  local copies, waits for them, and re-layouts: 5.37 us -> 1.32 us
  waiting for transfers between devices: 21.9 us -> 23.8 us
  starting transfers between devices: 25.9 us -> 27.4 us
  Pallas kernels: 11.6 us -> 12.9 us
    unnamed x14 -> x4, local copies, waits for them, and re-layouts: 4.67 us -> 0.01 us
    ppermute x3 -> x4, waiting for transfers between devices: 3.32 us -> 5.95 us  [the longest x1 3.14 us: shards(): lax.ppermute(half(high_kernel, moved[1], ROWS // 2), 'kv', kv_pairs(3, 0))]
    pallas_call x8 -> x10, Pallas kernels: 11.6 us -> 12.9 us  [call(): pl.pallas_call(kernel, out_shape=[jax.ShapeDtypeStruct(s, t) for s, t in...]
    ppermute x3 -> x4, starting transfers between devices: 11.4 us -> 12.1 us  [the longest x2 6.47 us: shards(): moved = [lax.ppermute(hidden, 'kv', kv_pairs(d, 0)) for d in (1, 3)]]
  transfers between devices with their start and end apart: 20 -> 22, of which waited for: 8 -> 10; matrix products, arithmetic and copies ran while one was open for 1% -> 2% of each run, Pallas kernels for 11% -> 13%
where the time goes in v7:
time: 67.1 us; the launch traced here: 66.1 us
  starting transfers between devices  27.4 us (41%)
  waiting for transfers between devices  23.8 us (35%)
  Pallas kernels  12.9 us (19%)
  local copies, waits for them, and re-layouts  1.32 us (2%)
  between operations  0.75 us (1%)
    pallas_call x10, Pallas kernels, call(): pl.pallas_call(kernel, out_shape=[jax.ShapeDtypeStruct(s, t) for s, t in...  12.9 us
    ppermute x2, starting transfers between devices, shards(): moved = [lax.ppermute(hidden, 'kv', kv_pairs(d, 0)) for d in (1, 3)]  6.47 us
    ppermute x3, starting transfers between devices, shards(): ks = [lax.ppermute(k, 'ctx', ctx_pairs(0, d, 0)) for d in (1, 2, 3)]  5.65 us
    ppermute x3, waiting for transfers between devices, shards(): vs = [lax.ppermute(v, 'ctx', ctx_pairs(d, 0, 0)) for d in (1, 2, 3)]  5.48 us
    ppermute x1, waiting for transfers between devices, shards(): pair = lax.ppermute(kv, 'ctx', ctx_pairs(0, 0, 1))  4.34 us
    ppermute x3, waiting for transfers between devices, shards(): lax.ppermute(ks, 'ctx', ctx_pairs(d, 0, 0))  3.61 us
    ppermute x3, starting transfers between devices, shards(): lax.ppermute(vs, 'ctx', ctx_pairs(0, d, 0))  3.5 us
    ppermute x3, waiting for transfers between devices, shards(): lax.ppermute(vs, 'ctx', ctx_pairs(0, d, 0))  3.19 us
  transfers between devices with their start and end apart: 22, of which 10 were waited for; matrix products, arithmetic and copies ran while one was open for 2% of the time, Pallas kernels for 13%

profile of v7, /device:TPU:24, one launch (start us, length us, event | category | flops | bytes accessed | tf_op | source)
XLA Modules:
  0.0 66.1 jit_solution(6468907199737223594)
XLA Ops:
  0.7 3.3 %collective-permute-start.1 = (bf16[128,512]{1,0:T(8,128)(2,1)}, bf16[128,512]{1,0:T(8,128)(2,1)S(1)}, u32[]{:S(2)}, u32[]{:S(2)}) collective-permute-start(bf16[128,512]{1,0:T(8,128)(2,1)} %refs_0_.1), channel_id=1, source_target_pairs={{0,2},{1,3},{2,4},{3,5},{4,6},{5,7},{6,0},{7,1},{8,10},{9,11},{10,... | collective-permute-start | bytes 393224 | tf_op jit(solution)/shard_map/ppermute | solution.py:398
  4.0 3.1 %collective-permute-start.3 = (bf16[128,512]{1,0:T(8,128)(2,1)}, bf16[128,512]{1,0:T(8,128)(2,1)S(1)}, u32[]{:S(2)}, u32[]{:S(2)}) collective-permute-start(bf16[128,512]{1,0:T(8,128)(2,1)} %refs_0_.1), channel_id=1, source_target_pairs={{0,6},{1,7},{2,0},{3,1},{4,2},{5,3},{6,4},{7,5},{8,14},{9,15},{10,... | collective-permute-start | bytes 393224 | tf_op jit(solution)/shard_map/ppermute | solution.py:398
  7.1 1.3 %reshape.18.refs_5_ = bf16[1,4096]{1,0:T(2,128)(2,1)} reshape(bf16[4096]{0:T(1024)(128)(2,1)} %param.12) | data formatting | bytes 16384 | tf_op jit(solution)/shard_map/reshape | solution.py:410
  8.4 1.7 %shard_map.95 = (bf16[128,512]{1,0:T(8,128)(2,1)S(1)}, bf16[4096,128]{1,0:T(8,128)(2,1)S(1)}, bf16[4096,128]{1,0:T(8,128)(2,1)S(1)}, bf16[16,128]{1,0:T(8,128)(2,1)S(1)}, bf16[16,4096]{1,0:T(8,128)(2,1)S(1)}) custom-call(bf16[128,512]{1,0:T(8,128)(2,1)} %refs_0_.1, bf16[4096,128]{1,0:T(8,128)(2,1)} %refs_1_.1, bf16[4096,128]{1,0:T(8,128)(2,1)} %refs_2_.1, ...), custom_call_target="tpu_custom_call" | custom-call | flops 1048576 | bytes 4194304 | tf_op jit(solution)/shard_map/pallas_call | solution.py:51
  10.2 1.2 %collective-permute-done.1.source_ref.refs_2_ = bf16[128,512]{1,0:T(8,128)(2,1)S(1)} collective-permute-done((bf16[128,512]{1,0:T(8,128)(2,1)}, bf16[128,512]{1,0:T(8,128)(2,1)S(1)}, u32[]{:S(2)}, u32[]{:S(2)}) %collective-permute-start.1) | collective-permute-done | bytes 131104 | tf_op jit(solution)/shard_map/ppermute | solution.py:398
  11.3 2.9 %collective-permute-start.5 = (bf16[64,512]{1,0:T(8,128)(2,1)S(1)}, bf16[64,512]{1,0:T(8,128)(2,1)S(1)}, u32[]{:S(2)}, u32[]{:S(2)}) collective-permute-start(bf16[64,512]{1,0:T(8,128)(2,1)S(1)} %shard_map.96), channel_id=1, source_target_pairs={{0,2},{1,3},{2,4},{3,5},{4,6},{5,7},{6,0},{7,1},{8,10},{9,11},{10,... | collective-permute-start | bytes 196616 | tf_op jit(solution)/shard_map/ppermute | solution.py:399
  14.8 2.7 %collective-permute-start.7 = (bf16[64,512]{1,0:T(8,128)(2,1)S(1)}, bf16[64,512]{1,0:T(8,128)(2,1)S(1)}, u32[]{:S(2)}, u32[]{:S(2)}) collective-permute-start(bf16[64,512]{1,0:T(8,128)(2,1)S(1)} %shard_map.97), channel_id=1, source_target_pairs={{0,6},{1,7},{2,0},{3,1},{4,2},{5,3},{6,4},{7,5},{8,14},{9,15},{10,... | collective-permute-start | bytes 196616 | tf_op jit(solution)/shard_map/ppermute | solution.py:400
  18.0 1.2 %collective-permute-done.5.refs_6_ = bf16[64,512]{1,0:T(8,128)(2,1)S(1)} collective-permute-done((bf16[64,512]{1,0:T(8,128)(2,1)S(1)}, bf16[64,512]{1,0:T(8,128)(2,1)S(1)}, u32[]{:S(2)}, u32[]{:S(2)}) %collective-permute-start.5) | collective-permute-done | bytes 65568 | tf_op jit(solution)/shard_map/ppermute | solution.py:399
  19.2 3.1 %collective-permute-done.7.refs_8_ = bf16[64,512]{1,0:T(8,128)(2,1)S(1)} collective-permute-done((bf16[64,512]{1,0:T(8,128)(2,1)S(1)}, bf16[64,512]{1,0:T(8,128)(2,1)S(1)}, u32[]{:S(2)}, u32[]{:S(2)}) %collective-permute-start.7) | collective-permute-done | bytes 65568 | tf_op jit(solution)/shard_map/ppermute | solution.py:400
  22.4 1.2 %collective-permute-done.8.refs_9_ = bf16[64,512]{1,0:T(8,128)(2,1)S(1)} collective-permute-done((bf16[64,512]{1,0:T(8,128)(2,1)S(1)}, bf16[64,512]{1,0:T(8,128)(2,1)S(1)}, u32[]{:S(2)}, u32[]{:S(2)}) %collective-permute-start.8) | collective-permute-done | bytes 65568 | tf_op jit(solution)/shard_map/ppermute | solution.py:423
  24.5 4.3 %collective-permute-done.9.other_ref = bf16[144,256]{1,0:T(8,128)(2,1)S(1)} collective-permute-done((bf16[144,256]{1,0:T(8,128)(2,1)S(1)}, bf16[144,256]{1,0:T(8,128)(2,1)S(1)}, u32[]{:S(2)}, u32[]{:S(2)}) %collective-permute-start.9) | collective-permute-done | bytes 73760 | tf_op jit(solution)/shard_map/ppermute | solution.py:434
  29.2 1.5 %collective-permute-start.10 = (bf16[272,128]{1,0:T(8,128)(2,1)S(1)}, bf16[272,128]{1,0:T(8,128)(2,1)S(1)}, u32[]{:S(2)}, u32[]{:S(2)}) collective-permute-start(bf16[272,128]{1,0:T(8,128)(2,1)S(1)} %get-tuple-element.41.refs_0_), channel_id=1, source_target_pairs={{0,16},{8,24},{16,32},{24,40},{32,48},{40,56},{48,0},{56,8},{64,80... | collective-permute-start | bytes 208904 | tf_op jit(solution)/shard_map/ppermute | solution.py:441
  30.7 2.7 %collective-permute-start.11 = (bf16[272,128]{1,0:T(8,128)(2,1)S(1)}, bf16[272,128]{1,0:T(8,128)(2,1)S(1)}, u32[]{:S(2)}, u32[]{:S(2)}) collective-permute-start(bf16[272,128]{1,0:T(8,128)(2,1)S(1)} %get-tuple-element.41.refs_0_), channel_id=1, source_target_pairs={{0,32},{8,40},{16,48},{24,56},{32,0},{40,8},{48,16},{56,24},{64,96... | collective-permute-start | bytes 208904 | tf_op jit(solution)/shard_map/ppermute | solution.py:441
  33.4 1.4 %collective-permute-start.12 = (bf16[272,128]{1,0:T(8,128)(2,1)S(1)}, bf16[272,128]{1,0:T(8,128)(2,1)S(1)}, u32[]{:S(2)}, u32[]{:S(2)}) collective-permute-start(bf16[272,128]{1,0:T(8,128)(2,1)S(1)} %get-tuple-element.41.refs_0_), channel_id=1, source_target_pairs={{0,48},{8,56},{16,0},{24,8},{32,16},{40,24},{48,32},{56,40},{64,11... | collective-permute-start | bytes 208904 | tf_op jit(solution)/shard_map/ppermute | solution.py:441
  34.9 2.6 %collective-permute-start.14 = (bf16[256,128]{1,0:T(8,128)(2,1)S(1)}, bf16[256,128]{1,0:T(8,128)(2,1)S(1)}, u32[]{:S(2)}, u32[]{:S(2)}) collective-permute-start(bf16[256,128]{1,0:T(8,128)(2,1)S(1)} %get-tuple-element.42.refs_4_), channel_id=1, source_target_pairs={{0,128},{8,136},{16,144},{24,152},{32,160},{40,168},{48,176},{56,1... | collective-permute-start | bytes 196616 | tf_op jit(solution)/shard_map/ppermute | solution.py:442
  37.5 3.2 %collective-permute-done.14.refs_6_ = bf16[256,128]{1,0:T(8,128)(2,1)S(1)} collective-permute-done((bf16[256,128]{1,0:T(8,128)(2,1)S(1)}, bf16[256,128]{1,0:T(8,128)(2,1)S(1)}, u32[]{:S(2)}, u32[]{:S(2)}) %collective-permute-start.14) | collective-permute-done | bytes 65568 | tf_op jit(solution)/shard_map/ppermute | solution.py:442
  40.6 2.3 %collective-permute-done.15.refs_7_ = bf16[256,128]{1,0:T(8,128)(2,1)S(1)} collective-permute-done((bf16[256,128]{1,0:T(8,128)(2,1)S(1)}, bf16[256,128]{1,0:T(8,128)(2,1)S(1)}, u32[]{:S(2)}, u32[]{:S(2)}) %collective-permute-start.15) | collective-permute-done | bytes 65568 | tf_op jit(solution)/shard_map/ppermute | solution.py:442
  44.8 1.1 %collective-permute-start.18 = (bf16[1040,128]{1,0:T(8,128)(2,1)S(1)}, bf16[1040,128]{1,0:T(8,128)(2,1)S(1)}, u32[]{:S(2)}, u32[]{:S(2)}) collective-permute-start(bf16[1040,128]{1,0:T(8,128)(2,1)S(1)} %get-tuple-element.43.refs_1_), channel_id=1, source_target_pairs={{0,192},{8,200},{16,208},{24,216},{32,224},{40,232},{48,240},{56,2... | collective-permute-start | bytes 798728 | tf_op jit(solution)/shard_map/ppermute | solution.py:461
  45.9 2.6 %collective-permute-start.21 = (bf16[1024,128]{1,0:T(8,128)(2,1)S(1)}, bf16[1024,128]{1,0:T(8,128)(2,1)S(1)}, u32[]{:S(2)}, u32[]{:S(2)}) collective-permute-start(bf16[1024,128]{1,0:T(8,128)(2,1)S(1)} %get-tuple-element.44.refs_4_.refs_5_), channel_id=1, source_target_pairs={{0,48},{8,56},{16,0},{24,8},{32,16},{40,24},{48,32},{56,40},{64,11... | collective-permute-start | bytes 786440 | tf_op jit(solution)/shard_map/ppermute | solution.py:462
  48.5 1.4 %shard_map.99 = (bf16[4,256,128]{2,1,0:T(8,128)(2,1)S(1)}, f32[128,128]{1,0:T(8,128)S(1)}, f32[128,128]{1,0:T(8,128)S(1)}) custom-call(bf16[144,4096]{1,0:T(8,128)(2,1)S(1)} %get-tuple-element.38.x_ref, bf16[4096,512]{1,0:T(8,128)(2,1)S(1)} %copy-done, bf16[16,128]{1,0:T(8,128)(2,1)S(1)} %get-tuple-element.37.refs_13_.code_ref.refs_10_, s32[1,256]{1,0:T(1,128)S(1)} %bitcast.3), custom_call_target="tpu_custom_call" | custom-call | flops 1073741824 | bytes 5242880 | tf_op jit(solution)/shard_map/pallas_call | solution.py:51
  50.5 3.2 %collective-permute-done.19.refs_5_.refs_6_ = bf16[1024,128]{1,0:T(8,128)(2,1)S(1)} collective-permute-done((bf16[1024,128]{1,0:T(8,128)(2,1)S(1)}, bf16[1024,128]{1,0:T(8,128)(2,1)S(1)}, u32[]{:S(2)}, u32[]{:S(2)}) %collective-permute-start.19) | collective-permute-done | bytes 262176 | tf_op jit(solution)/shard_map/ppermute | solution.py:462
  54.5 3.6 %collective-permute-done.18.refs_3_.refs_4_ = bf16[1040,128]{1,0:T(8,128)(2,1)S(1)} collective-permute-done((bf16[1040,128]{1,0:T(8,128)(2,1)S(1)}, bf16[1040,128]{1,0:T(8,128)(2,1)S(1)}, u32[]{:S(2)}, u32[]{:S(2)}) %collective-permute-start.18) | collective-permute-done | bytes 266272 | tf_op jit(solution)/shard_map/ppermute | solution.py:461
  58.1 4.4 %shard_map.103 = (f32[4,256,128]{2,1,0:T(8,128)S(1)}, f32[4,256,128]{2,1,0:T(8,128)S(1)}, f32[4,256,128]{2,1,0:T(8,128)S(1)}) custom-call(bf16[4,256,128]{2,1,0:T(8,128)(2,1)S(1)} %get-tuple-element.39.q_ref.refs_0_, bf16[1040,128]{1,0:T(8,128)(2,1)S(1)} %get-tuple-element.43.refs_1_, bf16[1040,128]{1,0:T(8,128)(2,1)S(1)} %collective-permute-done.16.refs_2_, ...), custom_call_target="tpu_custom_call" | custom-call | flops 2147483648 | bytes 4194304 | tf_op jit(solution)/shard_map/pallas_call | solution.py:51
  62.5 3.6 %shard_map.104 = (bf16[128,512]{1,0:T(8,128)(2,1)}, bf16[128,512]{1,0:T(8,128)(2,1)}) custom-call(bf16[4,256,128]{2,1,0:T(8,128)(2,1)S(1)} %get-tuple-element.39.q_ref.refs_0_, bf16[1040,128]{1,0:T(8,128)(2,1)S(1)} %get-tuple-element.43.refs_1_, bf16[1040,128]{1,0:T(8,128)(2,1)S(1)} %collective-permute-done.16.refs_2_, ...), custom_call_target="tpu_custom_call" | custom-call | flops 2147483648 | bytes 4194304 | tf_op jit(solution)/shard_map/pallas_call | solution.py:51
  (35 shorter events, 5.5 us)
Async XLA Ops:
  0.6 47.9 %copy-start.1 = (s32[256]{0:T(256)S(1)}, s32[256]{0:T(256)}, u32[]{:S(2)}) copy-start(s32[256]{0:T(256)} %param.11) | copy-start | bytes 3076
  0.6 47.9 %copy-start = (bf16[4096,512]{1,0:T(8,128)(2,1)S(1)}, bf16[4096,512]{1,0:T(8,128)(2,1)}, u32[]{:S(2)}) copy-start(bf16[4096,512]{1,0:T(8,128)(2,1)} %wq_ref.1) | copy-start | bytes 12582916
  0.7 10.7 %collective-permute-start.1 = (bf16[128,512]{1,0:T(8,128)(2,1)}, bf16[128,512]{1,0:T(8,128)(2,1)S(1)}, u32[]{:S(2)}, u32[]{:S(2)}) collective-permute-start(bf16[128,512]{1,0:T(8,128)(2,1)} %refs_0_.1), channel_id=1, source_target_pairs={{0,2},{1,3},{2,4},{3,5},{4,6},{5,7},{6,0},{7,1},{8,10},{9,11},{10,... | collective-permute-start | bytes 393224 | tf_op jit(solution)/shard_map/ppermute | solution.py:398
  4.0 10.7 %collective-permute-start.3 = (bf16[128,512]{1,0:T(8,128)(2,1)}, bf16[128,512]{1,0:T(8,128)(2,1)S(1)}, u32[]{:S(2)}, u32[]{:S(2)}) collective-permute-start(bf16[128,512]{1,0:T(8,128)(2,1)} %refs_0_.1), channel_id=1, source_target_pairs={{0,6},{1,7},{2,0},{3,1},{4,2},{5,3},{6,4},{7,5},{8,14},{9,15},{10,... | collective-permute-start | bytes 393224 | tf_op jit(solution)/shard_map/ppermute | solution.py:398
  11.3 7.8 %collective-permute-start.5 = (bf16[64,512]{1,0:T(8,128)(2,1)S(1)}, bf16[64,512]{1,0:T(8,128)(2,1)S(1)}, u32[]{:S(2)}, u32[]{:S(2)}) collective-permute-start(bf16[64,512]{1,0:T(8,128)(2,1)S(1)} %shard_map.96), channel_id=1, source_target_pairs={{0,2},{1,3},{2,4},{3,5},{4,6},{5,7},{6,0},{7,1},{8,10},{9,11},{10,... | collective-permute-start | bytes 196616 | tf_op jit(solution)/shard_map/ppermute | solution.py:399
  14.3 8.1 %collective-permute-start = (bf16[128,512]{1,0:T(8,128)(2,1)S(1)}, bf16[128,512]{1,0:T(8,128)(2,1)S(1)}, u32[]{:S(2)}, u32[]{:S(2)}) collective-permute-start(bf16[128,512]{1,0:T(8,128)(2,1)S(1)} %get-tuple-element.30.refs_0_), channel_id=1, source_target_pairs={{0,1},{1,0},{2,3},{3,2},{4,5},{5,4},{6,7},{7,6},{8,9},{9,8},{10,11... | collective-permute-start | bytes 393224 | tf_op jit(solution)/shard_map/ppermute | solution.py:423
  14.8 7.6 %collective-permute-start.7 = (bf16[64,512]{1,0:T(8,128)(2,1)S(1)}, bf16[64,512]{1,0:T(8,128)(2,1)S(1)}, u32[]{:S(2)}, u32[]{:S(2)}) collective-permute-start(bf16[64,512]{1,0:T(8,128)(2,1)S(1)} %shard_map.97), channel_id=1, source_target_pairs={{0,6},{1,7},{2,0},{3,1},{4,2},{5,3},{6,4},{7,5},{8,14},{9,15},{10,... | collective-permute-start | bytes 196616 | tf_op jit(solution)/shard_map/ppermute | solution.py:400
  17.5 6.1 %collective-permute-start.2 = (bf16[128,512]{1,0:T(8,128)(2,1)S(1)}, bf16[128,512]{1,0:T(8,128)(2,1)S(1)}, u32[]{:S(2)}, u32[]{:S(2)}) collective-permute-start(bf16[128,512]{1,0:T(8,128)(2,1)S(1)} %collective-permute-done.1.source_ref.refs_2_), channel_id=1, source_target_pairs={{0,1},{1,0},{2,3},{3,2},{4,5},{5,4},{6,7},{7,6},{8,9},{9,8},{10,11... | collective-permute-start | bytes 393224 | tf_op jit(solution)/shard_map/ppermute | solution.py:423
  17.5 6.1 %collective-permute-start.4 = (bf16[128,512]{1,0:T(8,128)(2,1)S(1)}, bf16[128,512]{1,0:T(8,128)(2,1)S(1)}, u32[]{:S(2)}, u32[]{:S(2)}) collective-permute-start(bf16[128,512]{1,0:T(8,128)(2,1)S(1)} %collective-permute-done.3.source_ref.refs_4_), channel_id=1, source_target_pairs={{0,1},{1,0},{2,3},{3,2},{4,5},{5,4},{6,7},{7,6},{8,9},{9,8},{10,11... | collective-permute-start | bytes 393224 | tf_op jit(solution)/shard_map/ppermute | solution.py:423
  19.2 3.2 %collective-permute-start.6 = (bf16[64,512]{1,0:T(8,128)(2,1)S(1)}, bf16[64,512]{1,0:T(8,128)(2,1)S(1)}, u32[]{:S(2)}, u32[]{:S(2)}) collective-permute-start(bf16[64,512]{1,0:T(8,128)(2,1)S(1)} %collective-permute-done.5.refs_6_), channel_id=1, source_target_pairs={{0,1},{1,0},{2,3},{3,2},{4,5},{5,4},{6,7},{7,6},{8,9},{9,8},{10,11... | collective-permute-start | bytes 196616 | tf_op jit(solution)/shard_map/ppermute | solution.py:423
  22.3 1.3 %collective-permute-start.8 = (bf16[64,512]{1,0:T(8,128)(2,1)S(1)}, bf16[64,512]{1,0:T(8,128)(2,1)S(1)}, u32[]{:S(2)}, u32[]{:S(2)}) collective-permute-start(bf16[64,512]{1,0:T(8,128)(2,1)S(1)} %collective-permute-done.7.refs_8_), channel_id=1, source_target_pairs={{0,1},{1,0},{2,3},{3,2},{4,5},{5,4},{6,7},{7,6},{8,9},{9,8},{10,11... | collective-permute-start | bytes 196616 | tf_op jit(solution)/shard_map/ppermute | solution.py:423
  24.4 4.4 %collective-permute-start.9 = (bf16[144,256]{1,0:T(8,128)(2,1)S(1)}, bf16[144,256]{1,0:T(8,128)(2,1)S(1)}, u32[]{:S(2)}, u32[]{:S(2)}) collective-permute-start(bf16[144,256]{1,0:T(8,128)(2,1)S(1)} %get-tuple-element.40.own_ref.kv_ref), channel_id=1, source_target_pairs={{0,8},{8,0},{16,24},{24,16},{32,40},{40,32},{48,56},{56,48},{64,72... | collective-permute-start | bytes 221192 | tf_op jit(solution)/shard_map/ppermute | solution.py:434
  28.9 8.5 %collective-permute-start.13 = (bf16[256,128]{1,0:T(8,128)(2,1)S(1)}, bf16[256,128]{1,0:T(8,128)(2,1)S(1)}, u32[]{:S(2)}, u32[]{:S(2)}) collective-permute-start(bf16[256,128]{1,0:T(8,128)(2,1)S(1)} %get-tuple-element.42.refs_4_), channel_id=1, source_target_pairs={{0,64},{8,72},{16,80},{24,88},{32,96},{40,104},{48,112},{56,120},{... | collective-permute-start | bytes 196616 | tf_op jit(solution)/shard_map/ppermute | solution.py:442
  29.2 13.7 %collective-permute-start.10 = (bf16[272,128]{1,0:T(8,128)(2,1)S(1)}, bf16[272,128]{1,0:T(8,128)(2,1)S(1)}, u32[]{:S(2)}, u32[]{:S(2)}) collective-permute-start(bf16[272,128]{1,0:T(8,128)(2,1)S(1)} %get-tuple-element.41.refs_0_), channel_id=1, source_target_pairs={{0,16},{8,24},{16,32},{24,40},{32,48},{40,56},{48,0},{56,8},{64,80... | collective-permute-start | bytes 208904 | tf_op jit(solution)/shard_map/ppermute | solution.py:441
  30.7 12.2 %collective-permute-start.11 = (bf16[272,128]{1,0:T(8,128)(2,1)S(1)}, bf16[272,128]{1,0:T(8,128)(2,1)S(1)}, u32[]{:S(2)}, u32[]{:S(2)}) collective-permute-start(bf16[272,128]{1,0:T(8,128)(2,1)S(1)} %get-tuple-element.41.refs_0_), channel_id=1, source_target_pairs={{0,32},{8,40},{16,48},{24,56},{32,0},{40,8},{48,16},{56,24},{64,96... | collective-permute-start | bytes 208904 | tf_op jit(solution)/shard_map/ppermute | solution.py:441
  33.4 9.5 %collective-permute-start.12 = (bf16[272,128]{1,0:T(8,128)(2,1)S(1)}, bf16[272,128]{1,0:T(8,128)(2,1)S(1)}, u32[]{:S(2)}, u32[]{:S(2)}) collective-permute-start(bf16[272,128]{1,0:T(8,128)(2,1)S(1)} %get-tuple-element.41.refs_0_), channel_id=1, source_target_pairs={{0,48},{8,56},{16,0},{24,8},{32,16},{40,24},{48,32},{56,40},{64,11... | collective-permute-start | bytes 208904 | tf_op jit(solution)/shard_map/ppermute | solution.py:441
  34.9 5.8 %collective-permute-start.14 = (bf16[256,128]{1,0:T(8,128)(2,1)S(1)}, bf16[256,128]{1,0:T(8,128)(2,1)S(1)}, u32[]{:S(2)}, u32[]{:S(2)}) collective-permute-start(bf16[256,128]{1,0:T(8,128)(2,1)S(1)} %get-tuple-element.42.refs_4_), channel_id=1, source_target_pairs={{0,128},{8,136},{16,144},{24,152},{32,160},{40,168},{48,176},{56,1... | collective-permute-start | bytes 196616 | tf_op jit(solution)/shard_map/ppermute | solution.py:442
  37.4 5.5 %collective-permute-start.15 = (bf16[256,128]{1,0:T(8,128)(2,1)S(1)}, bf16[256,128]{1,0:T(8,128)(2,1)S(1)}, u32[]{:S(2)}, u32[]{:S(2)}) collective-permute-start(bf16[256,128]{1,0:T(8,128)(2,1)S(1)} %get-tuple-element.42.refs_4_), channel_id=1, source_target_pairs={{0,192},{8,200},{16,208},{24,216},{32,224},{40,232},{48,240},{56,2... | collective-permute-start | bytes 196616 | tf_op jit(solution)/shard_map/ppermute | solution.py:442
  43.0 10.6 %collective-permute-start.19 = (bf16[1024,128]{1,0:T(8,128)(2,1)S(1)}, bf16[1024,128]{1,0:T(8,128)(2,1)S(1)}, u32[]{:S(2)}, u32[]{:S(2)}) collective-permute-start(bf16[1024,128]{1,0:T(8,128)(2,1)S(1)} %get-tuple-element.44.refs_4_.refs_5_), channel_id=1, source_target_pairs={{0,16},{8,24},{16,32},{24,40},{32,48},{40,56},{48,0},{56,8},{64,80... | collective-permute-start | bytes 786440 | tf_op jit(solution)/shard_map/ppermute | solution.py:462
  43.8 10.6 %collective-permute-start.16 = (bf16[1040,128]{1,0:T(8,128)(2,1)S(1)}, bf16[1040,128]{1,0:T(8,128)(2,1)S(1)}, u32[]{:S(2)}, u32[]{:S(2)}) collective-permute-start(bf16[1040,128]{1,0:T(8,128)(2,1)S(1)} %get-tuple-element.43.refs_1_), channel_id=1, source_target_pairs={{0,64},{8,72},{16,80},{24,88},{32,96},{40,104},{48,112},{56,120},{... | collective-permute-start | bytes 798728 | tf_op jit(solution)/shard_map/ppermute | solution.py:461
  44.8 13.3 %collective-permute-start.18 = (bf16[1040,128]{1,0:T(8,128)(2,1)S(1)}, bf16[1040,128]{1,0:T(8,128)(2,1)S(1)}, u32[]{:S(2)}, u32[]{:S(2)}) collective-permute-start(bf16[1040,128]{1,0:T(8,128)(2,1)S(1)} %get-tuple-element.43.refs_1_), channel_id=1, source_target_pairs={{0,192},{8,200},{16,208},{24,216},{32,224},{40,232},{48,240},{56,2... | collective-permute-start | bytes 798728 | tf_op jit(solution)/shard_map/ppermute | solution.py:461
  45.9 8.6 %collective-permute-start.21 = (bf16[1024,128]{1,0:T(8,128)(2,1)S(1)}, bf16[1024,128]{1,0:T(8,128)(2,1)S(1)}, u32[]{:S(2)}, u32[]{:S(2)}) collective-permute-start(bf16[1024,128]{1,0:T(8,128)(2,1)S(1)} %get-tuple-element.44.refs_4_.refs_5_), channel_id=1, source_target_pairs={{0,48},{8,56},{16,0},{24,8},{32,16},{40,24},{48,32},{56,40},{64,11... | collective-permute-start | bytes 786440 | tf_op jit(solution)/shard_map/ppermute | solution.py:462
  49.9 12.6 %collective-permute-start.17 = (bf16[1040,128]{1,0:T(8,128)(2,1)S(1)}, bf16[1040,128]{1,0:T(8,128)(2,1)S(1)}, u32[]{:S(2)}, u32[]{:S(2)}) collective-permute-start(bf16[1040,128]{1,0:T(8,128)(2,1)S(1)} %get-tuple-element.43.refs_1_), channel_id=1, source_target_pairs={{0,128},{8,136},{16,144},{24,152},{32,160},{40,168},{48,176},{56,1... | collective-permute-start | bytes 798728 | tf_op jit(solution)/shard_map/ppermute | solution.py:461
  53.6 8.9 %collective-permute-start.20 = (bf16[1024,128]{1,0:T(8,128)(2,1)S(1)}, bf16[1024,128]{1,0:T(8,128)(2,1)S(1)}, u32[]{:S(2)}, u32[]{:S(2)}) collective-permute-start(bf16[1024,128]{1,0:T(8,128)(2,1)S(1)} %get-tuple-element.44.refs_4_.refs_5_), channel_id=1, source_target_pairs={{0,32},{8,40},{16,48},{24,56},{32,0},{40,8},{48,16},{56,24},{64,96... | collective-permute-start | bytes 786440 | tf_op jit(solution)/shard_map/ppermute | solution.py:462

commit v8 on v7

--- a/solution.py
+++ b/solution.py
@@ -102,22 +102,34 @@
     out_ref[...] = source_ref[rows : 2 * rows, :]
 
 
-def half(kernel, array, rows):
-    (out,) = call(kernel, [((rows, array.shape[1]), BF16)], [array], (1 << 10, 1 << 16))
+def half(kernel, array):
+    (out,) = call(kernel, [((ROWS // 2, WIDTH), BF16)], [array], (1 << 10, 1 << 16))
     return out
 
 
+def join_kernel(*refs):
+    out_ref = refs[-1]
+    rows = refs[0].shape[0]
+    for i, ref in enumerate(refs[:-1]):
+        out_ref[i * rows : (i + 1) * rows, :] = ref[...]
+
+
+def join(*arrays):
+    rows = sum(a.shape[0] for a in arrays)
+    (out,) = call(join_kernel, [((rows, WIDTH), BF16)], arrays, (1 << 10, 1 << 19))
+    return out
+
+
 def kv_kernel(*refs):
-    pieces = refs[:10]
-    pad_ref, wk_ref, wv_ref, code_ref = refs[10:14]
-    x_ref, kv_ref, mkv_ref = refs[14:]
+    early, early_other, late, late_other, pad_ref, wk_ref, wv_ref, code_ref = refs[:8]
+    x_ref, kv_ref, mkv_ref = refs[8:]
     me = lax.axis_index("kv")
-    spots = ((0, 0, ROWS), (1, 0, ROWS), (3, 0, ROWS), (2, 0, ROWS // 2), (2, ROWS // 2, ROWS // 2))
-    for i, (dz, start, count) in enumerate(spots):
-        for dc in range(2):
+    for dc, (first, second) in enumerate(((early, late), (early_other, late_other))):
+        for dz in range(4):
             source = lax.rem(me // 2 + 4 - dz, 4) * 2 + lax.rem(me + dc, 2)
             lanes = pl.ds(pl.multiple_of(source * WIDTH, WIDTH), WIDTH)
-            x_ref[start : start + count, lanes] = pieces[2 * i + dc][...]
+            i = (0, 1, None, 2)[dz]
+            x_ref[:ROWS, lanes] = second[...] if i is None else first[i * ROWS : (i + 1) * ROWS, :]
     x_ref[ROWS:, :] = pad_ref[...]
     x = x_ref[...]
     for part, w_ref in enumerate((wk_ref, wv_ref)):
@@ -395,9 +407,9 @@
     ids = block_ids.reshape(1, ROWS)
     order = decode_order.reshape(1, ROWS)
     cuts = step_cut.reshape(1, -1)
-    moved = [lax.ppermute(hidden, "kv", kv_pairs(d, 0)) for d in (1, 3)]
-    moved.append(lax.ppermute(half(low_kernel, moved[0], ROWS // 2), "kv", kv_pairs(1, 0)))
-    moved.append(lax.ppermute(half(high_kernel, moved[1], ROWS // 2), "kv", kv_pairs(3, 0)))
+    one, three = [lax.ppermute(hidden, "kv", kv_pairs(d, 0)) for d in (1, 3)]
+    low = lax.ppermute(half(low_kernel, one), "kv", kv_pairs(1, 0))
+    high = lax.ppermute(half(high_kernel, three), "kv", kv_pairs(3, 0))
     own, wk, wv, code, pad = call(
         prep_kernel,
         [
@@ -417,10 +429,10 @@
         ],
         pl.ANY,
     )
-    pieces = []
-    for piece in (own, *moved):
-        piece, _ = lax.optimization_barrier((piece, pad))
-        pieces += [piece, lax.ppermute(piece, "kv", kv_pairs(0, 1))]
+    early = join(own, one, three)
+    early_other = lax.ppermute(early, "kv", kv_pairs(0, 1))
+    late = join(low, high)
+    late_other = lax.ppermute(late, "kv", kv_pairs(0, 1))
     x, kv, mask_kv = call(
         kv_kernel,
         [
@@ -428,7 +440,7 @@
             ((ROWS + PAD, 2 * HEAD), BF16),
             ((PAD, 2 * HEAD), BF16),
         ],
-        [*pieces, pad, wk, wv, code],
+        [early, early_other, late, late_other, pad, wk, wv, code],
         (1 << 29, 3 << 20),
     )
     pair = lax.ppermute(kv, "ctx", ctx_pairs(0, 0, 1))

time: 67.1 us -> 69 us (1.028)
  waiting for transfers between devices: 23.8 us -> 27.1 us
  starting transfers between devices: 27.4 us -> 26.5 us
    ppermute x9 -> x6, waiting for transfers between devices: 7.17 us -> 11.6 us  [the longest x2 4.57 us: shards(): one, three = [lax.ppermute(hidden, 'kv', kv_pairs(d, 0)) for d in (1, 3)]]
    ppermute x9 -> x6, starting transfers between devices: 12.7 us -> 10.9 us  [the longest x2 6.47 us: shards(): one, three = [lax.ppermute(hidden, 'kv', kv_pairs(d, 0)) for d in (1, 3)]]
    ppermute x1, starting transfers between devices: 0.09 us -> 1.22 us  [shards(): pair = lax.ppermute(kv, 'ctx', ctx_pairs(0, 0, 1))]
    ppermute x1, waiting for transfers between devices: 4.34 us -> 3.22 us  [shards(): pair = lax.ppermute(kv, 'ctx', ctx_pairs(0, 0, 1))]
    pallas_call x10 -> x12, Pallas kernels: 12.9 us -> 12.9 us  [call(): pl.pallas_call(kernel, out_shape=[jax.ShapeDtypeStruct(s, t) for s, t in...]
  transfers between devices with their start and end apart: 22 -> 19, of which waited for: 10 -> 10; matrix products, arithmetic and copies ran while one was open for 2% -> 2% of each run, Pallas kernels for 13% -> 12%
where the time goes in v8:
time: 69 us; the launch traced here: 68.6 us
  waiting for transfers between devices  27.1 us (39%)
  starting transfers between devices  26.5 us (38%)
  Pallas kernels  12.9 us (19%)
  local copies, waits for them, and re-layouts  1.32 us (2%)
  between operations  0.77 us (1%)
    pallas_call x12, Pallas kernels, call(): pl.pallas_call(kernel, out_shape=[jax.ShapeDtypeStruct(s, t) for s, t in...  12.9 us
    ppermute x2, starting transfers between devices, shards(): one, three = [lax.ppermute(hidden, 'kv', kv_pairs(d, 0)) for d in (1, 3)]  6.47 us
    ppermute x3, starting transfers between devices, shards(): ks = [lax.ppermute(k, 'ctx', ctx_pairs(0, d, 0)) for d in (1, 2, 3)]  5.65 us
    ppermute x3, waiting for transfers between devices, shards(): vs = [lax.ppermute(v, 'ctx', ctx_pairs(d, 0, 0)) for d in (1, 2, 3)]  5.48 us
    ppermute x2, waiting for transfers between devices, shards(): one, three = [lax.ppermute(hidden, 'kv', kv_pairs(d, 0)) for d in (1, 3)]  4.57 us
    ppermute x1, starting transfers between devices, shards(): low = lax.ppermute(half(low_kernel, one), 'kv', kv_pairs(1, 0))  3.81 us
    ppermute x3, waiting for transfers between devices, shards(): lax.ppermute(ks, 'ctx', ctx_pairs(d, 0, 0))  3.66 us
    ppermute x3, starting transfers between devices, shards(): lax.ppermute(vs, 'ctx', ctx_pairs(0, d, 0))  3.32 us
  transfers between devices with their start and end apart: 19, of which 10 were waited for; matrix products, arithmetic and copies ran while one was open for 2% of the time, Pallas kernels for 12%

profile of v8, /device:TPU:24, one launch (start us, length us, event | category | flops | bytes accessed | tf_op | source)
XLA Modules:
  0.0 68.6 jit_solution(5320490752700640089)
XLA Ops:
  0.7 3.3 %collective-permute-start = (bf16[128,512]{1,0:T(8,128)(2,1)}, bf16[128,512]{1,0:T(8,128)(2,1)S(1)}, u32[]{:S(2)}, u32[]{:S(2)}) collective-permute-start(bf16[128,512]{1,0:T(8,128)(2,1)} %refs_0_.1), channel_id=1, source_target_pairs={{0,2},{1,3},{2,4},{3,5},{4,6},{5,7},{6,0},{7,1},{8,10},{9,11},{10,... | collective-permute-start | bytes 393224 | tf_op jit(solution)/shard_map/ppermute | solution.py:410
  4.0 3.1 %collective-permute-start.1 = (bf16[128,512]{1,0:T(8,128)(2,1)}, bf16[128,512]{1,0:T(8,128)(2,1)S(1)}, u32[]{:S(2)}, u32[]{:S(2)}) collective-permute-start(bf16[128,512]{1,0:T(8,128)(2,1)} %refs_0_.1), channel_id=1, source_target_pairs={{0,6},{1,7},{2,0},{3,1},{4,2},{5,3},{6,4},{7,5},{8,14},{9,15},{10,... | collective-permute-start | bytes 393224 | tf_op jit(solution)/shard_map/ppermute | solution.py:410
  7.1 1.3 %reshape.18.refs_5_ = bf16[1,4096]{1,0:T(2,128)(2,1)} reshape(bf16[4096]{0:T(1024)(128)(2,1)} %param.12) | data formatting | bytes 16384 | tf_op jit(solution)/shard_map/reshape | solution.py:422
  8.4 1.7 %shard_map.95 = (bf16[128,512]{1,0:T(8,128)(2,1)S(1)}, bf16[4096,128]{1,0:T(8,128)(2,1)S(1)}, bf16[4096,128]{1,0:T(8,128)(2,1)S(1)}, bf16[16,128]{1,0:T(8,128)(2,1)S(1)}, bf16[16,4096]{1,0:T(8,128)(2,1)S(1)}) custom-call(bf16[128,512]{1,0:T(8,128)(2,1)} %refs_0_.1, bf16[4096,128]{1,0:T(8,128)(2,1)} %refs_1_.1, bf16[4096,128]{1,0:T(8,128)(2,1)} %refs_2_.1, ...), custom_call_target="tpu_custom_call" | custom-call | flops 1048576 | bytes 4194304 | tf_op jit(solution)/shard_map/pallas_call | solution.py:51
  10.2 1.2 %collective-permute-done.refs_1_.source_ref = bf16[128,512]{1,0:T(8,128)(2,1)S(1)} collective-permute-done((bf16[128,512]{1,0:T(8,128)(2,1)}, bf16[128,512]{1,0:T(8,128)(2,1)S(1)}, u32[]{:S(2)}, u32[]{:S(2)}) %collective-permute-start) | collective-permute-done | bytes 131104 | tf_op jit(solution)/shard_map/ppermute | solution.py:410
  11.3 3.4 %collective-permute-done.1.refs_2_.source_ref = bf16[128,512]{1,0:T(8,128)(2,1)S(1)} collective-permute-done((bf16[128,512]{1,0:T(8,128)(2,1)}, bf16[128,512]{1,0:T(8,128)(2,1)S(1)}, u32[]{:S(2)}, u32[]{:S(2)}) %collective-permute-start.1) | collective-permute-done | bytes 131104 | tf_op jit(solution)/shard_map/ppermute | solution.py:410
  14.9 3.8 %collective-permute-start.3 = (bf16[64,512]{1,0:T(8,128)(2,1)S(1)}, bf16[64,512]{1,0:T(8,128)(2,1)S(1)}, u32[]{:S(2)}, u32[]{:S(2)}) collective-permute-start(bf16[64,512]{1,0:T(8,128)(2,1)S(1)} %shard_map.97), channel_id=1, source_target_pairs={{0,2},{1,3},{2,4},{3,5},{4,6},{5,7},{6,0},{7,1},{8,10},{9,11},{10,... | collective-permute-start | bytes 196616 | tf_op jit(solution)/shard_map/ppermute | solution.py:411
  19.1 2.6 %collective-permute-done.3.refs_0_ = bf16[64,512]{1,0:T(8,128)(2,1)S(1)} collective-permute-done((bf16[64,512]{1,0:T(8,128)(2,1)S(1)}, bf16[64,512]{1,0:T(8,128)(2,1)S(1)}, u32[]{:S(2)}, u32[]{:S(2)}) %collective-permute-start.3) | collective-permute-done | bytes 65568 | tf_op jit(solution)/shard_map/ppermute | solution.py:411
  21.7 3.1 %collective-permute-done.4.refs_1_ = bf16[64,512]{1,0:T(8,128)(2,1)S(1)} collective-permute-done((bf16[64,512]{1,0:T(8,128)(2,1)S(1)}, bf16[64,512]{1,0:T(8,128)(2,1)S(1)}, u32[]{:S(2)}, u32[]{:S(2)}) %collective-permute-start.4) | collective-permute-done | bytes 65568 | tf_op jit(solution)/shard_map/ppermute | solution.py:412
  24.9 1.3 %collective-permute-done.5.refs_3_ = bf16[128,512]{1,0:T(8,128)(2,1)S(1)} collective-permute-done((bf16[128,512]{1,0:T(8,128)(2,1)S(1)}, bf16[128,512]{1,0:T(8,128)(2,1)S(1)}, u32[]{:S(2)}, u32[]{:S(2)}) %collective-permute-start.5) | collective-permute-done | bytes 131104 | tf_op jit(solution)/shard_map/ppermute | solution.py:435
  27.1 1.2 %collective-permute-start.6 = (bf16[144,256]{1,0:T(8,128)(2,1)S(1)}, bf16[144,256]{1,0:T(8,128)(2,1)S(1)}, u32[]{:S(2)}, u32[]{:S(2)}) collective-permute-start(bf16[144,256]{1,0:T(8,128)(2,1)S(1)} %get-tuple-element.30.own_ref.kv_ref), channel_id=1, source_target_pairs={{0,8},{8,0},{16,24},{24,16},{32,40},{40,32},{48,56},{56,48},{64,72... | collective-permute-start | bytes 221192 | tf_op jit(solution)/shard_map/ppermute | solution.py:446
  28.3 3.2 %collective-permute-done.6.other_ref = bf16[144,256]{1,0:T(8,128)(2,1)S(1)} collective-permute-done((bf16[144,256]{1,0:T(8,128)(2,1)S(1)}, bf16[144,256]{1,0:T(8,128)(2,1)S(1)}, u32[]{:S(2)}, u32[]{:S(2)}) %collective-permute-start.6) | collective-permute-done | bytes 73760 | tf_op jit(solution)/shard_map/ppermute | solution.py:446
  31.9 1.5 %collective-permute-start.7 = (bf16[272,128]{1,0:T(8,128)(2,1)S(1)}, bf16[272,128]{1,0:T(8,128)(2,1)S(1)}, u32[]{:S(2)}, u32[]{:S(2)}) collective-permute-start(bf16[272,128]{1,0:T(8,128)(2,1)S(1)} %get-tuple-element.31.refs_0_), channel_id=1, source_target_pairs={{0,16},{8,24},{16,32},{24,40},{32,48},{40,56},{48,0},{56,8},{64,80... | collective-permute-start | bytes 208904 | tf_op jit(solution)/shard_map/ppermute | solution.py:453
  33.4 2.7 %collective-permute-start.8 = (bf16[272,128]{1,0:T(8,128)(2,1)S(1)}, bf16[272,128]{1,0:T(8,128)(2,1)S(1)}, u32[]{:S(2)}, u32[]{:S(2)}) collective-permute-start(bf16[272,128]{1,0:T(8,128)(2,1)S(1)} %get-tuple-element.31.refs_0_), channel_id=1, source_target_pairs={{0,32},{8,40},{16,48},{24,56},{32,0},{40,8},{48,16},{56,24},{64,96... | collective-permute-start | bytes 208904 | tf_op jit(solution)/shard_map/ppermute | solution.py:453
  36.1 1.4 %collective-permute-start.9 = (bf16[272,128]{1,0:T(8,128)(2,1)S(1)}, bf16[272,128]{1,0:T(8,128)(2,1)S(1)}, u32[]{:S(2)}, u32[]{:S(2)}) collective-permute-start(bf16[272,128]{1,0:T(8,128)(2,1)S(1)} %get-tuple-element.31.refs_0_), channel_id=1, source_target_pairs={{0,48},{8,56},{16,0},{24,8},{32,16},{40,24},{48,32},{56,40},{64,11... | collective-permute-start | bytes 208904 | tf_op jit(solution)/shard_map/ppermute | solution.py:453
  37.5 2.6 %collective-permute-start.11 = (bf16[256,128]{1,0:T(8,128)(2,1)S(1)}, bf16[256,128]{1,0:T(8,128)(2,1)S(1)}, u32[]{:S(2)}, u32[]{:S(2)}) collective-permute-start(bf16[256,128]{1,0:T(8,128)(2,1)S(1)} %get-tuple-element.32.refs_4_), channel_id=1, source_target_pairs={{0,128},{8,136},{16,144},{24,152},{32,160},{40,168},{48,176},{56,1... | collective-permute-start | bytes 196616 | tf_op jit(solution)/shard_map/ppermute | solution.py:454
  40.1 3.2 %collective-permute-done.11.refs_6_ = bf16[256,128]{1,0:T(8,128)(2,1)S(1)} collective-permute-done((bf16[256,128]{1,0:T(8,128)(2,1)S(1)}, bf16[256,128]{1,0:T(8,128)(2,1)S(1)}, u32[]{:S(2)}, u32[]{:S(2)}) %collective-permute-start.11) | collective-permute-done | bytes 65568 | tf_op jit(solution)/shard_map/ppermute | solution.py:454
  43.3 2.3 %collective-permute-done.12.refs_7_ = bf16[256,128]{1,0:T(8,128)(2,1)S(1)} collective-permute-done((bf16[256,128]{1,0:T(8,128)(2,1)S(1)}, bf16[256,128]{1,0:T(8,128)(2,1)S(1)}, u32[]{:S(2)}, u32[]{:S(2)}) %collective-permute-start.12) | collective-permute-done | bytes 65568 | tf_op jit(solution)/shard_map/ppermute | solution.py:454
  48.4 2.6 %collective-permute-start.18 = (bf16[1024,128]{1,0:T(8,128)(2,1)S(1)}, bf16[1024,128]{1,0:T(8,128)(2,1)S(1)}, u32[]{:S(2)}, u32[]{:S(2)}) collective-permute-start(bf16[1024,128]{1,0:T(8,128)(2,1)S(1)} %get-tuple-element.34.refs_4_.refs_5_), channel_id=1, source_target_pairs={{0,48},{8,56},{16,0},{24,8},{32,16},{40,24},{48,32},{56,40},{64,11... | collective-permute-start | bytes 786440 | tf_op jit(solution)/shard_map/ppermute | solution.py:474
  51.0 1.4 %shard_map.101 = (bf16[4,256,128]{2,1,0:T(8,128)(2,1)S(1)}, f32[128,128]{1,0:T(8,128)S(1)}, f32[128,128]{1,0:T(8,128)S(1)}) custom-call(bf16[144,4096]{1,0:T(8,128)(2,1)S(1)} %get-tuple-element.28.x_ref, bf16[4096,512]{1,0:T(8,128)(2,1)S(1)} %copy-done, bf16[16,128]{1,0:T(8,128)(2,1)S(1)} %get-tuple-element.27.refs_7_.code_ref.refs_10_, s32[1,256]{1,0:T(1,128)S(1)} %bitcast.3), custom_call_target="tpu_custom_call" | custom-call | flops 1073741824 | bytes 5242880 | tf_op jit(solution)/shard_map/pallas_call | solution.py:51
  53.0 3.2 %collective-permute-done.16.refs_5_.refs_6_ = bf16[1024,128]{1,0:T(8,128)(2,1)S(1)} collective-permute-done((bf16[1024,128]{1,0:T(8,128)(2,1)S(1)}, bf16[1024,128]{1,0:T(8,128)(2,1)S(1)}, u32[]{:S(2)}, u32[]{:S(2)}) %collective-permute-start.16) | collective-permute-done | bytes 262176 | tf_op jit(solution)/shard_map/ppermute | solution.py:474
  57.0 3.7 %collective-permute-done.15.refs_3_.refs_4_ = bf16[1040,128]{1,0:T(8,128)(2,1)S(1)} collective-permute-done((bf16[1040,128]{1,0:T(8,128)(2,1)S(1)}, bf16[1040,128]{1,0:T(8,128)(2,1)S(1)}, u32[]{:S(2)}, u32[]{:S(2)}) %collective-permute-start.15) | collective-permute-done | bytes 266272 | tf_op jit(solution)/shard_map/ppermute | solution.py:473
  60.6 4.3 %shard_map.105 = (f32[4,256,128]{2,1,0:T(8,128)S(1)}, f32[4,256,128]{2,1,0:T(8,128)S(1)}, f32[4,256,128]{2,1,0:T(8,128)S(1)}) custom-call(bf16[4,256,128]{2,1,0:T(8,128)(2,1)S(1)} %get-tuple-element.29.q_ref.refs_0_, bf16[1040,128]{1,0:T(8,128)(2,1)S(1)} %get-tuple-element.33.refs_1_, bf16[1040,128]{1,0:T(8,128)(2,1)S(1)} %collective-permute-done.13.refs_2_, ...), custom_call_target="tpu_custom_call" | custom-call | flops 2147483648 | bytes 4194304 | tf_op jit(solution)/shard_map/pallas_call | solution.py:51
  65.0 3.6 %shard_map.106 = (bf16[128,512]{1,0:T(8,128)(2,1)}, bf16[128,512]{1,0:T(8,128)(2,1)}) custom-call(bf16[4,256,128]{2,1,0:T(8,128)(2,1)S(1)} %get-tuple-element.29.q_ref.refs_0_, bf16[1040,128]{1,0:T(8,128)(2,1)S(1)} %get-tuple-element.33.refs_1_, bf16[1040,128]{1,0:T(8,128)(2,1)S(1)} %collective-permute-done.13.refs_2_, ...), custom_call_target="tpu_custom_call" | custom-call | flops 2147483648 | bytes 4194304 | tf_op jit(solution)/shard_map/pallas_call | solution.py:51
  (31 shorter events, 5.9 us)
Async XLA Ops:
  0.6 50.4 %copy-start.1 = (s32[256]{0:T(256)S(1)}, s32[256]{0:T(256)}, u32[]{:S(2)}) copy-start(s32[256]{0:T(256)} %param.11) | copy-start | bytes 3076
  0.6 50.4 %copy-start = (bf16[4096,512]{1,0:T(8,128)(2,1)S(1)}, bf16[4096,512]{1,0:T(8,128)(2,1)}, u32[]{:S(2)}) copy-start(bf16[4096,512]{1,0:T(8,128)(2,1)} %wq_ref.1) | copy-start | bytes 12582916
  0.7 10.7 %collective-permute-start = (bf16[128,512]{1,0:T(8,128)(2,1)}, bf16[128,512]{1,0:T(8,128)(2,1)S(1)}, u32[]{:S(2)}, u32[]{:S(2)}) collective-permute-start(bf16[128,512]{1,0:T(8,128)(2,1)} %refs_0_.1), channel_id=1, source_target_pairs={{0,2},{1,3},{2,4},{3,5},{4,6},{5,7},{6,0},{7,1},{8,10},{9,11},{10,... | collective-permute-start | bytes 393224 | tf_op jit(solution)/shard_map/ppermute | solution.py:410
  4.0 10.7 %collective-permute-start.1 = (bf16[128,512]{1,0:T(8,128)(2,1)}, bf16[128,512]{1,0:T(8,128)(2,1)S(1)}, u32[]{:S(2)}, u32[]{:S(2)}) collective-permute-start(bf16[128,512]{1,0:T(8,128)(2,1)} %refs_0_.1), channel_id=1, source_target_pairs={{0,6},{1,7},{2,0},{3,1},{4,2},{5,3},{6,4},{7,5},{8,14},{9,15},{10,... | collective-permute-start | bytes 393224 | tf_op jit(solution)/shard_map/ppermute | solution.py:410
  14.8 11.5 %collective-permute-start.2 = (bf16[384,512]{1,0:T(8,128)(2,1)S(1)}, bf16[384,512]{1,0:T(8,128)(2,1)S(1)}, u32[]{:S(2)}, u32[]{:S(2)}) collective-permute-start(bf16[384,512]{1,0:T(8,128)(2,1)S(1)} %shard_map.96.refs_0_), channel_id=1, source_target_pairs={{0,1},{1,0},{2,3},{3,2},{4,5},{5,4},{6,7},{7,6},{8,9},{9,8},{10,11... | collective-permute-start | bytes 1179656 | tf_op jit(solution)/shard_map/ppermute | solution.py:433
  14.9 6.8 %collective-permute-start.3 = (bf16[64,512]{1,0:T(8,128)(2,1)S(1)}, bf16[64,512]{1,0:T(8,128)(2,1)S(1)}, u32[]{:S(2)}, u32[]{:S(2)}) collective-permute-start(bf16[64,512]{1,0:T(8,128)(2,1)S(1)} %shard_map.97), channel_id=1, source_target_pairs={{0,2},{1,3},{2,4},{3,5},{4,6},{5,7},{6,0},{7,1},{8,10},{9,11},{10,... | collective-permute-start | bytes 196616 | tf_op jit(solution)/shard_map/ppermute | solution.py:411
  18.7 6.1 %collective-permute-start.4 = (bf16[64,512]{1,0:T(8,128)(2,1)S(1)}, bf16[64,512]{1,0:T(8,128)(2,1)S(1)}, u32[]{:S(2)}, u32[]{:S(2)}) collective-permute-start(bf16[64,512]{1,0:T(8,128)(2,1)S(1)} %shard_map.98), channel_id=1, source_target_pairs={{0,6},{1,7},{2,0},{3,1},{4,2},{5,3},{6,4},{7,5},{8,14},{9,15},{10,... | collective-permute-start | bytes 196616 | tf_op jit(solution)/shard_map/ppermute | solution.py:412
  24.8 1.4 %collective-permute-start.5 = (bf16[128,512]{1,0:T(8,128)(2,1)S(1)}, bf16[128,512]{1,0:T(8,128)(2,1)S(1)}, u32[]{:S(2)}, u32[]{:S(2)}) collective-permute-start(bf16[128,512]{1,0:T(8,128)(2,1)S(1)} %shard_map.99.refs_2_), channel_id=1, source_target_pairs={{0,1},{1,0},{2,3},{3,2},{4,5},{5,4},{6,7},{7,6},{8,9},{9,8},{10,11... | collective-permute-start | bytes 393224 | tf_op jit(solution)/shard_map/ppermute | solution.py:435
  27.1 4.4 %collective-permute-start.6 = (bf16[144,256]{1,0:T(8,128)(2,1)S(1)}, bf16[144,256]{1,0:T(8,128)(2,1)S(1)}, u32[]{:S(2)}, u32[]{:S(2)}) collective-permute-start(bf16[144,256]{1,0:T(8,128)(2,1)S(1)} %get-tuple-element.30.own_ref.kv_ref), channel_id=1, source_target_pairs={{0,8},{8,0},{16,24},{24,16},{32,40},{40,32},{48,56},{56,48},{64,72... | collective-permute-start | bytes 221192 | tf_op jit(solution)/shard_map/ppermute | solution.py:446
  31.6 8.5 %collective-permute-start.10 = (bf16[256,128]{1,0:T(8,128)(2,1)S(1)}, bf16[256,128]{1,0:T(8,128)(2,1)S(1)}, u32[]{:S(2)}, u32[]{:S(2)}) collective-permute-start(bf16[256,128]{1,0:T(8,128)(2,1)S(1)} %get-tuple-element.32.refs_4_), channel_id=1, source_target_pairs={{0,64},{8,72},{16,80},{24,88},{32,96},{40,104},{48,112},{56,120},{... | collective-permute-start | bytes 196616 | tf_op jit(solution)/shard_map/ppermute | solution.py:454
  31.9 13.7 %collective-permute-start.7 = (bf16[272,128]{1,0:T(8,128)(2,1)S(1)}, bf16[272,128]{1,0:T(8,128)(2,1)S(1)}, u32[]{:S(2)}, u32[]{:S(2)}) collective-permute-start(bf16[272,128]{1,0:T(8,128)(2,1)S(1)} %get-tuple-element.31.refs_0_), channel_id=1, source_target_pairs={{0,16},{8,24},{16,32},{24,40},{32,48},{40,56},{48,0},{56,8},{64,80... | collective-permute-start | bytes 208904 | tf_op jit(solution)/shard_map/ppermute | solution.py:453
  33.4 12.2 %collective-permute-start.8 = (bf16[272,128]{1,0:T(8,128)(2,1)S(1)}, bf16[272,128]{1,0:T(8,128)(2,1)S(1)}, u32[]{:S(2)}, u32[]{:S(2)}) collective-permute-start(bf16[272,128]{1,0:T(8,128)(2,1)S(1)} %get-tuple-element.31.refs_0_), channel_id=1, source_target_pairs={{0,32},{8,40},{16,48},{24,56},{32,0},{40,8},{48,16},{56,24},{64,96... | collective-permute-start | bytes 208904 | tf_op jit(solution)/shard_map/ppermute | solution.py:453
  36.1 9.5 %collective-permute-start.9 = (bf16[272,128]{1,0:T(8,128)(2,1)S(1)}, bf16[272,128]{1,0:T(8,128)(2,1)S(1)}, u32[]{:S(2)}, u32[]{:S(2)}) collective-permute-start(bf16[272,128]{1,0:T(8,128)(2,1)S(1)} %get-tuple-element.31.refs_0_), channel_id=1, source_target_pairs={{0,48},{8,56},{16,0},{24,8},{32,16},{40,24},{48,32},{56,40},{64,11... | collective-permute-start | bytes 208904 | tf_op jit(solution)/shard_map/ppermute | solution.py:453
  37.5 5.8 %collective-permute-start.11 = (bf16[256,128]{1,0:T(8,128)(2,1)S(1)}, bf16[256,128]{1,0:T(8,128)(2,1)S(1)}, u32[]{:S(2)}, u32[]{:S(2)}) collective-permute-start(bf16[256,128]{1,0:T(8,128)(2,1)S(1)} %get-tuple-element.32.refs_4_), channel_id=1, source_target_pairs={{0,128},{8,136},{16,144},{24,152},{32,160},{40,168},{48,176},{56,1... | collective-permute-start | bytes 196616 | tf_op jit(solution)/shard_map/ppermute | solution.py:454
  40.1 5.5 %collective-permute-start.12 = (bf16[256,128]{1,0:T(8,128)(2,1)S(1)}, bf16[256,128]{1,0:T(8,128)(2,1)S(1)}, u32[]{:S(2)}, u32[]{:S(2)}) collective-permute-start(bf16[256,128]{1,0:T(8,128)(2,1)S(1)} %get-tuple-element.32.refs_4_), channel_id=1, source_target_pairs={{0,192},{8,200},{16,208},{24,216},{32,224},{40,232},{48,240},{56,2... | collective-permute-start | bytes 196616 | tf_op jit(solution)/shard_map/ppermute | solution.py:454
  45.7 10.5 %collective-permute-start.16 = (bf16[1024,128]{1,0:T(8,128)(2,1)S(1)}, bf16[1024,128]{1,0:T(8,128)(2,1)S(1)}, u32[]{:S(2)}, u32[]{:S(2)}) collective-permute-start(bf16[1024,128]{1,0:T(8,128)(2,1)S(1)} %get-tuple-element.34.refs_4_.refs_5_), channel_id=1, source_target_pairs={{0,16},{8,24},{16,32},{24,40},{32,48},{40,56},{48,0},{56,8},{64,80... | collective-permute-start | bytes 786440 | tf_op jit(solution)/shard_map/ppermute | solution.py:474
  46.3 10.7 %collective-permute-start.13 = (bf16[1040,128]{1,0:T(8,128)(2,1)S(1)}, bf16[1040,128]{1,0:T(8,128)(2,1)S(1)}, u32[]{:S(2)}, u32[]{:S(2)}) collective-permute-start(bf16[1040,128]{1,0:T(8,128)(2,1)S(1)} %get-tuple-element.33.refs_1_), channel_id=1, source_target_pairs={{0,64},{8,72},{16,80},{24,88},{32,96},{40,104},{48,112},{56,120},{... | collective-permute-start | bytes 798728 | tf_op jit(solution)/shard_map/ppermute | solution.py:473
  47.4 13.3 %collective-permute-start.15 = (bf16[1040,128]{1,0:T(8,128)(2,1)S(1)}, bf16[1040,128]{1,0:T(8,128)(2,1)S(1)}, u32[]{:S(2)}, u32[]{:S(2)}) collective-permute-start(bf16[1040,128]{1,0:T(8,128)(2,1)S(1)} %get-tuple-element.33.refs_1_), channel_id=1, source_target_pairs={{0,192},{8,200},{16,208},{24,216},{32,224},{40,232},{48,240},{56,2... | collective-permute-start | bytes 798728 | tf_op jit(solution)/shard_map/ppermute | solution.py:473
  48.4 8.6 %collective-permute-start.18 = (bf16[1024,128]{1,0:T(8,128)(2,1)S(1)}, bf16[1024,128]{1,0:T(8,128)(2,1)S(1)}, u32[]{:S(2)}, u32[]{:S(2)}) collective-permute-start(bf16[1024,128]{1,0:T(8,128)(2,1)S(1)} %get-tuple-element.34.refs_4_.refs_5_), channel_id=1, source_target_pairs={{0,48},{8,56},{16,0},{24,8},{32,16},{40,24},{48,32},{56,40},{64,11... | collective-permute-start | bytes 786440 | tf_op jit(solution)/shard_map/ppermute | solution.py:474
  52.4 12.6 %collective-permute-start.14 = (bf16[1040,128]{1,0:T(8,128)(2,1)S(1)}, bf16[1040,128]{1,0:T(8,128)(2,1)S(1)}, u32[]{:S(2)}, u32[]{:S(2)}) collective-permute-start(bf16[1040,128]{1,0:T(8,128)(2,1)S(1)} %get-tuple-element.33.refs_1_), channel_id=1, source_target_pairs={{0,128},{8,136},{16,144},{24,152},{32,160},{40,168},{48,176},{56,1... | collective-permute-start | bytes 798728 | tf_op jit(solution)/shard_map/ppermute | solution.py:473
  56.1 8.9 %collective-permute-start.17 = (bf16[1024,128]{1,0:T(8,128)(2,1)S(1)}, bf16[1024,128]{1,0:T(8,128)(2,1)S(1)}, u32[]{:S(2)}, u32[]{:S(2)}) collective-permute-start(bf16[1024,128]{1,0:T(8,128)(2,1)S(1)} %get-tuple-element.34.refs_4_.refs_5_), channel_id=1, source_target_pairs={{0,32},{8,40},{16,48},{24,56},{32,0},{40,8},{48,16},{56,24},{64,96... | collective-permute-start | bytes 786440 | tf_op jit(solution)/shard_map/ppermute | solution.py:474

commit v9 on v8

--- a/solution.py
+++ b/solution.py
@@ -93,20 +93,6 @@
     pad_ref[...] = jnp.broadcast_to(embed_ref[...], pad_ref.shape)
 
 
-def low_kernel(source_ref, out_ref):
-    out_ref[...] = source_ref[: out_ref.shape[0], :]
-
-
-def high_kernel(source_ref, out_ref):
-    rows = out_ref.shape[0]
-    out_ref[...] = source_ref[rows : 2 * rows, :]
-
-
-def half(kernel, array):
-    (out,) = call(kernel, [((ROWS // 2, WIDTH), BF16)], [array], (1 << 10, 1 << 16))
-    return out
-
-
 def join_kernel(*refs):
     out_ref = refs[-1]
     rows = refs[0].shape[0]
@@ -121,15 +107,14 @@
 
 
 def kv_kernel(*refs):
-    early, early_other, late, late_other, pad_ref, wk_ref, wv_ref, code_ref = refs[:8]
-    x_ref, kv_ref, mkv_ref = refs[8:]
+    mine, other, pad_ref, wk_ref, wv_ref, code_ref = refs[:6]
+    x_ref, kv_ref, mkv_ref = refs[6:]
     me = lax.axis_index("kv")
-    for dc, (first, second) in enumerate(((early, late), (early_other, late_other))):
+    for dc, ref in enumerate((mine, other)):
         for dz in range(4):
             source = lax.rem(me // 2 + 4 - dz, 4) * 2 + lax.rem(me + dc, 2)
             lanes = pl.ds(pl.multiple_of(source * WIDTH, WIDTH), WIDTH)
-            i = (0, 1, None, 2)[dz]
-            x_ref[:ROWS, lanes] = second[...] if i is None else first[i * ROWS : (i + 1) * ROWS, :]
+            x_ref[:ROWS, lanes] = ref[dz * ROWS : (dz + 1) * ROWS, :]
     x_ref[ROWS:, :] = pad_ref[...]
     x = x_ref[...]
     for part, w_ref in enumerate((wk_ref, wv_ref)):
@@ -283,6 +268,23 @@
     return mask
 
 
+def spots_piece(where, k_of, v_of, spots):
+    def keys():
+        return jnp.concatenate([k_of[dy][dx * 2 * ROWS : (dx + 1) * 2 * ROWS, :] for dy, dx in spots], axis=0)
+
+    def values():
+        return jnp.concatenate([v_of[dx][dy * 2 * ROWS : (dy + 1) * 2 * ROWS, :] for dy, dx in spots], axis=0)
+
+    return keys, values, shard_mask(where, spots), None
+
+
+def first_kernel(*refs):
+    q_ref = refs[0]
+    k_of, v_of = dict(zip((0, 1), refs[1:3])), dict(zip((0, 1), refs[3:5]))
+    piece = spots_piece(place(), k_of, v_of, ((0, 0), (0, 1), (1, 0), (1, 1)))
+    pipeline(q_ref, [piece], refs[5:8], refs[8:11], None)
+
+
 def far_kernel(*refs):
     q_ref = refs[0]
     k_refs = dict(zip((0, 1, 3), refs[1:4]))
@@ -358,17 +360,11 @@
     def rim_mask(parts):
         return [jnp.where(bias[:, j * ROWS : (j + 1) * ROWS] < -1.0, LOW, part) for j, part in enumerate(parts)]
 
-    near = (0, 1, 3)
-    pieces = [(lambda: k_rim, lambda: v_rim, rim_mask, None)]
-    for dy in near:
-        pieces.append(
-            (
-                lambda dy=dy: blocks_of(k_refs[dy], near),
-                lambda dy=dy: jnp.concatenate([blocks_of(v_refs[dx], (dy,)) for dx in near], axis=0),
-                shard_mask((me, y, x, z), [(dy, dx) for dx in near]) if dy < 3 else None,
-                y >= dy if dy == 3 else None,
-            )
-        )
+    spots = ((0, 3), (1, 3), (3, 0), (3, 1), (3, 3))
+    pieces = [
+        (lambda: k_rim, lambda: v_rim, rim_mask, None),
+        spots_piece((me, y, x, z), k_refs, v_refs, spots),
+    ]
     pipeline(q_ref, pieces, state_in, state, None)
 
 
@@ -407,9 +403,7 @@
     ids = block_ids.reshape(1, ROWS)
     order = decode_order.reshape(1, ROWS)
     cuts = step_cut.reshape(1, -1)
-    one, three = [lax.ppermute(hidden, "kv", kv_pairs(d, 0)) for d in (1, 3)]
-    low = lax.ppermute(half(low_kernel, one), "kv", kv_pairs(1, 0))
-    high = lax.ppermute(half(high_kernel, three), "kv", kv_pairs(3, 0))
+    moved = [lax.ppermute(hidden, "kv", kv_pairs(d, 0)) for d in (1, 2, 3)]
     own, wk, wv, code, pad = call(
         prep_kernel,
         [
@@ -429,10 +423,8 @@
         ],
         pl.ANY,
     )
-    early = join(own, one, three)
-    early_other = lax.ppermute(early, "kv", kv_pairs(0, 1))
-    late = join(low, high)
-    late_other = lax.ppermute(late, "kv", kv_pairs(0, 1))
+    mine = join(own, *moved)
+    other = lax.ppermute(mine, "kv", kv_pairs(0, 1))
     x, kv, mask_kv = call(
         kv_kernel,
         [
@@ -440,7 +432,7 @@
             ((ROWS + PAD, 2 * HEAD), BF16),
             ((PAD, 2 * HEAD), BF16),
         ],
-        [early, early_other, late, late_other, pad, wk, wv, code],
+        [mine, other, pad, wk, wv, code],
         (1 << 29, 3 << 20),
     )
     pair = lax.ppermute(kv, "ctx", ctx_pairs(0, 0, 1))
@@ -473,10 +465,16 @@
     all_k = [ks] + [lax.ppermute(ks, "ctx", ctx_pairs(d, 0, 0)) for d in (1, 2, 3)]
     all_v = [vs] + [lax.ppermute(vs, "ctx", ctx_pairs(0, d, 0)) for d in (1, 2, 3)]
     state = [((GROUP, 2 * ROWS, HEAD), F32)] * 3
+    first = call(
+        first_kernel,
+        state,
+        [q, *all_k[:2], *all_v[:2], *near],
+        (1 << 30, 2 << 20),
+    )
     far = call(
         far_kernel,
         state,
-        [q, *[all_k[d] for d in (0, 1, 3)], *[all_v[d] for d in (0, 1, 3)], *near, code, own_cut, mask_kv],
+        [q, *[all_k[d] for d in (0, 1, 3)], *[all_v[d] for d in (0, 1, 3)], *first, code, own_cut, mask_kv],
         (1 << 31, 4 << 20),
     )
     return tuple(

time: 69 us -> 67.7 us (0.981); the launches traced: 68.6 us -> 66.4 us
  waiting for transfers between devices: 27.1 us -> 25.3 us
    ppermute x3, waiting for transfers between devices: 3.66 us -> 0.01 us  [shards(): lax.ppermute(ks, 'ctx', ctx_pairs(d, 0, 0))]
    ppermute x3, waiting for transfers between devices: 3.18 us -> 6.19 us  [shards(): lax.ppermute(vs, 'ctx', ctx_pairs(0, d, 0))]
    ppermute x6 -> x4, waiting for transfers between devices: 11.6 us -> 8.57 us  [the longest x3 6.68 us: shards(): moved = [lax.ppermute(hidden, 'kv', kv_pairs(d, 0)) for d in (1, 2, 3)]]
    ppermute x1, starting transfers between devices: 1.22 us -> 0.09 us  [shards(): pair = lax.ppermute(kv, 'ctx', ctx_pairs(0, 0, 1))]
    ppermute x1, waiting for transfers between devices: 3.22 us -> 4.34 us  [shards(): pair = lax.ppermute(kv, 'ctx', ctx_pairs(0, 0, 1))]
    ppermute x6 -> x4, starting transfers between devices: 10.9 us -> 11.5 us  [the longest x3 11.4 us: shards(): moved = [lax.ppermute(hidden, 'kv', kv_pairs(d, 0)) for d in (1, 2, 3)]]
    pallas_call x12 -> x10, Pallas kernels: 12.9 us -> 13 us  [call(): pl.pallas_call(kernel, out_shape=[jax.ShapeDtypeStruct(s, t) for s, t in...]
  transfers between devices with their start and end apart: 19 -> 17, of which waited for: 10 -> 8; matrix products, arithmetic and copies ran while one was open for 2% -> 2% of each run, Pallas kernels for 12% -> 13%
where the time goes in v9:
time: 67.7 us; the launch traced here: 66.4 us
  starting transfers between devices  26 us (38%)
  waiting for transfers between devices  25.3 us (37%)
  Pallas kernels  13 us (19%)
  local copies, waits for them, and re-layouts  1.32 us (2%)
  between operations  0.76 us (1%)
    pallas_call x10, Pallas kernels, call(): pl.pallas_call(kernel, out_shape=[jax.ShapeDtypeStruct(s, t) for s, t in...  13 us
    ppermute x3, starting transfers between devices, shards(): moved = [lax.ppermute(hidden, 'kv', kv_pairs(d, 0)) for d in (1, 2, 3)]  11.4 us
    ppermute x3, waiting for transfers between devices, shards(): moved = [lax.ppermute(hidden, 'kv', kv_pairs(d, 0)) for d in (1, 2, 3)]  6.68 us
    ppermute x3, waiting for transfers between devices, shards(): lax.ppermute(vs, 'ctx', ctx_pairs(0, d, 0))  6.19 us
    ppermute x3, waiting for transfers between devices, shards(): vs = [lax.ppermute(v, 'ctx', ctx_pairs(d, 0, 0)) for d in (1, 2, 3)]  6.13 us
    ppermute x3, starting transfers between devices, shards(): ks = [lax.ppermute(k, 'ctx', ctx_pairs(0, d, 0)) for d in (1, 2, 3)]  5.65 us
    ppermute x1, waiting for transfers between devices, shards(): pair = lax.ppermute(kv, 'ctx', ctx_pairs(0, 0, 1))  4.34 us
    ppermute x3, starting transfers between devices, shards(): vs = [lax.ppermute(v, 'ctx', ctx_pairs(d, 0, 0)) for d in (1, 2, 3)]  3.34 us
  transfers between devices with their start and end apart: 17, of which 8 were waited for; matrix products, arithmetic and copies ran while one was open for 2% of the time, Pallas kernels for 13%

profile of v9, /device:TPU:24, one launch (start us, length us, event | category | flops | bytes accessed | tf_op | source)
XLA Modules:
  0.0 66.4 jit_solution(8800599548280680888)
XLA Ops:
  0.7 3.3 %collective-permute-start = (bf16[128,512]{1,0:T(8,128)(2,1)}, bf16[128,512]{1,0:T(8,128)(2,1)S(1)}, u32[]{:S(2)}, u32[]{:S(2)}) collective-permute-start(bf16[128,512]{1,0:T(8,128)(2,1)} %refs_0_.1), channel_id=1, source_target_pairs={{0,2},{1,3},{2,4},{3,5},{4,6},{5,7},{6,0},{7,1},{8,10},{9,11},{10,... | collective-permute-start | bytes 393224 | tf_op jit(solution)/shard_map/ppermute | solution.py:406
  4.0 5.4 %collective-permute-start.1 = (bf16[128,512]{1,0:T(8,128)(2,1)}, bf16[128,512]{1,0:T(8,128)(2,1)S(1)}, u32[]{:S(2)}, u32[]{:S(2)}) collective-permute-start(bf16[128,512]{1,0:T(8,128)(2,1)} %refs_0_.1), channel_id=1, source_target_pairs={{0,4},{1,5},{2,6},{3,7},{4,0},{5,1},{6,2},{7,3},{8,12},{9,13},{10,... | collective-permute-start | bytes 393224 | tf_op jit(solution)/shard_map/ppermute | solution.py:406
  9.4 2.7 %collective-permute-start.2 = (bf16[128,512]{1,0:T(8,128)(2,1)}, bf16[128,512]{1,0:T(8,128)(2,1)S(1)}, u32[]{:S(2)}, u32[]{:S(2)}) collective-permute-start(bf16[128,512]{1,0:T(8,128)(2,1)} %refs_0_.1), channel_id=1, source_target_pairs={{0,6},{1,7},{2,0},{3,1},{4,2},{5,3},{6,4},{7,5},{8,14},{9,15},{10,... | collective-permute-start | bytes 393224 | tf_op jit(solution)/shard_map/ppermute | solution.py:406
  12.1 1.3 %reshape.18.refs_5_ = bf16[1,4096]{1,0:T(2,128)(2,1)} reshape(bf16[4096]{0:T(1024)(128)(2,1)} %param.12) | data formatting | bytes 16384 | tf_op jit(solution)/shard_map/reshape | solution.py:416
  13.4 1.7 %shard_map.95 = (bf16[128,512]{1,0:T(8,128)(2,1)S(1)}, bf16[4096,128]{1,0:T(8,128)(2,1)S(1)}, bf16[4096,128]{1,0:T(8,128)(2,1)S(1)}, bf16[16,128]{1,0:T(8,128)(2,1)S(1)}, bf16[16,4096]{1,0:T(8,128)(2,1)S(1)}) custom-call(bf16[128,512]{1,0:T(8,128)(2,1)} %refs_0_.1, bf16[4096,128]{1,0:T(8,128)(2,1)} %refs_1_.1, bf16[4096,128]{1,0:T(8,128)(2,1)} %refs_2_.1, ...), custom_call_target="tpu_custom_call" | custom-call | flops 1048576 | bytes 4194304 | tf_op jit(solution)/shard_map/pallas_call | solution.py:51
  15.1 3.4 %collective-permute-done.1.refs_2_ = bf16[128,512]{1,0:T(8,128)(2,1)S(1)} collective-permute-done((bf16[128,512]{1,0:T(8,128)(2,1)}, bf16[128,512]{1,0:T(8,128)(2,1)S(1)}, u32[]{:S(2)}, u32[]{:S(2)}) %collective-permute-start.1) | collective-permute-done | bytes 131104 | tf_op jit(solution)/shard_map/ppermute | solution.py:406
  18.5 3.3 %collective-permute-done.2.refs_3_ = bf16[128,512]{1,0:T(8,128)(2,1)S(1)} collective-permute-done((bf16[128,512]{1,0:T(8,128)(2,1)}, bf16[128,512]{1,0:T(8,128)(2,1)S(1)}, u32[]{:S(2)}, u32[]{:S(2)}) %collective-permute-start.2) | collective-permute-done | bytes 131104 | tf_op jit(solution)/shard_map/ppermute | solution.py:406
  21.9 1.9 %collective-permute-done.3.refs_1_ = bf16[512,512]{1,0:T(8,128)(2,1)S(1)} collective-permute-done((bf16[512,512]{1,0:T(8,128)(2,1)S(1)}, bf16[512,512]{1,0:T(8,128)(2,1)S(1)}, u32[]{:S(2)}, u32[]{:S(2)}) %collective-permute-start.3) | collective-permute-done | bytes 524320 | tf_op jit(solution)/shard_map/ppermute | solution.py:427
  23.8 0.9 %shard_map.97 = (bf16[144,4096]{1,0:T(8,128)(2,1)S(1)}, bf16[144,256]{1,0:T(8,128)(2,1)S(1)}, bf16[16,256]{1,0:T(8,128)(2,1)S(1)}) custom-call(bf16[512,512]{1,0:T(8,128)(2,1)S(1)} %shard_map.96.refs_0_, bf16[512,512]{1,0:T(8,128)(2,1)S(1)} %collective-permute-done.3.refs_1_, bf16[16,4096]{1,0:T(8,128)(2,1)S(1)} %get-tuple-element.27.refs_2_, ...), custom_call_target="tpu_custom_call" | custom-call | flops 536870912 | bytes 3145728 | tf_op jit(solution)/shard_map/pallas_call | solution.py:51
  24.8 4.3 %collective-permute-done.4.other_ref = bf16[144,256]{1,0:T(8,128)(2,1)S(1)} collective-permute-done((bf16[144,256]{1,0:T(8,128)(2,1)S(1)}, bf16[144,256]{1,0:T(8,128)(2,1)S(1)}, u32[]{:S(2)}, u32[]{:S(2)}) %collective-permute-start.4) | collective-permute-done | bytes 73760 | tf_op jit(solution)/shard_map/ppermute | solution.py:438
  30.0 1.5 %collective-permute-start.5 = (bf16[272,128]{1,0:T(8,128)(2,1)S(1)}, bf16[272,128]{1,0:T(8,128)(2,1)S(1)}, u32[]{:S(2)}, u32[]{:S(2)}) collective-permute-start(bf16[272,128]{1,0:T(8,128)(2,1)S(1)} %get-tuple-element.34.refs_0_), channel_id=1, source_target_pairs={{0,16},{8,24},{16,32},{24,40},{32,48},{40,56},{48,0},{56,8},{64,80... | collective-permute-start | bytes 208904 | tf_op jit(solution)/shard_map/ppermute | solution.py:445
  31.5 2.7 %collective-permute-start.6 = (bf16[272,128]{1,0:T(8,128)(2,1)S(1)}, bf16[272,128]{1,0:T(8,128)(2,1)S(1)}, u32[]{:S(2)}, u32[]{:S(2)}) collective-permute-start(bf16[272,128]{1,0:T(8,128)(2,1)S(1)} %get-tuple-element.34.refs_0_), channel_id=1, source_target_pairs={{0,32},{8,40},{16,48},{24,56},{32,0},{40,8},{48,16},{56,24},{64,96... | collective-permute-start | bytes 208904 | tf_op jit(solution)/shard_map/ppermute | solution.py:445
  34.2 1.4 %collective-permute-start.7 = (bf16[272,128]{1,0:T(8,128)(2,1)S(1)}, bf16[272,128]{1,0:T(8,128)(2,1)S(1)}, u32[]{:S(2)}, u32[]{:S(2)}) collective-permute-start(bf16[272,128]{1,0:T(8,128)(2,1)S(1)} %get-tuple-element.34.refs_0_), channel_id=1, source_target_pairs={{0,48},{8,56},{16,0},{24,8},{32,16},{40,24},{48,32},{56,40},{64,11... | collective-permute-start | bytes 208904 | tf_op jit(solution)/shard_map/ppermute | solution.py:445
  35.6 2.5 %collective-permute-start.8 = (bf16[256,128]{1,0:T(8,128)(2,1)S(1)}, bf16[256,128]{1,0:T(8,128)(2,1)S(1)}, u32[]{:S(2)}, u32[]{:S(2)}) collective-permute-start(bf16[256,128]{1,0:T(8,128)(2,1)S(1)} %get-tuple-element.35.refs_4_), channel_id=1, source_target_pairs={{0,64},{8,72},{16,80},{24,88},{32,96},{40,104},{48,112},{56,120},{... | collective-permute-start | bytes 196616 | tf_op jit(solution)/shard_map/ppermute | solution.py:446
  38.2 2.5 %collective-permute-done.8.refs_5_ = bf16[256,128]{1,0:T(8,128)(2,1)S(1)} collective-permute-done((bf16[256,128]{1,0:T(8,128)(2,1)S(1)}, bf16[256,128]{1,0:T(8,128)(2,1)S(1)}, u32[]{:S(2)}, u32[]{:S(2)}) %collective-permute-start.8) | collective-permute-done | bytes 65568 | tf_op jit(solution)/shard_map/ppermute | solution.py:446
  40.7 3.6 %collective-permute-done.9.refs_6_ = bf16[256,128]{1,0:T(8,128)(2,1)S(1)} collective-permute-done((bf16[256,128]{1,0:T(8,128)(2,1)S(1)}, bf16[256,128]{1,0:T(8,128)(2,1)S(1)}, u32[]{:S(2)}, u32[]{:S(2)}) %collective-permute-start.9) | collective-permute-done | bytes 65568 | tf_op jit(solution)/shard_map/ppermute | solution.py:446
  45.2 1.9 %collective-permute-start.13 = (bf16[1040,128]{1,0:T(8,128)(2,1)S(1)}, bf16[1040,128]{1,0:T(8,128)(2,1)S(1)}, u32[]{:S(2)}, u32[]{:S(2)}) collective-permute-start(bf16[1040,128]{1,0:T(8,128)(2,1)S(1)} %get-tuple-element.36.refs_1_), channel_id=1, source_target_pairs={{0,192},{8,200},{16,208},{24,216},{32,224},{40,232},{48,240},{56,2... | collective-permute-start | bytes 798728 | tf_op jit(solution)/shard_map/ppermute | solution.py:465
  47.2 2.5 %collective-permute-start.16 = (bf16[1024,128]{1,0:T(8,128)(2,1)S(1)}, bf16[1024,128]{1,0:T(8,128)(2,1)S(1)}, u32[]{:S(2)}, u32[]{:S(2)}) collective-permute-start(bf16[1024,128]{1,0:T(8,128)(2,1)S(1)} %get-tuple-element.37.refs_3_.refs_4_.refs_5_), channel_id=1, source_target_pairs={{0,48},{8,56},{16,0},{24,8},{32,16},{40,24},{48,32},{56,40},{64,11... | collective-permute-start | bytes 786440 | tf_op jit(solution)/shard_map/ppermute | solution.py:466
  49.7 1.4 %shard_map.98 = (bf16[4,256,128]{2,1,0:T(8,128)(2,1)S(1)}, f32[128,128]{1,0:T(8,128)S(1)}, f32[128,128]{1,0:T(8,128)S(1)}) custom-call(bf16[144,4096]{1,0:T(8,128)(2,1)S(1)} %get-tuple-element.31.x_ref, bf16[4096,512]{1,0:T(8,128)(2,1)S(1)} %copy-done, bf16[16,128]{1,0:T(8,128)(2,1)S(1)} %get-tuple-element.30.refs_5_.code_ref.refs_10_, s32[1,256]{1,0:T(1,128)S(1)} %bitcast.3), custom_call_target="tpu_custom_call" | custom-call | flops 1073741824 | bytes 5242880 | tf_op jit(solution)/shard_map/pallas_call | solution.py:51
  52.1 2.8 %collective-permute-done.14.refs_4_.refs_5_.refs_6_ = bf16[1024,128]{1,0:T(8,128)(2,1)S(1)} collective-permute-done((bf16[1024,128]{1,0:T(8,128)(2,1)S(1)}, bf16[1024,128]{1,0:T(8,128)(2,1)S(1)}, u32[]{:S(2)}, u32[]{:S(2)}) %collective-permute-start.14) | collective-permute-done | bytes 262176 | tf_op jit(solution)/shard_map/ppermute | solution.py:466
  54.9 1.7 %shard_map.102 = (f32[4,256,128]{2,1,0:T(8,128)S(1)}, f32[4,256,128]{2,1,0:T(8,128)S(1)}, f32[4,256,128]{2,1,0:T(8,128)S(1)}) custom-call(bf16[4,256,128]{2,1,0:T(8,128)(2,1)S(1)} %get-tuple-element.32.q_ref.refs_0_, bf16[1040,128]{1,0:T(8,128)(2,1)S(1)} %get-tuple-element.36.refs_1_, bf16[1040,128]{1,0:T(8,128)(2,1)S(1)} %collective-permute-done.11.refs_2_, ...), custom_call_target="tpu_custom_call" | custom-call | flops 1073741824 | bytes 2097152 | tf_op jit(solution)/shard_map/pallas_call | solution.py:51
  56.6 2.8 %shard_map.103 = (f32[4,256,128]{2,1,0:T(8,128)S(1)}, f32[4,256,128]{2,1,0:T(8,128)S(1)}, f32[4,256,128]{2,1,0:T(8,128)S(1)}) custom-call(bf16[4,256,128]{2,1,0:T(8,128)(2,1)S(1)} %get-tuple-element.32.q_ref.refs_0_, bf16[1040,128]{1,0:T(8,128)(2,1)S(1)} %get-tuple-element.36.refs_1_, bf16[1040,128]{1,0:T(8,128)(2,1)S(1)} %collective-permute-done.11.refs_2_, ...), custom_call_target="tpu_custom_call" | custom-call | flops 2147483648 | bytes 4194304 | tf_op jit(solution)/shard_map/pallas_call | solution.py:51
  59.4 3.3 %collective-permute-done.15.refs_7_ = bf16[1024,128]{1,0:T(8,128)(2,1)S(1)} collective-permute-done((bf16[1024,128]{1,0:T(8,128)(2,1)S(1)}, bf16[1024,128]{1,0:T(8,128)(2,1)S(1)}, u32[]{:S(2)}, u32[]{:S(2)}) %collective-permute-start.15) | collective-permute-done | bytes 262176 | tf_op jit(solution)/shard_map/ppermute | solution.py:466
  62.8 3.6 %shard_map.104 = (bf16[128,512]{1,0:T(8,128)(2,1)}, bf16[128,512]{1,0:T(8,128)(2,1)}) custom-call(bf16[4,256,128]{2,1,0:T(8,128)(2,1)S(1)} %get-tuple-element.32.q_ref.refs_0_, bf16[1040,128]{1,0:T(8,128)(2,1)S(1)} %get-tuple-element.36.refs_1_, bf16[1040,128]{1,0:T(8,128)(2,1)S(1)} %collective-permute-done.11.refs_2_, ...), custom_call_target="tpu_custom_call" | custom-call | flops 2147483648 | bytes 4194304 | tf_op jit(solution)/shard_map/pallas_call | solution.py:51
  (25 shorter events, 3.0 us)
Async XLA Ops:
  0.6 49.1 %copy-start.1 = (s32[256]{0:T(256)S(1)}, s32[256]{0:T(256)}, u32[]{:S(2)}) copy-start(s32[256]{0:T(256)} %param.11) | copy-start | bytes 3076
  0.6 49.1 %copy-start = (bf16[4096,512]{1,0:T(8,128)(2,1)S(1)}, bf16[4096,512]{1,0:T(8,128)(2,1)}, u32[]{:S(2)}) copy-start(bf16[4096,512]{1,0:T(8,128)(2,1)} %wq_ref.1) | copy-start | bytes 12582916
  0.7 14.5 %collective-permute-start = (bf16[128,512]{1,0:T(8,128)(2,1)}, bf16[128,512]{1,0:T(8,128)(2,1)S(1)}, u32[]{:S(2)}, u32[]{:S(2)}) collective-permute-start(bf16[128,512]{1,0:T(8,128)(2,1)} %refs_0_.1), channel_id=1, source_target_pairs={{0,2},{1,3},{2,4},{3,5},{4,6},{5,7},{6,0},{7,1},{8,10},{9,11},{10,... | collective-permute-start | bytes 393224 | tf_op jit(solution)/shard_map/ppermute | solution.py:406
  4.0 14.5 %collective-permute-start.1 = (bf16[128,512]{1,0:T(8,128)(2,1)}, bf16[128,512]{1,0:T(8,128)(2,1)S(1)}, u32[]{:S(2)}, u32[]{:S(2)}) collective-permute-start(bf16[128,512]{1,0:T(8,128)(2,1)} %refs_0_.1), channel_id=1, source_target_pairs={{0,4},{1,5},{2,6},{3,7},{4,0},{5,1},{6,2},{7,3},{8,12},{9,13},{10,... | collective-permute-start | bytes 393224 | tf_op jit(solution)/shard_map/ppermute | solution.py:406
  9.4 12.4 %collective-permute-start.2 = (bf16[128,512]{1,0:T(8,128)(2,1)}, bf16[128,512]{1,0:T(8,128)(2,1)S(1)}, u32[]{:S(2)}, u32[]{:S(2)}) collective-permute-start(bf16[128,512]{1,0:T(8,128)(2,1)} %refs_0_.1), channel_id=1, source_target_pairs={{0,6},{1,7},{2,0},{3,1},{4,2},{5,3},{6,4},{7,5},{8,14},{9,15},{10,... | collective-permute-start | bytes 393224 | tf_op jit(solution)/shard_map/ppermute | solution.py:406
  21.8 2.0 %collective-permute-start.3 = (bf16[512,512]{1,0:T(8,128)(2,1)S(1)}, bf16[512,512]{1,0:T(8,128)(2,1)S(1)}, u32[]{:S(2)}, u32[]{:S(2)}) collective-permute-start(bf16[512,512]{1,0:T(8,128)(2,1)S(1)} %shard_map.96.refs_0_), channel_id=1, source_target_pairs={{0,1},{1,0},{2,3},{3,2},{4,5},{5,4},{6,7},{7,6},{8,9},{9,8},{10,11... | collective-permute-start | bytes 1572872 | tf_op jit(solution)/shard_map/ppermute | solution.py:427
  24.7 4.4 %collective-permute-start.4 = (bf16[144,256]{1,0:T(8,128)(2,1)S(1)}, bf16[144,256]{1,0:T(8,128)(2,1)S(1)}, u32[]{:S(2)}, u32[]{:S(2)}) collective-permute-start(bf16[144,256]{1,0:T(8,128)(2,1)S(1)} %get-tuple-element.33.own_ref.kv_ref), channel_id=1, source_target_pairs={{0,8},{8,0},{16,24},{24,16},{32,40},{40,32},{48,56},{56,48},{64,72... | collective-permute-start | bytes 221192 | tf_op jit(solution)/shard_map/ppermute | solution.py:438
  29.2 9.0 %collective-permute-start.10 = (bf16[256,128]{1,0:T(8,128)(2,1)S(1)}, bf16[256,128]{1,0:T(8,128)(2,1)S(1)}, u32[]{:S(2)}, u32[]{:S(2)}) collective-permute-start(bf16[256,128]{1,0:T(8,128)(2,1)S(1)} %get-tuple-element.35.refs_4_), channel_id=1, source_target_pairs={{0,192},{8,200},{16,208},{24,216},{32,224},{40,232},{48,240},{56,2... | collective-permute-start | bytes 196616 | tf_op jit(solution)/shard_map/ppermute | solution.py:446
  30.0 14.3 %collective-permute-start.5 = (bf16[272,128]{1,0:T(8,128)(2,1)S(1)}, bf16[272,128]{1,0:T(8,128)(2,1)S(1)}, u32[]{:S(2)}, u32[]{:S(2)}) collective-permute-start(bf16[272,128]{1,0:T(8,128)(2,1)S(1)} %get-tuple-element.34.refs_0_), channel_id=1, source_target_pairs={{0,16},{8,24},{16,32},{24,40},{32,48},{40,56},{48,0},{56,8},{64,80... | collective-permute-start | bytes 208904 | tf_op jit(solution)/shard_map/ppermute | solution.py:445
  31.5 12.8 %collective-permute-start.6 = (bf16[272,128]{1,0:T(8,128)(2,1)S(1)}, bf16[272,128]{1,0:T(8,128)(2,1)S(1)}, u32[]{:S(2)}, u32[]{:S(2)}) collective-permute-start(bf16[272,128]{1,0:T(8,128)(2,1)S(1)} %get-tuple-element.34.refs_0_), channel_id=1, source_target_pairs={{0,32},{8,40},{16,48},{24,56},{32,0},{40,8},{48,16},{56,24},{64,96... | collective-permute-start | bytes 208904 | tf_op jit(solution)/shard_map/ppermute | solution.py:445
  34.2 10.1 %collective-permute-start.7 = (bf16[272,128]{1,0:T(8,128)(2,1)S(1)}, bf16[272,128]{1,0:T(8,128)(2,1)S(1)}, u32[]{:S(2)}, u32[]{:S(2)}) collective-permute-start(bf16[272,128]{1,0:T(8,128)(2,1)S(1)} %get-tuple-element.34.refs_0_), channel_id=1, source_target_pairs={{0,48},{8,56},{16,0},{24,8},{32,16},{40,24},{48,32},{56,40},{64,11... | collective-permute-start | bytes 208904 | tf_op jit(solution)/shard_map/ppermute | solution.py:445
  35.6 5.0 %collective-permute-start.8 = (bf16[256,128]{1,0:T(8,128)(2,1)S(1)}, bf16[256,128]{1,0:T(8,128)(2,1)S(1)}, u32[]{:S(2)}, u32[]{:S(2)}) collective-permute-start(bf16[256,128]{1,0:T(8,128)(2,1)S(1)} %get-tuple-element.35.refs_4_), channel_id=1, source_target_pairs={{0,64},{8,72},{16,80},{24,88},{32,96},{40,104},{48,112},{56,120},{... | collective-permute-start | bytes 196616 | tf_op jit(solution)/shard_map/ppermute | solution.py:446
  38.1 6.2 %collective-permute-start.9 = (bf16[256,128]{1,0:T(8,128)(2,1)S(1)}, bf16[256,128]{1,0:T(8,128)(2,1)S(1)}, u32[]{:S(2)}, u32[]{:S(2)}) collective-permute-start(bf16[256,128]{1,0:T(8,128)(2,1)S(1)} %get-tuple-element.35.refs_4_), channel_id=1, source_target_pairs={{0,128},{8,136},{16,144},{24,152},{32,160},{40,168},{48,176},{56,1... | collective-permute-start | bytes 196616 | tf_op jit(solution)/shard_map/ppermute | solution.py:446
  44.4 10.6 %collective-permute-start.11 = (bf16[1040,128]{1,0:T(8,128)(2,1)S(1)}, bf16[1040,128]{1,0:T(8,128)(2,1)S(1)}, u32[]{:S(2)}, u32[]{:S(2)}) collective-permute-start(bf16[1040,128]{1,0:T(8,128)(2,1)S(1)} %get-tuple-element.36.refs_1_), channel_id=1, source_target_pairs={{0,64},{8,72},{16,80},{24,88},{32,96},{40,104},{48,112},{56,120},{... | collective-permute-start | bytes 798728 | tf_op jit(solution)/shard_map/ppermute | solution.py:465
  44.5 10.5 %collective-permute-start.14 = (bf16[1024,128]{1,0:T(8,128)(2,1)S(1)}, bf16[1024,128]{1,0:T(8,128)(2,1)S(1)}, u32[]{:S(2)}, u32[]{:S(2)}) collective-permute-start(bf16[1024,128]{1,0:T(8,128)(2,1)S(1)} %get-tuple-element.37.refs_3_.refs_4_.refs_5_), channel_id=1, source_target_pairs={{0,16},{8,24},{16,32},{24,40},{32,48},{40,56},{48,0},{56,8},{64,80... | collective-permute-start | bytes 786440 | tf_op jit(solution)/shard_map/ppermute | solution.py:466
  45.2 11.4 %collective-permute-start.13 = (bf16[1040,128]{1,0:T(8,128)(2,1)S(1)}, bf16[1040,128]{1,0:T(8,128)(2,1)S(1)}, u32[]{:S(2)}, u32[]{:S(2)}) collective-permute-start(bf16[1040,128]{1,0:T(8,128)(2,1)S(1)} %get-tuple-element.36.refs_1_), channel_id=1, source_target_pairs={{0,192},{8,200},{16,208},{24,216},{32,224},{40,232},{48,240},{56,2... | collective-permute-start | bytes 798728 | tf_op jit(solution)/shard_map/ppermute | solution.py:465
  47.2 9.4 %collective-permute-start.16 = (bf16[1024,128]{1,0:T(8,128)(2,1)S(1)}, bf16[1024,128]{1,0:T(8,128)(2,1)S(1)}, u32[]{:S(2)}, u32[]{:S(2)}) collective-permute-start(bf16[1024,128]{1,0:T(8,128)(2,1)S(1)} %get-tuple-element.37.refs_3_.refs_4_.refs_5_), channel_id=1, source_target_pairs={{0,48},{8,56},{16,0},{24,8},{32,16},{40,24},{48,32},{56,40},{64,11... | collective-permute-start | bytes 786440 | tf_op jit(solution)/shard_map/ppermute | solution.py:466
  52.0 10.8 %collective-permute-start.12 = (bf16[1040,128]{1,0:T(8,128)(2,1)S(1)}, bf16[1040,128]{1,0:T(8,128)(2,1)S(1)}, u32[]{:S(2)}, u32[]{:S(2)}) collective-permute-start(bf16[1040,128]{1,0:T(8,128)(2,1)S(1)} %get-tuple-element.36.refs_1_), channel_id=1, source_target_pairs={{0,128},{8,136},{16,144},{24,152},{32,160},{40,168},{48,176},{56,1... | collective-permute-start | bytes 798728 | tf_op jit(solution)/shard_map/ppermute | solution.py:465
  54.9 7.9 %collective-permute-start.15 = (bf16[1024,128]{1,0:T(8,128)(2,1)S(1)}, bf16[1024,128]{1,0:T(8,128)(2,1)S(1)}, u32[]{:S(2)}, u32[]{:S(2)}) collective-permute-start(bf16[1024,128]{1,0:T(8,128)(2,1)S(1)} %get-tuple-element.37.refs_3_.refs_4_.refs_5_), channel_id=1, source_target_pairs={{0,32},{8,40},{16,48},{24,56},{32,0},{40,8},{48,16},{56,24},{64,96... | collective-permute-start | bytes 786440 | tf_op jit(solution)/shard_map/ppermute | solution.py:466

commit v10 on v9

--- a/solution.py
+++ b/solution.py
@@ -38,6 +38,19 @@
     return pairs
 
 
+def cross_pairs(first, d):
+    pairs = []
+    for i in range(256):
+        c, g = i // 8, i % 8
+        y, x, z = c // 8, (c // 2) % 4, c % 2
+        if (g % 2 == 0) == first:
+            x = (x + d) % 4
+        else:
+            y = (y + d) % 4
+        pairs.append((i, ((y * 4 + x) * 2 + z) * 8 + g))
+    return pairs
+
+
 def dot(a, b):
     return jnp.dot(a, b, preferred_element_type=F32)
 
@@ -107,8 +120,8 @@
 
 
 def kv_kernel(*refs):
-    mine, other, pad_ref, wk_ref, wv_ref, code_ref = refs[:6]
-    x_ref, kv_ref, mkv_ref = refs[6:]
+    mine, other, pad_ref, wk_ref, wv_ref = refs[:5]
+    x_ref, kv_ref, mkv_ref, keep_ref, give_ref = refs[5:]
     me = lax.axis_index("kv")
     for dc, ref in enumerate((mine, other)):
         for dz in range(4):
@@ -117,40 +130,77 @@
             x_ref[:ROWS, lanes] = ref[dz * ROWS : (dz + 1) * ROWS, :]
     x_ref[ROWS:, :] = pad_ref[...]
     x = x_ref[...]
-    for part, w_ref in enumerate((wk_ref, wv_ref)):
+    products = [dot(x, w_ref[...]).astype(BF16) for w_ref in (wk_ref, wv_ref)]
+    for part, product in enumerate(products):
         lanes = slice(part * HEAD, (part + 1) * HEAD)
-        product = dot(x, w_ref[...]).astype(BF16)
-        kv_ref[:ROWS, lanes] = product[:ROWS]
-        kv_ref[ROWS:, lanes] = code_ref[...]
+        kv_ref[:, lanes] = product[:ROWS]
         mkv_ref[:, lanes] = product[ROWS:]
-
-
-def pair_kernel(own_ref, other_ref, k_ref, v_ref):
-    for i, ref in enumerate((own_ref, other_ref)):
-        rows = slice(i * ROWS, (i + 1) * ROWS)
-        k_ref[rows, :] = ref[:ROWS, :HEAD]
-        v_ref[rows, :] = ref[:ROWS, HEAD:]
-    row = lax.broadcasted_iota(jnp.int32, (PAD, HEAD), 0)
-    first = ref_tail(own_ref, ROWS)
-    code = jnp.where(lax.rem(row, 4) < 2, first, ref_tail(other_ref, ROWS))
-    k_ref[2 * ROWS :, :] = code.astype(BF16)
+    even = lax.rem(me, 2) == 0
+
+    @pl.when(even)
+    def _():
+        keep_ref[...] = products[0][:ROWS]
+        give_ref[...] = products[1][:ROWS]
+
+    @pl.when(jnp.logical_not(even))
+    def _():
+        keep_ref[...] = products[1][:ROWS]
+        give_ref[...] = products[0][:ROWS]
+
+
+def merge_kernel(keep_ref, got_ref, code_ref, out_ref):
+    for ref, lanes in ((keep_ref, slice(0, HEAD)), (got_ref, slice(HEAD, 2 * HEAD))):
+        out_ref[:ROWS, lanes] = ref[...]
+        out_ref[ROWS:, lanes] = code_ref[...]
+
+
+def pair_kernel(own_ref, other_ref, out_ref):
+    out_ref[:ROWS, :] = own_ref[:ROWS, :]
+    out_ref[ROWS : 2 * ROWS, :] = other_ref[:ROWS, :]
+    row = lax.broadcasted_iota(jnp.int32, (PAD, 2 * HEAD), 0)
+    code = jnp.where(lax.rem(row, 4) < 2, own_ref[ROWS:, :].astype(F32), other_ref[ROWS:, :].astype(F32))
+    out_ref[2 * ROWS :, :] = code.astype(BF16)
+
+
+def stack_kernel(a_ref, b_ref, c_ref, d_ref, out_ref, over_ref):
+    row = lax.broadcasted_iota(jnp.int32, (PAD, 2 * HEAD), 0)
+    code = jnp.zeros((PAD, 2 * HEAD), F32)
+    for i, ref in enumerate((a_ref, b_ref, c_ref, d_ref)):
+        rows = slice(i * 2 * ROWS, (i + 1) * 2 * ROWS)
+        out_ref[rows, :] = ref[: 2 * ROWS, :]
+        over_ref[rows, :] = ref[: 2 * ROWS, HEAD:]
+        code = jnp.where(row // 4 == i, ref[2 * ROWS :, :].astype(F32), code)
+    out_ref[8 * ROWS :, :] = code.astype(BF16)
+    over_ref[8 * ROWS :, :] = code[:, :HEAD].astype(BF16)
 
 
 def ref_tail(ref, start):
     return ref[start:, :HEAD].astype(F32)
 
 
-def stack_kernel(*refs):
-    ks, vs = refs[:4], refs[4:8]
-    k_ref, v_ref = refs[8:]
-    row = lax.broadcasted_iota(jnp.int32, (PAD, HEAD), 0)
-    code = jnp.zeros((PAD, HEAD), F32)
-    for i in range(4):
-        rows = slice(i * 2 * ROWS, (i + 1) * 2 * ROWS)
-        k_ref[rows, :] = ks[i][: 2 * ROWS, :]
-        v_ref[rows, :] = vs[i][...]
-        code = jnp.where(row // 4 == i, ref_tail(ks[i], 2 * ROWS), code)
-    k_ref[8 * ROWS :, :] = code.astype(BF16)
+def over_kernel(source_ref, out_ref):
+    out_ref[...] = source_ref[:, HEAD:]
+
+
+def sort_out(direct, swapped, keys, values):
+    even = lax.rem(lax.axis_index("kv"), 2) == 0
+
+    @pl.when(even)
+    def _():
+        for a, b, k, v in zip(direct, swapped, keys, values):
+            k[...] = a[:, :HEAD]
+            v[...] = b[: v.shape[0], :]
+
+    @pl.when(jnp.logical_not(even))
+    def _():
+        for a, b, k, v in zip(direct, swapped, keys, values):
+            v[...] = a[:, :HEAD]
+            k[...] = b[: k.shape[0], :]
+
+
+def mask_rows(mkv_ref):
+    rows = mkv_ref[0:1, :].astype(F32)
+    return rows[:, :HEAD], rows[:, HEAD:]
 
 
 def q_kernel(x_ref, wq_ref, code_ref, cut_ref, q_ref, flag_ref, own_cut_ref):
@@ -176,9 +226,8 @@
 def near_kernel(q_ref, kv_ref, mkv_ref, flag_ref, code_ref, top_ref, total_ref, accum_ref):
     masked = flag_ref[...] > 0.5
 
-    def both(lanes):
-        clean = kv_ref[:ROWS, lanes]
-        fixed = jnp.broadcast_to(mkv_ref[0:1, lanes].astype(F32), (ROWS, HEAD))
+    def both(clean, fixed):
+        fixed = jnp.broadcast_to(fixed, (ROWS, HEAD))
         return jnp.concatenate([clean, jnp.where(masked, fixed, clean.astype(F32)).astype(BF16)], axis=0)
 
     row = code_ref[...].astype(F32)[0:1]
@@ -189,8 +238,9 @@
     clean_bias = jnp.concatenate([jnp.where(key <= query, zero, low), low], axis=1)
     noisy_bias = jnp.concatenate([jnp.where(key < query, zero, low), jnp.where(key == query, zero, low)], axis=1)
     bias = jnp.concatenate([clean_bias, noisy_bias], axis=0)
-    keys = both(slice(0, HEAD))
-    values = both(slice(HEAD, 2 * HEAD))
+    k_fixed, v_fixed = mask_rows(mkv_ref)
+    keys = both(kv_ref[:, :HEAD], k_fixed)
+    values = both(kv_ref[:, HEAD:], v_fixed)
     for h in range(GROUP):
         scores = jnp.where(bias < -1.0, LOW, dot_t(q_ref[h], keys))
         top = jnp.max(scores, axis=1, keepdims=True)
@@ -279,19 +329,24 @@
 
 
 def first_kernel(*refs):
-    q_ref = refs[0]
-    k_of, v_of = dict(zip((0, 1), refs[1:3])), dict(zip((0, 1), refs[3:5]))
+    q_ref, direct, swapped = refs[0], refs[1:3], refs[3:5]
+    keys, values = refs[11:13], refs[13:15]
+    sort_out(direct, swapped, keys, values)
+    k_of, v_of = dict(zip((0, 1), keys)), dict(zip((0, 1), values))
     piece = spots_piece(place(), k_of, v_of, ((0, 0), (0, 1), (1, 0), (1, 1)))
     pipeline(q_ref, [piece], refs[5:8], refs[8:11], None)
 
 
 def far_kernel(*refs):
-    q_ref = refs[0]
-    k_refs = dict(zip((0, 1, 3), refs[1:4]))
-    v_refs = dict(zip((0, 1, 3), refs[4:7]))
+    q_ref, direct, swapped = refs[0], refs[1:4], refs[4:7]
     state_in = refs[7:10]
     code_ref, own_cut_ref, mkv_ref = refs[10:13]
     state = refs[13:16]
+    keys, values = refs[16:19], refs[19:22]
+    sort_out(direct, swapped, keys, values)
+    k_refs = dict(zip((0, 1, 3), keys))
+    v_refs = dict(zip((0, 1, 3), values))
+    k_fixed, v_fixed = mask_rows(mkv_ref)
     me, y, x, z = place()
 
     wrap = (z == 0) & (x == 0)
@@ -323,17 +378,17 @@
     old_masked = column(jnp.where(old_order >= first_cut, 1.0, 0.0))[ROWS - BLOCK :]
     new_masked = column(jnp.where(new_order >= last_cut, 1.0, 0.0))[:BLOCK]
 
-    def noisy(masked, clean, lanes):
-        fixed = jnp.broadcast_to(mkv_ref[0:1, lanes].astype(F32), clean.shape)
+    def noisy(masked, clean, fixed):
+        fixed = jnp.broadcast_to(fixed, clean.shape)
         flag = jnp.broadcast_to(masked, clean.shape) > 0.5
         return jnp.where(flag, fixed, clean.astype(F32)).astype(BF16)
 
-    def rim(old, new, lanes):
-        parts = [old, new, noisy(old_masked, old[ROWS - BLOCK :], lanes), noisy(new_masked, new, lanes)]
+    def rim(old, new, fixed):
+        parts = [old, new, noisy(old_masked, old[ROWS - BLOCK :], fixed), noisy(new_masked, new, fixed)]
         return jnp.concatenate(parts + [jnp.zeros((BLOCK, HEAD), BF16)], axis=0)
 
-    k_rim = rim(k_old, k_new, slice(0, HEAD))
-    v_rim = rim(v_old, v_new, slice(HEAD, 2 * HEAD))
+    k_rim = rim(k_old, k_new, k_fixed)
+    v_rim = rim(v_old, v_new, v_fixed)
     lane = lax.broadcasted_iota(jnp.int32, (8, ROWS), 1)
     mixed = jnp.where(
         lane < 32,
@@ -369,10 +424,12 @@
 
 
 def last_kernel(*refs):
-    q_ref, k_refs, v_refs = refs[0], refs[1:5], refs[5:9]
+    q_ref, direct, swapped = refs[0], refs[1:5], refs[5:9]
     state_in = refs[9:12]
     clean_ref, noisy_ref = refs[12:14]
-    state = refs[14:]
+    state = refs[14:17]
+    k_refs, v_refs = refs[17:21], refs[21:25]
+    sort_out(direct, swapped, k_refs, v_refs)
     where = place()
     near = (0, 1, 3)
     pieces = [
@@ -425,65 +482,74 @@
     )
     mine = join(own, *moved)
     other = lax.ppermute(mine, "kv", kv_pairs(0, 1))
-    x, kv, mask_kv = call(
+    x, kv, mask_kv, keep, give = call(
         kv_kernel,
         [
             ((ROWS + PAD, 8 * WIDTH), BF16),
-            ((ROWS + PAD, 2 * HEAD), BF16),
+            ((ROWS, 2 * HEAD), BF16),
             ((PAD, 2 * HEAD), BF16),
+            ((ROWS, HEAD), BF16),
+            ((ROWS, HEAD), BF16),
         ],
-        [mine, other, pad, wk, wv, code],
+        [mine, other, pad, wk, wv],
         (1 << 29, 3 << 20),
     )
-    pair = lax.ppermute(kv, "ctx", ctx_pairs(0, 0, 1))
-    k, v = call(
-        pair_kernel,
-        [((2 * ROWS + PAD, HEAD), BF16), ((2 * ROWS, HEAD), BF16)],
-        [kv, pair],
-        (1 << 10, 1 << 18),
-    )
-    ks = [lax.ppermute(k, "ctx", ctx_pairs(0, d, 0)) for d in (1, 2, 3)]
-    vs = [lax.ppermute(v, "ctx", ctx_pairs(d, 0, 0)) for d in (1, 2, 3)]
-    ks, vs = call(
+    got = lax.ppermute(give, "kv", kv_pairs(0, 1))
+    (lot,) = call(merge_kernel, [((ROWS + PAD, 2 * HEAD), BF16)], [keep, got, code], (1 << 10, 1 << 18))
+    pair = lax.ppermute(lot, "ctx", ctx_pairs(0, 0, 1))
+    (both,) = call(pair_kernel, [((2 * ROWS + PAD, 2 * HEAD), BF16)], [lot, pair], (1 << 10, 1 << 18))
+    axes = ("ctx", "kv")
+    parts = [both] + [lax.ppermute(both, axes, cross_pairs(True, d)) for d in (1, 2, 3)]
+    tall = 8 * ROWS + PAD
+    held_here, over = call(
         stack_kernel,
-        [((8 * ROWS + PAD, HEAD), BF16), ((8 * ROWS, HEAD), BF16)],
-        [k, *ks, v, *vs],
+        [((tall, 2 * HEAD), BF16), ((tall, HEAD), BF16)],
+        parts,
         (1 << 10, 1 << 20),
     )
+    direct = [held_here] + [lax.ppermute(held_here, axes, cross_pairs(False, d)) for d in (1, 2, 3)]
+    swapped = [lax.ppermute(over, "kv", kv_pairs(0, 1)), None, None, None]
     q, flag, own_cut = call(
         q_kernel,
         [((GROUP, 2 * ROWS, HEAD), BF16), ((ROWS, HEAD), F32), ((ROWS, HEAD), F32)],
         [x, q_weight, code, cuts],
         (1 << 30, 5 << 20),
     )
+    state = [((GROUP, 2 * ROWS, HEAD), F32)] * 3
+
+    def room(count):
+        return [pltpu.VMEM((tall, HEAD), BF16)] * (2 * count)
+
     near = call(
         near_kernel,
-        [((GROUP, 2 * ROWS, HEAD), F32)] * 3,
+        state,
         [q, kv, mask_kv, flag, code],
         (1 << 30, 2 << 20),
     )
-    all_k = [ks] + [lax.ppermute(ks, "ctx", ctx_pairs(d, 0, 0)) for d in (1, 2, 3)]
-    all_v = [vs] + [lax.ppermute(vs, "ctx", ctx_pairs(0, d, 0)) for d in (1, 2, 3)]
-    state = [((GROUP, 2 * ROWS, HEAD), F32)] * 3
-    first = call(
-        first_kernel,
-        state,
-        [q, *all_k[:2], *all_v[:2], *near],
-        (1 << 30, 2 << 20),
-    )
+    def cross(i, before):
+        direct[i], _ = lax.optimization_barrier((direct[i], before[0]))
+        (over,) = call(over_kernel, [((tall, HEAD), BF16)], [direct[i]], (1 << 10, 1 << 19))
+        swapped[i] = lax.ppermute(over, "kv", kv_pairs(0, 1))
+
+    cross(1, near)
+    cross(3, near)
+    first = call(first_kernel, state, [q, *direct[:2], *swapped[:2], *near], (1 << 30, 2 << 20), room(2))
+    cross(2, first)
+    some = (0, 1, 3)
     far = call(
         far_kernel,
         state,
-        [q, *[all_k[d] for d in (0, 1, 3)], *[all_v[d] for d in (0, 1, 3)], *first, code, own_cut, mask_kv],
+        [q, *[direct[d] for d in some], *[swapped[d] for d in some], *first, code, own_cut, mask_kv],
         (1 << 31, 4 << 20),
+        room(3),
     )
     return tuple(
         call(
             last_kernel,
             [((ROWS, GROUP * HEAD), BF16)] * 2,
-            [q, *all_k, *all_v, *far],
+            [q, *direct, *swapped, *far],
             (1 << 31, 4 << 20),
-            [pltpu.VMEM((GROUP, 2 * ROWS, HEAD), F32)] * 3,
+            [pltpu.VMEM((GROUP, 2 * ROWS, HEAD), F32)] * 3 + room(4),
         )
     )
 

time: 67.7 us -> 66.1 us (0.976); the launches traced: 66.4 us -> 65.5 us
  starting transfers between devices: 26 us -> 21.9 us
  waiting for transfers between devices: 25.3 us -> 28.1 us
    ppermute x13 -> x12, starting transfers between devices: 14.5 us -> 10.4 us  [the longest x3 5.73 us: shards(): lax.ppermute(both, axes, cross_pairs(True, d))]
    ppermute x13 -> x12, waiting for transfers between devices: 16.7 us -> 19.5 us  [the longest x3 10.5 us: shards(): lax.ppermute(held_here, axes, cross_pairs(False, d))]
    pallas_call x10 -> x14, Pallas kernels: 13 us -> 13.4 us  [call(): pl.pallas_call(kernel, out_shape=[jax.ShapeDtypeStruct(s, t) for s, t in...]
  transfers between devices with their start and end apart: 17 -> 16, of which waited for: 8 -> 10; matrix products, arithmetic and copies ran while one was open for 2% -> 2% of each run, Pallas kernels for 13% -> 13%
where the time goes in v10:
time: 66.1 us; the launch traced here: 65.5 us
  waiting for transfers between devices  28.1 us (43%)
  starting transfers between devices  21.9 us (33%)
  Pallas kernels  13.4 us (20%)
  local copies, waits for them, and re-layouts  1.32 us (2%)
  between operations  0.8 us (1%)
    pallas_call x14, Pallas kernels, call(): pl.pallas_call(kernel, out_shape=[jax.ShapeDtypeStruct(s, t) for s, t in...  13.4 us
    ppermute x3, starting transfers between devices, shards(): moved = [lax.ppermute(hidden, 'kv', kv_pairs(d, 0)) for d in (1, 2, 3)]  11.4 us
    ppermute x3, waiting for transfers between devices, shards(): lax.ppermute(held_here, axes, cross_pairs(False, d))  10.5 us
    ppermute x3, waiting for transfers between devices, shards(): moved = [lax.ppermute(hidden, 'kv', kv_pairs(d, 0)) for d in (1, 2, 3)]  6.68 us
    ppermute x3, starting transfers between devices, shards(): lax.ppermute(both, axes, cross_pairs(True, d))  5.73 us
    ppermute x1, waiting for transfers between devices, shards(): pair = lax.ppermute(lot, 'ctx', ctx_pairs(0, 0, 1))  4.34 us
    ppermute x3, waiting for transfers between devices, shards(): lax.ppermute(both, axes, cross_pairs(True, d))  3.62 us
    ppermute x3, starting transfers between devices, shards(): lax.ppermute(held_here, axes, cross_pairs(False, d))  3.34 us
  transfers between devices with their start and end apart: 16, of which 10 were waited for; matrix products, arithmetic and copies ran while one was open for 2% of the time, Pallas kernels for 13%

profile of v10, /device:TPU:24, one launch (start us, length us, event | category | flops | bytes accessed | tf_op | source)
XLA Modules:
  0.0 65.5 jit_solution(14487773618926190343)
XLA Ops:
  0.7 3.3 %collective-permute-start = (bf16[128,512]{1,0:T(8,128)(2,1)}, bf16[128,512]{1,0:T(8,128)(2,1)S(1)}, u32[]{:S(2)}, u32[]{:S(2)}) collective-permute-start(bf16[128,512]{1,0:T(8,128)(2,1)} %refs_0_.1), channel_id=1, source_target_pairs={{0,2},{1,3},{2,4},{3,5},{4,6},{5,7},{6,0},{7,1},{8,10},{9,11},{10,... | collective-permute-start | bytes 393224 | tf_op jit(solution)/shard_map/ppermute | solution.py:463
  4.0 5.4 %collective-permute-start.1 = (bf16[128,512]{1,0:T(8,128)(2,1)}, bf16[128,512]{1,0:T(8,128)(2,1)S(1)}, u32[]{:S(2)}, u32[]{:S(2)}) collective-permute-start(bf16[128,512]{1,0:T(8,128)(2,1)} %refs_0_.1), channel_id=1, source_target_pairs={{0,4},{1,5},{2,6},{3,7},{4,0},{5,1},{6,2},{7,3},{8,12},{9,13},{10,... | collective-permute-start | bytes 393224 | tf_op jit(solution)/shard_map/ppermute | solution.py:463
  9.4 2.7 %collective-permute-start.2 = (bf16[128,512]{1,0:T(8,128)(2,1)}, bf16[128,512]{1,0:T(8,128)(2,1)S(1)}, u32[]{:S(2)}, u32[]{:S(2)}) collective-permute-start(bf16[128,512]{1,0:T(8,128)(2,1)} %refs_0_.1), channel_id=1, source_target_pairs={{0,6},{1,7},{2,0},{3,1},{4,2},{5,3},{6,4},{7,5},{8,14},{9,15},{10,... | collective-permute-start | bytes 393224 | tf_op jit(solution)/shard_map/ppermute | solution.py:463
  12.1 1.3 %reshape.18.refs_5_ = bf16[1,4096]{1,0:T(2,128)(2,1)} reshape(bf16[4096]{0:T(1024)(128)(2,1)} %param.12) | data formatting | bytes 16384 | tf_op jit(solution)/shard_map/reshape | solution.py:473
  13.4 1.7 %shard_map.95 = (bf16[128,512]{1,0:T(8,128)(2,1)S(1)}, bf16[4096,128]{1,0:T(8,128)(2,1)S(1)}, bf16[4096,128]{1,0:T(8,128)(2,1)S(1)}, bf16[16,128]{1,0:T(8,128)(2,1)S(1)}, bf16[16,4096]{1,0:T(8,128)(2,1)S(1)}) custom-call(bf16[128,512]{1,0:T(8,128)(2,1)} %refs_0_.1, bf16[4096,128]{1,0:T(8,128)(2,1)} %refs_1_.1, bf16[4096,128]{1,0:T(8,128)(2,1)} %refs_2_.1, ...), custom_call_target="tpu_custom_call" | custom-call | flops 1048576 | bytes 4194304 | tf_op jit(solution)/shard_map/pallas_call | solution.py:64
  15.1 3.4 %collective-permute-done.1.refs_2_ = bf16[128,512]{1,0:T(8,128)(2,1)S(1)} collective-permute-done((bf16[128,512]{1,0:T(8,128)(2,1)}, bf16[128,512]{1,0:T(8,128)(2,1)S(1)}, u32[]{:S(2)}, u32[]{:S(2)}) %collective-permute-start.1) | collective-permute-done | bytes 131104 | tf_op jit(solution)/shard_map/ppermute | solution.py:463
  18.5 3.3 %collective-permute-done.2.refs_3_ = bf16[128,512]{1,0:T(8,128)(2,1)S(1)} collective-permute-done((bf16[128,512]{1,0:T(8,128)(2,1)}, bf16[128,512]{1,0:T(8,128)(2,1)S(1)}, u32[]{:S(2)}, u32[]{:S(2)}) %collective-permute-start.2) | collective-permute-done | bytes 131104 | tf_op jit(solution)/shard_map/ppermute | solution.py:463
  21.9 1.9 %collective-permute-done.3.refs_1_ = bf16[512,512]{1,0:T(8,128)(2,1)S(1)} collective-permute-done((bf16[512,512]{1,0:T(8,128)(2,1)S(1)}, bf16[512,512]{1,0:T(8,128)(2,1)S(1)}, u32[]{:S(2)}, u32[]{:S(2)}) %collective-permute-start.3) | collective-permute-done | bytes 524320 | tf_op jit(solution)/shard_map/ppermute | solution.py:484
  23.8 0.9 %shard_map.97 = (bf16[144,4096]{1,0:T(8,128)(2,1)S(1)}, bf16[128,256]{1,0:T(8,128)(2,1)S(1)}, bf16[16,256]{1,0:T(8,128)(2,1)S(1)}, bf16[128,128]{1,0:T(8,128)(2,1)S(1)}, bf16[128,128]{1,0:T(8,128)(2,1)S(1)}) custom-call(bf16[512,512]{1,0:T(8,128)(2,1)S(1)} %shard_map.96.refs_0_, bf16[512,512]{1,0:T(8,128)(2,1)S(1)} %collective-permute-done.3.refs_1_, ...), custom_call_target="tpu_custom_call" | custom-call | flops 536870912 | bytes 3145728 | tf_op jit(solution)/shard_map/pallas_call | solution.py:64
  24.9 1.1 %collective-permute-done.4.got_ref = bf16[128,128]{1,0:T(8,128)(2,1)S(1)} collective-permute-done((bf16[128,128]{1,0:T(8,128)(2,1)S(1)}, bf16[128,128]{1,0:T(8,128)(2,1)S(1)}, u32[]{:S(2)}, u32[]{:S(2)}) %collective-permute-start.4) | collective-permute-done | bytes 32800 | tf_op jit(solution)/shard_map/ppermute | solution.py:497
  26.1 4.3 %collective-permute-done.5.other_ref = bf16[144,256]{1,0:T(8,128)(2,1)S(1)} collective-permute-done((bf16[144,256]{1,0:T(8,128)(2,1)S(1)}, bf16[144,256]{1,0:T(8,128)(2,1)S(1)}, u32[]{:S(2)}, u32[]{:S(2)}) %collective-permute-start.5) | collective-permute-done | bytes 73760 | tf_op jit(solution)/shard_map/ppermute | solution.py:499
  30.5 1.6 %collective-permute-start.6 = (bf16[272,256]{1,0:T(8,128)(2,1)S(1)}, bf16[272,256]{1,0:T(8,128)(2,1)S(1)}, u32[]{:S(2)}, u32[]{:S(2)}) collective-permute-start(bf16[272,256]{1,0:T(8,128)(2,1)S(1)} %shard_map.100.a_ref), channel_id=1, source_target_pairs={{0,16},{1,65},{2,18},{3,67},{4,20},{5,69},{6,22},{7,71},{8,24},{9,... | collective-permute-start | bytes 417800 | tf_op jit(solution)/shard_map/ppermute | solution.py:502
  32.0 2.7 %collective-permute-start.7 = (bf16[272,256]{1,0:T(8,128)(2,1)S(1)}, bf16[272,256]{1,0:T(8,128)(2,1)S(1)}, u32[]{:S(2)}, u32[]{:S(2)}) collective-permute-start(bf16[272,256]{1,0:T(8,128)(2,1)S(1)} %shard_map.100.a_ref), channel_id=1, source_target_pairs={{0,32},{1,129},{2,34},{3,131},{4,36},{5,133},{6,38},{7,135},{8,40}... | collective-permute-start | bytes 417800 | tf_op jit(solution)/shard_map/ppermute | solution.py:502
  34.8 1.4 %collective-permute-start.8 = (bf16[272,256]{1,0:T(8,128)(2,1)S(1)}, bf16[272,256]{1,0:T(8,128)(2,1)S(1)}, u32[]{:S(2)}, u32[]{:S(2)}) collective-permute-start(bf16[272,256]{1,0:T(8,128)(2,1)S(1)} %shard_map.100.a_ref), channel_id=1, source_target_pairs={{0,48},{1,193},{2,50},{3,195},{4,52},{5,197},{6,54},{7,199},{8,56}... | collective-permute-start | bytes 417800 | tf_op jit(solution)/shard_map/ppermute | solution.py:502
  36.8 2.5 %collective-permute-done.7.c_ref = bf16[272,256]{1,0:T(8,128)(2,1)S(1)} collective-permute-done((bf16[272,256]{1,0:T(8,128)(2,1)S(1)}, bf16[272,256]{1,0:T(8,128)(2,1)S(1)}, u32[]{:S(2)}, u32[]{:S(2)}) %collective-permute-start.7) | collective-permute-done | bytes 139296 | tf_op jit(solution)/shard_map/ppermute | solution.py:502
  40.2 1.8 %collective-permute-start.13 = (bf16[1040,256]{1,0:T(8,128)(2,1)S(1)}, bf16[1040,256]{1,0:T(8,128)(2,1)S(1)}, u32[]{:S(2)}, u32[]{:S(2)}) collective-permute-start(bf16[1040,256]{1,0:T(8,128)(2,1)S(1)} %get-tuple-element.38.refs_1_), channel_id=1, source_target_pairs={{0,192},{1,49},{2,194},{3,51},{4,196},{5,53},{6,198},{7,55},{8,200... | collective-permute-start | bytes 1597448 | tf_op jit(solution)/shard_map/ppermute | solution.py:510
  42.0 1.2 %collective-permute-start.10 = (bf16[1040,256]{1,0:T(8,128)(2,1)S(1)}, bf16[1040,256]{1,0:T(8,128)(2,1)S(1)}, u32[]{:S(2)}, u32[]{:S(2)}) collective-permute-start(bf16[1040,256]{1,0:T(8,128)(2,1)S(1)} %get-tuple-element.38.refs_1_), channel_id=1, source_target_pairs={{0,128},{1,33},{2,130},{3,35},{4,132},{5,37},{6,134},{7,39},{8,136... | collective-permute-start | bytes 1597448 | tf_op jit(solution)/shard_map/ppermute | solution.py:510
  43.3 1.4 %shard_map.98 = (bf16[4,256,128]{2,1,0:T(8,128)(2,1)S(1)}, f32[128,128]{1,0:T(8,128)S(1)}, f32[128,128]{1,0:T(8,128)S(1)}) custom-call(bf16[144,4096]{1,0:T(8,128)(2,1)S(1)} %get-tuple-element.33.x_ref, bf16[4096,512]{1,0:T(8,128)(2,1)S(1)} %copy-done, bf16[16,128]{1,0:T(8,128)(2,1)S(1)} %get-tuple-element.34.code_ref.refs_10_, s32[1,256]{1,0:T(1,128)S(1)} %bitcast.3), custom_call_target="tpu_custom_call" | custom-call | flops 1073741824 | bytes 5242880 | tf_op jit(solution)/shard_map/pallas_call | solution.py:64
  44.7 0.8 %shard_map.102 = (f32[4,256,128]{2,1,0:T(8,128)S(1)}, f32[4,256,128]{2,1,0:T(8,128)S(1)}, f32[4,256,128]{2,1,0:T(8,128)S(1)}) custom-call(bf16[4,256,128]{2,1,0:T(8,128)(2,1)S(1)} %get-tuple-element.35.q_ref.refs_0_, bf16[128,256]{1,0:T(8,128)(2,1)S(1)} %get-tuple-element.39.kv_ref, bf16[16,256]{1,0:T(8,128)(2,1)S(1)} %get-tuple-element.40.mkv_ref.refs_12_, ...), custom_call_target="tpu_custom_call" | custom-call | flops 1073741824 | bytes 2097152 | tf_op jit(solution)/shard_map/pallas_call | solution.py:64
  45.6 3.7 %collective-permute-done.9.source_ref.refs_2_ = bf16[1040,256]{1,0:T(8,128)(2,1)S(1)} collective-permute-done((bf16[1040,256]{1,0:T(8,128)(2,1)S(1)}, bf16[1040,256]{1,0:T(8,128)(2,1)S(1)}, u32[]{:S(2)}, u32[]{:S(2)}) %collective-permute-start.9) | collective-permute-done | bytes 532512 | tf_op jit(solution)/shard_map/ppermute | solution.py:510
  49.6 6.8 %collective-permute-done.13.source_ref.refs_3_.refs_4_ = bf16[1040,256]{1,0:T(8,128)(2,1)S(1)} collective-permute-done((bf16[1040,256]{1,0:T(8,128)(2,1)S(1)}, bf16[1040,256]{1,0:T(8,128)(2,1)S(1)}, u32[]{:S(2)}, u32[]{:S(2)}) %collective-permute-start.13) | collective-permute-done | bytes 532512 | tf_op jit(solution)/shard_map/ppermute | solution.py:510
  56.6 1.7 %shard_map.104 = (f32[4,256,128]{2,1,0:T(8,128)S(1)}, f32[4,256,128]{2,1,0:T(8,128)S(1)}, f32[4,256,128]{2,1,0:T(8,128)S(1)}) custom-call(bf16[4,256,128]{2,1,0:T(8,128)(2,1)S(1)} %get-tuple-element.35.q_ref.refs_0_, bf16[1040,256]{1,0:T(8,128)(2,1)S(1)} %get-tuple-element.38.refs_1_, bf16[1040,256]{1,0:T(8,128)(2,1)S(1)} %collective-permute-done.9.source_ref.refs_2_, ...), custom_call_target="tpu_custom_call" | custom-call | flops 1073741824 | bytes 2097152 | tf_op jit(solution)/shard_map/pallas_call | solution.py:64
  58.9 2.9 %shard_map.107 = (f32[4,256,128]{2,1,0:T(8,128)S(1)}, f32[4,256,128]{2,1,0:T(8,128)S(1)}, f32[4,256,128]{2,1,0:T(8,128)S(1)}) custom-call(bf16[4,256,128]{2,1,0:T(8,128)(2,1)S(1)} %get-tuple-element.35.q_ref.refs_0_, bf16[1040,256]{1,0:T(8,128)(2,1)S(1)} %get-tuple-element.38.refs_1_, bf16[1040,256]{1,0:T(8,128)(2,1)S(1)} %collective-permute-done.9.source_ref.refs_2_, ...), custom_call_target="tpu_custom_call" | custom-call | flops 2147483648 | bytes 4194304 | tf_op jit(solution)/shard_map/pallas_call | solution.py:64
  61.8 3.7 %shard_map.108 = (bf16[128,512]{1,0:T(8,128)(2,1)}, bf16[128,512]{1,0:T(8,128)(2,1)}) custom-call(bf16[4,256,128]{2,1,0:T(8,128)(2,1)S(1)} %get-tuple-element.35.q_ref.refs_0_, bf16[1040,256]{1,0:T(8,128)(2,1)S(1)} %get-tuple-element.38.refs_1_, bf16[1040,256]{1,0:T(8,128)(2,1)S(1)} %collective-permute-done.9.source_ref.refs_2_, ...), custom_call_target="tpu_custom_call" | custom-call | flops 2147483648 | bytes 4194304 | tf_op jit(solution)/shard_map/pallas_call | solution.py:64
  (27 shorter events, 3.2 us)
Async XLA Ops:
  0.6 42.6 %copy-start.1 = (s32[256]{0:T(256)S(1)}, s32[256]{0:T(256)}, u32[]{:S(2)}) copy-start(s32[256]{0:T(256)} %param.11) | copy-start | bytes 3076
  0.6 42.6 %copy-start = (bf16[4096,512]{1,0:T(8,128)(2,1)S(1)}, bf16[4096,512]{1,0:T(8,128)(2,1)}, u32[]{:S(2)}) copy-start(bf16[4096,512]{1,0:T(8,128)(2,1)} %wq_ref.1) | copy-start | bytes 12582916
  0.7 14.5 %collective-permute-start = (bf16[128,512]{1,0:T(8,128)(2,1)}, bf16[128,512]{1,0:T(8,128)(2,1)S(1)}, u32[]{:S(2)}, u32[]{:S(2)}) collective-permute-start(bf16[128,512]{1,0:T(8,128)(2,1)} %refs_0_.1), channel_id=1, source_target_pairs={{0,2},{1,3},{2,4},{3,5},{4,6},{5,7},{6,0},{7,1},{8,10},{9,11},{10,... | collective-permute-start | bytes 393224 | tf_op jit(solution)/shard_map/ppermute | solution.py:463
  4.0 14.5 %collective-permute-start.1 = (bf16[128,512]{1,0:T(8,128)(2,1)}, bf16[128,512]{1,0:T(8,128)(2,1)S(1)}, u32[]{:S(2)}, u32[]{:S(2)}) collective-permute-start(bf16[128,512]{1,0:T(8,128)(2,1)} %refs_0_.1), channel_id=1, source_target_pairs={{0,4},{1,5},{2,6},{3,7},{4,0},{5,1},{6,2},{7,3},{8,12},{9,13},{10,... | collective-permute-start | bytes 393224 | tf_op jit(solution)/shard_map/ppermute | solution.py:463
  9.4 12.4 %collective-permute-start.2 = (bf16[128,512]{1,0:T(8,128)(2,1)}, bf16[128,512]{1,0:T(8,128)(2,1)S(1)}, u32[]{:S(2)}, u32[]{:S(2)}) collective-permute-start(bf16[128,512]{1,0:T(8,128)(2,1)} %refs_0_.1), channel_id=1, source_target_pairs={{0,6},{1,7},{2,0},{3,1},{4,2},{5,3},{6,4},{7,5},{8,14},{9,15},{10,... | collective-permute-start | bytes 393224 | tf_op jit(solution)/shard_map/ppermute | solution.py:463
  21.8 2.0 %collective-permute-start.3 = (bf16[512,512]{1,0:T(8,128)(2,1)S(1)}, bf16[512,512]{1,0:T(8,128)(2,1)S(1)}, u32[]{:S(2)}, u32[]{:S(2)}) collective-permute-start(bf16[512,512]{1,0:T(8,128)(2,1)S(1)} %shard_map.96.refs_0_), channel_id=1, source_target_pairs={{0,1},{1,0},{2,3},{3,2},{4,5},{5,4},{6,7},{7,6},{8,9},{9,8},{10,11... | collective-permute-start | bytes 1572872 | tf_op jit(solution)/shard_map/ppermute | solution.py:484
  24.7 1.3 %collective-permute-start.4 = (bf16[128,128]{1,0:T(8,128)(2,1)S(1)}, bf16[128,128]{1,0:T(8,128)(2,1)S(1)}, u32[]{:S(2)}, u32[]{:S(2)}) collective-permute-start(bf16[128,128]{1,0:T(8,128)(2,1)S(1)} %get-tuple-element.37), channel_id=1, source_target_pairs={{0,1},{1,0},{2,3},{3,2},{4,5},{5,4},{6,7},{7,6},{8,9},{9,8},{10,11... | collective-permute-start | bytes 98312 | tf_op jit(solution)/shard_map/ppermute | solution.py:497
  26.0 4.4 %collective-permute-start.5 = (bf16[144,256]{1,0:T(8,128)(2,1)S(1)}, bf16[144,256]{1,0:T(8,128)(2,1)S(1)}, u32[]{:S(2)}, u32[]{:S(2)}) collective-permute-start(bf16[144,256]{1,0:T(8,128)(2,1)S(1)} %shard_map.99.own_ref), channel_id=1, source_target_pairs={{0,8},{8,0},{16,24},{24,16},{32,40},{40,32},{48,56},{56,48},{64,72... | collective-permute-start | bytes 221192 | tf_op jit(solution)/shard_map/ppermute | solution.py:499
  30.5 6.3 %collective-permute-start.6 = (bf16[272,256]{1,0:T(8,128)(2,1)S(1)}, bf16[272,256]{1,0:T(8,128)(2,1)S(1)}, u32[]{:S(2)}, u32[]{:S(2)}) collective-permute-start(bf16[272,256]{1,0:T(8,128)(2,1)S(1)} %shard_map.100.a_ref), channel_id=1, source_target_pairs={{0,16},{1,65},{2,18},{3,67},{4,20},{5,69},{6,22},{7,71},{8,24},{9,... | collective-permute-start | bytes 417800 | tf_op jit(solution)/shard_map/ppermute | solution.py:502
  32.0 7.3 %collective-permute-start.7 = (bf16[272,256]{1,0:T(8,128)(2,1)S(1)}, bf16[272,256]{1,0:T(8,128)(2,1)S(1)}, u32[]{:S(2)}, u32[]{:S(2)}) collective-permute-start(bf16[272,256]{1,0:T(8,128)(2,1)S(1)} %shard_map.100.a_ref), channel_id=1, source_target_pairs={{0,32},{1,129},{2,34},{3,131},{4,36},{5,133},{6,38},{7,135},{8,40}... | collective-permute-start | bytes 417800 | tf_op jit(solution)/shard_map/ppermute | solution.py:502
  34.8 5.1 %collective-permute-start.8 = (bf16[272,256]{1,0:T(8,128)(2,1)S(1)}, bf16[272,256]{1,0:T(8,128)(2,1)S(1)}, u32[]{:S(2)}, u32[]{:S(2)}) collective-permute-start(bf16[272,256]{1,0:T(8,128)(2,1)S(1)} %shard_map.100.a_ref), channel_id=1, source_target_pairs={{0,48},{1,193},{2,50},{3,195},{4,52},{5,197},{6,54},{7,199},{8,56}... | collective-permute-start | bytes 417800 | tf_op jit(solution)/shard_map/ppermute | solution.py:502
  39.9 9.3 %collective-permute-start.9 = (bf16[1040,256]{1,0:T(8,128)(2,1)S(1)}, bf16[1040,256]{1,0:T(8,128)(2,1)S(1)}, u32[]{:S(2)}, u32[]{:S(2)}) collective-permute-start(bf16[1040,256]{1,0:T(8,128)(2,1)S(1)} %get-tuple-element.38.refs_1_), channel_id=1, source_target_pairs={{0,64},{1,17},{2,66},{3,19},{4,68},{5,21},{6,70},{7,23},{8,72},{9,... | collective-permute-start | bytes 1597448 | tf_op jit(solution)/shard_map/ppermute | solution.py:510
  40.2 16.2 %collective-permute-start.13 = (bf16[1040,256]{1,0:T(8,128)(2,1)S(1)}, bf16[1040,256]{1,0:T(8,128)(2,1)S(1)}, u32[]{:S(2)}, u32[]{:S(2)}) collective-permute-start(bf16[1040,256]{1,0:T(8,128)(2,1)S(1)} %get-tuple-element.38.refs_1_), channel_id=1, source_target_pairs={{0,192},{1,49},{2,194},{3,51},{4,196},{5,53},{6,198},{7,55},{8,200... | collective-permute-start | bytes 1597448 | tf_op jit(solution)/shard_map/ppermute | solution.py:510
  42.0 16.3 %collective-permute-start.10 = (bf16[1040,256]{1,0:T(8,128)(2,1)S(1)}, bf16[1040,256]{1,0:T(8,128)(2,1)S(1)}, u32[]{:S(2)}, u32[]{:S(2)}) collective-permute-start(bf16[1040,256]{1,0:T(8,128)(2,1)S(1)} %get-tuple-element.38.refs_1_), channel_id=1, source_target_pairs={{0,128},{1,33},{2,130},{3,35},{4,132},{5,37},{6,134},{7,39},{8,136... | collective-permute-start | bytes 1597448 | tf_op jit(solution)/shard_map/ppermute | solution.py:510
  45.5 11.1 %collective-permute-start.11 = (bf16[1040,128]{1,0:T(8,128)(2,1)S(1)}, bf16[1040,128]{1,0:T(8,128)(2,1)S(1)}, u32[]{:S(2)}, u32[]{:S(2)}) collective-permute-start(bf16[1040,128]{1,0:T(8,128)(2,1)S(1)} %get-tuple-element.44), channel_id=1, source_target_pairs={{0,1},{1,0},{2,3},{3,2},{4,5},{5,4},{6,7},{7,6},{8,9},{9,8},{10,11... | collective-permute-start | bytes 798728 | tf_op jit(solution)/shard_map/ppermute | solution.py:511
  49.3 7.3 %collective-permute-start.12 = (bf16[1040,128]{1,0:T(8,128)(2,1)S(1)}, bf16[1040,128]{1,0:T(8,128)(2,1)S(1)}, u32[]{:S(2)}, u32[]{:S(2)}) collective-permute-start(bf16[1040,128]{1,0:T(8,128)(2,1)S(1)} %shard_map.103), channel_id=1, source_target_pairs={{0,1},{1,0},{2,3},{3,2},{4,5},{5,4},{6,7},{7,6},{8,9},{9,8},{10,11... | collective-permute-start | bytes 798728 | tf_op jit(solution)/shard_map/ppermute | solution.py:532
  56.4 2.4 %collective-permute-start.15 = (bf16[1040,128]{1,0:T(8,128)(2,1)S(1)}, bf16[1040,128]{1,0:T(8,128)(2,1)S(1)}, u32[]{:S(2)}, u32[]{:S(2)}) collective-permute-start(bf16[1040,128]{1,0:T(8,128)(2,1)S(1)} %shard_map.106), channel_id=1, source_target_pairs={{0,1},{1,0},{2,3},{3,2},{4,5},{5,4},{6,7},{7,6},{8,9},{9,8},{10,11... | collective-permute-start | bytes 798728 | tf_op jit(solution)/shard_map/ppermute | solution.py:532
  58.3 3.5 %collective-permute-start.14 = (bf16[1040,128]{1,0:T(8,128)(2,1)S(1)}, bf16[1040,128]{1,0:T(8,128)(2,1)S(1)}, u32[]{:S(2)}, u32[]{:S(2)}) collective-permute-start(bf16[1040,128]{1,0:T(8,128)(2,1)S(1)} %shard_map.105), channel_id=1, source_target_pairs={{0,1},{1,0},{2,3},{3,2},{4,5},{5,4},{6,7},{7,6},{8,9},{9,8},{10,11... | collective-permute-start | bytes 798728 | tf_op jit(solution)/shard_map/ppermute | solution.py:532

commit v11 on v9

--- a/solution.py
+++ b/solution.py
@@ -93,28 +93,16 @@
     pad_ref[...] = jnp.broadcast_to(embed_ref[...], pad_ref.shape)
 
 
-def join_kernel(*refs):
-    out_ref = refs[-1]
-    rows = refs[0].shape[0]
-    for i, ref in enumerate(refs[:-1]):
-        out_ref[i * rows : (i + 1) * rows, :] = ref[...]
-
-
-def join(*arrays):
-    rows = sum(a.shape[0] for a in arrays)
-    (out,) = call(join_kernel, [((rows, WIDTH), BF16)], arrays, (1 << 10, 1 << 19))
-    return out
-
-
 def kv_kernel(*refs):
-    mine, other, pad_ref, wk_ref, wv_ref, code_ref = refs[:6]
-    x_ref, kv_ref, mkv_ref = refs[6:]
+    pieces = refs[:8]
+    pad_ref, wk_ref, wv_ref, code_ref = refs[8:12]
+    x_ref, kv_ref, mkv_ref = refs[12:]
     me = lax.axis_index("kv")
-    for dc, ref in enumerate((mine, other)):
-        for dz in range(4):
+    for dz in range(4):
+        for dc in range(2):
             source = lax.rem(me // 2 + 4 - dz, 4) * 2 + lax.rem(me + dc, 2)
             lanes = pl.ds(pl.multiple_of(source * WIDTH, WIDTH), WIDTH)
-            x_ref[:ROWS, lanes] = ref[dz * ROWS : (dz + 1) * ROWS, :]
+            x_ref[:ROWS, lanes] = pieces[2 * dz + dc][...]
     x_ref[ROWS:, :] = pad_ref[...]
     x = x_ref[...]
     for part, w_ref in enumerate((wk_ref, wv_ref)):
@@ -368,27 +356,20 @@
     pipeline(q_ref, pieces, state_in, state, None)
 
 
-def last_kernel(*refs):
-    q_ref, k_refs, v_refs = refs[0], refs[1:5], refs[5:9]
-    state_in = refs[9:12]
-    clean_ref, noisy_ref = refs[12:14]
-    state = refs[14:]
+def third_kernel(*refs):
+    q_ref, k_ref, v_refs = refs[0], refs[1], refs[2:5]
     where = place()
     near = (0, 1, 3)
-    pieces = [
-        (
-            lambda: blocks_of(k_refs[2], range(4)),
-            lambda: jnp.concatenate([blocks_of(v_refs[dx], (2,)) for dx in range(4)], axis=0),
-            None,
-            where[1] >= 2,
-        ),
-        (
-            lambda: jnp.concatenate([blocks_of(k_refs[dy], (2,)) for dy in near], axis=0),
-            lambda: blocks_of(v_refs[2], near),
-            shard_mask(where, [(dy, 2) for dy in near]),
-            None,
-        ),
-    ]
+    piece = spots_piece(where, {2: k_ref}, dict(zip(near, v_refs)), [(2, dx) for dx in near])
+    pipeline(q_ref, [piece], refs[5:8], refs[8:11], None)
+
+
+def last_kernel(*refs):
+    q_ref, k_refs, v_ref = refs[0], refs[1:5], refs[5]
+    state_in = refs[6:9]
+    clean_ref, noisy_ref = refs[9:11]
+    state = refs[11:]
+    piece = spots_piece(place(), dict(enumerate(k_refs)), {2: v_ref}, [(dy, 2) for dy in range(4)])
 
     def finish(h, accum, total):
         lanes = slice(h * HEAD, (h + 1) * HEAD)
@@ -396,7 +377,7 @@
         clean_ref[:, lanes] = result[:ROWS]
         noisy_ref[:, lanes] = result[ROWS:]
 
-    pipeline(q_ref, pieces, state_in, state, finish)
+    pipeline(q_ref, [piece], state_in, state, finish)
 
 
 def shards(hidden, block_ids, decode_order, step_cut, mask_embed, q_weight, k_weight, v_weight):
@@ -423,8 +404,10 @@
         ],
         pl.ANY,
     )
-    mine = join(own, *moved)
-    other = lax.ppermute(mine, "kv", kv_pairs(0, 1))
+    pieces = []
+    for piece in (own, *moved):
+        piece, _ = lax.optimization_barrier((piece, pad))
+        pieces += [piece, lax.ppermute(piece, "kv", kv_pairs(0, 1))]
     x, kv, mask_kv = call(
         kv_kernel,
         [
@@ -432,7 +415,7 @@
             ((ROWS + PAD, 2 * HEAD), BF16),
             ((PAD, 2 * HEAD), BF16),
         ],
-        [mine, other, pad, wk, wv, code],
+        [*pieces, pad, wk, wv, code],
         (1 << 29, 3 << 20),
     )
     pair = lax.ppermute(kv, "ctx", ctx_pairs(0, 0, 1))
@@ -477,11 +460,17 @@
         [q, *[all_k[d] for d in (0, 1, 3)], *[all_v[d] for d in (0, 1, 3)], *first, code, own_cut, mask_kv],
         (1 << 31, 4 << 20),
     )
+    third = call(
+        third_kernel,
+        state,
+        [q, all_k[2], *[all_v[d] for d in (0, 1, 3)], *far],
+        (1 << 30, 2 << 20),
+    )
     return tuple(
         call(
             last_kernel,
             [((ROWS, GROUP * HEAD), BF16)] * 2,
-            [q, *all_k, *all_v, *far],
+            [q, *all_k, all_v[2], *third],
             (1 << 31, 4 << 20),
             [pltpu.VMEM((GROUP, 2 * ROWS, HEAD), F32)] * 3,
         )

time: 67.7 us -> 64.9 us (0.959); the launches traced: 66.4 us -> 64.7 us
  waiting for transfers between devices: 25.3 us -> 23.4 us
    ppermute x3, waiting for transfers between devices: 6.19 us -> 3.02 us  [shards(): lax.ppermute(vs, 'ctx', ctx_pairs(0, d, 0))]
    ppermute x3, waiting for transfers between devices: 0.01 us -> 3.18 us  [shards(): lax.ppermute(ks, 'ctx', ctx_pairs(d, 0, 0))]
    ppermute x1 -> x4, waiting for transfers between devices: 1.89 us -> 1.33 us  [shards(): pieces += [piece, lax.ppermute(piece, 'kv', kv_pairs(0, 1))]]
  transfers between devices with their start and end apart: 17 -> 20, of which waited for: 8 -> 8; matrix products, arithmetic and copies ran while one was open for 2% -> 2% of each run, Pallas kernels for 13% -> 15%
where the time goes in v11:
time: 64.9 us; the launch traced here: 64.7 us
  starting transfers between devices  25.9 us (40%)
  waiting for transfers between devices  23.4 us (36%)
  Pallas kernels  13.3 us (20%)
  local copies, waits for them, and re-layouts  1.32 us (2%)
  between operations  0.77 us (1%)
    pallas_call x10, Pallas kernels, call(): pl.pallas_call(kernel, out_shape=[jax.ShapeDtypeStruct(s, t) for s, t in...  13.3 us
    ppermute x3, starting transfers between devices, shards(): moved = [lax.ppermute(hidden, 'kv', kv_pairs(d, 0)) for d in (1, 2, 3)]  11.4 us
    ppermute x3, waiting for transfers between devices, shards(): moved = [lax.ppermute(hidden, 'kv', kv_pairs(d, 0)) for d in (1, 2, 3)]  6.09 us
    ppermute x3, waiting for transfers between devices, shards(): vs = [lax.ppermute(v, 'ctx', ctx_pairs(d, 0, 0)) for d in (1, 2, 3)]  5.48 us
    ppermute x3, starting transfers between devices, shards(): ks = [lax.ppermute(k, 'ctx', ctx_pairs(0, d, 0)) for d in (1, 2, 3)]  5.05 us
    ppermute x1, waiting for transfers between devices, shards(): pair = lax.ppermute(kv, 'ctx', ctx_pairs(0, 0, 1))  4.34 us
    ppermute x3, starting transfers between devices, shards(): lax.ppermute(vs, 'ctx', ctx_pairs(0, d, 0))  3.69 us
    ppermute x3, waiting for transfers between devices, shards(): lax.ppermute(ks, 'ctx', ctx_pairs(d, 0, 0))  3.18 us
  transfers between devices with their start and end apart: 20, of which 8 were waited for; matrix products, arithmetic and copies ran while one was open for 2% of the time, Pallas kernels for 15%

profile of v11, /device:TPU:24, one launch (start us, length us, event | category | flops | bytes accessed | tf_op | source)
XLA Modules:
  0.0 64.7 jit_solution(12629553004169440160)
XLA Ops:
  0.7 3.3 %collective-permute-start.1 = (bf16[128,512]{1,0:T(8,128)(2,1)}, bf16[128,512]{1,0:T(8,128)(2,1)S(1)}, u32[]{:S(2)}, u32[]{:S(2)}) collective-permute-start(bf16[128,512]{1,0:T(8,128)(2,1)} %refs_0_.1), channel_id=1, source_target_pairs={{0,2},{1,3},{2,4},{3,5},{4,6},{5,7},{6,0},{7,1},{8,10},{9,11},{10,... | collective-permute-start | bytes 393224 | tf_op jit(solution)/shard_map/ppermute | solution.py:387
  4.0 5.4 %collective-permute-start.3 = (bf16[128,512]{1,0:T(8,128)(2,1)}, bf16[128,512]{1,0:T(8,128)(2,1)S(1)}, u32[]{:S(2)}, u32[]{:S(2)}) collective-permute-start(bf16[128,512]{1,0:T(8,128)(2,1)} %refs_0_.1), channel_id=1, source_target_pairs={{0,4},{1,5},{2,6},{3,7},{4,0},{5,1},{6,2},{7,3},{8,12},{9,13},{10,... | collective-permute-start | bytes 393224 | tf_op jit(solution)/shard_map/ppermute | solution.py:387
  9.4 2.7 %collective-permute-start.5 = (bf16[128,512]{1,0:T(8,128)(2,1)}, bf16[128,512]{1,0:T(8,128)(2,1)S(1)}, u32[]{:S(2)}, u32[]{:S(2)}) collective-permute-start(bf16[128,512]{1,0:T(8,128)(2,1)} %refs_0_.1), channel_id=1, source_target_pairs={{0,6},{1,7},{2,0},{3,1},{4,2},{5,3},{6,4},{7,5},{8,14},{9,15},{10,... | collective-permute-start | bytes 393224 | tf_op jit(solution)/shard_map/ppermute | solution.py:387
  12.1 1.3 %reshape.18.refs_5_ = bf16[1,4096]{1,0:T(2,128)(2,1)} reshape(bf16[4096]{0:T(1024)(128)(2,1)} %param.12) | data formatting | bytes 16384 | tf_op jit(solution)/shard_map/reshape | solution.py:397
  13.4 1.7 %shard_map.95 = (bf16[128,512]{1,0:T(8,128)(2,1)S(1)}, bf16[4096,128]{1,0:T(8,128)(2,1)S(1)}, bf16[4096,128]{1,0:T(8,128)(2,1)S(1)}, bf16[16,128]{1,0:T(8,128)(2,1)S(1)}, bf16[16,4096]{1,0:T(8,128)(2,1)S(1)}) custom-call(bf16[128,512]{1,0:T(8,128)(2,1)} %refs_0_.1, bf16[4096,128]{1,0:T(8,128)(2,1)} %refs_1_.1, bf16[4096,128]{1,0:T(8,128)(2,1)} %refs_2_.1, ...), custom_call_target="tpu_custom_call" | custom-call | flops 1048576 | bytes 4194304 | tf_op jit(solution)/shard_map/pallas_call | solution.py:51
  15.7 2.8 %collective-permute-done.3.refs_4_ = bf16[128,512]{1,0:T(8,128)(2,1)S(1)} collective-permute-done((bf16[128,512]{1,0:T(8,128)(2,1)}, bf16[128,512]{1,0:T(8,128)(2,1)S(1)}, u32[]{:S(2)}, u32[]{:S(2)}) %collective-permute-start.3) | collective-permute-done | bytes 131104 | tf_op jit(solution)/shard_map/ppermute | solution.py:387
  18.5 3.3 %collective-permute-done.5.refs_6_ = bf16[128,512]{1,0:T(8,128)(2,1)S(1)} collective-permute-done((bf16[128,512]{1,0:T(8,128)(2,1)}, bf16[128,512]{1,0:T(8,128)(2,1)S(1)}, u32[]{:S(2)}, u32[]{:S(2)}) %collective-permute-start.5) | collective-permute-done | bytes 131104 | tf_op jit(solution)/shard_map/ppermute | solution.py:387
  21.8 1.3 %collective-permute-done.6.refs_7_ = bf16[128,512]{1,0:T(8,128)(2,1)S(1)} collective-permute-done((bf16[128,512]{1,0:T(8,128)(2,1)S(1)}, bf16[128,512]{1,0:T(8,128)(2,1)S(1)}, u32[]{:S(2)}, u32[]{:S(2)}) %collective-permute-start.6) | collective-permute-done | bytes 131104 | tf_op jit(solution)/shard_map/ppermute | solution.py:410
  24.1 4.3 %collective-permute-done.7.other_ref = bf16[144,256]{1,0:T(8,128)(2,1)S(1)} collective-permute-done((bf16[144,256]{1,0:T(8,128)(2,1)S(1)}, bf16[144,256]{1,0:T(8,128)(2,1)S(1)}, u32[]{:S(2)}, u32[]{:S(2)}) %collective-permute-start.7) | collective-permute-done | bytes 73760 | tf_op jit(solution)/shard_map/ppermute | solution.py:421
  28.8 2.8 %collective-permute-start.10 = (bf16[272,128]{1,0:T(8,128)(2,1)S(1)}, bf16[272,128]{1,0:T(8,128)(2,1)S(1)}, u32[]{:S(2)}, u32[]{:S(2)}) collective-permute-start(bf16[272,128]{1,0:T(8,128)(2,1)S(1)} %get-tuple-element.45.refs_0_), channel_id=1, source_target_pairs={{0,48},{8,56},{16,0},{24,8},{32,16},{40,24},{48,32},{56,40},{64,11... | collective-permute-start | bytes 208904 | tf_op jit(solution)/shard_map/ppermute | solution.py:428
  31.5 2.3 %collective-permute-start.9 = (bf16[272,128]{1,0:T(8,128)(2,1)S(1)}, bf16[272,128]{1,0:T(8,128)(2,1)S(1)}, u32[]{:S(2)}, u32[]{:S(2)}) collective-permute-start(bf16[272,128]{1,0:T(8,128)(2,1)S(1)} %get-tuple-element.45.refs_0_), channel_id=1, source_target_pairs={{0,32},{8,40},{16,48},{24,56},{32,0},{40,8},{48,16},{56,24},{64,96... | collective-permute-start | bytes 208904 | tf_op jit(solution)/shard_map/ppermute | solution.py:428
  33.8 2.6 %collective-permute-start.12 = (bf16[256,128]{1,0:T(8,128)(2,1)S(1)}, bf16[256,128]{1,0:T(8,128)(2,1)S(1)}, u32[]{:S(2)}, u32[]{:S(2)}) collective-permute-start(bf16[256,128]{1,0:T(8,128)(2,1)S(1)} %get-tuple-element.46.refs_4_), channel_id=1, source_target_pairs={{0,128},{8,136},{16,144},{24,152},{32,160},{40,168},{48,176},{56,1... | collective-permute-start | bytes 196616 | tf_op jit(solution)/shard_map/ppermute | solution.py:429
  36.4 3.2 %collective-permute-done.12.refs_6_ = bf16[256,128]{1,0:T(8,128)(2,1)S(1)} collective-permute-done((bf16[256,128]{1,0:T(8,128)(2,1)S(1)}, bf16[256,128]{1,0:T(8,128)(2,1)S(1)}, u32[]{:S(2)}, u32[]{:S(2)}) %collective-permute-start.12) | collective-permute-done | bytes 65568 | tf_op jit(solution)/shard_map/ppermute | solution.py:429
  39.6 2.3 %collective-permute-done.13.refs_7_ = bf16[256,128]{1,0:T(8,128)(2,1)S(1)} collective-permute-done((bf16[256,128]{1,0:T(8,128)(2,1)S(1)}, bf16[256,128]{1,0:T(8,128)(2,1)S(1)}, u32[]{:S(2)}, u32[]{:S(2)}) %collective-permute-start.13) | collective-permute-done | bytes 65568 | tf_op jit(solution)/shard_map/ppermute | solution.py:429
  42.7 2.3 %collective-permute-start.18 = (bf16[1024,128]{1,0:T(8,128)(2,1)S(1)}, bf16[1024,128]{1,0:T(8,128)(2,1)S(1)}, u32[]{:S(2)}, u32[]{:S(2)}) collective-permute-start(bf16[1024,128]{1,0:T(8,128)(2,1)S(1)} %get-tuple-element.48.refs_3_.refs_4_.refs_2_), channel_id=1, source_target_pairs={{0,16},{8,24},{16,32},{24,40},{32,48},{40,56},{48,0},{56,8},{64,80... | collective-permute-start | bytes 786440 | tf_op jit(solution)/shard_map/ppermute | solution.py:449
  45.0 0.9 %collective-permute-start.16 = (bf16[1040,128]{1,0:T(8,128)(2,1)S(1)}, bf16[1040,128]{1,0:T(8,128)(2,1)S(1)}, u32[]{:S(2)}, u32[]{:S(2)}) collective-permute-start(bf16[1040,128]{1,0:T(8,128)(2,1)S(1)} %get-tuple-element.47.refs_1_), channel_id=1, source_target_pairs={{0,192},{8,200},{16,208},{24,216},{32,224},{40,232},{48,240},{56,2... | collective-permute-start | bytes 798728 | tf_op jit(solution)/shard_map/ppermute | solution.py:448
  45.9 1.4 %collective-permute-start.19 = (bf16[1024,128]{1,0:T(8,128)(2,1)S(1)}, bf16[1024,128]{1,0:T(8,128)(2,1)S(1)}, u32[]{:S(2)}, u32[]{:S(2)}) collective-permute-start(bf16[1024,128]{1,0:T(8,128)(2,1)S(1)} %get-tuple-element.48.refs_3_.refs_4_.refs_2_), channel_id=1, source_target_pairs={{0,48},{8,56},{16,0},{24,8},{32,16},{40,24},{48,32},{56,40},{64,11... | collective-permute-start | bytes 786440 | tf_op jit(solution)/shard_map/ppermute | solution.py:449
  47.3 1.4 %shard_map.97 = (bf16[4,256,128]{2,1,0:T(8,128)(2,1)S(1)}, f32[128,128]{1,0:T(8,128)S(1)}, f32[128,128]{1,0:T(8,128)S(1)}) custom-call(bf16[144,4096]{1,0:T(8,128)(2,1)S(1)} %get-tuple-element.42.x_ref, bf16[4096,512]{1,0:T(8,128)(2,1)S(1)} %copy-done, bf16[16,128]{1,0:T(8,128)(2,1)S(1)} %get-tuple-element.41.refs_11_.code_ref.refs_10_, s32[1,256]{1,0:T(1,128)S(1)} %bitcast.3), custom_call_target="tpu_custom_call" | custom-call | flops 1073741824 | bytes 5242880 | tf_op jit(solution)/shard_map/pallas_call | solution.py:51
  50.1 3.0 %collective-permute-done.18.refs_4_.refs_5_.refs_3_ = bf16[1024,128]{1,0:T(8,128)(2,1)S(1)} collective-permute-done((bf16[1024,128]{1,0:T(8,128)(2,1)S(1)}, bf16[1024,128]{1,0:T(8,128)(2,1)S(1)}, u32[]{:S(2)}, u32[]{:S(2)}) %collective-permute-start.18) | collective-permute-done | bytes 262176 | tf_op jit(solution)/shard_map/ppermute | solution.py:449
  53.1 1.7 %shard_map.101 = (f32[4,256,128]{2,1,0:T(8,128)S(1)}, f32[4,256,128]{2,1,0:T(8,128)S(1)}, f32[4,256,128]{2,1,0:T(8,128)S(1)}) custom-call(bf16[4,256,128]{2,1,0:T(8,128)(2,1)S(1)} %get-tuple-element.43.q_ref.refs_0_, bf16[1040,128]{1,0:T(8,128)(2,1)S(1)} %get-tuple-element.47.refs_1_, bf16[1040,128]{1,0:T(8,128)(2,1)S(1)} %collective-permute-done.14.refs_2_, ...), custom_call_target="tpu_custom_call" | custom-call | flops 1073741824 | bytes 2097152 | tf_op jit(solution)/shard_map/pallas_call | solution.py:51
  54.8 3.2 %collective-permute-done.16.refs_3_.refs_4_ = bf16[1040,128]{1,0:T(8,128)(2,1)S(1)} collective-permute-done((bf16[1040,128]{1,0:T(8,128)(2,1)S(1)}, bf16[1040,128]{1,0:T(8,128)(2,1)S(1)}, u32[]{:S(2)}, u32[]{:S(2)}) %collective-permute-start.16) | collective-permute-done | bytes 266272 | tf_op jit(solution)/shard_map/ppermute | solution.py:448
  58.0 2.8 %shard_map.102 = (f32[4,256,128]{2,1,0:T(8,128)S(1)}, f32[4,256,128]{2,1,0:T(8,128)S(1)}, f32[4,256,128]{2,1,0:T(8,128)S(1)}) custom-call(bf16[4,256,128]{2,1,0:T(8,128)(2,1)S(1)} %get-tuple-element.43.q_ref.refs_0_, bf16[1040,128]{1,0:T(8,128)(2,1)S(1)} %get-tuple-element.47.refs_1_, bf16[1040,128]{1,0:T(8,128)(2,1)S(1)} %collective-permute-done.14.refs_2_, ...), custom_call_target="tpu_custom_call" | custom-call | flops 2147483648 | bytes 4194304 | tf_op jit(solution)/shard_map/pallas_call | solution.py:51
  60.8 1.5 %shard_map.103 = (f32[4,256,128]{2,1,0:T(8,128)S(1)}, f32[4,256,128]{2,1,0:T(8,128)S(1)}, f32[4,256,128]{2,1,0:T(8,128)S(1)}) custom-call(bf16[4,256,128]{2,1,0:T(8,128)(2,1)S(1)} %get-tuple-element.43.q_ref.refs_0_, bf16[1040,128]{1,0:T(8,128)(2,1)S(1)} %collective-permute-done.15.refs_1_.refs_3_, ...), custom_call_target="tpu_custom_call" | custom-call | flops 1073741824 | bytes 2097152 | tf_op jit(solution)/shard_map/pallas_call | solution.py:51
  62.3 2.4 %shard_map.104 = (bf16[128,512]{1,0:T(8,128)(2,1)}, bf16[128,512]{1,0:T(8,128)(2,1)}) custom-call(bf16[4,256,128]{2,1,0:T(8,128)(2,1)S(1)} %get-tuple-element.43.q_ref.refs_0_, bf16[1040,128]{1,0:T(8,128)(2,1)S(1)} %get-tuple-element.47.refs_1_, bf16[1040,128]{1,0:T(8,128)(2,1)S(1)} %collective-permute-done.14.refs_2_, ...), custom_call_target="tpu_custom_call" | custom-call | flops 2147483648 | bytes 4194304 | tf_op jit(solution)/shard_map/pallas_call | solution.py:51
  (31 shorter events, 4.1 us)
Async XLA Ops:
  0.6 46.7 %copy-start.1 = (s32[256]{0:T(256)S(1)}, s32[256]{0:T(256)}, u32[]{:S(2)}) copy-start(s32[256]{0:T(256)} %param.11) | copy-start | bytes 3076
  0.6 46.7 %copy-start = (bf16[4096,512]{1,0:T(8,128)(2,1)S(1)}, bf16[4096,512]{1,0:T(8,128)(2,1)}, u32[]{:S(2)}) copy-start(bf16[4096,512]{1,0:T(8,128)(2,1)} %wq_ref.1) | copy-start | bytes 12582916
  0.7 14.6 %collective-permute-start.1 = (bf16[128,512]{1,0:T(8,128)(2,1)}, bf16[128,512]{1,0:T(8,128)(2,1)S(1)}, u32[]{:S(2)}, u32[]{:S(2)}) collective-permute-start(bf16[128,512]{1,0:T(8,128)(2,1)} %refs_0_.1), channel_id=1, source_target_pairs={{0,2},{1,3},{2,4},{3,5},{4,6},{5,7},{6,0},{7,1},{8,10},{9,11},{10,... | collective-permute-start | bytes 393224 | tf_op jit(solution)/shard_map/ppermute | solution.py:387
  4.0 14.5 %collective-permute-start.3 = (bf16[128,512]{1,0:T(8,128)(2,1)}, bf16[128,512]{1,0:T(8,128)(2,1)S(1)}, u32[]{:S(2)}, u32[]{:S(2)}) collective-permute-start(bf16[128,512]{1,0:T(8,128)(2,1)} %refs_0_.1), channel_id=1, source_target_pairs={{0,4},{1,5},{2,6},{3,7},{4,0},{5,1},{6,2},{7,3},{8,12},{9,13},{10,... | collective-permute-start | bytes 393224 | tf_op jit(solution)/shard_map/ppermute | solution.py:387
  9.4 12.4 %collective-permute-start.5 = (bf16[128,512]{1,0:T(8,128)(2,1)}, bf16[128,512]{1,0:T(8,128)(2,1)S(1)}, u32[]{:S(2)}, u32[]{:S(2)}) collective-permute-start(bf16[128,512]{1,0:T(8,128)(2,1)} %refs_0_.1), channel_id=1, source_target_pairs={{0,6},{1,7},{2,0},{3,1},{4,2},{5,3},{6,4},{7,5},{8,14},{9,15},{10,... | collective-permute-start | bytes 393224 | tf_op jit(solution)/shard_map/ppermute | solution.py:387
  15.1 6.7 %collective-permute-start = (bf16[128,512]{1,0:T(8,128)(2,1)S(1)}, bf16[128,512]{1,0:T(8,128)(2,1)S(1)}, u32[]{:S(2)}, u32[]{:S(2)}) collective-permute-start(bf16[128,512]{1,0:T(8,128)(2,1)S(1)} %get-tuple-element.35.refs_0_), channel_id=1, source_target_pairs={{0,1},{1,0},{2,3},{3,2},{4,5},{5,4},{6,7},{7,6},{8,9},{9,8},{10,11... | collective-permute-start | bytes 393224 | tf_op jit(solution)/shard_map/ppermute | solution.py:410
  15.2 6.6 %collective-permute-start.2 = (bf16[128,512]{1,0:T(8,128)(2,1)S(1)}, bf16[128,512]{1,0:T(8,128)(2,1)S(1)}, u32[]{:S(2)}, u32[]{:S(2)}) collective-permute-start(bf16[128,512]{1,0:T(8,128)(2,1)S(1)} %collective-permute-done.1.refs_2_), channel_id=1, source_target_pairs={{0,1},{1,0},{2,3},{3,2},{4,5},{5,4},{6,7},{7,6},{8,9},{9,8},{10,11... | collective-permute-start | bytes 393224 | tf_op jit(solution)/shard_map/ppermute | solution.py:410
  18.5 3.3 %collective-permute-start.4 = (bf16[128,512]{1,0:T(8,128)(2,1)S(1)}, bf16[128,512]{1,0:T(8,128)(2,1)S(1)}, u32[]{:S(2)}, u32[]{:S(2)}) collective-permute-start(bf16[128,512]{1,0:T(8,128)(2,1)S(1)} %collective-permute-done.3.refs_4_), channel_id=1, source_target_pairs={{0,1},{1,0},{2,3},{3,2},{4,5},{5,4},{6,7},{7,6},{8,9},{9,8},{10,11... | collective-permute-start | bytes 393224 | tf_op jit(solution)/shard_map/ppermute | solution.py:410
  21.8 1.3 %collective-permute-start.6 = (bf16[128,512]{1,0:T(8,128)(2,1)S(1)}, bf16[128,512]{1,0:T(8,128)(2,1)S(1)}, u32[]{:S(2)}, u32[]{:S(2)}) collective-permute-start(bf16[128,512]{1,0:T(8,128)(2,1)S(1)} %collective-permute-done.5.refs_6_), channel_id=1, source_target_pairs={{0,1},{1,0},{2,3},{3,2},{4,5},{5,4},{6,7},{7,6},{8,9},{9,8},{10,11... | collective-permute-start | bytes 393224 | tf_op jit(solution)/shard_map/ppermute | solution.py:410
  24.0 4.4 %collective-permute-start.7 = (bf16[144,256]{1,0:T(8,128)(2,1)S(1)}, bf16[144,256]{1,0:T(8,128)(2,1)S(1)}, u32[]{:S(2)}, u32[]{:S(2)}) collective-permute-start(bf16[144,256]{1,0:T(8,128)(2,1)S(1)} %get-tuple-element.44.own_ref.kv_ref), channel_id=1, source_target_pairs={{0,8},{8,0},{16,24},{24,16},{32,40},{40,32},{48,56},{56,48},{64,72... | collective-permute-start | bytes 221192 | tf_op jit(solution)/shard_map/ppermute | solution.py:421
  28.5 7.9 %collective-permute-start.11 = (bf16[256,128]{1,0:T(8,128)(2,1)S(1)}, bf16[256,128]{1,0:T(8,128)(2,1)S(1)}, u32[]{:S(2)}, u32[]{:S(2)}) collective-permute-start(bf16[256,128]{1,0:T(8,128)(2,1)S(1)} %get-tuple-element.46.refs_4_), channel_id=1, source_target_pairs={{0,64},{8,72},{16,80},{24,88},{32,96},{40,104},{48,112},{56,120},{... | collective-permute-start | bytes 196616 | tf_op jit(solution)/shard_map/ppermute | solution.py:429
  28.8 13.1 %collective-permute-start.10 = (bf16[272,128]{1,0:T(8,128)(2,1)S(1)}, bf16[272,128]{1,0:T(8,128)(2,1)S(1)}, u32[]{:S(2)}, u32[]{:S(2)}) collective-permute-start(bf16[272,128]{1,0:T(8,128)(2,1)S(1)} %get-tuple-element.45.refs_0_), channel_id=1, source_target_pairs={{0,48},{8,56},{16,0},{24,8},{32,16},{40,24},{48,32},{56,40},{64,11... | collective-permute-start | bytes 208904 | tf_op jit(solution)/shard_map/ppermute | solution.py:428
  31.5 10.4 %collective-permute-start.8 = (bf16[272,128]{1,0:T(8,128)(2,1)S(1)}, bf16[272,128]{1,0:T(8,128)(2,1)S(1)}, u32[]{:S(2)}, u32[]{:S(2)}) collective-permute-start(bf16[272,128]{1,0:T(8,128)(2,1)S(1)} %get-tuple-element.45.refs_0_), channel_id=1, source_target_pairs={{0,16},{8,24},{16,32},{24,40},{32,48},{40,56},{48,0},{56,8},{64,80... | collective-permute-start | bytes 208904 | tf_op jit(solution)/shard_map/ppermute | solution.py:428
  31.5 10.4 %collective-permute-start.9 = (bf16[272,128]{1,0:T(8,128)(2,1)S(1)}, bf16[272,128]{1,0:T(8,128)(2,1)S(1)}, u32[]{:S(2)}, u32[]{:S(2)}) collective-permute-start(bf16[272,128]{1,0:T(8,128)(2,1)S(1)} %get-tuple-element.45.refs_0_), channel_id=1, source_target_pairs={{0,32},{8,40},{16,48},{24,56},{32,0},{40,8},{48,16},{56,24},{64,96... | collective-permute-start | bytes 208904 | tf_op jit(solution)/shard_map/ppermute | solution.py:428
  33.8 5.8 %collective-permute-start.12 = (bf16[256,128]{1,0:T(8,128)(2,1)S(1)}, bf16[256,128]{1,0:T(8,128)(2,1)S(1)}, u32[]{:S(2)}, u32[]{:S(2)}) collective-permute-start(bf16[256,128]{1,0:T(8,128)(2,1)S(1)} %get-tuple-element.46.refs_4_), channel_id=1, source_target_pairs={{0,128},{8,136},{16,144},{24,152},{32,160},{40,168},{48,176},{56,1... | collective-permute-start | bytes 196616 | tf_op jit(solution)/shard_map/ppermute | solution.py:429
  36.4 5.5 %collective-permute-start.13 = (bf16[256,128]{1,0:T(8,128)(2,1)S(1)}, bf16[256,128]{1,0:T(8,128)(2,1)S(1)}, u32[]{:S(2)}, u32[]{:S(2)}) collective-permute-start(bf16[256,128]{1,0:T(8,128)(2,1)S(1)} %get-tuple-element.46.refs_4_), channel_id=1, source_target_pairs={{0,192},{8,200},{16,208},{24,216},{32,224},{40,232},{48,240},{56,2... | collective-permute-start | bytes 196616 | tf_op jit(solution)/shard_map/ppermute | solution.py:429
  41.9 11.2 %collective-permute-start.14 = (bf16[1040,128]{1,0:T(8,128)(2,1)S(1)}, bf16[1040,128]{1,0:T(8,128)(2,1)S(1)}, u32[]{:S(2)}, u32[]{:S(2)}) collective-permute-start(bf16[1040,128]{1,0:T(8,128)(2,1)S(1)} %get-tuple-element.47.refs_1_), channel_id=1, source_target_pairs={{0,64},{8,72},{16,80},{24,88},{32,96},{40,104},{48,112},{56,120},{... | collective-permute-start | bytes 798728 | tf_op jit(solution)/shard_map/ppermute | solution.py:448
  42.7 10.4 %collective-permute-start.18 = (bf16[1024,128]{1,0:T(8,128)(2,1)S(1)}, bf16[1024,128]{1,0:T(8,128)(2,1)S(1)}, u32[]{:S(2)}, u32[]{:S(2)}) collective-permute-start(bf16[1024,128]{1,0:T(8,128)(2,1)S(1)} %get-tuple-element.48.refs_3_.refs_4_.refs_2_), channel_id=1, source_target_pairs={{0,16},{8,24},{16,32},{24,40},{32,48},{40,56},{48,0},{56,8},{64,80... | collective-permute-start | bytes 786440 | tf_op jit(solution)/shard_map/ppermute | solution.py:449
  45.0 13.0 %collective-permute-start.16 = (bf16[1040,128]{1,0:T(8,128)(2,1)S(1)}, bf16[1040,128]{1,0:T(8,128)(2,1)S(1)}, u32[]{:S(2)}, u32[]{:S(2)}) collective-permute-start(bf16[1040,128]{1,0:T(8,128)(2,1)S(1)} %get-tuple-element.47.refs_1_), channel_id=1, source_target_pairs={{0,192},{8,200},{16,208},{24,216},{32,224},{40,232},{48,240},{56,2... | collective-permute-start | bytes 798728 | tf_op jit(solution)/shard_map/ppermute | solution.py:448
  45.9 8.9 %collective-permute-start.19 = (bf16[1024,128]{1,0:T(8,128)(2,1)S(1)}, bf16[1024,128]{1,0:T(8,128)(2,1)S(1)}, u32[]{:S(2)}, u32[]{:S(2)}) collective-permute-start(bf16[1024,128]{1,0:T(8,128)(2,1)S(1)} %get-tuple-element.48.refs_3_.refs_4_.refs_2_), channel_id=1, source_target_pairs={{0,48},{8,56},{16,0},{24,8},{32,16},{40,24},{48,32},{56,40},{64,11... | collective-permute-start | bytes 786440 | tf_op jit(solution)/shard_map/ppermute | solution.py:449
  49.6 11.2 %collective-permute-start.15 = (bf16[1040,128]{1,0:T(8,128)(2,1)S(1)}, bf16[1040,128]{1,0:T(8,128)(2,1)S(1)}, u32[]{:S(2)}, u32[]{:S(2)}) collective-permute-start(bf16[1040,128]{1,0:T(8,128)(2,1)S(1)} %get-tuple-element.47.refs_1_), channel_id=1, source_target_pairs={{0,128},{8,136},{16,144},{24,152},{32,160},{40,168},{48,176},{56,1... | collective-permute-start | bytes 798728 | tf_op jit(solution)/shard_map/ppermute | solution.py:448
  53.1 9.2 %collective-permute-start.17 = (bf16[1024,128]{1,0:T(8,128)(2,1)S(1)}, bf16[1024,128]{1,0:T(8,128)(2,1)S(1)}, u32[]{:S(2)}, u32[]{:S(2)}) collective-permute-start(bf16[1024,128]{1,0:T(8,128)(2,1)S(1)} %get-tuple-element.48.refs_3_.refs_4_.refs_2_), channel_id=1, source_target_pairs={{0,32},{8,40},{16,48},{24,56},{32,0},{40,8},{48,16},{56,24},{64,96... | collective-permute-start | bytes 786440 | tf_op jit(solution)/shard_map/ppermute | solution.py:449

commit v12 on v11

--- a/solution.py
+++ b/solution.py
@@ -26,7 +26,7 @@
     pairs = []
     for i in range(32):
         y, x, z = i // 8, (i // 2) % 4, i % 2
-        pairs.append((i, (((y + dy) % 4) * 4 + (x + dx) % 4) * 2 + (z + dz) % 2))
+        pairs.append((i, ((y ^ dy) * 4 + (x ^ dx)) * 2 + (z ^ dz)))
     return pairs
 
 
@@ -34,7 +34,7 @@
     pairs = []
     for i in range(8):
         z, c = i // 2, i % 2
-        pairs.append((i, ((z + dz) % 4) * 2 + (c + dc) % 2))
+        pairs.append((i, (z ^ dz) * 2 + (c ^ dc)))
     return pairs
 
 
@@ -100,7 +100,7 @@
     me = lax.axis_index("kv")
     for dz in range(4):
         for dc in range(2):
-            source = lax.rem(me // 2 + 4 - dz, 4) * 2 + lax.rem(me + dc, 2)
+            source = jnp.bitwise_xor(me, 2 * dz + dc)
             lanes = pl.ds(pl.multiple_of(source * WIDTH, WIDTH), WIDTH)
             x_ref[:ROWS, lanes] = pieces[2 * dz + dc][...]
     x_ref[ROWS:, :] = pad_ref[...]
@@ -249,7 +249,7 @@
         kept = []
         for j, part in enumerate(parts):
             dy, dx = spots[j // 2]
-            there = lax.rem(y + 4 - dy, 4) * 8 + lax.rem(x + 4 - dx, 4) * 2 + lax.rem(z + j, 2)
+            there = jnp.bitwise_xor(me, dy * 8 + dx * 2 + j % 2)
             kept.append(jnp.where(there < me - 1, part, LOW))
         return kept
 
@@ -282,25 +282,34 @@
     state = refs[13:16]
     me, y, x, z = place()
 
-    wrap = (z == 0) & (x == 0)
-    beyond = (z == 1) & (x == 3)
-
-    def block(ref, index):
-        return ref[index * ROWS : (index + 1) * ROWS, :]
-
-    k_old = jnp.where(wrap, block(k_refs[1], 3), jnp.where(z == 0, block(k_refs[0], 3), block(k_refs[0], 1)))
-    v_old = jnp.where(wrap, block(v_refs[1], 3), jnp.where(z == 0, block(v_refs[1], 1), block(v_refs[0], 1)))
-    k_new = jnp.where(beyond, block(k_refs[3], 7), jnp.where(z == 1, block(k_refs[0], 7), block(k_refs[0], 1)))
-    v_new = jnp.where(beyond, block(v_refs[3], 7), jnp.where(z == 1, block(v_refs[3], 1), block(v_refs[0], 1)))
+    spots = ((0, 0), (0, 1), (0, 3), (1, 3), (3, 3))
+    old_far = jnp.bitwise_xor(me, jnp.maximum(me - 1, 0)) // 2
+    new_far = jnp.bitwise_xor(me, jnp.minimum(me + 1, LAST)) // 2
+
+    def pick(far, of):
+        chosen = of(*spots[0])
+        for dy, dx in spots[1:]:
+            chosen = jnp.where(far == dy * 4 + dx, of(dy, dx), chosen)
+        return chosen
+
+    def k_block(dy, dx):
+        return k_refs[dy][(dx * 2 + 1) * ROWS : (dx * 2 + 2) * ROWS, :]
+
+    def v_block(dy, dx):
+        return v_refs[dx][(dy * 2 + 1) * ROWS : (dy * 2 + 2) * ROWS, :]
+
+    k_old, v_old = pick(old_far, k_block), pick(old_far, v_block)
+    k_new, v_new = pick(new_far, k_block), pick(new_far, v_block)
     k_new, v_new = k_new[:BLOCK], v_new[:BLOCK]
 
     own = code_ref[...].astype(F32)[0:1]
     tails = {dy: ref_tail(k_refs[dy], 8 * ROWS) for dy in (0, 1, 3)}
 
     def line(i):
-        old = jnp.where(wrap, tails[1][6 + i : 7 + i], jnp.where(z == 0, tails[0][6 + i : 7 + i], tails[0][2 + i : 3 + i]))
-        new = jnp.where(beyond, tails[3][14 + i : 15 + i], jnp.where(z == 1, tails[0][14 + i : 15 + i], tails[0][2 + i : 3 + i]))
-        return old, new
+        def row(dy, dx):
+            return tails[dy][dx * 4 + 2 + i : dx * 4 + 3 + i]
+
+        return pick(old_far, row), pick(new_far, row)
 
     old_ids, new_ids = line(0)
     old_order, new_order = line(1)

time: 64.9 us -> 63.6 us (0.980)
  the two profiles are of different devices: /device:TPU:24 before, /device:TPU:16 now
where the time goes in v12:
time: 63.6 us; the launch traced here: 63.4 us
  starting transfers between devices  27.9 us (44%)
  waiting for transfers between devices  20.1 us (32%)
  Pallas kernels  13.3 us (21%)
  local copies, waits for them, and re-layouts  1.32 us (2%)
  between operations  0.77 us (1%)
    pallas_call x10, Pallas kernels, call(): pl.pallas_call(kernel, out_shape=[jax.ShapeDtypeStruct(s, t) for s, t in...  13.3 us
    ppermute x3, starting transfers between devices, shards(): moved = [lax.ppermute(hidden, 'kv', kv_pairs(d, 0)) for d in (1, 2, 3)]  8.75 us
    ppermute x3, waiting for transfers between devices, shards(): moved = [lax.ppermute(hidden, 'kv', kv_pairs(d, 0)) for d in (1, 2, 3)]  7.63 us
    ppermute x3, waiting for transfers between devices, shards(): lax.ppermute(vs, 'ctx', ctx_pairs(0, d, 0))  4.91 us
    ppermute x3, starting transfers between devices, shards(): ks = [lax.ppermute(k, 'ctx', ctx_pairs(0, d, 0)) for d in (1, 2, 3)]  4.7 us
    ppermute x3, starting transfers between devices, shards(): lax.ppermute(ks, 'ctx', ctx_pairs(d, 0, 0))  4.27 us
    ppermute x3, starting transfers between devices, shards(): lax.ppermute(vs, 'ctx', ctx_pairs(0, d, 0))  4.23 us
    ppermute x3, starting transfers between devices, shards(): vs = [lax.ppermute(v, 'ctx', ctx_pairs(d, 0, 0)) for d in (1, 2, 3)]  3.58 us
  transfers between devices with their start and end apart: 20, of which 6 were waited for; matrix products, arithmetic and copies ran while one was open for 2% of the time, Pallas kernels for 16%

profile of v12, /device:TPU:16, one launch (start us, length us, event | category | flops | bytes accessed | tf_op | source)
XLA Modules:
  0.0 63.4 jit_solution(8159483083092957582)
XLA Ops:
  0.7 3.4 %collective-permute-start.1 = (bf16[128,512]{1,0:T(8,128)(2,1)}, bf16[128,512]{1,0:T(8,128)(2,1)S(1)}, u32[]{:S(2)}, u32[]{:S(2)}) collective-permute-start(bf16[128,512]{1,0:T(8,128)(2,1)} %refs_0_.1), channel_id=1, source_target_pairs={{0,2},{1,3},{2,0},{3,1},{4,6},{5,7},{6,4},{7,5},{8,10},{9,11},{10,... | collective-permute-start | bytes 393224 | tf_op jit(solution)/shard_map/ppermute | solution.py:396
  4.0 5.4 %collective-permute-start.3 = (bf16[128,512]{1,0:T(8,128)(2,1)}, bf16[128,512]{1,0:T(8,128)(2,1)S(1)}, u32[]{:S(2)}, u32[]{:S(2)}) collective-permute-start(bf16[128,512]{1,0:T(8,128)(2,1)} %refs_0_.1), channel_id=1, source_target_pairs={{0,4},{1,5},{2,6},{3,7},{4,0},{5,1},{6,2},{7,3},{8,12},{9,13},{10,... | collective-permute-start | bytes 393224 | tf_op jit(solution)/shard_map/ppermute | solution.py:396
  9.4 1.3 %reshape.18.refs_5_ = bf16[1,4096]{1,0:T(2,128)(2,1)} reshape(bf16[4096]{0:T(1024)(128)(2,1)} %param.12) | data formatting | bytes 16384 | tf_op jit(solution)/shard_map/reshape | solution.py:406
  10.7 1.7 %shard_map.95 = (bf16[128,512]{1,0:T(8,128)(2,1)S(1)}, bf16[4096,128]{1,0:T(8,128)(2,1)S(1)}, bf16[4096,128]{1,0:T(8,128)(2,1)S(1)}, bf16[16,128]{1,0:T(8,128)(2,1)S(1)}, bf16[16,4096]{1,0:T(8,128)(2,1)S(1)}) custom-call(bf16[128,512]{1,0:T(8,128)(2,1)} %refs_0_.1, bf16[4096,128]{1,0:T(8,128)(2,1)} %refs_1_.1, bf16[4096,128]{1,0:T(8,128)(2,1)} %refs_2_.1, ...), custom_call_target="tpu_custom_call" | custom-call | flops 1048576 | bytes 4194304 | tf_op jit(solution)/shard_map/pallas_call | solution.py:51
  13.1 5.9 %collective-permute-done.3.refs_4_ = bf16[128,512]{1,0:T(8,128)(2,1)S(1)} collective-permute-done((bf16[128,512]{1,0:T(8,128)(2,1)}, bf16[128,512]{1,0:T(8,128)(2,1)S(1)}, u32[]{:S(2)}, u32[]{:S(2)}) %collective-permute-start.3) | collective-permute-done | bytes 131104 | tf_op jit(solution)/shard_map/ppermute | solution.py:396
  18.9 1.8 %collective-permute-done.5.refs_6_ = bf16[128,512]{1,0:T(8,128)(2,1)S(1)} collective-permute-done((bf16[128,512]{1,0:T(8,128)(2,1)}, bf16[128,512]{1,0:T(8,128)(2,1)S(1)}, u32[]{:S(2)}, u32[]{:S(2)}) %collective-permute-start.5) | collective-permute-done | bytes 131104 | tf_op jit(solution)/shard_map/ppermute | solution.py:396
  20.7 1.3 %collective-permute-done.6.refs_7_ = bf16[128,512]{1,0:T(8,128)(2,1)S(1)} collective-permute-done((bf16[128,512]{1,0:T(8,128)(2,1)S(1)}, bf16[128,512]{1,0:T(8,128)(2,1)S(1)}, u32[]{:S(2)}, u32[]{:S(2)}) %collective-permute-start.6) | collective-permute-done | bytes 131104 | tf_op jit(solution)/shard_map/ppermute | solution.py:419
  22.9 1.8 %collective-permute-start.7 = (bf16[144,256]{1,0:T(8,128)(2,1)S(1)}, bf16[144,256]{1,0:T(8,128)(2,1)S(1)}, u32[]{:S(2)}, u32[]{:S(2)}) collective-permute-start(bf16[144,256]{1,0:T(8,128)(2,1)S(1)} %get-tuple-element.44.own_ref.kv_ref), channel_id=1, source_target_pairs={{0,8},{8,0},{16,24},{24,16},{32,40},{40,32},{48,56},{56,48},{64,72... | collective-permute-start | bytes 221192 | tf_op jit(solution)/shard_map/ppermute | solution.py:430
  24.7 2.7 %collective-permute-done.7.other_ref = bf16[144,256]{1,0:T(8,128)(2,1)S(1)} collective-permute-done((bf16[144,256]{1,0:T(8,128)(2,1)S(1)}, bf16[144,256]{1,0:T(8,128)(2,1)S(1)}, u32[]{:S(2)}, u32[]{:S(2)}) %collective-permute-start.7) | collective-permute-done | bytes 73760 | tf_op jit(solution)/shard_map/ppermute | solution.py:430
  27.4 1.4 %collective-permute-start.11 = (bf16[256,128]{1,0:T(8,128)(2,1)S(1)}, bf16[256,128]{1,0:T(8,128)(2,1)S(1)}, u32[]{:S(2)}, u32[]{:S(2)}) collective-permute-start(bf16[256,128]{1,0:T(8,128)(2,1)S(1)} %get-tuple-element.46.refs_4_), channel_id=1, source_target_pairs={{0,64},{8,72},{16,80},{24,88},{32,96},{40,104},{48,112},{56,120},{... | collective-permute-start | bytes 196616 | tf_op jit(solution)/shard_map/ppermute | solution.py:438
  28.7 2.8 %collective-permute-start.10 = (bf16[272,128]{1,0:T(8,128)(2,1)S(1)}, bf16[272,128]{1,0:T(8,128)(2,1)S(1)}, u32[]{:S(2)}, u32[]{:S(2)}) collective-permute-start(bf16[272,128]{1,0:T(8,128)(2,1)S(1)} %get-tuple-element.45.refs_0_), channel_id=1, source_target_pairs={{0,48},{8,56},{16,32},{24,40},{32,16},{40,24},{48,0},{56,8},{64,11... | collective-permute-start | bytes 208904 | tf_op jit(solution)/shard_map/ppermute | solution.py:437
  31.7 1.7 %collective-permute-start.9 = (bf16[272,128]{1,0:T(8,128)(2,1)S(1)}, bf16[272,128]{1,0:T(8,128)(2,1)S(1)}, u32[]{:S(2)}, u32[]{:S(2)}) collective-permute-start(bf16[272,128]{1,0:T(8,128)(2,1)S(1)} %get-tuple-element.45.refs_0_), channel_id=1, source_target_pairs={{0,32},{8,40},{16,48},{24,56},{32,0},{40,8},{48,16},{56,24},{64,96... | collective-permute-start | bytes 208904 | tf_op jit(solution)/shard_map/ppermute | solution.py:437
  34.1 1.6 %collective-permute-start.13 = (bf16[256,128]{1,0:T(8,128)(2,1)S(1)}, bf16[256,128]{1,0:T(8,128)(2,1)S(1)}, u32[]{:S(2)}, u32[]{:S(2)}) collective-permute-start(bf16[256,128]{1,0:T(8,128)(2,1)S(1)} %get-tuple-element.46.refs_4_), channel_id=1, source_target_pairs={{0,192},{8,200},{16,208},{24,216},{32,224},{40,232},{48,240},{56,2... | collective-permute-start | bytes 196616 | tf_op jit(solution)/shard_map/ppermute | solution.py:438
  35.6 3.6 %collective-permute-done.12.refs_6_ = bf16[256,128]{1,0:T(8,128)(2,1)S(1)} collective-permute-done((bf16[256,128]{1,0:T(8,128)(2,1)S(1)}, bf16[256,128]{1,0:T(8,128)(2,1)S(1)}, u32[]{:S(2)}, u32[]{:S(2)}) %collective-permute-start.12) | collective-permute-done | bytes 65568 | tf_op jit(solution)/shard_map/ppermute | solution.py:438
  39.3 1.5 %collective-permute-start.14 = (bf16[1040,128]{1,0:T(8,128)(2,1)S(1)}, bf16[1040,128]{1,0:T(8,128)(2,1)S(1)}, u32[]{:S(2)}, u32[]{:S(2)}) collective-permute-start(bf16[1040,128]{1,0:T(8,128)(2,1)S(1)} %get-tuple-element.47.refs_1_), channel_id=1, source_target_pairs={{0,64},{8,72},{16,80},{24,88},{32,96},{40,104},{48,112},{56,120},{... | collective-permute-start | bytes 798728 | tf_op jit(solution)/shard_map/ppermute | solution.py:457
  41.1 2.4 %collective-permute-start.16 = (bf16[1040,128]{1,0:T(8,128)(2,1)S(1)}, bf16[1040,128]{1,0:T(8,128)(2,1)S(1)}, u32[]{:S(2)}, u32[]{:S(2)}) collective-permute-start(bf16[1040,128]{1,0:T(8,128)(2,1)S(1)} %get-tuple-element.47.refs_1_), channel_id=1, source_target_pairs={{0,192},{8,200},{16,208},{24,216},{32,224},{40,232},{48,240},{56,2... | collective-permute-start | bytes 798728 | tf_op jit(solution)/shard_map/ppermute | solution.py:457
  43.4 2.5 %collective-permute-start.19 = (bf16[1024,128]{1,0:T(8,128)(2,1)S(1)}, bf16[1024,128]{1,0:T(8,128)(2,1)S(1)}, u32[]{:S(2)}, u32[]{:S(2)}) collective-permute-start(bf16[1024,128]{1,0:T(8,128)(2,1)S(1)} %get-tuple-element.48.refs_3_.refs_4_.refs_2_), channel_id=1, source_target_pairs={{0,48},{8,56},{16,32},{24,40},{32,16},{40,24},{48,0},{56,8},{64,11... | collective-permute-start | bytes 786440 | tf_op jit(solution)/shard_map/ppermute | solution.py:458
  45.9 1.4 %shard_map.97 = (bf16[4,256,128]{2,1,0:T(8,128)(2,1)S(1)}, f32[128,128]{1,0:T(8,128)S(1)}, f32[128,128]{1,0:T(8,128)S(1)}) custom-call(bf16[144,4096]{1,0:T(8,128)(2,1)S(1)} %get-tuple-element.42.x_ref, bf16[4096,512]{1,0:T(8,128)(2,1)S(1)} %copy-done, bf16[16,128]{1,0:T(8,128)(2,1)S(1)} %get-tuple-element.41.refs_11_.code_ref.refs_10_, s32[1,256]{1,0:T(1,128)S(1)} %bitcast.3), custom_call_target="tpu_custom_call" | custom-call | flops 1073741824 | bytes 5242880 | tf_op jit(solution)/shard_map/pallas_call | solution.py:51
  48.6 1.5 %collective-permute-start.17 = (bf16[1024,128]{1,0:T(8,128)(2,1)S(1)}, bf16[1024,128]{1,0:T(8,128)(2,1)S(1)}, u32[]{:S(2)}, u32[]{:S(2)}) collective-permute-start(bf16[1024,128]{1,0:T(8,128)(2,1)S(1)} %get-tuple-element.48.refs_3_.refs_4_.refs_2_), channel_id=1, source_target_pairs={{0,32},{8,40},{16,48},{24,56},{32,0},{40,8},{48,16},{56,24},{64,96... | collective-permute-start | bytes 786440 | tf_op jit(solution)/shard_map/ppermute | solution.py:458
  50.0 1.7 %shard_map.101 = (f32[4,256,128]{2,1,0:T(8,128)S(1)}, f32[4,256,128]{2,1,0:T(8,128)S(1)}, f32[4,256,128]{2,1,0:T(8,128)S(1)}) custom-call(bf16[4,256,128]{2,1,0:T(8,128)(2,1)S(1)} %get-tuple-element.43.q_ref.refs_0_, bf16[1040,128]{1,0:T(8,128)(2,1)S(1)} %get-tuple-element.47.refs_1_, bf16[1040,128]{1,0:T(8,128)(2,1)S(1)} %collective-permute-done.14.refs_2_, ...), custom_call_target="tpu_custom_call" | custom-call | flops 1073741824 | bytes 2097152 | tf_op jit(solution)/shard_map/pallas_call | solution.py:51
  51.7 4.9 %collective-permute-done.19.refs_6_.refs_4_ = bf16[1024,128]{1,0:T(8,128)(2,1)S(1)} collective-permute-done((bf16[1024,128]{1,0:T(8,128)(2,1)S(1)}, bf16[1024,128]{1,0:T(8,128)(2,1)S(1)}, u32[]{:S(2)}, u32[]{:S(2)}) %collective-permute-start.19) | collective-permute-done | bytes 262176 | tf_op jit(solution)/shard_map/ppermute | solution.py:458
  56.6 2.8 %shard_map.102 = (f32[4,256,128]{2,1,0:T(8,128)S(1)}, f32[4,256,128]{2,1,0:T(8,128)S(1)}, f32[4,256,128]{2,1,0:T(8,128)S(1)}) custom-call(bf16[4,256,128]{2,1,0:T(8,128)(2,1)S(1)} %get-tuple-element.43.q_ref.refs_0_, bf16[1040,128]{1,0:T(8,128)(2,1)S(1)} %get-tuple-element.47.refs_1_, bf16[1040,128]{1,0:T(8,128)(2,1)S(1)} %collective-permute-done.14.refs_2_, ...), custom_call_target="tpu_custom_call" | custom-call | flops 2147483648 | bytes 4194304 | tf_op jit(solution)/shard_map/pallas_call | solution.py:51
  59.5 1.5 %shard_map.103 = (f32[4,256,128]{2,1,0:T(8,128)S(1)}, f32[4,256,128]{2,1,0:T(8,128)S(1)}, f32[4,256,128]{2,1,0:T(8,128)S(1)}) custom-call(bf16[4,256,128]{2,1,0:T(8,128)(2,1)S(1)} %get-tuple-element.43.q_ref.refs_0_, bf16[1040,128]{1,0:T(8,128)(2,1)S(1)} %collective-permute-done.15.refs_1_.refs_3_, ...), custom_call_target="tpu_custom_call" | custom-call | flops 1073741824 | bytes 2097152 | tf_op jit(solution)/shard_map/pallas_call | solution.py:51
  61.0 2.5 %shard_map.104 = (bf16[128,512]{1,0:T(8,128)(2,1)}, bf16[128,512]{1,0:T(8,128)(2,1)}) custom-call(bf16[4,256,128]{2,1,0:T(8,128)(2,1)S(1)} %get-tuple-element.43.q_ref.refs_0_, bf16[1040,128]{1,0:T(8,128)(2,1)S(1)} %get-tuple-element.47.refs_1_, bf16[1040,128]{1,0:T(8,128)(2,1)S(1)} %collective-permute-done.14.refs_2_, ...), custom_call_target="tpu_custom_call" | custom-call | flops 2147483648 | bytes 4194304 | tf_op jit(solution)/shard_map/pallas_call | solution.py:51
  (31 shorter events, 3.9 us)
Async XLA Ops:
  0.6 45.3 %copy-start.1 = (s32[256]{0:T(256)S(1)}, s32[256]{0:T(256)}, u32[]{:S(2)}) copy-start(s32[256]{0:T(256)} %param.11) | copy-start | bytes 3076
  0.6 45.3 %copy-start = (bf16[4096,512]{1,0:T(8,128)(2,1)S(1)}, bf16[4096,512]{1,0:T(8,128)(2,1)}, u32[]{:S(2)}) copy-start(bf16[4096,512]{1,0:T(8,128)(2,1)} %wq_ref.1) | copy-start | bytes 12582916
  0.7 11.9 %collective-permute-start.1 = (bf16[128,512]{1,0:T(8,128)(2,1)}, bf16[128,512]{1,0:T(8,128)(2,1)S(1)}, u32[]{:S(2)}, u32[]{:S(2)}) collective-permute-start(bf16[128,512]{1,0:T(8,128)(2,1)} %refs_0_.1), channel_id=1, source_target_pairs={{0,2},{1,3},{2,0},{3,1},{4,6},{5,7},{6,4},{7,5},{8,10},{9,11},{10,... | collective-permute-start | bytes 393224 | tf_op jit(solution)/shard_map/ppermute | solution.py:396
  4.0 14.9 %collective-permute-start.3 = (bf16[128,512]{1,0:T(8,128)(2,1)}, bf16[128,512]{1,0:T(8,128)(2,1)S(1)}, u32[]{:S(2)}, u32[]{:S(2)}) collective-permute-start(bf16[128,512]{1,0:T(8,128)(2,1)} %refs_0_.1), channel_id=1, source_target_pairs={{0,4},{1,5},{2,6},{3,7},{4,0},{5,1},{6,2},{7,3},{8,12},{9,13},{10,... | collective-permute-start | bytes 393224 | tf_op jit(solution)/shard_map/ppermute | solution.py:396
  9.4 11.3 %collective-permute-start.5 = (bf16[128,512]{1,0:T(8,128)(2,1)}, bf16[128,512]{1,0:T(8,128)(2,1)S(1)}, u32[]{:S(2)}, u32[]{:S(2)}) collective-permute-start(bf16[128,512]{1,0:T(8,128)(2,1)} %refs_0_.1), channel_id=1, source_target_pairs={{0,6},{1,7},{2,4},{3,5},{4,2},{5,3},{6,0},{7,1},{8,14},{9,15},{10,... | collective-permute-start | bytes 393224 | tf_op jit(solution)/shard_map/ppermute | solution.py:396
  12.5 8.2 %collective-permute-start = (bf16[128,512]{1,0:T(8,128)(2,1)S(1)}, bf16[128,512]{1,0:T(8,128)(2,1)S(1)}, u32[]{:S(2)}, u32[]{:S(2)}) collective-permute-start(bf16[128,512]{1,0:T(8,128)(2,1)S(1)} %get-tuple-element.35.refs_0_), channel_id=1, source_target_pairs={{0,1},{1,0},{2,3},{3,2},{4,5},{5,4},{6,7},{7,6},{8,9},{9,8},{10,11... | collective-permute-start | bytes 393224 | tf_op jit(solution)/shard_map/ppermute | solution.py:419
  12.6 8.1 %collective-permute-start.2 = (bf16[128,512]{1,0:T(8,128)(2,1)S(1)}, bf16[128,512]{1,0:T(8,128)(2,1)S(1)}, u32[]{:S(2)}, u32[]{:S(2)}) collective-permute-start(bf16[128,512]{1,0:T(8,128)(2,1)S(1)} %collective-permute-done.1.refs_2_), channel_id=1, source_target_pairs={{0,1},{1,0},{2,3},{3,2},{4,5},{5,4},{6,7},{7,6},{8,9},{9,8},{10,11... | collective-permute-start | bytes 393224 | tf_op jit(solution)/shard_map/ppermute | solution.py:419
  18.9 1.8 %collective-permute-start.4 = (bf16[128,512]{1,0:T(8,128)(2,1)S(1)}, bf16[128,512]{1,0:T(8,128)(2,1)S(1)}, u32[]{:S(2)}, u32[]{:S(2)}) collective-permute-start(bf16[128,512]{1,0:T(8,128)(2,1)S(1)} %collective-permute-done.3.refs_4_), channel_id=1, source_target_pairs={{0,1},{1,0},{2,3},{3,2},{4,5},{5,4},{6,7},{7,6},{8,9},{9,8},{10,11... | collective-permute-start | bytes 393224 | tf_op jit(solution)/shard_map/ppermute | solution.py:419
  20.7 1.3 %collective-permute-start.6 = (bf16[128,512]{1,0:T(8,128)(2,1)S(1)}, bf16[128,512]{1,0:T(8,128)(2,1)S(1)}, u32[]{:S(2)}, u32[]{:S(2)}) collective-permute-start(bf16[128,512]{1,0:T(8,128)(2,1)S(1)} %collective-permute-done.5.refs_6_), channel_id=1, source_target_pairs={{0,1},{1,0},{2,3},{3,2},{4,5},{5,4},{6,7},{7,6},{8,9},{9,8},{10,11... | collective-permute-start | bytes 393224 | tf_op jit(solution)/shard_map/ppermute | solution.py:419
  22.9 4.4 %collective-permute-start.7 = (bf16[144,256]{1,0:T(8,128)(2,1)S(1)}, bf16[144,256]{1,0:T(8,128)(2,1)S(1)}, u32[]{:S(2)}, u32[]{:S(2)}) collective-permute-start(bf16[144,256]{1,0:T(8,128)(2,1)S(1)} %get-tuple-element.44.own_ref.kv_ref), channel_id=1, source_target_pairs={{0,8},{8,0},{16,24},{24,16},{32,40},{40,32},{48,56},{56,48},{64,72... | collective-permute-start | bytes 221192 | tf_op jit(solution)/shard_map/ppermute | solution.py:430
  27.4 6.7 %collective-permute-start.11 = (bf16[256,128]{1,0:T(8,128)(2,1)S(1)}, bf16[256,128]{1,0:T(8,128)(2,1)S(1)}, u32[]{:S(2)}, u32[]{:S(2)}) collective-permute-start(bf16[256,128]{1,0:T(8,128)(2,1)S(1)} %get-tuple-element.46.refs_4_), channel_id=1, source_target_pairs={{0,64},{8,72},{16,80},{24,88},{32,96},{40,104},{48,112},{56,120},{... | collective-permute-start | bytes 196616 | tf_op jit(solution)/shard_map/ppermute | solution.py:438
  28.7 10.5 %collective-permute-start.10 = (bf16[272,128]{1,0:T(8,128)(2,1)S(1)}, bf16[272,128]{1,0:T(8,128)(2,1)S(1)}, u32[]{:S(2)}, u32[]{:S(2)}) collective-permute-start(bf16[272,128]{1,0:T(8,128)(2,1)S(1)} %get-tuple-element.45.refs_0_), channel_id=1, source_target_pairs={{0,48},{8,56},{16,32},{24,40},{32,16},{40,24},{48,0},{56,8},{64,11... | collective-permute-start | bytes 208904 | tf_op jit(solution)/shard_map/ppermute | solution.py:437
  31.5 7.7 %collective-permute-start.8 = (bf16[272,128]{1,0:T(8,128)(2,1)S(1)}, bf16[272,128]{1,0:T(8,128)(2,1)S(1)}, u32[]{:S(2)}, u32[]{:S(2)}) collective-permute-start(bf16[272,128]{1,0:T(8,128)(2,1)S(1)} %get-tuple-element.45.refs_0_), channel_id=1, source_target_pairs={{0,16},{8,24},{16,0},{24,8},{32,48},{40,56},{48,32},{56,40},{64,80... | collective-permute-start | bytes 208904 | tf_op jit(solution)/shard_map/ppermute | solution.py:437
  31.7 7.5 %collective-permute-start.9 = (bf16[272,128]{1,0:T(8,128)(2,1)S(1)}, bf16[272,128]{1,0:T(8,128)(2,1)S(1)}, u32[]{:S(2)}, u32[]{:S(2)}) collective-permute-start(bf16[272,128]{1,0:T(8,128)(2,1)S(1)} %get-tuple-element.45.refs_0_), channel_id=1, source_target_pairs={{0,32},{8,40},{16,48},{24,56},{32,0},{40,8},{48,16},{56,24},{64,96... | collective-permute-start | bytes 208904 | tf_op jit(solution)/shard_map/ppermute | solution.py:437
  33.4 5.8 %collective-permute-start.12 = (bf16[256,128]{1,0:T(8,128)(2,1)S(1)}, bf16[256,128]{1,0:T(8,128)(2,1)S(1)}, u32[]{:S(2)}, u32[]{:S(2)}) collective-permute-start(bf16[256,128]{1,0:T(8,128)(2,1)S(1)} %get-tuple-element.46.refs_4_), channel_id=1, source_target_pairs={{0,128},{8,136},{16,144},{24,152},{32,160},{40,168},{48,176},{56,1... | collective-permute-start | bytes 196616 | tf_op jit(solution)/shard_map/ppermute | solution.py:438
  34.1 5.1 %collective-permute-start.13 = (bf16[256,128]{1,0:T(8,128)(2,1)S(1)}, bf16[256,128]{1,0:T(8,128)(2,1)S(1)}, u32[]{:S(2)}, u32[]{:S(2)}) collective-permute-start(bf16[256,128]{1,0:T(8,128)(2,1)S(1)} %get-tuple-element.46.refs_4_), channel_id=1, source_target_pairs={{0,192},{8,200},{16,208},{24,216},{32,224},{40,232},{48,240},{56,2... | collective-permute-start | bytes 196616 | tf_op jit(solution)/shard_map/ppermute | solution.py:438
  39.3 10.8 %collective-permute-start.14 = (bf16[1040,128]{1,0:T(8,128)(2,1)S(1)}, bf16[1040,128]{1,0:T(8,128)(2,1)S(1)}, u32[]{:S(2)}, u32[]{:S(2)}) collective-permute-start(bf16[1040,128]{1,0:T(8,128)(2,1)S(1)} %get-tuple-element.47.refs_1_), channel_id=1, source_target_pairs={{0,64},{8,72},{16,80},{24,88},{32,96},{40,104},{48,112},{56,120},{... | collective-permute-start | bytes 798728 | tf_op jit(solution)/shard_map/ppermute | solution.py:457
  40.8 7.8 %collective-permute-start.18 = (bf16[1024,128]{1,0:T(8,128)(2,1)S(1)}, bf16[1024,128]{1,0:T(8,128)(2,1)S(1)}, u32[]{:S(2)}, u32[]{:S(2)}) collective-permute-start(bf16[1024,128]{1,0:T(8,128)(2,1)S(1)} %get-tuple-element.48.refs_3_.refs_4_.refs_2_), channel_id=1, source_target_pairs={{0,16},{8,24},{16,0},{24,8},{32,48},{40,56},{48,32},{56,40},{64,80... | collective-permute-start | bytes 786440 | tf_op jit(solution)/shard_map/ppermute | solution.py:458
  41.1 15.6 %collective-permute-start.16 = (bf16[1040,128]{1,0:T(8,128)(2,1)S(1)}, bf16[1040,128]{1,0:T(8,128)(2,1)S(1)}, u32[]{:S(2)}, u32[]{:S(2)}) collective-permute-start(bf16[1040,128]{1,0:T(8,128)(2,1)S(1)} %get-tuple-element.47.refs_1_), channel_id=1, source_target_pairs={{0,192},{8,200},{16,208},{24,216},{32,224},{40,232},{48,240},{56,2... | collective-permute-start | bytes 798728 | tf_op jit(solution)/shard_map/ppermute | solution.py:457
  43.4 13.2 %collective-permute-start.19 = (bf16[1024,128]{1,0:T(8,128)(2,1)S(1)}, bf16[1024,128]{1,0:T(8,128)(2,1)S(1)}, u32[]{:S(2)}, u32[]{:S(2)}) collective-permute-start(bf16[1024,128]{1,0:T(8,128)(2,1)S(1)} %get-tuple-element.48.refs_3_.refs_4_.refs_2_), channel_id=1, source_target_pairs={{0,48},{8,56},{16,32},{24,40},{32,16},{40,24},{48,0},{56,8},{64,11... | collective-permute-start | bytes 786440 | tf_op jit(solution)/shard_map/ppermute | solution.py:458
  48.2 11.3 %collective-permute-start.15 = (bf16[1040,128]{1,0:T(8,128)(2,1)S(1)}, bf16[1040,128]{1,0:T(8,128)(2,1)S(1)}, u32[]{:S(2)}, u32[]{:S(2)}) collective-permute-start(bf16[1040,128]{1,0:T(8,128)(2,1)S(1)} %get-tuple-element.47.refs_1_), channel_id=1, source_target_pairs={{0,128},{8,136},{16,144},{24,152},{32,160},{40,168},{48,176},{56,1... | collective-permute-start | bytes 798728 | tf_op jit(solution)/shard_map/ppermute | solution.py:457
  48.6 12.4 %collective-permute-start.17 = (bf16[1024,128]{1,0:T(8,128)(2,1)S(1)}, bf16[1024,128]{1,0:T(8,128)(2,1)S(1)}, u32[]{:S(2)}, u32[]{:S(2)}) collective-permute-start(bf16[1024,128]{1,0:T(8,128)(2,1)S(1)} %get-tuple-element.48.refs_3_.refs_4_.refs_2_), channel_id=1, source_target_pairs={{0,32},{8,40},{16,48},{24,56},{32,0},{40,8},{48,16},{56,24},{64,96... | collective-permute-start | bytes 786440 | tf_op jit(solution)/shard_map/ppermute | solution.py:458

commit v13 on v12

--- a/solution.py
+++ b/solution.py
@@ -184,7 +184,7 @@
         top = jnp.max(scores, axis=1, keepdims=True)
         probs = jnp.exp2((scores - top) * POWER)
         top_ref[h] = jnp.broadcast_to(top, (2 * ROWS, HEAD))
-        total_ref[h] = probs[:, :HEAD] + probs[:, HEAD:]
+        total_ref[h] = jnp.broadcast_to(jnp.sum(probs, axis=1, keepdims=True), (2 * ROWS, HEAD))
         accum_ref[h] = dot(probs.astype(BF16), values)
 
 
@@ -218,11 +218,11 @@
         factor = jnp.exp2((old - top) * POWER)
         level = top if seen is None else jnp.where(seen, top, -LOW)
         probs = [jnp.exp2((part - level) * POWER) for part in parts]
-        total = source[1][h] * factor
-        for part in probs:
-            total = total + part
         probs = jnp.concatenate([part.astype(BF16) for part in probs], axis=1)
-        accum = source[2][h] * factor + dot(probs, values())
+        right = values()
+        product = dot(probs, jnp.concatenate([right, jnp.ones(right.shape, BF16)], axis=1))
+        total = source[1][h] * factor + product[:, HEAD:]
+        accum = source[2][h] * factor + product[:, :HEAD]
         if last and finish is not None:
             finish(h, accum, total)
         else:
@@ -269,7 +269,7 @@
 def first_kernel(*refs):
     q_ref = refs[0]
     k_of, v_of = dict(zip((0, 1), refs[1:3])), dict(zip((0, 1), refs[3:5]))
-    piece = spots_piece(place(), k_of, v_of, ((0, 0), (0, 1), (1, 0), (1, 1)))
+    piece = spots_piece(place(), k_of, v_of, ((0, 1), (1, 0), (1, 1)))
     pipeline(q_ref, [piece], refs[5:8], refs[8:11], None)
 
 
@@ -369,7 +369,8 @@
     q_ref, k_ref, v_refs = refs[0], refs[1], refs[2:5]
     where = place()
     near = (0, 1, 3)
-    piece = spots_piece(where, {2: k_ref}, dict(zip(near, v_refs)), [(2, dx) for dx in near])
+    keys, values, _, _ = spots_piece(where, {2: k_ref}, dict(zip(near, v_refs)), [(2, dx) for dx in near])
+    piece = (keys, values, None, where[1] >= 2)
     pipeline(q_ref, [piece], refs[5:8], refs[8:11], None)
 
 
@@ -382,7 +383,7 @@
 
     def finish(h, accum, total):
         lanes = slice(h * HEAD, (h + 1) * HEAD)
-        result = (accum / jnp.sum(total, axis=1, keepdims=True)).astype(BF16)
+        result = (accum / total).astype(BF16)
         clean_ref[:, lanes] = result[:ROWS]
         noisy_ref[:, lanes] = result[ROWS:]
 

time: 63.6 us -> 63 us (level)
  Pallas kernels: 13.3 us -> 12.4 us
    pallas_call x10, Pallas kernels: 13.3 us -> 12.4 us  [call(): pl.pallas_call(kernel, out_shape=[jax.ShapeDtypeStruct(s, t) for s, t in...]
  transfers between devices with their start and end apart: 20 -> 20, of which waited for: 6 -> 6; matrix products, arithmetic and copies ran while one was open for 2% -> 2% of each run, Pallas kernels for 16% -> 15%
where the time goes in v13:
time: 63 us; the launch traced here: 62.9 us
  starting transfers between devices  27.9 us (44%)
  waiting for transfers between devices  20.4 us (32%)
  Pallas kernels  12.4 us (20%)
  local copies, waits for them, and re-layouts  1.32 us (2%)
  between operations  0.78 us (1%)
    pallas_call x10, Pallas kernels, call(): pl.pallas_call(kernel, out_shape=[jax.ShapeDtypeStruct(s, t) for s, t in...  12.4 us
    ppermute x3, starting transfers between devices, shards(): moved = [lax.ppermute(hidden, 'kv', kv_pairs(d, 0)) for d in (1, 2, 3)]  8.75 us
    ppermute x3, waiting for transfers between devices, shards(): moved = [lax.ppermute(hidden, 'kv', kv_pairs(d, 0)) for d in (1, 2, 3)]  7.63 us
    ppermute x3, waiting for transfers between devices, shards(): lax.ppermute(vs, 'ctx', ctx_pairs(0, d, 0))  5.25 us
    ppermute x3, starting transfers between devices, shards(): ks = [lax.ppermute(k, 'ctx', ctx_pairs(0, d, 0)) for d in (1, 2, 3)]  4.7 us
    ppermute x3, starting transfers between devices, shards(): lax.ppermute(ks, 'ctx', ctx_pairs(d, 0, 0))  4.27 us
    ppermute x3, starting transfers between devices, shards(): lax.ppermute(vs, 'ctx', ctx_pairs(0, d, 0))  4.23 us
    ppermute x3, starting transfers between devices, shards(): vs = [lax.ppermute(v, 'ctx', ctx_pairs(d, 0, 0)) for d in (1, 2, 3)]  3.58 us
  transfers between devices with their start and end apart: 20, of which 6 were waited for; matrix products, arithmetic and copies ran while one was open for 2% of the time, Pallas kernels for 15%

profile of v13, /device:TPU:16, one launch (start us, length us, event | category | flops | bytes accessed | tf_op | source)
XLA Modules:
  0.0 62.9 jit_solution(7295954792200829537)
XLA Ops:
  0.7 3.4 %collective-permute-start.1 = (bf16[128,512]{1,0:T(8,128)(2,1)}, bf16[128,512]{1,0:T(8,128)(2,1)S(1)}, u32[]{:S(2)}, u32[]{:S(2)}) collective-permute-start(bf16[128,512]{1,0:T(8,128)(2,1)} %refs_0_.1), channel_id=1, source_target_pairs={{0,2},{1,3},{2,0},{3,1},{4,6},{5,7},{6,4},{7,5},{8,10},{9,11},{10,... | collective-permute-start | bytes 393224 | tf_op jit(solution)/shard_map/ppermute | solution.py:397
  4.0 5.4 %collective-permute-start.3 = (bf16[128,512]{1,0:T(8,128)(2,1)}, bf16[128,512]{1,0:T(8,128)(2,1)S(1)}, u32[]{:S(2)}, u32[]{:S(2)}) collective-permute-start(bf16[128,512]{1,0:T(8,128)(2,1)} %refs_0_.1), channel_id=1, source_target_pairs={{0,4},{1,5},{2,6},{3,7},{4,0},{5,1},{6,2},{7,3},{8,12},{9,13},{10,... | collective-permute-start | bytes 393224 | tf_op jit(solution)/shard_map/ppermute | solution.py:397
  9.4 1.3 %reshape.18.refs_5_ = bf16[1,4096]{1,0:T(2,128)(2,1)} reshape(bf16[4096]{0:T(1024)(128)(2,1)} %param.12) | data formatting | bytes 16384 | tf_op jit(solution)/shard_map/reshape | solution.py:407
  10.7 1.7 %shard_map.95 = (bf16[128,512]{1,0:T(8,128)(2,1)S(1)}, bf16[4096,128]{1,0:T(8,128)(2,1)S(1)}, bf16[4096,128]{1,0:T(8,128)(2,1)S(1)}, bf16[16,128]{1,0:T(8,128)(2,1)S(1)}, bf16[16,4096]{1,0:T(8,128)(2,1)S(1)}) custom-call(bf16[128,512]{1,0:T(8,128)(2,1)} %refs_0_.1, bf16[4096,128]{1,0:T(8,128)(2,1)} %refs_1_.1, bf16[4096,128]{1,0:T(8,128)(2,1)} %refs_2_.1, ...), custom_call_target="tpu_custom_call" | custom-call | flops 1048576 | bytes 4194304 | tf_op jit(solution)/shard_map/pallas_call | solution.py:51
  13.1 5.9 %collective-permute-done.3.refs_4_ = bf16[128,512]{1,0:T(8,128)(2,1)S(1)} collective-permute-done((bf16[128,512]{1,0:T(8,128)(2,1)}, bf16[128,512]{1,0:T(8,128)(2,1)S(1)}, u32[]{:S(2)}, u32[]{:S(2)}) %collective-permute-start.3) | collective-permute-done | bytes 131104 | tf_op jit(solution)/shard_map/ppermute | solution.py:397
  18.9 1.8 %collective-permute-done.5.refs_6_ = bf16[128,512]{1,0:T(8,128)(2,1)S(1)} collective-permute-done((bf16[128,512]{1,0:T(8,128)(2,1)}, bf16[128,512]{1,0:T(8,128)(2,1)S(1)}, u32[]{:S(2)}, u32[]{:S(2)}) %collective-permute-start.5) | collective-permute-done | bytes 131104 | tf_op jit(solution)/shard_map/ppermute | solution.py:397
  20.7 1.3 %collective-permute-done.6.refs_7_ = bf16[128,512]{1,0:T(8,128)(2,1)S(1)} collective-permute-done((bf16[128,512]{1,0:T(8,128)(2,1)S(1)}, bf16[128,512]{1,0:T(8,128)(2,1)S(1)}, u32[]{:S(2)}, u32[]{:S(2)}) %collective-permute-start.6) | collective-permute-done | bytes 131104 | tf_op jit(solution)/shard_map/ppermute | solution.py:420
  22.9 1.8 %collective-permute-start.7 = (bf16[144,256]{1,0:T(8,128)(2,1)S(1)}, bf16[144,256]{1,0:T(8,128)(2,1)S(1)}, u32[]{:S(2)}, u32[]{:S(2)}) collective-permute-start(bf16[144,256]{1,0:T(8,128)(2,1)S(1)} %get-tuple-element.44.own_ref.kv_ref), channel_id=1, source_target_pairs={{0,8},{8,0},{16,24},{24,16},{32,40},{40,32},{48,56},{56,48},{64,72... | collective-permute-start | bytes 221192 | tf_op jit(solution)/shard_map/ppermute | solution.py:431
  24.7 2.7 %collective-permute-done.7.other_ref = bf16[144,256]{1,0:T(8,128)(2,1)S(1)} collective-permute-done((bf16[144,256]{1,0:T(8,128)(2,1)S(1)}, bf16[144,256]{1,0:T(8,128)(2,1)S(1)}, u32[]{:S(2)}, u32[]{:S(2)}) %collective-permute-start.7) | collective-permute-done | bytes 73760 | tf_op jit(solution)/shard_map/ppermute | solution.py:431
  27.4 1.4 %collective-permute-start.11 = (bf16[256,128]{1,0:T(8,128)(2,1)S(1)}, bf16[256,128]{1,0:T(8,128)(2,1)S(1)}, u32[]{:S(2)}, u32[]{:S(2)}) collective-permute-start(bf16[256,128]{1,0:T(8,128)(2,1)S(1)} %get-tuple-element.46.refs_4_), channel_id=1, source_target_pairs={{0,64},{8,72},{16,80},{24,88},{32,96},{40,104},{48,112},{56,120},{... | collective-permute-start | bytes 196616 | tf_op jit(solution)/shard_map/ppermute | solution.py:439
  28.7 2.8 %collective-permute-start.10 = (bf16[272,128]{1,0:T(8,128)(2,1)S(1)}, bf16[272,128]{1,0:T(8,128)(2,1)S(1)}, u32[]{:S(2)}, u32[]{:S(2)}) collective-permute-start(bf16[272,128]{1,0:T(8,128)(2,1)S(1)} %get-tuple-element.45.refs_0_), channel_id=1, source_target_pairs={{0,48},{8,56},{16,32},{24,40},{32,16},{40,24},{48,0},{56,8},{64,11... | collective-permute-start | bytes 208904 | tf_op jit(solution)/shard_map/ppermute | solution.py:438
  31.7 1.7 %collective-permute-start.9 = (bf16[272,128]{1,0:T(8,128)(2,1)S(1)}, bf16[272,128]{1,0:T(8,128)(2,1)S(1)}, u32[]{:S(2)}, u32[]{:S(2)}) collective-permute-start(bf16[272,128]{1,0:T(8,128)(2,1)S(1)} %get-tuple-element.45.refs_0_), channel_id=1, source_target_pairs={{0,32},{8,40},{16,48},{24,56},{32,0},{40,8},{48,16},{56,24},{64,96... | collective-permute-start | bytes 208904 | tf_op jit(solution)/shard_map/ppermute | solution.py:438
  34.1 1.6 %collective-permute-start.13 = (bf16[256,128]{1,0:T(8,128)(2,1)S(1)}, bf16[256,128]{1,0:T(8,128)(2,1)S(1)}, u32[]{:S(2)}, u32[]{:S(2)}) collective-permute-start(bf16[256,128]{1,0:T(8,128)(2,1)S(1)} %get-tuple-element.46.refs_4_), channel_id=1, source_target_pairs={{0,192},{8,200},{16,208},{24,216},{32,224},{40,232},{48,240},{56,2... | collective-permute-start | bytes 196616 | tf_op jit(solution)/shard_map/ppermute | solution.py:439
  35.6 3.6 %collective-permute-done.12.refs_6_ = bf16[256,128]{1,0:T(8,128)(2,1)S(1)} collective-permute-done((bf16[256,128]{1,0:T(8,128)(2,1)S(1)}, bf16[256,128]{1,0:T(8,128)(2,1)S(1)}, u32[]{:S(2)}, u32[]{:S(2)}) %collective-permute-start.12) | collective-permute-done | bytes 65568 | tf_op jit(solution)/shard_map/ppermute | solution.py:439
  39.3 1.5 %collective-permute-start.14 = (bf16[1040,128]{1,0:T(8,128)(2,1)S(1)}, bf16[1040,128]{1,0:T(8,128)(2,1)S(1)}, u32[]{:S(2)}, u32[]{:S(2)}) collective-permute-start(bf16[1040,128]{1,0:T(8,128)(2,1)S(1)} %get-tuple-element.47.refs_1_), channel_id=1, source_target_pairs={{0,64},{8,72},{16,80},{24,88},{32,96},{40,104},{48,112},{56,120},{... | collective-permute-start | bytes 798728 | tf_op jit(solution)/shard_map/ppermute | solution.py:458
  41.1 2.4 %collective-permute-start.16 = (bf16[1040,128]{1,0:T(8,128)(2,1)S(1)}, bf16[1040,128]{1,0:T(8,128)(2,1)S(1)}, u32[]{:S(2)}, u32[]{:S(2)}) collective-permute-start(bf16[1040,128]{1,0:T(8,128)(2,1)S(1)} %get-tuple-element.47.refs_1_), channel_id=1, source_target_pairs={{0,192},{8,200},{16,208},{24,216},{32,224},{40,232},{48,240},{56,2... | collective-permute-start | bytes 798728 | tf_op jit(solution)/shard_map/ppermute | solution.py:458
  43.4 2.5 %collective-permute-start.19 = (bf16[1024,128]{1,0:T(8,128)(2,1)S(1)}, bf16[1024,128]{1,0:T(8,128)(2,1)S(1)}, u32[]{:S(2)}, u32[]{:S(2)}) collective-permute-start(bf16[1024,128]{1,0:T(8,128)(2,1)S(1)} %get-tuple-element.48.refs_3_.refs_4_.refs_2_), channel_id=1, source_target_pairs={{0,48},{8,56},{16,32},{24,40},{32,16},{40,24},{48,0},{56,8},{64,11... | collective-permute-start | bytes 786440 | tf_op jit(solution)/shard_map/ppermute | solution.py:459
  45.9 1.4 %shard_map.97 = (bf16[4,256,128]{2,1,0:T(8,128)(2,1)S(1)}, f32[128,128]{1,0:T(8,128)S(1)}, f32[128,128]{1,0:T(8,128)S(1)}) custom-call(bf16[144,4096]{1,0:T(8,128)(2,1)S(1)} %get-tuple-element.42.x_ref, bf16[4096,512]{1,0:T(8,128)(2,1)S(1)} %copy-done, bf16[16,128]{1,0:T(8,128)(2,1)S(1)} %get-tuple-element.41.refs_11_.code_ref.refs_10_, s32[1,256]{1,0:T(1,128)S(1)} %bitcast.3), custom_call_target="tpu_custom_call" | custom-call | flops 1073741824 | bytes 5242880 | tf_op jit(solution)/shard_map/pallas_call | solution.py:51
  48.6 1.5 %collective-permute-start.17 = (bf16[1024,128]{1,0:T(8,128)(2,1)S(1)}, bf16[1024,128]{1,0:T(8,128)(2,1)S(1)}, u32[]{:S(2)}, u32[]{:S(2)}) collective-permute-start(bf16[1024,128]{1,0:T(8,128)(2,1)S(1)} %get-tuple-element.48.refs_3_.refs_4_.refs_2_), channel_id=1, source_target_pairs={{0,32},{8,40},{16,48},{24,56},{32,0},{40,8},{48,16},{56,24},{64,96... | collective-permute-start | bytes 786440 | tf_op jit(solution)/shard_map/ppermute | solution.py:459
  50.0 1.3 %shard_map.101 = (f32[4,256,128]{2,1,0:T(8,128)S(1)}, f32[4,256,128]{2,1,0:T(8,128)S(1)}, f32[4,256,128]{2,1,0:T(8,128)S(1)}) custom-call(bf16[4,256,128]{2,1,0:T(8,128)(2,1)S(1)} %get-tuple-element.43.q_ref.refs_0_, bf16[1040,128]{1,0:T(8,128)(2,1)S(1)} %get-tuple-element.47.refs_1_, bf16[1040,128]{1,0:T(8,128)(2,1)S(1)} %collective-permute-done.14.refs_2_, ...), custom_call_target="tpu_custom_call" | custom-call | flops 1073741824 | bytes 2097152 | tf_op jit(solution)/shard_map/pallas_call | solution.py:51
  51.4 5.2 %collective-permute-done.19.refs_6_.refs_4_ = bf16[1024,128]{1,0:T(8,128)(2,1)S(1)} collective-permute-done((bf16[1024,128]{1,0:T(8,128)(2,1)S(1)}, bf16[1024,128]{1,0:T(8,128)(2,1)S(1)}, u32[]{:S(2)}, u32[]{:S(2)}) %collective-permute-start.19) | collective-permute-done | bytes 262176 | tf_op jit(solution)/shard_map/ppermute | solution.py:459
  56.6 2.6 %shard_map.102 = (f32[4,256,128]{2,1,0:T(8,128)S(1)}, f32[4,256,128]{2,1,0:T(8,128)S(1)}, f32[4,256,128]{2,1,0:T(8,128)S(1)}) custom-call(bf16[4,256,128]{2,1,0:T(8,128)(2,1)S(1)} %get-tuple-element.43.q_ref.refs_0_, bf16[1040,128]{1,0:T(8,128)(2,1)S(1)} %get-tuple-element.47.refs_1_, bf16[1040,128]{1,0:T(8,128)(2,1)S(1)} %collective-permute-done.14.refs_2_, ...), custom_call_target="tpu_custom_call" | custom-call | flops 2147483648 | bytes 4194304 | tf_op jit(solution)/shard_map/pallas_call | solution.py:51
  59.3 1.3 %shard_map.103 = (f32[4,256,128]{2,1,0:T(8,128)S(1)}, f32[4,256,128]{2,1,0:T(8,128)S(1)}, f32[4,256,128]{2,1,0:T(8,128)S(1)}) custom-call(bf16[4,256,128]{2,1,0:T(8,128)(2,1)S(1)} %get-tuple-element.43.q_ref.refs_0_, bf16[1040,128]{1,0:T(8,128)(2,1)S(1)} %collective-permute-done.15.refs_1_.refs_3_, ...), custom_call_target="tpu_custom_call" | custom-call | flops 1073741824 | bytes 2097152 | tf_op jit(solution)/shard_map/pallas_call | solution.py:51
  60.6 2.3 %shard_map.104 = (bf16[128,512]{1,0:T(8,128)(2,1)}, bf16[128,512]{1,0:T(8,128)(2,1)}) custom-call(bf16[4,256,128]{2,1,0:T(8,128)(2,1)S(1)} %get-tuple-element.43.q_ref.refs_0_, bf16[1040,128]{1,0:T(8,128)(2,1)S(1)} %get-tuple-element.47.refs_1_, bf16[1040,128]{1,0:T(8,128)(2,1)S(1)} %collective-permute-done.14.refs_2_, ...), custom_call_target="tpu_custom_call" | custom-call | flops 2147483648 | bytes 4194304 | tf_op jit(solution)/shard_map/pallas_call | solution.py:51
  (31 shorter events, 3.9 us)
Async XLA Ops:
  0.6 45.3 %copy-start.1 = (s32[256]{0:T(256)S(1)}, s32[256]{0:T(256)}, u32[]{:S(2)}) copy-start(s32[256]{0:T(256)} %param.11) | copy-start | bytes 3076
  0.6 45.3 %copy-start = (bf16[4096,512]{1,0:T(8,128)(2,1)S(1)}, bf16[4096,512]{1,0:T(8,128)(2,1)}, u32[]{:S(2)}) copy-start(bf16[4096,512]{1,0:T(8,128)(2,1)} %wq_ref.1) | copy-start | bytes 12582916
  0.7 11.9 %collective-permute-start.1 = (bf16[128,512]{1,0:T(8,128)(2,1)}, bf16[128,512]{1,0:T(8,128)(2,1)S(1)}, u32[]{:S(2)}, u32[]{:S(2)}) collective-permute-start(bf16[128,512]{1,0:T(8,128)(2,1)} %refs_0_.1), channel_id=1, source_target_pairs={{0,2},{1,3},{2,0},{3,1},{4,6},{5,7},{6,4},{7,5},{8,10},{9,11},{10,... | collective-permute-start | bytes 393224 | tf_op jit(solution)/shard_map/ppermute | solution.py:397
  4.0 14.9 %collective-permute-start.3 = (bf16[128,512]{1,0:T(8,128)(2,1)}, bf16[128,512]{1,0:T(8,128)(2,1)S(1)}, u32[]{:S(2)}, u32[]{:S(2)}) collective-permute-start(bf16[128,512]{1,0:T(8,128)(2,1)} %refs_0_.1), channel_id=1, source_target_pairs={{0,4},{1,5},{2,6},{3,7},{4,0},{5,1},{6,2},{7,3},{8,12},{9,13},{10,... | collective-permute-start | bytes 393224 | tf_op jit(solution)/shard_map/ppermute | solution.py:397
  9.4 11.3 %collective-permute-start.5 = (bf16[128,512]{1,0:T(8,128)(2,1)}, bf16[128,512]{1,0:T(8,128)(2,1)S(1)}, u32[]{:S(2)}, u32[]{:S(2)}) collective-permute-start(bf16[128,512]{1,0:T(8,128)(2,1)} %refs_0_.1), channel_id=1, source_target_pairs={{0,6},{1,7},{2,4},{3,5},{4,2},{5,3},{6,0},{7,1},{8,14},{9,15},{10,... | collective-permute-start | bytes 393224 | tf_op jit(solution)/shard_map/ppermute | solution.py:397
  12.5 8.2 %collective-permute-start = (bf16[128,512]{1,0:T(8,128)(2,1)S(1)}, bf16[128,512]{1,0:T(8,128)(2,1)S(1)}, u32[]{:S(2)}, u32[]{:S(2)}) collective-permute-start(bf16[128,512]{1,0:T(8,128)(2,1)S(1)} %get-tuple-element.35.refs_0_), channel_id=1, source_target_pairs={{0,1},{1,0},{2,3},{3,2},{4,5},{5,4},{6,7},{7,6},{8,9},{9,8},{10,11... | collective-permute-start | bytes 393224 | tf_op jit(solution)/shard_map/ppermute | solution.py:420
  12.6 8.1 %collective-permute-start.2 = (bf16[128,512]{1,0:T(8,128)(2,1)S(1)}, bf16[128,512]{1,0:T(8,128)(2,1)S(1)}, u32[]{:S(2)}, u32[]{:S(2)}) collective-permute-start(bf16[128,512]{1,0:T(8,128)(2,1)S(1)} %collective-permute-done.1.refs_2_), channel_id=1, source_target_pairs={{0,1},{1,0},{2,3},{3,2},{4,5},{5,4},{6,7},{7,6},{8,9},{9,8},{10,11... | collective-permute-start | bytes 393224 | tf_op jit(solution)/shard_map/ppermute | solution.py:420
  18.9 1.8 %collective-permute-start.4 = (bf16[128,512]{1,0:T(8,128)(2,1)S(1)}, bf16[128,512]{1,0:T(8,128)(2,1)S(1)}, u32[]{:S(2)}, u32[]{:S(2)}) collective-permute-start(bf16[128,512]{1,0:T(8,128)(2,1)S(1)} %collective-permute-done.3.refs_4_), channel_id=1, source_target_pairs={{0,1},{1,0},{2,3},{3,2},{4,5},{5,4},{6,7},{7,6},{8,9},{9,8},{10,11... | collective-permute-start | bytes 393224 | tf_op jit(solution)/shard_map/ppermute | solution.py:420
  20.7 1.3 %collective-permute-start.6 = (bf16[128,512]{1,0:T(8,128)(2,1)S(1)}, bf16[128,512]{1,0:T(8,128)(2,1)S(1)}, u32[]{:S(2)}, u32[]{:S(2)}) collective-permute-start(bf16[128,512]{1,0:T(8,128)(2,1)S(1)} %collective-permute-done.5.refs_6_), channel_id=1, source_target_pairs={{0,1},{1,0},{2,3},{3,2},{4,5},{5,4},{6,7},{7,6},{8,9},{9,8},{10,11... | collective-permute-start | bytes 393224 | tf_op jit(solution)/shard_map/ppermute | solution.py:420
  22.9 4.4 %collective-permute-start.7 = (bf16[144,256]{1,0:T(8,128)(2,1)S(1)}, bf16[144,256]{1,0:T(8,128)(2,1)S(1)}, u32[]{:S(2)}, u32[]{:S(2)}) collective-permute-start(bf16[144,256]{1,0:T(8,128)(2,1)S(1)} %get-tuple-element.44.own_ref.kv_ref), channel_id=1, source_target_pairs={{0,8},{8,0},{16,24},{24,16},{32,40},{40,32},{48,56},{56,48},{64,72... | collective-permute-start | bytes 221192 | tf_op jit(solution)/shard_map/ppermute | solution.py:431
  27.4 6.7 %collective-permute-start.11 = (bf16[256,128]{1,0:T(8,128)(2,1)S(1)}, bf16[256,128]{1,0:T(8,128)(2,1)S(1)}, u32[]{:S(2)}, u32[]{:S(2)}) collective-permute-start(bf16[256,128]{1,0:T(8,128)(2,1)S(1)} %get-tuple-element.46.refs_4_), channel_id=1, source_target_pairs={{0,64},{8,72},{16,80},{24,88},{32,96},{40,104},{48,112},{56,120},{... | collective-permute-start | bytes 196616 | tf_op jit(solution)/shard_map/ppermute | solution.py:439
  28.7 10.5 %collective-permute-start.10 = (bf16[272,128]{1,0:T(8,128)(2,1)S(1)}, bf16[272,128]{1,0:T(8,128)(2,1)S(1)}, u32[]{:S(2)}, u32[]{:S(2)}) collective-permute-start(bf16[272,128]{1,0:T(8,128)(2,1)S(1)} %get-tuple-element.45.refs_0_), channel_id=1, source_target_pairs={{0,48},{8,56},{16,32},{24,40},{32,16},{40,24},{48,0},{56,8},{64,11... | collective-permute-start | bytes 208904 | tf_op jit(solution)/shard_map/ppermute | solution.py:438
  31.5 7.7 %collective-permute-start.8 = (bf16[272,128]{1,0:T(8,128)(2,1)S(1)}, bf16[272,128]{1,0:T(8,128)(2,1)S(1)}, u32[]{:S(2)}, u32[]{:S(2)}) collective-permute-start(bf16[272,128]{1,0:T(8,128)(2,1)S(1)} %get-tuple-element.45.refs_0_), channel_id=1, source_target_pairs={{0,16},{8,24},{16,0},{24,8},{32,48},{40,56},{48,32},{56,40},{64,80... | collective-permute-start | bytes 208904 | tf_op jit(solution)/shard_map/ppermute | solution.py:438
  31.7 7.5 %collective-permute-start.9 = (bf16[272,128]{1,0:T(8,128)(2,1)S(1)}, bf16[272,128]{1,0:T(8,128)(2,1)S(1)}, u32[]{:S(2)}, u32[]{:S(2)}) collective-permute-start(bf16[272,128]{1,0:T(8,128)(2,1)S(1)} %get-tuple-element.45.refs_0_), channel_id=1, source_target_pairs={{0,32},{8,40},{16,48},{24,56},{32,0},{40,8},{48,16},{56,24},{64,96... | collective-permute-start | bytes 208904 | tf_op jit(solution)/shard_map/ppermute | solution.py:438
  33.4 5.8 %collective-permute-start.12 = (bf16[256,128]{1,0:T(8,128)(2,1)S(1)}, bf16[256,128]{1,0:T(8,128)(2,1)S(1)}, u32[]{:S(2)}, u32[]{:S(2)}) collective-permute-start(bf16[256,128]{1,0:T(8,128)(2,1)S(1)} %get-tuple-element.46.refs_4_), channel_id=1, source_target_pairs={{0,128},{8,136},{16,144},{24,152},{32,160},{40,168},{48,176},{56,1... | collective-permute-start | bytes 196616 | tf_op jit(solution)/shard_map/ppermute | solution.py:439
  34.1 5.1 %collective-permute-start.13 = (bf16[256,128]{1,0:T(8,128)(2,1)S(1)}, bf16[256,128]{1,0:T(8,128)(2,1)S(1)}, u32[]{:S(2)}, u32[]{:S(2)}) collective-permute-start(bf16[256,128]{1,0:T(8,128)(2,1)S(1)} %get-tuple-element.46.refs_4_), channel_id=1, source_target_pairs={{0,192},{8,200},{16,208},{24,216},{32,224},{40,232},{48,240},{56,2... | collective-permute-start | bytes 196616 | tf_op jit(solution)/shard_map/ppermute | solution.py:439
  39.3 10.8 %collective-permute-start.14 = (bf16[1040,128]{1,0:T(8,128)(2,1)S(1)}, bf16[1040,128]{1,0:T(8,128)(2,1)S(1)}, u32[]{:S(2)}, u32[]{:S(2)}) collective-permute-start(bf16[1040,128]{1,0:T(8,128)(2,1)S(1)} %get-tuple-element.47.refs_1_), channel_id=1, source_target_pairs={{0,64},{8,72},{16,80},{24,88},{32,96},{40,104},{48,112},{56,120},{... | collective-permute-start | bytes 798728 | tf_op jit(solution)/shard_map/ppermute | solution.py:458
  40.8 7.8 %collective-permute-start.18 = (bf16[1024,128]{1,0:T(8,128)(2,1)S(1)}, bf16[1024,128]{1,0:T(8,128)(2,1)S(1)}, u32[]{:S(2)}, u32[]{:S(2)}) collective-permute-start(bf16[1024,128]{1,0:T(8,128)(2,1)S(1)} %get-tuple-element.48.refs_3_.refs_4_.refs_2_), channel_id=1, source_target_pairs={{0,16},{8,24},{16,0},{24,8},{32,48},{40,56},{48,32},{56,40},{64,80... | collective-permute-start | bytes 786440 | tf_op jit(solution)/shard_map/ppermute | solution.py:459
  41.1 15.6 %collective-permute-start.16 = (bf16[1040,128]{1,0:T(8,128)(2,1)S(1)}, bf16[1040,128]{1,0:T(8,128)(2,1)S(1)}, u32[]{:S(2)}, u32[]{:S(2)}) collective-permute-start(bf16[1040,128]{1,0:T(8,128)(2,1)S(1)} %get-tuple-element.47.refs_1_), channel_id=1, source_target_pairs={{0,192},{8,200},{16,208},{24,216},{32,224},{40,232},{48,240},{56,2... | collective-permute-start | bytes 798728 | tf_op jit(solution)/shard_map/ppermute | solution.py:458
  43.4 13.2 %collective-permute-start.19 = (bf16[1024,128]{1,0:T(8,128)(2,1)S(1)}, bf16[1024,128]{1,0:T(8,128)(2,1)S(1)}, u32[]{:S(2)}, u32[]{:S(2)}) collective-permute-start(bf16[1024,128]{1,0:T(8,128)(2,1)S(1)} %get-tuple-element.48.refs_3_.refs_4_.refs_2_), channel_id=1, source_target_pairs={{0,48},{8,56},{16,32},{24,40},{32,16},{40,24},{48,0},{56,8},{64,11... | collective-permute-start | bytes 786440 | tf_op jit(solution)/shard_map/ppermute | solution.py:459
  48.2 11.1 %collective-permute-start.15 = (bf16[1040,128]{1,0:T(8,128)(2,1)S(1)}, bf16[1040,128]{1,0:T(8,128)(2,1)S(1)}, u32[]{:S(2)}, u32[]{:S(2)}) collective-permute-start(bf16[1040,128]{1,0:T(8,128)(2,1)S(1)} %get-tuple-element.47.refs_1_), channel_id=1, source_target_pairs={{0,128},{8,136},{16,144},{24,152},{32,160},{40,168},{48,176},{56,1... | collective-permute-start | bytes 798728 | tf_op jit(solution)/shard_map/ppermute | solution.py:458
  48.6 12.0 %collective-permute-start.17 = (bf16[1024,128]{1,0:T(8,128)(2,1)S(1)}, bf16[1024,128]{1,0:T(8,128)(2,1)S(1)}, u32[]{:S(2)}, u32[]{:S(2)}) collective-permute-start(bf16[1024,128]{1,0:T(8,128)(2,1)S(1)} %get-tuple-element.48.refs_3_.refs_4_.refs_2_), channel_id=1, source_target_pairs={{0,32},{8,40},{16,48},{24,56},{32,0},{40,8},{48,16},{56,24},{64,96... | collective-permute-start | bytes 786440 | tf_op jit(solution)/shard_map/ppermute | solution.py:459

commit v14 on v13

--- a/solution.py
+++ b/solution.py
@@ -394,7 +394,8 @@
     ids = block_ids.reshape(1, ROWS)
     order = decode_order.reshape(1, ROWS)
     cuts = step_cut.reshape(1, -1)
-    moved = [lax.ppermute(hidden, "kv", kv_pairs(d, 0)) for d in (1, 2, 3)]
+    two, one, three = [lax.ppermute(hidden, "kv", kv_pairs(d, 0)) for d in (2, 1, 3)]
+    moved = [one, two, three]
     own, wk, wv, code, pad = call(
         prep_kernel,
         [
@@ -429,6 +430,19 @@
         (1 << 29, 3 << 20),
     )
     pair = lax.ppermute(kv, "ctx", ctx_pairs(0, 0, 1))
+    q, flag, own_cut = call(
+        q_kernel,
+        [((GROUP, 2 * ROWS, HEAD), BF16), ((ROWS, HEAD), F32), ((ROWS, HEAD), F32)],
+        [x, q_weight, code, cuts],
+        (1 << 30, 5 << 20),
+    )
+    near = call(
+        near_kernel,
+        [((GROUP, 2 * ROWS, HEAD), F32)] * 3,
+        [q, kv, mask_kv, flag, code],
+        (1 << 30, 2 << 20),
+    )
+    pair, _ = lax.optimization_barrier((pair, flag))
     k, v = call(
         pair_kernel,
         [((2 * ROWS + PAD, HEAD), BF16), ((2 * ROWS, HEAD), BF16)],
@@ -442,18 +456,6 @@
         [((8 * ROWS + PAD, HEAD), BF16), ((8 * ROWS, HEAD), BF16)],
         [k, *ks, v, *vs],
         (1 << 10, 1 << 20),
-    )
-    q, flag, own_cut = call(
-        q_kernel,
-        [((GROUP, 2 * ROWS, HEAD), BF16), ((ROWS, HEAD), F32), ((ROWS, HEAD), F32)],
-        [x, q_weight, code, cuts],
-        (1 << 30, 5 << 20),
-    )
-    near = call(
-        near_kernel,
-        [((GROUP, 2 * ROWS, HEAD), F32)] * 3,
-        [q, kv, mask_kv, flag, code],
-        (1 << 30, 2 << 20),
     )
     all_k = [ks] + [lax.ppermute(ks, "ctx", ctx_pairs(d, 0, 0)) for d in (1, 2, 3)]
     all_v = [vs] + [lax.ppermute(vs, "ctx", ctx_pairs(0, d, 0)) for d in (1, 2, 3)]

time: 63 us -> 62.6 us (level)
  the two profiles are of different devices: /device:TPU:16 before, /device:TPU:24 now
where the time goes in v14:
time: 62.6 us; the launch traced here: 62.3 us
  starting transfers between devices  29.8 us (48%)
  waiting for transfers between devices  17.8 us (28%)
  Pallas kernels  12.5 us (20%)
  local copies, waits for them, and re-layouts  1.32 us (2%)
  between operations  0.77 us (1%)
    pallas_call x10, Pallas kernels, call(): pl.pallas_call(kernel, out_shape=[jax.ShapeDtypeStruct(s, t) for s, t in...  12.5 us
    ppermute x3, starting transfers between devices, shards(): lax.ppermute(hidden, 'kv', kv_pairs(d, 0))  8.75 us
    ppermute x3, waiting for transfers between devices, shards(): lax.ppermute(hidden, 'kv', kv_pairs(d, 0))  7.63 us
    ppermute x3, waiting for transfers between devices, shards(): lax.ppermute(vs, 'ctx', ctx_pairs(0, d, 0))  5.11 us
    ppermute x3, starting transfers between devices, shards(): vs = [lax.ppermute(v, 'ctx', ctx_pairs(d, 0, 0)) for d in (1, 2, 3)]  4.79 us
    ppermute x3, starting transfers between devices, shards(): lax.ppermute(vs, 'ctx', ctx_pairs(0, d, 0))  4.71 us
    ppermute x3, starting transfers between devices, shards(): ks = [lax.ppermute(k, 'ctx', ctx_pairs(0, d, 0)) for d in (1, 2, 3)]  4.7 us
    ppermute x3, starting transfers between devices, shards(): lax.ppermute(ks, 'ctx', ctx_pairs(d, 0, 0))  4.51 us
  transfers between devices with their start and end apart: 20, of which 7 were waited for; matrix products, arithmetic and copies ran while one was open for 2% of the time, Pallas kernels for 15%

profile of v14, /device:TPU:24, one launch (start us, length us, event | category | flops | bytes accessed | tf_op | source)
XLA Modules:
  0.0 62.3 jit_solution(13201342126248308920)
XLA Ops:
  0.7 3.4 %collective-permute-start.1 = (bf16[128,512]{1,0:T(8,128)(2,1)}, bf16[128,512]{1,0:T(8,128)(2,1)S(1)}, u32[]{:S(2)}, u32[]{:S(2)}) collective-permute-start(bf16[128,512]{1,0:T(8,128)(2,1)} %refs_0_.1), channel_id=1, source_target_pairs={{0,2},{1,3},{2,0},{3,1},{4,6},{5,7},{6,4},{7,5},{8,10},{9,11},{10,... | collective-permute-start | bytes 393224 | tf_op jit(solution)/shard_map/ppermute | solution.py:397
  4.0 5.4 %collective-permute-start.3 = (bf16[128,512]{1,0:T(8,128)(2,1)}, bf16[128,512]{1,0:T(8,128)(2,1)S(1)}, u32[]{:S(2)}, u32[]{:S(2)}) collective-permute-start(bf16[128,512]{1,0:T(8,128)(2,1)} %refs_0_.1), channel_id=1, source_target_pairs={{0,4},{1,5},{2,6},{3,7},{4,0},{5,1},{6,2},{7,3},{8,12},{9,13},{10,... | collective-permute-start | bytes 393224 | tf_op jit(solution)/shard_map/ppermute | solution.py:397
  9.4 1.3 %reshape.18.refs_5_ = bf16[1,4096]{1,0:T(2,128)(2,1)} reshape(bf16[4096]{0:T(1024)(128)(2,1)} %param.12) | data formatting | bytes 16384 | tf_op jit(solution)/shard_map/reshape | solution.py:408
  10.7 1.7 %shard_map.95 = (bf16[128,512]{1,0:T(8,128)(2,1)S(1)}, bf16[4096,128]{1,0:T(8,128)(2,1)S(1)}, bf16[4096,128]{1,0:T(8,128)(2,1)S(1)}, bf16[16,128]{1,0:T(8,128)(2,1)S(1)}, bf16[16,4096]{1,0:T(8,128)(2,1)S(1)}) custom-call(bf16[128,512]{1,0:T(8,128)(2,1)} %refs_0_.1, bf16[4096,128]{1,0:T(8,128)(2,1)} %refs_1_.1, bf16[4096,128]{1,0:T(8,128)(2,1)} %refs_2_.1, ...), custom_call_target="tpu_custom_call" | custom-call | flops 1048576 | bytes 4194304 | tf_op jit(solution)/shard_map/pallas_call | solution.py:51
  13.1 5.9 %collective-permute-done.3.refs_4_ = bf16[128,512]{1,0:T(8,128)(2,1)S(1)} collective-permute-done((bf16[128,512]{1,0:T(8,128)(2,1)}, bf16[128,512]{1,0:T(8,128)(2,1)S(1)}, u32[]{:S(2)}, u32[]{:S(2)}) %collective-permute-start.3) | collective-permute-done | bytes 131104 | tf_op jit(solution)/shard_map/ppermute | solution.py:397
  18.9 1.8 %collective-permute-done.5.refs_6_ = bf16[128,512]{1,0:T(8,128)(2,1)S(1)} collective-permute-done((bf16[128,512]{1,0:T(8,128)(2,1)}, bf16[128,512]{1,0:T(8,128)(2,1)S(1)}, u32[]{:S(2)}, u32[]{:S(2)}) %collective-permute-start.5) | collective-permute-done | bytes 131104 | tf_op jit(solution)/shard_map/ppermute | solution.py:397
  20.7 1.3 %collective-permute-done.6.refs_7_ = bf16[128,512]{1,0:T(8,128)(2,1)S(1)} collective-permute-done((bf16[128,512]{1,0:T(8,128)(2,1)S(1)}, bf16[128,512]{1,0:T(8,128)(2,1)S(1)}, u32[]{:S(2)}, u32[]{:S(2)}) %collective-permute-start.6) | collective-permute-done | bytes 131104 | tf_op jit(solution)/shard_map/ppermute | solution.py:421
  22.9 1.8 %collective-permute-start.7 = (bf16[144,256]{1,0:T(8,128)(2,1)S(1)}, bf16[144,256]{1,0:T(8,128)(2,1)S(1)}, u32[]{:S(2)}, u32[]{:S(2)}) collective-permute-start(bf16[144,256]{1,0:T(8,128)(2,1)S(1)} %get-tuple-element.45.own_ref.kv_ref), channel_id=1, source_target_pairs={{0,8},{8,0},{16,24},{24,16},{32,40},{40,32},{48,56},{56,48},{64,72... | collective-permute-start | bytes 221192 | tf_op jit(solution)/shard_map/ppermute | solution.py:432
  24.7 1.4 %shard_map.97 = (bf16[4,256,128]{2,1,0:T(8,128)(2,1)S(1)}, f32[128,128]{1,0:T(8,128)S(1)}, f32[128,128]{1,0:T(8,128)S(1)}) custom-call(bf16[144,4096]{1,0:T(8,128)(2,1)S(1)} %get-tuple-element.43.x_ref, bf16[4096,512]{1,0:T(8,128)(2,1)S(1)} %copy-done, bf16[16,128]{1,0:T(8,128)(2,1)S(1)} %get-tuple-element.42.refs_11_.code_ref.refs_10_, s32[1,256]{1,0:T(1,128)S(1)} %bitcast.3), custom_call_target="tpu_custom_call" | custom-call | flops 1073741824 | bytes 5242880 | tf_op jit(solution)/shard_map/pallas_call | solution.py:51
  26.1 1.2 %collective-permute-done.7.other_ref = bf16[144,256]{1,0:T(8,128)(2,1)S(1)} collective-permute-done((bf16[144,256]{1,0:T(8,128)(2,1)S(1)}, bf16[144,256]{1,0:T(8,128)(2,1)S(1)}, u32[]{:S(2)}, u32[]{:S(2)}) %collective-permute-start.7) | collective-permute-done | bytes 73760 | tf_op jit(solution)/shard_map/ppermute | solution.py:432
  28.2 2.8 %collective-permute-start.10 = (bf16[272,128]{1,0:T(8,128)(2,1)S(1)}, bf16[272,128]{1,0:T(8,128)(2,1)S(1)}, u32[]{:S(2)}, u32[]{:S(2)}) collective-permute-start(bf16[272,128]{1,0:T(8,128)(2,1)S(1)} %get-tuple-element.48.refs_0_), channel_id=1, source_target_pairs={{0,48},{8,56},{16,32},{24,40},{32,16},{40,24},{48,0},{56,8},{64,11... | collective-permute-start | bytes 208904 | tf_op jit(solution)/shard_map/ppermute | solution.py:452
  31.2 1.7 %collective-permute-start.9 = (bf16[272,128]{1,0:T(8,128)(2,1)S(1)}, bf16[272,128]{1,0:T(8,128)(2,1)S(1)}, u32[]{:S(2)}, u32[]{:S(2)}) collective-permute-start(bf16[272,128]{1,0:T(8,128)(2,1)S(1)} %get-tuple-element.48.refs_0_), channel_id=1, source_target_pairs={{0,32},{8,40},{16,48},{24,56},{32,0},{40,8},{48,16},{56,24},{64,96... | collective-permute-start | bytes 208904 | tf_op jit(solution)/shard_map/ppermute | solution.py:452
  32.9 0.9 %collective-permute-start.12 = (bf16[256,128]{1,0:T(8,128)(2,1)S(1)}, bf16[256,128]{1,0:T(8,128)(2,1)S(1)}, u32[]{:S(2)}, u32[]{:S(2)}) collective-permute-start(bf16[256,128]{1,0:T(8,128)(2,1)S(1)} %get-tuple-element.49.refs_4_), channel_id=1, source_target_pairs={{0,128},{8,136},{16,144},{24,152},{32,160},{40,168},{48,176},{56,1... | collective-permute-start | bytes 196616 | tf_op jit(solution)/shard_map/ppermute | solution.py:453
  33.8 3.0 %collective-permute-start.13 = (bf16[256,128]{1,0:T(8,128)(2,1)S(1)}, bf16[256,128]{1,0:T(8,128)(2,1)S(1)}, u32[]{:S(2)}, u32[]{:S(2)}) collective-permute-start(bf16[256,128]{1,0:T(8,128)(2,1)S(1)} %get-tuple-element.49.refs_4_), channel_id=1, source_target_pairs={{0,192},{8,200},{16,208},{24,216},{32,224},{40,232},{48,240},{56,2... | collective-permute-start | bytes 196616 | tf_op jit(solution)/shard_map/ppermute | solution.py:453
  36.8 1.8 %collective-permute-done.12.refs_6_ = bf16[256,128]{1,0:T(8,128)(2,1)S(1)} collective-permute-done((bf16[256,128]{1,0:T(8,128)(2,1)S(1)}, bf16[256,128]{1,0:T(8,128)(2,1)S(1)}, u32[]{:S(2)}, u32[]{:S(2)}) %collective-permute-start.12) | collective-permute-done | bytes 65568 | tf_op jit(solution)/shard_map/ppermute | solution.py:453
  40.4 2.5 %collective-permute-start.16 = (bf16[1040,128]{1,0:T(8,128)(2,1)S(1)}, bf16[1040,128]{1,0:T(8,128)(2,1)S(1)}, u32[]{:S(2)}, u32[]{:S(2)}) collective-permute-start(bf16[1040,128]{1,0:T(8,128)(2,1)S(1)} %get-tuple-element.50.refs_1_), channel_id=1, source_target_pairs={{0,192},{8,200},{16,208},{24,216},{32,224},{40,232},{48,240},{56,2... | collective-permute-start | bytes 798728 | tf_op jit(solution)/shard_map/ppermute | solution.py:460
  42.9 2.6 %collective-permute-start.19 = (bf16[1024,128]{1,0:T(8,128)(2,1)S(1)}, bf16[1024,128]{1,0:T(8,128)(2,1)S(1)}, u32[]{:S(2)}, u32[]{:S(2)}) collective-permute-start(bf16[1024,128]{1,0:T(8,128)(2,1)S(1)} %get-tuple-element.51.refs_3_.refs_4_.refs_2_), channel_id=1, source_target_pairs={{0,48},{8,56},{16,32},{24,40},{32,16},{40,24},{48,0},{56,8},{64,11... | collective-permute-start | bytes 786440 | tf_op jit(solution)/shard_map/ppermute | solution.py:461
  46.3 1.4 %collective-permute-start.15 = (bf16[1040,128]{1,0:T(8,128)(2,1)S(1)}, bf16[1040,128]{1,0:T(8,128)(2,1)S(1)}, u32[]{:S(2)}, u32[]{:S(2)}) collective-permute-start(bf16[1040,128]{1,0:T(8,128)(2,1)S(1)} %get-tuple-element.50.refs_1_), channel_id=1, source_target_pairs={{0,128},{8,136},{16,144},{24,152},{32,160},{40,168},{48,176},{56,1... | collective-permute-start | bytes 798728 | tf_op jit(solution)/shard_map/ppermute | solution.py:460
  47.6 1.9 %collective-permute-start.17 = (bf16[1024,128]{1,0:T(8,128)(2,1)S(1)}, bf16[1024,128]{1,0:T(8,128)(2,1)S(1)}, u32[]{:S(2)}, u32[]{:S(2)}) collective-permute-start(bf16[1024,128]{1,0:T(8,128)(2,1)S(1)} %get-tuple-element.51.refs_3_.refs_4_.refs_2_), channel_id=1, source_target_pairs={{0,32},{8,40},{16,48},{24,56},{32,0},{40,8},{48,16},{56,24},{64,96... | collective-permute-start | bytes 786440 | tf_op jit(solution)/shard_map/ppermute | solution.py:461
  49.5 1.3 %shard_map.101 = (f32[4,256,128]{2,1,0:T(8,128)S(1)}, f32[4,256,128]{2,1,0:T(8,128)S(1)}, f32[4,256,128]{2,1,0:T(8,128)S(1)}) custom-call(bf16[4,256,128]{2,1,0:T(8,128)(2,1)S(1)} %get-tuple-element.44.q_ref.refs_0_, bf16[1040,128]{1,0:T(8,128)(2,1)S(1)} %get-tuple-element.50.refs_1_, bf16[1040,128]{1,0:T(8,128)(2,1)S(1)} %collective-permute-done.14.refs_2_, ...), custom_call_target="tpu_custom_call" | custom-call | flops 1073741824 | bytes 2097152 | tf_op jit(solution)/shard_map/pallas_call | solution.py:51
  50.8 5.1 %collective-permute-done.19.refs_6_.refs_4_ = bf16[1024,128]{1,0:T(8,128)(2,1)S(1)} collective-permute-done((bf16[1024,128]{1,0:T(8,128)(2,1)S(1)}, bf16[1024,128]{1,0:T(8,128)(2,1)S(1)}, u32[]{:S(2)}, u32[]{:S(2)}) %collective-permute-start.19) | collective-permute-done | bytes 262176 | tf_op jit(solution)/shard_map/ppermute | solution.py:461
  55.9 2.7 %shard_map.102 = (f32[4,256,128]{2,1,0:T(8,128)S(1)}, f32[4,256,128]{2,1,0:T(8,128)S(1)}, f32[4,256,128]{2,1,0:T(8,128)S(1)}) custom-call(bf16[4,256,128]{2,1,0:T(8,128)(2,1)S(1)} %get-tuple-element.44.q_ref.refs_0_, bf16[1040,128]{1,0:T(8,128)(2,1)S(1)} %get-tuple-element.50.refs_1_, bf16[1040,128]{1,0:T(8,128)(2,1)S(1)} %collective-permute-done.14.refs_2_, ...), custom_call_target="tpu_custom_call" | custom-call | flops 2147483648 | bytes 4194304 | tf_op jit(solution)/shard_map/pallas_call | solution.py:51
  58.6 1.4 %shard_map.103 = (f32[4,256,128]{2,1,0:T(8,128)S(1)}, f32[4,256,128]{2,1,0:T(8,128)S(1)}, f32[4,256,128]{2,1,0:T(8,128)S(1)}) custom-call(bf16[4,256,128]{2,1,0:T(8,128)(2,1)S(1)} %get-tuple-element.44.q_ref.refs_0_, bf16[1040,128]{1,0:T(8,128)(2,1)S(1)} %collective-permute-done.15.refs_1_.refs_3_, ...), custom_call_target="tpu_custom_call" | custom-call | flops 1073741824 | bytes 2097152 | tf_op jit(solution)/shard_map/pallas_call | solution.py:51
  60.0 2.3 %shard_map.104 = (bf16[128,512]{1,0:T(8,128)(2,1)}, bf16[128,512]{1,0:T(8,128)(2,1)}) custom-call(bf16[4,256,128]{2,1,0:T(8,128)(2,1)S(1)} %get-tuple-element.44.q_ref.refs_0_, bf16[1040,128]{1,0:T(8,128)(2,1)S(1)} %get-tuple-element.50.refs_1_, bf16[1040,128]{1,0:T(8,128)(2,1)S(1)} %collective-permute-done.14.refs_2_, ...), custom_call_target="tpu_custom_call" | custom-call | flops 2147483648 | bytes 4194304 | tf_op jit(solution)/shard_map/pallas_call | solution.py:51
  (31 shorter events, 5.1 us)
Async XLA Ops:
  0.6 24.0 %copy-start.1 = (s32[256]{0:T(256)S(1)}, s32[256]{0:T(256)}, u32[]{:S(2)}) copy-start(s32[256]{0:T(256)} %param.11) | copy-start | bytes 3076
  0.6 24.0 %copy-start = (bf16[4096,512]{1,0:T(8,128)(2,1)S(1)}, bf16[4096,512]{1,0:T(8,128)(2,1)}, u32[]{:S(2)}) copy-start(bf16[4096,512]{1,0:T(8,128)(2,1)} %wq_ref.1) | copy-start | bytes 12582916
  0.7 11.9 %collective-permute-start.1 = (bf16[128,512]{1,0:T(8,128)(2,1)}, bf16[128,512]{1,0:T(8,128)(2,1)S(1)}, u32[]{:S(2)}, u32[]{:S(2)}) collective-permute-start(bf16[128,512]{1,0:T(8,128)(2,1)} %refs_0_.1), channel_id=1, source_target_pairs={{0,2},{1,3},{2,0},{3,1},{4,6},{5,7},{6,4},{7,5},{8,10},{9,11},{10,... | collective-permute-start | bytes 393224 | tf_op jit(solution)/shard_map/ppermute | solution.py:397
  4.0 14.9 %collective-permute-start.3 = (bf16[128,512]{1,0:T(8,128)(2,1)}, bf16[128,512]{1,0:T(8,128)(2,1)S(1)}, u32[]{:S(2)}, u32[]{:S(2)}) collective-permute-start(bf16[128,512]{1,0:T(8,128)(2,1)} %refs_0_.1), channel_id=1, source_target_pairs={{0,4},{1,5},{2,6},{3,7},{4,0},{5,1},{6,2},{7,3},{8,12},{9,13},{10,... | collective-permute-start | bytes 393224 | tf_op jit(solution)/shard_map/ppermute | solution.py:397
  9.4 11.3 %collective-permute-start.5 = (bf16[128,512]{1,0:T(8,128)(2,1)}, bf16[128,512]{1,0:T(8,128)(2,1)S(1)}, u32[]{:S(2)}, u32[]{:S(2)}) collective-permute-start(bf16[128,512]{1,0:T(8,128)(2,1)} %refs_0_.1), channel_id=1, source_target_pairs={{0,6},{1,7},{2,4},{3,5},{4,2},{5,3},{6,0},{7,1},{8,14},{9,15},{10,... | collective-permute-start | bytes 393224 | tf_op jit(solution)/shard_map/ppermute | solution.py:397
  12.5 8.2 %collective-permute-start = (bf16[128,512]{1,0:T(8,128)(2,1)S(1)}, bf16[128,512]{1,0:T(8,128)(2,1)S(1)}, u32[]{:S(2)}, u32[]{:S(2)}) collective-permute-start(bf16[128,512]{1,0:T(8,128)(2,1)S(1)} %get-tuple-element.36.refs_0_), channel_id=1, source_target_pairs={{0,1},{1,0},{2,3},{3,2},{4,5},{5,4},{6,7},{7,6},{8,9},{9,8},{10,11... | collective-permute-start | bytes 393224 | tf_op jit(solution)/shard_map/ppermute | solution.py:421
  12.6 8.1 %collective-permute-start.2 = (bf16[128,512]{1,0:T(8,128)(2,1)S(1)}, bf16[128,512]{1,0:T(8,128)(2,1)S(1)}, u32[]{:S(2)}, u32[]{:S(2)}) collective-permute-start(bf16[128,512]{1,0:T(8,128)(2,1)S(1)} %collective-permute-done.1.refs_2_), channel_id=1, source_target_pairs={{0,1},{1,0},{2,3},{3,2},{4,5},{5,4},{6,7},{7,6},{8,9},{9,8},{10,11... | collective-permute-start | bytes 393224 | tf_op jit(solution)/shard_map/ppermute | solution.py:421
  18.9 1.8 %collective-permute-start.4 = (bf16[128,512]{1,0:T(8,128)(2,1)S(1)}, bf16[128,512]{1,0:T(8,128)(2,1)S(1)}, u32[]{:S(2)}, u32[]{:S(2)}) collective-permute-start(bf16[128,512]{1,0:T(8,128)(2,1)S(1)} %collective-permute-done.3.refs_4_), channel_id=1, source_target_pairs={{0,1},{1,0},{2,3},{3,2},{4,5},{5,4},{6,7},{7,6},{8,9},{9,8},{10,11... | collective-permute-start | bytes 393224 | tf_op jit(solution)/shard_map/ppermute | solution.py:421
  20.7 1.3 %collective-permute-start.6 = (bf16[128,512]{1,0:T(8,128)(2,1)S(1)}, bf16[128,512]{1,0:T(8,128)(2,1)S(1)}, u32[]{:S(2)}, u32[]{:S(2)}) collective-permute-start(bf16[128,512]{1,0:T(8,128)(2,1)S(1)} %collective-permute-done.5.refs_6_), channel_id=1, source_target_pairs={{0,1},{1,0},{2,3},{3,2},{4,5},{5,4},{6,7},{7,6},{8,9},{9,8},{10,11... | collective-permute-start | bytes 393224 | tf_op jit(solution)/shard_map/ppermute | solution.py:421
  22.9 4.4 %collective-permute-start.7 = (bf16[144,256]{1,0:T(8,128)(2,1)S(1)}, bf16[144,256]{1,0:T(8,128)(2,1)S(1)}, u32[]{:S(2)}, u32[]{:S(2)}) collective-permute-start(bf16[144,256]{1,0:T(8,128)(2,1)S(1)} %get-tuple-element.45.own_ref.kv_ref), channel_id=1, source_target_pairs={{0,8},{8,0},{16,24},{24,16},{32,40},{40,32},{48,56},{56,48},{64,72... | collective-permute-start | bytes 221192 | tf_op jit(solution)/shard_map/ppermute | solution.py:432
  27.4 6.5 %collective-permute-start.11 = (bf16[256,128]{1,0:T(8,128)(2,1)S(1)}, bf16[256,128]{1,0:T(8,128)(2,1)S(1)}, u32[]{:S(2)}, u32[]{:S(2)}) collective-permute-start(bf16[256,128]{1,0:T(8,128)(2,1)S(1)} %get-tuple-element.49.refs_4_), channel_id=1, source_target_pairs={{0,64},{8,72},{16,80},{24,88},{32,96},{40,104},{48,112},{56,120},{... | collective-permute-start | bytes 196616 | tf_op jit(solution)/shard_map/ppermute | solution.py:453
  28.2 11.2 %collective-permute-start.10 = (bf16[272,128]{1,0:T(8,128)(2,1)S(1)}, bf16[272,128]{1,0:T(8,128)(2,1)S(1)}, u32[]{:S(2)}, u32[]{:S(2)}) collective-permute-start(bf16[272,128]{1,0:T(8,128)(2,1)S(1)} %get-tuple-element.48.refs_0_), channel_id=1, source_target_pairs={{0,48},{8,56},{16,32},{24,40},{32,16},{40,24},{48,0},{56,8},{64,11... | collective-permute-start | bytes 208904 | tf_op jit(solution)/shard_map/ppermute | solution.py:452
  30.9 8.4 %collective-permute-start.8 = (bf16[272,128]{1,0:T(8,128)(2,1)S(1)}, bf16[272,128]{1,0:T(8,128)(2,1)S(1)}, u32[]{:S(2)}, u32[]{:S(2)}) collective-permute-start(bf16[272,128]{1,0:T(8,128)(2,1)S(1)} %get-tuple-element.48.refs_0_), channel_id=1, source_target_pairs={{0,16},{8,24},{16,0},{24,8},{32,48},{40,56},{48,32},{56,40},{64,80... | collective-permute-start | bytes 208904 | tf_op jit(solution)/shard_map/ppermute | solution.py:452
  31.2 8.2 %collective-permute-start.9 = (bf16[272,128]{1,0:T(8,128)(2,1)S(1)}, bf16[272,128]{1,0:T(8,128)(2,1)S(1)}, u32[]{:S(2)}, u32[]{:S(2)}) collective-permute-start(bf16[272,128]{1,0:T(8,128)(2,1)S(1)} %get-tuple-element.48.refs_0_), channel_id=1, source_target_pairs={{0,32},{8,40},{16,48},{24,56},{32,0},{40,8},{48,16},{56,24},{64,96... | collective-permute-start | bytes 208904 | tf_op jit(solution)/shard_map/ppermute | solution.py:452
  32.9 5.8 %collective-permute-start.12 = (bf16[256,128]{1,0:T(8,128)(2,1)S(1)}, bf16[256,128]{1,0:T(8,128)(2,1)S(1)}, u32[]{:S(2)}, u32[]{:S(2)}) collective-permute-start(bf16[256,128]{1,0:T(8,128)(2,1)S(1)} %get-tuple-element.49.refs_4_), channel_id=1, source_target_pairs={{0,128},{8,136},{16,144},{24,152},{32,160},{40,168},{48,176},{56,1... | collective-permute-start | bytes 196616 | tf_op jit(solution)/shard_map/ppermute | solution.py:453
  33.8 5.5 %collective-permute-start.13 = (bf16[256,128]{1,0:T(8,128)(2,1)S(1)}, bf16[256,128]{1,0:T(8,128)(2,1)S(1)}, u32[]{:S(2)}, u32[]{:S(2)}) collective-permute-start(bf16[256,128]{1,0:T(8,128)(2,1)S(1)} %get-tuple-element.49.refs_4_), channel_id=1, source_target_pairs={{0,192},{8,200},{16,208},{24,216},{32,224},{40,232},{48,240},{56,2... | collective-permute-start | bytes 196616 | tf_op jit(solution)/shard_map/ppermute | solution.py:453
  39.4 10.1 %collective-permute-start.14 = (bf16[1040,128]{1,0:T(8,128)(2,1)S(1)}, bf16[1040,128]{1,0:T(8,128)(2,1)S(1)}, u32[]{:S(2)}, u32[]{:S(2)}) collective-permute-start(bf16[1040,128]{1,0:T(8,128)(2,1)S(1)} %get-tuple-element.50.refs_1_), channel_id=1, source_target_pairs={{0,64},{8,72},{16,80},{24,88},{32,96},{40,104},{48,112},{56,120},{... | collective-permute-start | bytes 798728 | tf_op jit(solution)/shard_map/ppermute | solution.py:460
  40.1 7.5 %collective-permute-start.18 = (bf16[1024,128]{1,0:T(8,128)(2,1)S(1)}, bf16[1024,128]{1,0:T(8,128)(2,1)S(1)}, u32[]{:S(2)}, u32[]{:S(2)}) collective-permute-start(bf16[1024,128]{1,0:T(8,128)(2,1)S(1)} %get-tuple-element.51.refs_3_.refs_4_.refs_2_), channel_id=1, source_target_pairs={{0,16},{8,24},{16,0},{24,8},{32,48},{40,56},{48,32},{56,40},{64,80... | collective-permute-start | bytes 786440 | tf_op jit(solution)/shard_map/ppermute | solution.py:461
  40.4 15.6 %collective-permute-start.16 = (bf16[1040,128]{1,0:T(8,128)(2,1)S(1)}, bf16[1040,128]{1,0:T(8,128)(2,1)S(1)}, u32[]{:S(2)}, u32[]{:S(2)}) collective-permute-start(bf16[1040,128]{1,0:T(8,128)(2,1)S(1)} %get-tuple-element.50.refs_1_), channel_id=1, source_target_pairs={{0,192},{8,200},{16,208},{24,216},{32,224},{40,232},{48,240},{56,2... | collective-permute-start | bytes 798728 | tf_op jit(solution)/shard_map/ppermute | solution.py:460
  42.9 13.1 %collective-permute-start.19 = (bf16[1024,128]{1,0:T(8,128)(2,1)S(1)}, bf16[1024,128]{1,0:T(8,128)(2,1)S(1)}, u32[]{:S(2)}, u32[]{:S(2)}) collective-permute-start(bf16[1024,128]{1,0:T(8,128)(2,1)S(1)} %get-tuple-element.51.refs_3_.refs_4_.refs_2_), channel_id=1, source_target_pairs={{0,48},{8,56},{16,32},{24,40},{32,16},{40,24},{48,0},{56,8},{64,11... | collective-permute-start | bytes 786440 | tf_op jit(solution)/shard_map/ppermute | solution.py:461
  46.3 12.3 %collective-permute-start.15 = (bf16[1040,128]{1,0:T(8,128)(2,1)S(1)}, bf16[1040,128]{1,0:T(8,128)(2,1)S(1)}, u32[]{:S(2)}, u32[]{:S(2)}) collective-permute-start(bf16[1040,128]{1,0:T(8,128)(2,1)S(1)} %get-tuple-element.50.refs_1_), channel_id=1, source_target_pairs={{0,128},{8,136},{16,144},{24,152},{32,160},{40,168},{48,176},{56,1... | collective-permute-start | bytes 798728 | tf_op jit(solution)/shard_map/ppermute | solution.py:460
  47.6 12.4 %collective-permute-start.17 = (bf16[1024,128]{1,0:T(8,128)(2,1)S(1)}, bf16[1024,128]{1,0:T(8,128)(2,1)S(1)}, u32[]{:S(2)}, u32[]{:S(2)}) collective-permute-start(bf16[1024,128]{1,0:T(8,128)(2,1)S(1)} %get-tuple-element.51.refs_3_.refs_4_.refs_2_), channel_id=1, source_target_pairs={{0,32},{8,40},{16,48},{24,56},{32,0},{40,8},{48,16},{56,24},{64,96... | collective-permute-start | bytes 786440 | tf_op jit(solution)/shard_map/ppermute | solution.py:461

commit v15 on v14

--- a/solution.py
+++ b/solution.py
@@ -365,21 +365,18 @@
     pipeline(q_ref, pieces, state_in, state, None)
 
 
-def third_kernel(*refs):
-    q_ref, k_ref, v_refs = refs[0], refs[1], refs[2:5]
+def last_kernel(*refs):
+    q_ref, k_refs, v_refs = refs[0], refs[1:5], refs[5:9]
+    state_in = refs[9:12]
+    clean_ref, noisy_ref = refs[12:14]
+    state = refs[14:17]
     where = place()
-    near = (0, 1, 3)
-    keys, values, _, _ = spots_piece(where, {2: k_ref}, dict(zip(near, v_refs)), [(2, dx) for dx in near])
-    piece = (keys, values, None, where[1] >= 2)
-    pipeline(q_ref, [piece], refs[5:8], refs[8:11], None)
-
-
-def last_kernel(*refs):
-    q_ref, k_refs, v_ref = refs[0], refs[1:5], refs[5]
-    state_in = refs[6:9]
-    clean_ref, noisy_ref = refs[9:11]
-    state = refs[11:]
-    piece = spots_piece(place(), dict(enumerate(k_refs)), {2: v_ref}, [(dy, 2) for dy in range(4)])
+    k_of, v_of = dict(enumerate(k_refs)), dict(enumerate(v_refs))
+    keys, values, _, _ = spots_piece(where, k_of, v_of, [(2, dx) for dx in range(4)])
+    pieces = [
+        (keys, values, None, where[1] >= 2),
+        spots_piece(where, k_of, v_of, [(dy, 2) for dy in (0, 1, 3)]),
+    ]
 
     def finish(h, accum, total):
         lanes = slice(h * HEAD, (h + 1) * HEAD)
@@ -387,7 +384,7 @@
         clean_ref[:, lanes] = result[:ROWS]
         noisy_ref[:, lanes] = result[ROWS:]
 
-    pipeline(q_ref, [piece], state_in, state, finish)
+    pipeline(q_ref, pieces, state_in, state, finish)
 
 
 def shards(hidden, block_ids, decode_order, step_cut, mask_embed, q_weight, k_weight, v_weight):
@@ -472,17 +469,11 @@
         [q, *[all_k[d] for d in (0, 1, 3)], *[all_v[d] for d in (0, 1, 3)], *first, code, own_cut, mask_kv],
         (1 << 31, 4 << 20),
     )
-    third = call(
-        third_kernel,
-        state,
-        [q, all_k[2], *[all_v[d] for d in (0, 1, 3)], *far],
-        (1 << 30, 2 << 20),
-    )
     return tuple(
         call(
             last_kernel,
             [((ROWS, GROUP * HEAD), BF16)] * 2,
-            [q, *all_k, all_v[2], *third],
+            [q, *all_k, *all_v, *far],
             (1 << 31, 4 << 20),
             [pltpu.VMEM((GROUP, 2 * ROWS, HEAD), F32)] * 3,
         )

time: 62.6 us -> 63.3 us (1.011); the launches traced: 62.3 us -> 62 us
    pallas_call x10 -> x9, Pallas kernels: 12.5 us -> 12.3 us  [call(): pl.pallas_call(kernel, out_shape=[jax.ShapeDtypeStruct(s, t) for s, t in...]
  transfers between devices with their start and end apart: 20 -> 20, of which waited for: 7 -> 7; matrix products, arithmetic and copies ran while one was open for 2% -> 2% of each run, Pallas kernels for 15% -> 13%
where the time goes in v15:
time: 63.3 us; the launch traced here: 62 us
  starting transfers between devices  29.8 us (47%)
  waiting for transfers between devices  17.8 us (28%)
  Pallas kernels  12.3 us (19%)
  local copies, waits for them, and re-layouts  1.32 us (2%)
  between operations  0.77 us (1%)
    pallas_call x9, Pallas kernels, call(): pl.pallas_call(kernel, out_shape=[jax.ShapeDtypeStruct(s, t) for s, t in...  12.3 us
    ppermute x3, starting transfers between devices, shards(): lax.ppermute(hidden, 'kv', kv_pairs(d, 0))  8.75 us
    ppermute x3, waiting for transfers between devices, shards(): lax.ppermute(hidden, 'kv', kv_pairs(d, 0))  7.63 us
    ppermute x3, waiting for transfers between devices, shards(): lax.ppermute(vs, 'ctx', ctx_pairs(0, d, 0))  5.11 us
    ppermute x3, starting transfers between devices, shards(): vs = [lax.ppermute(v, 'ctx', ctx_pairs(d, 0, 0)) for d in (1, 2, 3)]  4.79 us
    ppermute x3, starting transfers between devices, shards(): lax.ppermute(vs, 'ctx', ctx_pairs(0, d, 0))  4.71 us
    ppermute x3, starting transfers between devices, shards(): ks = [lax.ppermute(k, 'ctx', ctx_pairs(0, d, 0)) for d in (1, 2, 3)]  4.7 us
    ppermute x3, starting transfers between devices, shards(): lax.ppermute(ks, 'ctx', ctx_pairs(d, 0, 0))  4.51 us
  transfers between devices with their start and end apart: 20, of which 7 were waited for; matrix products, arithmetic and copies ran while one was open for 2% of the time, Pallas kernels for 13%

profile of v15, /device:TPU:24, one launch (start us, length us, event | category | flops | bytes accessed | tf_op | source)
XLA Modules:
  0.0 62.0 jit_solution(3845544909012139604)
XLA Ops:
  0.7 3.4 %collective-permute-start.1 = (bf16[128,512]{1,0:T(8,128)(2,1)}, bf16[128,512]{1,0:T(8,128)(2,1)S(1)}, u32[]{:S(2)}, u32[]{:S(2)}) collective-permute-start(bf16[128,512]{1,0:T(8,128)(2,1)} %refs_0_.1), channel_id=1, source_target_pairs={{0,2},{1,3},{2,0},{3,1},{4,6},{5,7},{6,4},{7,5},{8,10},{9,11},{10,... | collective-permute-start | bytes 393224 | tf_op jit(solution)/shard_map/ppermute | solution.py:394
  4.0 5.4 %collective-permute-start.3 = (bf16[128,512]{1,0:T(8,128)(2,1)}, bf16[128,512]{1,0:T(8,128)(2,1)S(1)}, u32[]{:S(2)}, u32[]{:S(2)}) collective-permute-start(bf16[128,512]{1,0:T(8,128)(2,1)} %refs_0_.1), channel_id=1, source_target_pairs={{0,4},{1,5},{2,6},{3,7},{4,0},{5,1},{6,2},{7,3},{8,12},{9,13},{10,... | collective-permute-start | bytes 393224 | tf_op jit(solution)/shard_map/ppermute | solution.py:394
  9.4 1.3 %reshape.18.refs_5_ = bf16[1,4096]{1,0:T(2,128)(2,1)} reshape(bf16[4096]{0:T(1024)(128)(2,1)} %param.12) | data formatting | bytes 16384 | tf_op jit(solution)/shard_map/reshape | solution.py:405
  10.7 1.7 %shard_map.95 = (bf16[128,512]{1,0:T(8,128)(2,1)S(1)}, bf16[4096,128]{1,0:T(8,128)(2,1)S(1)}, bf16[4096,128]{1,0:T(8,128)(2,1)S(1)}, bf16[16,128]{1,0:T(8,128)(2,1)S(1)}, bf16[16,4096]{1,0:T(8,128)(2,1)S(1)}) custom-call(bf16[128,512]{1,0:T(8,128)(2,1)} %refs_0_.1, bf16[4096,128]{1,0:T(8,128)(2,1)} %refs_1_.1, bf16[4096,128]{1,0:T(8,128)(2,1)} %refs_2_.1, ...), custom_call_target="tpu_custom_call" | custom-call | flops 1048576 | bytes 4194304 | tf_op jit(solution)/shard_map/pallas_call | solution.py:51
  13.1 5.9 %collective-permute-done.3.refs_4_ = bf16[128,512]{1,0:T(8,128)(2,1)S(1)} collective-permute-done((bf16[128,512]{1,0:T(8,128)(2,1)}, bf16[128,512]{1,0:T(8,128)(2,1)S(1)}, u32[]{:S(2)}, u32[]{:S(2)}) %collective-permute-start.3) | collective-permute-done | bytes 131104 | tf_op jit(solution)/shard_map/ppermute | solution.py:394
  18.9 1.8 %collective-permute-done.5.refs_6_ = bf16[128,512]{1,0:T(8,128)(2,1)S(1)} collective-permute-done((bf16[128,512]{1,0:T(8,128)(2,1)}, bf16[128,512]{1,0:T(8,128)(2,1)S(1)}, u32[]{:S(2)}, u32[]{:S(2)}) %collective-permute-start.5) | collective-permute-done | bytes 131104 | tf_op jit(solution)/shard_map/ppermute | solution.py:394
  20.7 1.3 %collective-permute-done.6.refs_7_ = bf16[128,512]{1,0:T(8,128)(2,1)S(1)} collective-permute-done((bf16[128,512]{1,0:T(8,128)(2,1)S(1)}, bf16[128,512]{1,0:T(8,128)(2,1)S(1)}, u32[]{:S(2)}, u32[]{:S(2)}) %collective-permute-start.6) | collective-permute-done | bytes 131104 | tf_op jit(solution)/shard_map/ppermute | solution.py:418
  22.0 0.8 %shard_map.96 = (bf16[144,4096]{1,0:T(8,128)(2,1)S(1)}, bf16[144,256]{1,0:T(8,128)(2,1)S(1)}, bf16[16,256]{1,0:T(8,128)(2,1)S(1)}) custom-call(bf16[128,512]{1,0:T(8,128)(2,1)S(1)} %get-tuple-element.33.refs_0_, bf16[128,512]{1,0:T(8,128)(2,1)S(1)} %collective-permute-done.refs_1_, bf16[128,512]{1,0:T(8,128)(2,1)S(1)} %collective-permute-done.1.refs_2_, ...), custom_call_target="tpu_custom_call" | custom-call | flops 536870912 | bytes 3145728 | tf_op jit(solution)/shard_map/pallas_call | solution.py:51
  22.9 1.8 %collective-permute-start.7 = (bf16[144,256]{1,0:T(8,128)(2,1)S(1)}, bf16[144,256]{1,0:T(8,128)(2,1)S(1)}, u32[]{:S(2)}, u32[]{:S(2)}) collective-permute-start(bf16[144,256]{1,0:T(8,128)(2,1)S(1)} %get-tuple-element.42.own_ref.kv_ref), channel_id=1, source_target_pairs={{0,8},{8,0},{16,24},{24,16},{32,40},{40,32},{48,56},{56,48},{64,72... | collective-permute-start | bytes 221192 | tf_op jit(solution)/shard_map/ppermute | solution.py:429
  24.7 1.4 %shard_map.97 = (bf16[4,256,128]{2,1,0:T(8,128)(2,1)S(1)}, f32[128,128]{1,0:T(8,128)S(1)}, f32[128,128]{1,0:T(8,128)S(1)}) custom-call(bf16[144,4096]{1,0:T(8,128)(2,1)S(1)} %get-tuple-element.40.x_ref, bf16[4096,512]{1,0:T(8,128)(2,1)S(1)} %copy-done, bf16[16,128]{1,0:T(8,128)(2,1)S(1)} %get-tuple-element.39.refs_11_.code_ref.refs_10_, s32[1,256]{1,0:T(1,128)S(1)} %bitcast.3), custom_call_target="tpu_custom_call" | custom-call | flops 1073741824 | bytes 5242880 | tf_op jit(solution)/shard_map/pallas_call | solution.py:51
  26.1 1.2 %collective-permute-done.7.other_ref = bf16[144,256]{1,0:T(8,128)(2,1)S(1)} collective-permute-done((bf16[144,256]{1,0:T(8,128)(2,1)S(1)}, bf16[144,256]{1,0:T(8,128)(2,1)S(1)}, u32[]{:S(2)}, u32[]{:S(2)}) %collective-permute-start.7) | collective-permute-done | bytes 73760 | tf_op jit(solution)/shard_map/ppermute | solution.py:429
  28.2 2.8 %collective-permute-start.10 = (bf16[272,128]{1,0:T(8,128)(2,1)S(1)}, bf16[272,128]{1,0:T(8,128)(2,1)S(1)}, u32[]{:S(2)}, u32[]{:S(2)}) collective-permute-start(bf16[272,128]{1,0:T(8,128)(2,1)S(1)} %get-tuple-element.45.refs_0_), channel_id=1, source_target_pairs={{0,48},{8,56},{16,32},{24,40},{32,16},{40,24},{48,0},{56,8},{64,11... | collective-permute-start | bytes 208904 | tf_op jit(solution)/shard_map/ppermute | solution.py:449
  31.2 1.7 %collective-permute-start.9 = (bf16[272,128]{1,0:T(8,128)(2,1)S(1)}, bf16[272,128]{1,0:T(8,128)(2,1)S(1)}, u32[]{:S(2)}, u32[]{:S(2)}) collective-permute-start(bf16[272,128]{1,0:T(8,128)(2,1)S(1)} %get-tuple-element.45.refs_0_), channel_id=1, source_target_pairs={{0,32},{8,40},{16,48},{24,56},{32,0},{40,8},{48,16},{56,24},{64,96... | collective-permute-start | bytes 208904 | tf_op jit(solution)/shard_map/ppermute | solution.py:449
  32.9 0.9 %collective-permute-start.12 = (bf16[256,128]{1,0:T(8,128)(2,1)S(1)}, bf16[256,128]{1,0:T(8,128)(2,1)S(1)}, u32[]{:S(2)}, u32[]{:S(2)}) collective-permute-start(bf16[256,128]{1,0:T(8,128)(2,1)S(1)} %get-tuple-element.46.refs_4_), channel_id=1, source_target_pairs={{0,128},{8,136},{16,144},{24,152},{32,160},{40,168},{48,176},{56,1... | collective-permute-start | bytes 196616 | tf_op jit(solution)/shard_map/ppermute | solution.py:450
  33.8 3.0 %collective-permute-start.13 = (bf16[256,128]{1,0:T(8,128)(2,1)S(1)}, bf16[256,128]{1,0:T(8,128)(2,1)S(1)}, u32[]{:S(2)}, u32[]{:S(2)}) collective-permute-start(bf16[256,128]{1,0:T(8,128)(2,1)S(1)} %get-tuple-element.46.refs_4_), channel_id=1, source_target_pairs={{0,192},{8,200},{16,208},{24,216},{32,224},{40,232},{48,240},{56,2... | collective-permute-start | bytes 196616 | tf_op jit(solution)/shard_map/ppermute | solution.py:450
  36.8 1.8 %collective-permute-done.12.refs_6_ = bf16[256,128]{1,0:T(8,128)(2,1)S(1)} collective-permute-done((bf16[256,128]{1,0:T(8,128)(2,1)S(1)}, bf16[256,128]{1,0:T(8,128)(2,1)S(1)}, u32[]{:S(2)}, u32[]{:S(2)}) %collective-permute-start.12) | collective-permute-done | bytes 65568 | tf_op jit(solution)/shard_map/ppermute | solution.py:450
  40.4 2.5 %collective-permute-start.16 = (bf16[1040,128]{1,0:T(8,128)(2,1)S(1)}, bf16[1040,128]{1,0:T(8,128)(2,1)S(1)}, u32[]{:S(2)}, u32[]{:S(2)}) collective-permute-start(bf16[1040,128]{1,0:T(8,128)(2,1)S(1)} %get-tuple-element.47.refs_1_), channel_id=1, source_target_pairs={{0,192},{8,200},{16,208},{24,216},{32,224},{40,232},{48,240},{56,2... | collective-permute-start | bytes 798728 | tf_op jit(solution)/shard_map/ppermute | solution.py:457
  42.9 2.6 %collective-permute-start.19 = (bf16[1024,128]{1,0:T(8,128)(2,1)S(1)}, bf16[1024,128]{1,0:T(8,128)(2,1)S(1)}, u32[]{:S(2)}, u32[]{:S(2)}) collective-permute-start(bf16[1024,128]{1,0:T(8,128)(2,1)S(1)} %get-tuple-element.48.refs_3_.refs_4_.refs_5_), channel_id=1, source_target_pairs={{0,48},{8,56},{16,32},{24,40},{32,16},{40,24},{48,0},{56,8},{64,11... | collective-permute-start | bytes 786440 | tf_op jit(solution)/shard_map/ppermute | solution.py:458
  46.3 1.4 %collective-permute-start.15 = (bf16[1040,128]{1,0:T(8,128)(2,1)S(1)}, bf16[1040,128]{1,0:T(8,128)(2,1)S(1)}, u32[]{:S(2)}, u32[]{:S(2)}) collective-permute-start(bf16[1040,128]{1,0:T(8,128)(2,1)S(1)} %get-tuple-element.47.refs_1_), channel_id=1, source_target_pairs={{0,128},{8,136},{16,144},{24,152},{32,160},{40,168},{48,176},{56,1... | collective-permute-start | bytes 798728 | tf_op jit(solution)/shard_map/ppermute | solution.py:457
  47.6 1.9 %collective-permute-start.18 = (bf16[1024,128]{1,0:T(8,128)(2,1)S(1)}, bf16[1024,128]{1,0:T(8,128)(2,1)S(1)}, u32[]{:S(2)}, u32[]{:S(2)}) collective-permute-start(bf16[1024,128]{1,0:T(8,128)(2,1)S(1)} %get-tuple-element.48.refs_3_.refs_4_.refs_5_), channel_id=1, source_target_pairs={{0,32},{8,40},{16,48},{24,56},{32,0},{40,8},{48,16},{56,24},{64,96... | collective-permute-start | bytes 786440 | tf_op jit(solution)/shard_map/ppermute | solution.py:458
  49.5 1.3 %shard_map.101 = (f32[4,256,128]{2,1,0:T(8,128)S(1)}, f32[4,256,128]{2,1,0:T(8,128)S(1)}, f32[4,256,128]{2,1,0:T(8,128)S(1)}) custom-call(bf16[4,256,128]{2,1,0:T(8,128)(2,1)S(1)} %get-tuple-element.41.q_ref.refs_0_, bf16[1040,128]{1,0:T(8,128)(2,1)S(1)} %get-tuple-element.47.refs_1_, bf16[1040,128]{1,0:T(8,128)(2,1)S(1)} %collective-permute-done.14.refs_2_, ...), custom_call_target="tpu_custom_call" | custom-call | flops 1073741824 | bytes 2097152 | tf_op jit(solution)/shard_map/pallas_call | solution.py:51
  50.8 5.1 %collective-permute-done.19.refs_6_.refs_8_ = bf16[1024,128]{1,0:T(8,128)(2,1)S(1)} collective-permute-done((bf16[1024,128]{1,0:T(8,128)(2,1)S(1)}, bf16[1024,128]{1,0:T(8,128)(2,1)S(1)}, u32[]{:S(2)}, u32[]{:S(2)}) %collective-permute-start.19) | collective-permute-done | bytes 262176 | tf_op jit(solution)/shard_map/ppermute | solution.py:458
  55.9 2.7 %shard_map.102 = (f32[4,256,128]{2,1,0:T(8,128)S(1)}, f32[4,256,128]{2,1,0:T(8,128)S(1)}, f32[4,256,128]{2,1,0:T(8,128)S(1)}) custom-call(bf16[4,256,128]{2,1,0:T(8,128)(2,1)S(1)} %get-tuple-element.41.q_ref.refs_0_, bf16[1040,128]{1,0:T(8,128)(2,1)S(1)} %get-tuple-element.47.refs_1_, bf16[1040,128]{1,0:T(8,128)(2,1)S(1)} %collective-permute-done.14.refs_2_, ...), custom_call_target="tpu_custom_call" | custom-call | flops 2147483648 | bytes 4194304 | tf_op jit(solution)/shard_map/pallas_call | solution.py:51
  58.6 3.4 %shard_map.103 = (bf16[128,512]{1,0:T(8,128)(2,1)}, bf16[128,512]{1,0:T(8,128)(2,1)}) custom-call(bf16[4,256,128]{2,1,0:T(8,128)(2,1)S(1)} %get-tuple-element.41.q_ref.refs_0_, bf16[1040,128]{1,0:T(8,128)(2,1)S(1)} %get-tuple-element.47.refs_1_, bf16[1040,128]{1,0:T(8,128)(2,1)S(1)} %collective-permute-done.14.refs_2_, ...), custom_call_target="tpu_custom_call" | custom-call | flops 2147483648 | bytes 4194304 | tf_op jit(solution)/shard_map/pallas_call | solution.py:51
  (30 shorter events, 4.2 us)
Async XLA Ops:
  0.6 24.0 %copy-start.1 = (s32[256]{0:T(256)S(1)}, s32[256]{0:T(256)}, u32[]{:S(2)}) copy-start(s32[256]{0:T(256)} %param.11) | copy-start | bytes 3076
  0.6 24.0 %copy-start = (bf16[4096,512]{1,0:T(8,128)(2,1)S(1)}, bf16[4096,512]{1,0:T(8,128)(2,1)}, u32[]{:S(2)}) copy-start(bf16[4096,512]{1,0:T(8,128)(2,1)} %wq_ref.1) | copy-start | bytes 12582916
  0.7 11.9 %collective-permute-start.1 = (bf16[128,512]{1,0:T(8,128)(2,1)}, bf16[128,512]{1,0:T(8,128)(2,1)S(1)}, u32[]{:S(2)}, u32[]{:S(2)}) collective-permute-start(bf16[128,512]{1,0:T(8,128)(2,1)} %refs_0_.1), channel_id=1, source_target_pairs={{0,2},{1,3},{2,0},{3,1},{4,6},{5,7},{6,4},{7,5},{8,10},{9,11},{10,... | collective-permute-start | bytes 393224 | tf_op jit(solution)/shard_map/ppermute | solution.py:394
  4.0 14.9 %collective-permute-start.3 = (bf16[128,512]{1,0:T(8,128)(2,1)}, bf16[128,512]{1,0:T(8,128)(2,1)S(1)}, u32[]{:S(2)}, u32[]{:S(2)}) collective-permute-start(bf16[128,512]{1,0:T(8,128)(2,1)} %refs_0_.1), channel_id=1, source_target_pairs={{0,4},{1,5},{2,6},{3,7},{4,0},{5,1},{6,2},{7,3},{8,12},{9,13},{10,... | collective-permute-start | bytes 393224 | tf_op jit(solution)/shard_map/ppermute | solution.py:394
  9.4 11.3 %collective-permute-start.5 = (bf16[128,512]{1,0:T(8,128)(2,1)}, bf16[128,512]{1,0:T(8,128)(2,1)S(1)}, u32[]{:S(2)}, u32[]{:S(2)}) collective-permute-start(bf16[128,512]{1,0:T(8,128)(2,1)} %refs_0_.1), channel_id=1, source_target_pairs={{0,6},{1,7},{2,4},{3,5},{4,2},{5,3},{6,0},{7,1},{8,14},{9,15},{10,... | collective-permute-start | bytes 393224 | tf_op jit(solution)/shard_map/ppermute | solution.py:394
  12.5 8.2 %collective-permute-start = (bf16[128,512]{1,0:T(8,128)(2,1)S(1)}, bf16[128,512]{1,0:T(8,128)(2,1)S(1)}, u32[]{:S(2)}, u32[]{:S(2)}) collective-permute-start(bf16[128,512]{1,0:T(8,128)(2,1)S(1)} %get-tuple-element.33.refs_0_), channel_id=1, source_target_pairs={{0,1},{1,0},{2,3},{3,2},{4,5},{5,4},{6,7},{7,6},{8,9},{9,8},{10,11... | collective-permute-start | bytes 393224 | tf_op jit(solution)/shard_map/ppermute | solution.py:418
  12.6 8.1 %collective-permute-start.2 = (bf16[128,512]{1,0:T(8,128)(2,1)S(1)}, bf16[128,512]{1,0:T(8,128)(2,1)S(1)}, u32[]{:S(2)}, u32[]{:S(2)}) collective-permute-start(bf16[128,512]{1,0:T(8,128)(2,1)S(1)} %collective-permute-done.1.refs_2_), channel_id=1, source_target_pairs={{0,1},{1,0},{2,3},{3,2},{4,5},{5,4},{6,7},{7,6},{8,9},{9,8},{10,11... | collective-permute-start | bytes 393224 | tf_op jit(solution)/shard_map/ppermute | solution.py:418
  18.9 1.8 %collective-permute-start.4 = (bf16[128,512]{1,0:T(8,128)(2,1)S(1)}, bf16[128,512]{1,0:T(8,128)(2,1)S(1)}, u32[]{:S(2)}, u32[]{:S(2)}) collective-permute-start(bf16[128,512]{1,0:T(8,128)(2,1)S(1)} %collective-permute-done.3.refs_4_), channel_id=1, source_target_pairs={{0,1},{1,0},{2,3},{3,2},{4,5},{5,4},{6,7},{7,6},{8,9},{9,8},{10,11... | collective-permute-start | bytes 393224 | tf_op jit(solution)/shard_map/ppermute | solution.py:418
  20.7 1.3 %collective-permute-start.6 = (bf16[128,512]{1,0:T(8,128)(2,1)S(1)}, bf16[128,512]{1,0:T(8,128)(2,1)S(1)}, u32[]{:S(2)}, u32[]{:S(2)}) collective-permute-start(bf16[128,512]{1,0:T(8,128)(2,1)S(1)} %collective-permute-done.5.refs_6_), channel_id=1, source_target_pairs={{0,1},{1,0},{2,3},{3,2},{4,5},{5,4},{6,7},{7,6},{8,9},{9,8},{10,11... | collective-permute-start | bytes 393224 | tf_op jit(solution)/shard_map/ppermute | solution.py:418
  22.9 4.4 %collective-permute-start.7 = (bf16[144,256]{1,0:T(8,128)(2,1)S(1)}, bf16[144,256]{1,0:T(8,128)(2,1)S(1)}, u32[]{:S(2)}, u32[]{:S(2)}) collective-permute-start(bf16[144,256]{1,0:T(8,128)(2,1)S(1)} %get-tuple-element.42.own_ref.kv_ref), channel_id=1, source_target_pairs={{0,8},{8,0},{16,24},{24,16},{32,40},{40,32},{48,56},{56,48},{64,72... | collective-permute-start | bytes 221192 | tf_op jit(solution)/shard_map/ppermute | solution.py:429
  27.4 6.5 %collective-permute-start.11 = (bf16[256,128]{1,0:T(8,128)(2,1)S(1)}, bf16[256,128]{1,0:T(8,128)(2,1)S(1)}, u32[]{:S(2)}, u32[]{:S(2)}) collective-permute-start(bf16[256,128]{1,0:T(8,128)(2,1)S(1)} %get-tuple-element.46.refs_4_), channel_id=1, source_target_pairs={{0,64},{8,72},{16,80},{24,88},{32,96},{40,104},{48,112},{56,120},{... | collective-permute-start | bytes 196616 | tf_op jit(solution)/shard_map/ppermute | solution.py:450
  28.2 11.2 %collective-permute-start.10 = (bf16[272,128]{1,0:T(8,128)(2,1)S(1)}, bf16[272,128]{1,0:T(8,128)(2,1)S(1)}, u32[]{:S(2)}, u32[]{:S(2)}) collective-permute-start(bf16[272,128]{1,0:T(8,128)(2,1)S(1)} %get-tuple-element.45.refs_0_), channel_id=1, source_target_pairs={{0,48},{8,56},{16,32},{24,40},{32,16},{40,24},{48,0},{56,8},{64,11... | collective-permute-start | bytes 208904 | tf_op jit(solution)/shard_map/ppermute | solution.py:449
  30.9 8.4 %collective-permute-start.8 = (bf16[272,128]{1,0:T(8,128)(2,1)S(1)}, bf16[272,128]{1,0:T(8,128)(2,1)S(1)}, u32[]{:S(2)}, u32[]{:S(2)}) collective-permute-start(bf16[272,128]{1,0:T(8,128)(2,1)S(1)} %get-tuple-element.45.refs_0_), channel_id=1, source_target_pairs={{0,16},{8,24},{16,0},{24,8},{32,48},{40,56},{48,32},{56,40},{64,80... | collective-permute-start | bytes 208904 | tf_op jit(solution)/shard_map/ppermute | solution.py:449
  31.2 8.2 %collective-permute-start.9 = (bf16[272,128]{1,0:T(8,128)(2,1)S(1)}, bf16[272,128]{1,0:T(8,128)(2,1)S(1)}, u32[]{:S(2)}, u32[]{:S(2)}) collective-permute-start(bf16[272,128]{1,0:T(8,128)(2,1)S(1)} %get-tuple-element.45.refs_0_), channel_id=1, source_target_pairs={{0,32},{8,40},{16,48},{24,56},{32,0},{40,8},{48,16},{56,24},{64,96... | collective-permute-start | bytes 208904 | tf_op jit(solution)/shard_map/ppermute | solution.py:449
  32.9 5.8 %collective-permute-start.12 = (bf16[256,128]{1,0:T(8,128)(2,1)S(1)}, bf16[256,128]{1,0:T(8,128)(2,1)S(1)}, u32[]{:S(2)}, u32[]{:S(2)}) collective-permute-start(bf16[256,128]{1,0:T(8,128)(2,1)S(1)} %get-tuple-element.46.refs_4_), channel_id=1, source_target_pairs={{0,128},{8,136},{16,144},{24,152},{32,160},{40,168},{48,176},{56,1... | collective-permute-start | bytes 196616 | tf_op jit(solution)/shard_map/ppermute | solution.py:450
  33.8 5.5 %collective-permute-start.13 = (bf16[256,128]{1,0:T(8,128)(2,1)S(1)}, bf16[256,128]{1,0:T(8,128)(2,1)S(1)}, u32[]{:S(2)}, u32[]{:S(2)}) collective-permute-start(bf16[256,128]{1,0:T(8,128)(2,1)S(1)} %get-tuple-element.46.refs_4_), channel_id=1, source_target_pairs={{0,192},{8,200},{16,208},{24,216},{32,224},{40,232},{48,240},{56,2... | collective-permute-start | bytes 196616 | tf_op jit(solution)/shard_map/ppermute | solution.py:450
  39.4 10.1 %collective-permute-start.14 = (bf16[1040,128]{1,0:T(8,128)(2,1)S(1)}, bf16[1040,128]{1,0:T(8,128)(2,1)S(1)}, u32[]{:S(2)}, u32[]{:S(2)}) collective-permute-start(bf16[1040,128]{1,0:T(8,128)(2,1)S(1)} %get-tuple-element.47.refs_1_), channel_id=1, source_target_pairs={{0,64},{8,72},{16,80},{24,88},{32,96},{40,104},{48,112},{56,120},{... | collective-permute-start | bytes 798728 | tf_op jit(solution)/shard_map/ppermute | solution.py:457
  40.1 7.5 %collective-permute-start.17 = (bf16[1024,128]{1,0:T(8,128)(2,1)S(1)}, bf16[1024,128]{1,0:T(8,128)(2,1)S(1)}, u32[]{:S(2)}, u32[]{:S(2)}) collective-permute-start(bf16[1024,128]{1,0:T(8,128)(2,1)S(1)} %get-tuple-element.48.refs_3_.refs_4_.refs_5_), channel_id=1, source_target_pairs={{0,16},{8,24},{16,0},{24,8},{32,48},{40,56},{48,32},{56,40},{64,80... | collective-permute-start | bytes 786440 | tf_op jit(solution)/shard_map/ppermute | solution.py:458
  40.4 15.6 %collective-permute-start.16 = (bf16[1040,128]{1,0:T(8,128)(2,1)S(1)}, bf16[1040,128]{1,0:T(8,128)(2,1)S(1)}, u32[]{:S(2)}, u32[]{:S(2)}) collective-permute-start(bf16[1040,128]{1,0:T(8,128)(2,1)S(1)} %get-tuple-element.47.refs_1_), channel_id=1, source_target_pairs={{0,192},{8,200},{16,208},{24,216},{32,224},{40,232},{48,240},{56,2... | collective-permute-start | bytes 798728 | tf_op jit(solution)/shard_map/ppermute | solution.py:457
  42.9 13.1 %collective-permute-start.19 = (bf16[1024,128]{1,0:T(8,128)(2,1)S(1)}, bf16[1024,128]{1,0:T(8,128)(2,1)S(1)}, u32[]{:S(2)}, u32[]{:S(2)}) collective-permute-start(bf16[1024,128]{1,0:T(8,128)(2,1)S(1)} %get-tuple-element.48.refs_3_.refs_4_.refs_5_), channel_id=1, source_target_pairs={{0,48},{8,56},{16,32},{24,40},{32,16},{40,24},{48,0},{56,8},{64,11... | collective-permute-start | bytes 786440 | tf_op jit(solution)/shard_map/ppermute | solution.py:458
  46.3 12.3 %collective-permute-start.15 = (bf16[1040,128]{1,0:T(8,128)(2,1)S(1)}, bf16[1040,128]{1,0:T(8,128)(2,1)S(1)}, u32[]{:S(2)}, u32[]{:S(2)}) collective-permute-start(bf16[1040,128]{1,0:T(8,128)(2,1)S(1)} %get-tuple-element.47.refs_1_), channel_id=1, source_target_pairs={{0,128},{8,136},{16,144},{24,152},{32,160},{40,168},{48,176},{56,1... | collective-permute-start | bytes 798728 | tf_op jit(solution)/shard_map/ppermute | solution.py:457
  47.6 11.0 %collective-permute-start.18 = (bf16[1024,128]{1,0:T(8,128)(2,1)S(1)}, bf16[1024,128]{1,0:T(8,128)(2,1)S(1)}, u32[]{:S(2)}, u32[]{:S(2)}) collective-permute-start(bf16[1024,128]{1,0:T(8,128)(2,1)S(1)} %get-tuple-element.48.refs_3_.refs_4_.refs_5_), channel_id=1, source_target_pairs={{0,32},{8,40},{16,48},{24,56},{32,0},{40,8},{48,16},{56,24},{64,96... | collective-permute-start | bytes 786440 | tf_op jit(solution)/shard_map/ppermute | solution.py:458

commit v16 on v14

--- a/solution.py
+++ b/solution.py
@@ -46,8 +46,8 @@
     return lax.dot_general(a, b, (((1,), (1,)), ((), ())), preferred_element_type=F32)
 
 
-def call(kernel, outs, args, cost, scratch=(), space=pltpu.VMEM):
-    spec = pl.BlockSpec(memory_space=pltpu.VMEM)
+def call(kernel, outs, args, cost, scratch=(), space=pltpu.VMEM, out_space=pltpu.VMEM):
+    spec = pl.BlockSpec(memory_space=out_space)
     return pl.pallas_call(
         kernel,
         out_shape=[jax.ShapeDtypeStruct(s, t) for s, t in outs],
@@ -378,16 +378,23 @@
     q_ref, k_refs, v_ref = refs[0], refs[1:5], refs[5]
     state_in = refs[6:9]
     clean_ref, noisy_ref = refs[9:11]
-    state = refs[11:]
+    state = refs[11:14]
     piece = spots_piece(place(), dict(enumerate(k_refs)), {2: v_ref}, [(dy, 2) for dy in range(4)])
+
+    stage_ref, sems = refs[-2:]
+    copies = []
 
     def finish(h, accum, total):
         lanes = slice(h * HEAD, (h + 1) * HEAD)
-        result = (accum / total).astype(BF16)
-        clean_ref[:, lanes] = result[:ROWS]
-        noisy_ref[:, lanes] = result[ROWS:]
+        stage_ref[h] = (accum / total).astype(BF16)
+        for i, ref in enumerate((clean_ref, noisy_ref)):
+            source = stage_ref.at[h, i * ROWS : (i + 1) * ROWS]
+            copies.append(pltpu.make_async_copy(source, ref.at[:, lanes], sems.at[2 * h + i]))
+            copies[-1].start()
 
     pipeline(q_ref, [piece], state_in, state, finish)
+    for copy in copies:
+        copy.wait()
 
 
 def shards(hidden, block_ids, decode_order, step_cut, mask_embed, q_weight, k_weight, v_weight):
@@ -484,7 +491,9 @@
             [((ROWS, GROUP * HEAD), BF16)] * 2,
             [q, *all_k, all_v[2], *third],
             (1 << 31, 4 << 20),
-            [pltpu.VMEM((GROUP, 2 * ROWS, HEAD), F32)] * 3,
+            [pltpu.VMEM((GROUP, 2 * ROWS, HEAD), F32)] * 3
+            + [pltpu.VMEM((GROUP, 2 * ROWS, HEAD), BF16), pltpu.SemaphoreType.DMA((2 * GROUP,))],
+            out_space=pl.ANY,
         )
     )
 

time: 62.6 us -> 62.8 us (level)
  no operation moved by 1% of the time
where the time goes in v16:
time: 62.8 us; the launch traced here: 62.5 us
  starting transfers between devices  29.8 us (47%)
  waiting for transfers between devices  17.8 us (28%)
  Pallas kernels  12.6 us (20%)
  local copies, waits for them, and re-layouts  1.32 us (2%)
  between operations  0.93 us (1%)
    pallas_call x10, Pallas kernels, call(): pl.pallas_call(kernel, out_shape=[jax.ShapeDtypeStruct(s, t) for s, t in...  12.6 us
    ppermute x3, starting transfers between devices, shards(): lax.ppermute(hidden, 'kv', kv_pairs(d, 0))  8.75 us
    ppermute x3, waiting for transfers between devices, shards(): lax.ppermute(hidden, 'kv', kv_pairs(d, 0))  7.63 us
    ppermute x3, waiting for transfers between devices, shards(): lax.ppermute(vs, 'ctx', ctx_pairs(0, d, 0))  5.11 us
    ppermute x3, starting transfers between devices, shards(): vs = [lax.ppermute(v, 'ctx', ctx_pairs(d, 0, 0)) for d in (1, 2, 3)]  4.79 us
    ppermute x3, starting transfers between devices, shards(): lax.ppermute(vs, 'ctx', ctx_pairs(0, d, 0))  4.71 us
    ppermute x3, starting transfers between devices, shards(): ks = [lax.ppermute(k, 'ctx', ctx_pairs(0, d, 0)) for d in (1, 2, 3)]  4.7 us
    ppermute x3, starting transfers between devices, shards(): lax.ppermute(ks, 'ctx', ctx_pairs(d, 0, 0))  4.51 us
  transfers between devices with their start and end apart: 20, of which 7 were waited for; matrix products, arithmetic and copies ran while one was open for 2% of the time, Pallas kernels for 15%

profile of v16, /device:TPU:24, one launch (start us, length us, event | category | flops | bytes accessed | tf_op | source)
XLA Modules:
  0.0 62.5 jit_solution(7356689457897515499)
XLA Ops:
  0.7 3.4 %collective-permute-start.1 = (bf16[128,512]{1,0:T(8,128)(2,1)}, bf16[128,512]{1,0:T(8,128)(2,1)S(1)}, u32[]{:S(2)}, u32[]{:S(2)}) collective-permute-start(bf16[128,512]{1,0:T(8,128)(2,1)} %refs_0_.1), channel_id=1, source_target_pairs={{0,2},{1,3},{2,0},{3,1},{4,6},{5,7},{6,4},{7,5},{8,10},{9,11},{10,... | collective-permute-start | bytes 393224 | tf_op jit(solution)/shard_map/ppermute | solution.py:404
  4.0 5.4 %collective-permute-start.3 = (bf16[128,512]{1,0:T(8,128)(2,1)}, bf16[128,512]{1,0:T(8,128)(2,1)S(1)}, u32[]{:S(2)}, u32[]{:S(2)}) collective-permute-start(bf16[128,512]{1,0:T(8,128)(2,1)} %refs_0_.1), channel_id=1, source_target_pairs={{0,4},{1,5},{2,6},{3,7},{4,0},{5,1},{6,2},{7,3},{8,12},{9,13},{10,... | collective-permute-start | bytes 393224 | tf_op jit(solution)/shard_map/ppermute | solution.py:404
  9.4 1.3 %reshape.18.refs_5_ = bf16[1,4096]{1,0:T(2,128)(2,1)} reshape(bf16[4096]{0:T(1024)(128)(2,1)} %param.12) | data formatting | bytes 16384 | tf_op jit(solution)/shard_map/reshape | solution.py:415
  10.7 1.7 %shard_map.95 = (bf16[128,512]{1,0:T(8,128)(2,1)S(1)}, bf16[4096,128]{1,0:T(8,128)(2,1)S(1)}, bf16[4096,128]{1,0:T(8,128)(2,1)S(1)}, bf16[16,128]{1,0:T(8,128)(2,1)S(1)}, bf16[16,4096]{1,0:T(8,128)(2,1)S(1)}) custom-call(bf16[128,512]{1,0:T(8,128)(2,1)} %refs_0_.1, bf16[4096,128]{1,0:T(8,128)(2,1)} %refs_1_.1, bf16[4096,128]{1,0:T(8,128)(2,1)} %refs_2_.1, ...), custom_call_target="tpu_custom_call" | custom-call | flops 1048576 | bytes 4194304 | tf_op jit(solution)/shard_map/pallas_call | solution.py:51
  13.1 5.9 %collective-permute-done.3.refs_4_ = bf16[128,512]{1,0:T(8,128)(2,1)S(1)} collective-permute-done((bf16[128,512]{1,0:T(8,128)(2,1)}, bf16[128,512]{1,0:T(8,128)(2,1)S(1)}, u32[]{:S(2)}, u32[]{:S(2)}) %collective-permute-start.3) | collective-permute-done | bytes 131104 | tf_op jit(solution)/shard_map/ppermute | solution.py:404
  18.9 1.8 %collective-permute-done.5.refs_6_ = bf16[128,512]{1,0:T(8,128)(2,1)S(1)} collective-permute-done((bf16[128,512]{1,0:T(8,128)(2,1)}, bf16[128,512]{1,0:T(8,128)(2,1)S(1)}, u32[]{:S(2)}, u32[]{:S(2)}) %collective-permute-start.5) | collective-permute-done | bytes 131104 | tf_op jit(solution)/shard_map/ppermute | solution.py:404
  20.7 1.3 %collective-permute-done.6.refs_7_ = bf16[128,512]{1,0:T(8,128)(2,1)S(1)} collective-permute-done((bf16[128,512]{1,0:T(8,128)(2,1)S(1)}, bf16[128,512]{1,0:T(8,128)(2,1)S(1)}, u32[]{:S(2)}, u32[]{:S(2)}) %collective-permute-start.6) | collective-permute-done | bytes 131104 | tf_op jit(solution)/shard_map/ppermute | solution.py:428
  22.9 1.8 %collective-permute-start.7 = (bf16[144,256]{1,0:T(8,128)(2,1)S(1)}, bf16[144,256]{1,0:T(8,128)(2,1)S(1)}, u32[]{:S(2)}, u32[]{:S(2)}) collective-permute-start(bf16[144,256]{1,0:T(8,128)(2,1)S(1)} %get-tuple-element.45.own_ref.kv_ref), channel_id=1, source_target_pairs={{0,8},{8,0},{16,24},{24,16},{32,40},{40,32},{48,56},{56,48},{64,72... | collective-permute-start | bytes 221192 | tf_op jit(solution)/shard_map/ppermute | solution.py:439
  24.7 1.4 %shard_map.97 = (bf16[4,256,128]{2,1,0:T(8,128)(2,1)S(1)}, f32[128,128]{1,0:T(8,128)S(1)}, f32[128,128]{1,0:T(8,128)S(1)}) custom-call(bf16[144,4096]{1,0:T(8,128)(2,1)S(1)} %get-tuple-element.43.x_ref, bf16[4096,512]{1,0:T(8,128)(2,1)S(1)} %copy-done, bf16[16,128]{1,0:T(8,128)(2,1)S(1)} %get-tuple-element.42.refs_11_.code_ref.refs_10_, s32[1,256]{1,0:T(1,128)S(1)} %bitcast.3), custom_call_target="tpu_custom_call" | custom-call | flops 1073741824 | bytes 5242880 | tf_op jit(solution)/shard_map/pallas_call | solution.py:51
  26.1 1.2 %collective-permute-done.7.other_ref = bf16[144,256]{1,0:T(8,128)(2,1)S(1)} collective-permute-done((bf16[144,256]{1,0:T(8,128)(2,1)S(1)}, bf16[144,256]{1,0:T(8,128)(2,1)S(1)}, u32[]{:S(2)}, u32[]{:S(2)}) %collective-permute-start.7) | collective-permute-done | bytes 73760 | tf_op jit(solution)/shard_map/ppermute | solution.py:439
  28.2 2.8 %collective-permute-start.10 = (bf16[272,128]{1,0:T(8,128)(2,1)S(1)}, bf16[272,128]{1,0:T(8,128)(2,1)S(1)}, u32[]{:S(2)}, u32[]{:S(2)}) collective-permute-start(bf16[272,128]{1,0:T(8,128)(2,1)S(1)} %get-tuple-element.48.refs_0_), channel_id=1, source_target_pairs={{0,48},{8,56},{16,32},{24,40},{32,16},{40,24},{48,0},{56,8},{64,11... | collective-permute-start | bytes 208904 | tf_op jit(solution)/shard_map/ppermute | solution.py:459
  31.2 1.7 %collective-permute-start.9 = (bf16[272,128]{1,0:T(8,128)(2,1)S(1)}, bf16[272,128]{1,0:T(8,128)(2,1)S(1)}, u32[]{:S(2)}, u32[]{:S(2)}) collective-permute-start(bf16[272,128]{1,0:T(8,128)(2,1)S(1)} %get-tuple-element.48.refs_0_), channel_id=1, source_target_pairs={{0,32},{8,40},{16,48},{24,56},{32,0},{40,8},{48,16},{56,24},{64,96... | collective-permute-start | bytes 208904 | tf_op jit(solution)/shard_map/ppermute | solution.py:459
  32.9 0.9 %collective-permute-start.12 = (bf16[256,128]{1,0:T(8,128)(2,1)S(1)}, bf16[256,128]{1,0:T(8,128)(2,1)S(1)}, u32[]{:S(2)}, u32[]{:S(2)}) collective-permute-start(bf16[256,128]{1,0:T(8,128)(2,1)S(1)} %get-tuple-element.49.refs_4_), channel_id=1, source_target_pairs={{0,128},{8,136},{16,144},{24,152},{32,160},{40,168},{48,176},{56,1... | collective-permute-start | bytes 196616 | tf_op jit(solution)/shard_map/ppermute | solution.py:460
  33.8 3.0 %collective-permute-start.13 = (bf16[256,128]{1,0:T(8,128)(2,1)S(1)}, bf16[256,128]{1,0:T(8,128)(2,1)S(1)}, u32[]{:S(2)}, u32[]{:S(2)}) collective-permute-start(bf16[256,128]{1,0:T(8,128)(2,1)S(1)} %get-tuple-element.49.refs_4_), channel_id=1, source_target_pairs={{0,192},{8,200},{16,208},{24,216},{32,224},{40,232},{48,240},{56,2... | collective-permute-start | bytes 196616 | tf_op jit(solution)/shard_map/ppermute | solution.py:460
  36.8 1.8 %collective-permute-done.12.refs_6_ = bf16[256,128]{1,0:T(8,128)(2,1)S(1)} collective-permute-done((bf16[256,128]{1,0:T(8,128)(2,1)S(1)}, bf16[256,128]{1,0:T(8,128)(2,1)S(1)}, u32[]{:S(2)}, u32[]{:S(2)}) %collective-permute-start.12) | collective-permute-done | bytes 65568 | tf_op jit(solution)/shard_map/ppermute | solution.py:460
  40.4 2.5 %collective-permute-start.16 = (bf16[1040,128]{1,0:T(8,128)(2,1)S(1)}, bf16[1040,128]{1,0:T(8,128)(2,1)S(1)}, u32[]{:S(2)}, u32[]{:S(2)}) collective-permute-start(bf16[1040,128]{1,0:T(8,128)(2,1)S(1)} %get-tuple-element.50.refs_1_), channel_id=1, source_target_pairs={{0,192},{8,200},{16,208},{24,216},{32,224},{40,232},{48,240},{56,2... | collective-permute-start | bytes 798728 | tf_op jit(solution)/shard_map/ppermute | solution.py:467
  42.9 2.6 %collective-permute-start.19 = (bf16[1024,128]{1,0:T(8,128)(2,1)S(1)}, bf16[1024,128]{1,0:T(8,128)(2,1)S(1)}, u32[]{:S(2)}, u32[]{:S(2)}) collective-permute-start(bf16[1024,128]{1,0:T(8,128)(2,1)S(1)} %get-tuple-element.51.refs_3_.refs_4_.refs_2_), channel_id=1, source_target_pairs={{0,48},{8,56},{16,32},{24,40},{32,16},{40,24},{48,0},{56,8},{64,11... | collective-permute-start | bytes 786440 | tf_op jit(solution)/shard_map/ppermute | solution.py:468
  46.3 1.4 %collective-permute-start.15 = (bf16[1040,128]{1,0:T(8,128)(2,1)S(1)}, bf16[1040,128]{1,0:T(8,128)(2,1)S(1)}, u32[]{:S(2)}, u32[]{:S(2)}) collective-permute-start(bf16[1040,128]{1,0:T(8,128)(2,1)S(1)} %get-tuple-element.50.refs_1_), channel_id=1, source_target_pairs={{0,128},{8,136},{16,144},{24,152},{32,160},{40,168},{48,176},{56,1... | collective-permute-start | bytes 798728 | tf_op jit(solution)/shard_map/ppermute | solution.py:467
  47.6 1.9 %collective-permute-start.17 = (bf16[1024,128]{1,0:T(8,128)(2,1)S(1)}, bf16[1024,128]{1,0:T(8,128)(2,1)S(1)}, u32[]{:S(2)}, u32[]{:S(2)}) collective-permute-start(bf16[1024,128]{1,0:T(8,128)(2,1)S(1)} %get-tuple-element.51.refs_3_.refs_4_.refs_2_), channel_id=1, source_target_pairs={{0,32},{8,40},{16,48},{24,56},{32,0},{40,8},{48,16},{56,24},{64,96... | collective-permute-start | bytes 786440 | tf_op jit(solution)/shard_map/ppermute | solution.py:468
  49.5 1.3 %shard_map.101 = (f32[4,256,128]{2,1,0:T(8,128)S(1)}, f32[4,256,128]{2,1,0:T(8,128)S(1)}, f32[4,256,128]{2,1,0:T(8,128)S(1)}) custom-call(bf16[4,256,128]{2,1,0:T(8,128)(2,1)S(1)} %get-tuple-element.44.q_ref.refs_0_, bf16[1040,128]{1,0:T(8,128)(2,1)S(1)} %get-tuple-element.50.refs_1_, bf16[1040,128]{1,0:T(8,128)(2,1)S(1)} %collective-permute-done.14.refs_2_, ...), custom_call_target="tpu_custom_call" | custom-call | flops 1073741824 | bytes 2097152 | tf_op jit(solution)/shard_map/pallas_call | solution.py:51
  50.8 5.1 %collective-permute-done.19.refs_6_.refs_4_ = bf16[1024,128]{1,0:T(8,128)(2,1)S(1)} collective-permute-done((bf16[1024,128]{1,0:T(8,128)(2,1)S(1)}, bf16[1024,128]{1,0:T(8,128)(2,1)S(1)}, u32[]{:S(2)}, u32[]{:S(2)}) %collective-permute-start.19) | collective-permute-done | bytes 262176 | tf_op jit(solution)/shard_map/ppermute | solution.py:468
  55.9 2.7 %shard_map.102 = (f32[4,256,128]{2,1,0:T(8,128)S(1)}, f32[4,256,128]{2,1,0:T(8,128)S(1)}, f32[4,256,128]{2,1,0:T(8,128)S(1)}) custom-call(bf16[4,256,128]{2,1,0:T(8,128)(2,1)S(1)} %get-tuple-element.44.q_ref.refs_0_, bf16[1040,128]{1,0:T(8,128)(2,1)S(1)} %get-tuple-element.50.refs_1_, bf16[1040,128]{1,0:T(8,128)(2,1)S(1)} %collective-permute-done.14.refs_2_, ...), custom_call_target="tpu_custom_call" | custom-call | flops 2147483648 | bytes 4194304 | tf_op jit(solution)/shard_map/pallas_call | solution.py:51
  58.6 1.4 %shard_map.103 = (f32[4,256,128]{2,1,0:T(8,128)S(1)}, f32[4,256,128]{2,1,0:T(8,128)S(1)}, f32[4,256,128]{2,1,0:T(8,128)S(1)}) custom-call(bf16[4,256,128]{2,1,0:T(8,128)(2,1)S(1)} %get-tuple-element.44.q_ref.refs_0_, bf16[1040,128]{1,0:T(8,128)(2,1)S(1)} %collective-permute-done.15.refs_1_.refs_3_, ...), custom_call_target="tpu_custom_call" | custom-call | flops 1073741824 | bytes 2097152 | tf_op jit(solution)/shard_map/pallas_call | solution.py:51
  60.0 2.4 %shard_map.104 = (bf16[128,512]{1,0:T(8,128)(2,1)}, bf16[128,512]{1,0:T(8,128)(2,1)}) custom-call(bf16[4,256,128]{2,1,0:T(8,128)(2,1)S(1)} %get-tuple-element.44.q_ref.refs_0_, bf16[1040,128]{1,0:T(8,128)(2,1)S(1)} %get-tuple-element.50.refs_1_, bf16[1040,128]{1,0:T(8,128)(2,1)S(1)} %collective-permute-done.14.refs_2_, ...), custom_call_target="tpu_custom_call" | custom-call | flops 2147483648 | bytes 4194304 | tf_op jit(solution)/shard_map/pallas_call | solution.py:51
  (31 shorter events, 5.1 us)
Async XLA Ops:
  0.6 24.0 %copy-start.1 = (s32[256]{0:T(256)S(1)}, s32[256]{0:T(256)}, u32[]{:S(2)}) copy-start(s32[256]{0:T(256)} %param.11) | copy-start | bytes 3076
  0.6 24.0 %copy-start = (bf16[4096,512]{1,0:T(8,128)(2,1)S(1)}, bf16[4096,512]{1,0:T(8,128)(2,1)}, u32[]{:S(2)}) copy-start(bf16[4096,512]{1,0:T(8,128)(2,1)} %wq_ref.1) | copy-start | bytes 12582916
  0.7 11.9 %collective-permute-start.1 = (bf16[128,512]{1,0:T(8,128)(2,1)}, bf16[128,512]{1,0:T(8,128)(2,1)S(1)}, u32[]{:S(2)}, u32[]{:S(2)}) collective-permute-start(bf16[128,512]{1,0:T(8,128)(2,1)} %refs_0_.1), channel_id=1, source_target_pairs={{0,2},{1,3},{2,0},{3,1},{4,6},{5,7},{6,4},{7,5},{8,10},{9,11},{10,... | collective-permute-start | bytes 393224 | tf_op jit(solution)/shard_map/ppermute | solution.py:404
  4.0 14.9 %collective-permute-start.3 = (bf16[128,512]{1,0:T(8,128)(2,1)}, bf16[128,512]{1,0:T(8,128)(2,1)S(1)}, u32[]{:S(2)}, u32[]{:S(2)}) collective-permute-start(bf16[128,512]{1,0:T(8,128)(2,1)} %refs_0_.1), channel_id=1, source_target_pairs={{0,4},{1,5},{2,6},{3,7},{4,0},{5,1},{6,2},{7,3},{8,12},{9,13},{10,... | collective-permute-start | bytes 393224 | tf_op jit(solution)/shard_map/ppermute | solution.py:404
  9.4 11.3 %collective-permute-start.5 = (bf16[128,512]{1,0:T(8,128)(2,1)}, bf16[128,512]{1,0:T(8,128)(2,1)S(1)}, u32[]{:S(2)}, u32[]{:S(2)}) collective-permute-start(bf16[128,512]{1,0:T(8,128)(2,1)} %refs_0_.1), channel_id=1, source_target_pairs={{0,6},{1,7},{2,4},{3,5},{4,2},{5,3},{6,0},{7,1},{8,14},{9,15},{10,... | collective-permute-start | bytes 393224 | tf_op jit(solution)/shard_map/ppermute | solution.py:404
  12.5 8.2 %collective-permute-start = (bf16[128,512]{1,0:T(8,128)(2,1)S(1)}, bf16[128,512]{1,0:T(8,128)(2,1)S(1)}, u32[]{:S(2)}, u32[]{:S(2)}) collective-permute-start(bf16[128,512]{1,0:T(8,128)(2,1)S(1)} %get-tuple-element.36.refs_0_), channel_id=1, source_target_pairs={{0,1},{1,0},{2,3},{3,2},{4,5},{5,4},{6,7},{7,6},{8,9},{9,8},{10,11... | collective-permute-start | bytes 393224 | tf_op jit(solution)/shard_map/ppermute | solution.py:428
  12.6 8.1 %collective-permute-start.2 = (bf16[128,512]{1,0:T(8,128)(2,1)S(1)}, bf16[128,512]{1,0:T(8,128)(2,1)S(1)}, u32[]{:S(2)}, u32[]{:S(2)}) collective-permute-start(bf16[128,512]{1,0:T(8,128)(2,1)S(1)} %collective-permute-done.1.refs_2_), channel_id=1, source_target_pairs={{0,1},{1,0},{2,3},{3,2},{4,5},{5,4},{6,7},{7,6},{8,9},{9,8},{10,11... | collective-permute-start | bytes 393224 | tf_op jit(solution)/shard_map/ppermute | solution.py:428
  18.9 1.8 %collective-permute-start.4 = (bf16[128,512]{1,0:T(8,128)(2,1)S(1)}, bf16[128,512]{1,0:T(8,128)(2,1)S(1)}, u32[]{:S(2)}, u32[]{:S(2)}) collective-permute-start(bf16[128,512]{1,0:T(8,128)(2,1)S(1)} %collective-permute-done.3.refs_4_), channel_id=1, source_target_pairs={{0,1},{1,0},{2,3},{3,2},{4,5},{5,4},{6,7},{7,6},{8,9},{9,8},{10,11... | collective-permute-start | bytes 393224 | tf_op jit(solution)/shard_map/ppermute | solution.py:428
  20.7 1.3 %collective-permute-start.6 = (bf16[128,512]{1,0:T(8,128)(2,1)S(1)}, bf16[128,512]{1,0:T(8,128)(2,1)S(1)}, u32[]{:S(2)}, u32[]{:S(2)}) collective-permute-start(bf16[128,512]{1,0:T(8,128)(2,1)S(1)} %collective-permute-done.5.refs_6_), channel_id=1, source_target_pairs={{0,1},{1,0},{2,3},{3,2},{4,5},{5,4},{6,7},{7,6},{8,9},{9,8},{10,11... | collective-permute-start | bytes 393224 | tf_op jit(solution)/shard_map/ppermute | solution.py:428
  22.9 4.4 %collective-permute-start.7 = (bf16[144,256]{1,0:T(8,128)(2,1)S(1)}, bf16[144,256]{1,0:T(8,128)(2,1)S(1)}, u32[]{:S(2)}, u32[]{:S(2)}) collective-permute-start(bf16[144,256]{1,0:T(8,128)(2,1)S(1)} %get-tuple-element.45.own_ref.kv_ref), channel_id=1, source_target_pairs={{0,8},{8,0},{16,24},{24,16},{32,40},{40,32},{48,56},{56,48},{64,72... | collective-permute-start | bytes 221192 | tf_op jit(solution)/shard_map/ppermute | solution.py:439
  27.4 6.5 %collective-permute-start.11 = (bf16[256,128]{1,0:T(8,128)(2,1)S(1)}, bf16[256,128]{1,0:T(8,128)(2,1)S(1)}, u32[]{:S(2)}, u32[]{:S(2)}) collective-permute-start(bf16[256,128]{1,0:T(8,128)(2,1)S(1)} %get-tuple-element.49.refs_4_), channel_id=1, source_target_pairs={{0,64},{8,72},{16,80},{24,88},{32,96},{40,104},{48,112},{56,120},{... | collective-permute-start | bytes 196616 | tf_op jit(solution)/shard_map/ppermute | solution.py:460
  28.2 11.2 %collective-permute-start.10 = (bf16[272,128]{1,0:T(8,128)(2,1)S(1)}, bf16[272,128]{1,0:T(8,128)(2,1)S(1)}, u32[]{:S(2)}, u32[]{:S(2)}) collective-permute-start(bf16[272,128]{1,0:T(8,128)(2,1)S(1)} %get-tuple-element.48.refs_0_), channel_id=1, source_target_pairs={{0,48},{8,56},{16,32},{24,40},{32,16},{40,24},{48,0},{56,8},{64,11... | collective-permute-start | bytes 208904 | tf_op jit(solution)/shard_map/ppermute | solution.py:459
  30.9 8.4 %collective-permute-start.8 = (bf16[272,128]{1,0:T(8,128)(2,1)S(1)}, bf16[272,128]{1,0:T(8,128)(2,1)S(1)}, u32[]{:S(2)}, u32[]{:S(2)}) collective-permute-start(bf16[272,128]{1,0:T(8,128)(2,1)S(1)} %get-tuple-element.48.refs_0_), channel_id=1, source_target_pairs={{0,16},{8,24},{16,0},{24,8},{32,48},{40,56},{48,32},{56,40},{64,80... | collective-permute-start | bytes 208904 | tf_op jit(solution)/shard_map/ppermute | solution.py:459
  31.2 8.2 %collective-permute-start.9 = (bf16[272,128]{1,0:T(8,128)(2,1)S(1)}, bf16[272,128]{1,0:T(8,128)(2,1)S(1)}, u32[]{:S(2)}, u32[]{:S(2)}) collective-permute-start(bf16[272,128]{1,0:T(8,128)(2,1)S(1)} %get-tuple-element.48.refs_0_), channel_id=1, source_target_pairs={{0,32},{8,40},{16,48},{24,56},{32,0},{40,8},{48,16},{56,24},{64,96... | collective-permute-start | bytes 208904 | tf_op jit(solution)/shard_map/ppermute | solution.py:459
  32.9 5.8 %collective-permute-start.12 = (bf16[256,128]{1,0:T(8,128)(2,1)S(1)}, bf16[256,128]{1,0:T(8,128)(2,1)S(1)}, u32[]{:S(2)}, u32[]{:S(2)}) collective-permute-start(bf16[256,128]{1,0:T(8,128)(2,1)S(1)} %get-tuple-element.49.refs_4_), channel_id=1, source_target_pairs={{0,128},{8,136},{16,144},{24,152},{32,160},{40,168},{48,176},{56,1... | collective-permute-start | bytes 196616 | tf_op jit(solution)/shard_map/ppermute | solution.py:460
  33.8 5.5 %collective-permute-start.13 = (bf16[256,128]{1,0:T(8,128)(2,1)S(1)}, bf16[256,128]{1,0:T(8,128)(2,1)S(1)}, u32[]{:S(2)}, u32[]{:S(2)}) collective-permute-start(bf16[256,128]{1,0:T(8,128)(2,1)S(1)} %get-tuple-element.49.refs_4_), channel_id=1, source_target_pairs={{0,192},{8,200},{16,208},{24,216},{32,224},{40,232},{48,240},{56,2... | collective-permute-start | bytes 196616 | tf_op jit(solution)/shard_map/ppermute | solution.py:460
  39.4 10.1 %collective-permute-start.14 = (bf16[1040,128]{1,0:T(8,128)(2,1)S(1)}, bf16[1040,128]{1,0:T(8,128)(2,1)S(1)}, u32[]{:S(2)}, u32[]{:S(2)}) collective-permute-start(bf16[1040,128]{1,0:T(8,128)(2,1)S(1)} %get-tuple-element.50.refs_1_), channel_id=1, source_target_pairs={{0,64},{8,72},{16,80},{24,88},{32,96},{40,104},{48,112},{56,120},{... | collective-permute-start | bytes 798728 | tf_op jit(solution)/shard_map/ppermute | solution.py:467
  40.1 7.5 %collective-permute-start.18 = (bf16[1024,128]{1,0:T(8,128)(2,1)S(1)}, bf16[1024,128]{1,0:T(8,128)(2,1)S(1)}, u32[]{:S(2)}, u32[]{:S(2)}) collective-permute-start(bf16[1024,128]{1,0:T(8,128)(2,1)S(1)} %get-tuple-element.51.refs_3_.refs_4_.refs_2_), channel_id=1, source_target_pairs={{0,16},{8,24},{16,0},{24,8},{32,48},{40,56},{48,32},{56,40},{64,80... | collective-permute-start | bytes 786440 | tf_op jit(solution)/shard_map/ppermute | solution.py:468
  40.4 15.6 %collective-permute-start.16 = (bf16[1040,128]{1,0:T(8,128)(2,1)S(1)}, bf16[1040,128]{1,0:T(8,128)(2,1)S(1)}, u32[]{:S(2)}, u32[]{:S(2)}) collective-permute-start(bf16[1040,128]{1,0:T(8,128)(2,1)S(1)} %get-tuple-element.50.refs_1_), channel_id=1, source_target_pairs={{0,192},{8,200},{16,208},{24,216},{32,224},{40,232},{48,240},{56,2... | collective-permute-start | bytes 798728 | tf_op jit(solution)/shard_map/ppermute | solution.py:467
  42.9 13.1 %collective-permute-start.19 = (bf16[1024,128]{1,0:T(8,128)(2,1)S(1)}, bf16[1024,128]{1,0:T(8,128)(2,1)S(1)}, u32[]{:S(2)}, u32[]{:S(2)}) collective-permute-start(bf16[1024,128]{1,0:T(8,128)(2,1)S(1)} %get-tuple-element.51.refs_3_.refs_4_.refs_2_), channel_id=1, source_target_pairs={{0,48},{8,56},{16,32},{24,40},{32,16},{40,24},{48,0},{56,8},{64,11... | collective-permute-start | bytes 786440 | tf_op jit(solution)/shard_map/ppermute | solution.py:468
  46.3 12.3 %collective-permute-start.15 = (bf16[1040,128]{1,0:T(8,128)(2,1)S(1)}, bf16[1040,128]{1,0:T(8,128)(2,1)S(1)}, u32[]{:S(2)}, u32[]{:S(2)}) collective-permute-start(bf16[1040,128]{1,0:T(8,128)(2,1)S(1)} %get-tuple-element.50.refs_1_), channel_id=1, source_target_pairs={{0,128},{8,136},{16,144},{24,152},{32,160},{40,168},{48,176},{56,1... | collective-permute-start | bytes 798728 | tf_op jit(solution)/shard_map/ppermute | solution.py:467
  47.6 12.4 %collective-permute-start.17 = (bf16[1024,128]{1,0:T(8,128)(2,1)S(1)}, bf16[1024,128]{1,0:T(8,128)(2,1)S(1)}, u32[]{:S(2)}, u32[]{:S(2)}) collective-permute-start(bf16[1024,128]{1,0:T(8,128)(2,1)S(1)} %get-tuple-element.51.refs_3_.refs_4_.refs_2_), channel_id=1, source_target_pairs={{0,32},{8,40},{16,48},{24,56},{32,0},{40,8},{48,16},{56,24},{64,96... | collective-permute-start | bytes 786440 | tf_op jit(solution)/shard_map/ppermute | solution.py:468
